TPU v7x, 32 devices: a whole 2x2x4 slice. The times are simulated.
32 devices in a mesh: dp: 2 (over x), seq: 16 (over z, y, core).
Axes of the slice: x: 2, y: 2, z: 4, core: 2. Of those that a mesh axis runs over, the one named last changes fastest.
Arguments:
- block_in: bfloat16 [12, 2048, 1024], P('dp', 'seq'), may hold values from -6 to 6
- doc_starts: int32 [12, 4], P('dp'), may hold values from 0 to 2047, as said below
- cotangent: bfloat16 [12, 2048, 1024], P('dp', 'seq'), may hold values from -6 to 6
- norm1_gain: float32 [1024], replicated, may hold values from 0.5 to 1.5
- w_query: bfloat16 [1024, 512], replicated
- w_key: bfloat16 [1024, 512], replicated
- w_value: bfloat16 [1024, 1024], replicated, may hold values from -0.1875 to 0.1875
- w_outgate: bfloat16 [1024, 1024], replicated, may hold values from -0.1875 to 0.1875
- w_rank_down: bfloat16 [1024, 16], replicated, may hold values from -0.1875 to 0.1875
- w_rank_up: bfloat16 [16, 512], replicated, may hold values from -1.5 to 1.5
- decay_bias: float32 [512], replicated, may hold values from -1 to 8
- group_gain: float32 [256], replicated, may hold values from 0.5 to 1.5
- w_output: bfloat16 [1024, 1024], replicated, may hold values from -0.375 to 0.375
- norm2_gain: float32 [1024], replicated, may hold values from 0.5 to 1.5
- w_ffgate: bfloat16 [1024, 2816], replicated, may hold values from -0.1875 to 0.1875
- w_ffup: bfloat16 [1024, 2816], replicated, may hold values from -0.1875 to 0.1875
- w_ffdown: bfloat16 [2816, 1024], replicated, may hold values from -0.15625 to 0.15625
Outputs:
- block_out: bfloat16 [12, 2048, 1024], P('dp', 'seq')
- grad_in: float32 [12, 2048, 1024], P('dp', 'seq')
- grad_norm1: float32 [1024], P(('dp', 'seq'))
- grad_query: float32 [1024, 512], P(('dp', 'seq'))
- grad_key: float32 [1024, 512], P(('dp', 'seq'))
- grad_value: float32 [1024, 1024], P(('dp', 'seq'))
- grad_outgate: float32 [1024, 1024], P(('dp', 'seq'))
- grad_rank_down: float32 [1024, 16], P(('dp', 'seq'))
- grad_rank_up: float32 [16, 512], P(None, ('dp', 'seq'))
- grad_bias: float32 [512], P(('dp', 'seq'))
- grad_group: float32 [256], P(('dp', 'seq'))
- grad_output: float32 [1024, 1024], P(('dp', 'seq'))
- grad_norm2: float32 [1024], P(('dp', 'seq'))
- grad_ffgate: float32 [1024, 2816], P(('dp', 'seq'))
- grad_ffup: float32 [1024, 2816], P(('dp', 'seq'))
- grad_ffdown: float32 [2816, 1024], P(('dp', 'seq'))
Inputs may be any that keep to these rules, and one draw needn't show every extreme that they name: `doc_starts`: each row lists 4 positions where a document begins, in no order and possibly repeated; the first entry is 0. In every block of 6 rows (the rows of one index of dp) one row, drawn from the seed, lists only 0.
All inputs are finite; a program needn't handle non-finite values.
Results may differ from a plain program's by a relative error of at most 0.025.
Values sent between devices are 32-bit elements; how exact they have to be, the bound alone decides.
No kernel may reach another device: no remote copies, remote signals or barrier semaphores. Data moves between devices by JAX's collectives and lax.ppermute only.
A program may use at most 256 MiB of HBM per device.

v0:
```python
import jax
import jax.numpy as jnp
from jax import lax
from jax.sharding import PartitionSpec as P

HEADS = 4
SPAN = 64


epsilon = 1e-06
highest = lax.Precision.HIGHEST


def prefix(x, axis, combine, identity, reverse):
    peers, position = (lax.axis_size(axis), lax.axis_index(axis))
    everything = jax.tree.map(lambda part: lax.all_gather(part, axis), x)
    start = jax.tree.map(
        lambda part, zero: jnp.broadcast_to(jnp.asarray(zero, part.dtype), part.shape), x, identity
    )

    def step(k, before):
        at = peers - 1 - k if reverse else k
        reached = at > position if reverse else at < position
        new = combine(before, jax.tree.map(lambda part: part[at], everything))
        return jax.tree.map(lambda a, b: jnp.where(reached, a, b), new, before)

    return lax.fori_loop(0, peers, step, start)


def span_step(state, block):
    queries, key_rows, value_rows, log_decay, resets = block
    length = resets.shape[0]
    cumulative = jnp.cumsum(log_decay, axis=0)
    doc_ids = jnp.cumsum(resets)
    alive = (doc_ids == 0).astype(jnp.float32)
    scaled_q = queries * jnp.exp(cumulative)
    scaled_k = key_rows * jnp.exp(-cumulative)
    scores = jnp.einsum("ihc,jhc->hij", scaled_q, scaled_k, precision=highest)
    position = jnp.arange(length)
    visible = (doc_ids[:, None] == doc_ids[None, :]) & (position[:, None] >= position[None, :])
    scores = jnp.where(visible[None], scores, 0.0)
    inner = jnp.einsum("hij,jhe->ihe", scores, value_rows, precision=highest)
    outer = jnp.einsum("ihc,hce->ihe", scaled_q * alive[:, None, None], state, precision=highest)
    head_scale = queries.shape[-1] ** (-0.5)
    last_sum = cumulative[-1]
    tail_mask = (doc_ids == doc_ids[-1]).astype(jnp.float32)
    weighted = key_rows * jnp.exp(last_sum[None] - cumulative) * tail_mask[:, None, None]
    renewed = state * (jnp.exp(last_sum) * alive[-1])[:, :, None]
    renewed = renewed + jnp.einsum("jhc,jhe->hce", weighted, value_rows, precision=highest)
    return (renewed, head_scale * (inner + outer))


def run_spans(queries, key_rows, value_rows, log_decay, resets, state):
    length = resets.shape[0]
    blocks = length // SPAN
    heads_k = (blocks, SPAN, queries.shape[1], queries.shape[2])
    heads_v = (blocks, SPAN, value_rows.shape[1], value_rows.shape[2])
    final_state, outputs = lax.scan(
        jax.checkpoint(span_step),
        state,
        (
            queries.reshape(heads_k),
            key_rows.reshape(heads_k),
            value_rows.reshape(heads_v),
            log_decay.reshape(heads_k),
            resets.reshape(blocks, SPAN),
        ),
    )
    return (outputs.reshape(length, value_rows.shape[1], value_rows.shape[2]), final_state)


def project(left, right):
    return jnp.dot(left, right, preferred_element_type=jnp.float32)


def back_project(grads, weight):
    return lax.dot_general(
        grads, weight, (((1,), (1,)), ((), ())), preferred_element_type=jnp.float32
    )


def outer_sum(left, right):
    return lax.dot_general(
        left, right, (((0,), (0,)), ((), ())), preferred_element_type=jnp.float32
    )


def chain(earlier, later):
    return (earlier[0] * later[0], later[0][..., None] * earlier[1] + later[1])


def local(
    block_in,
    doc_starts,
    cotangent,
    norm1_gain,
    w_query,
    w_key,
    w_value,
    w_outgate,
    w_rank_down,
    w_rank_up,
    decay_bias,
    group_gain,
    w_output,
    norm2_gain,
    w_ffgate,
    w_ffup,
    w_ffdown,
):
    row_count, seg_len, width = block_in.shape
    tokens = row_count * seg_len
    key_width = w_query.shape[1]
    value_width = w_value.shape[1]
    head_k = key_width // HEADS
    head_v = value_width // HEADS
    head_scale = head_k ** (-0.5)
    inputs = block_in.reshape(tokens, width).astype(jnp.float32)
    positions = lax.axis_index("seq") * seg_len + jnp.arange(seg_len)
    resets = jnp.any(doc_starts[:, :, None] == positions[None, None, :], axis=1).astype(jnp.float32)
    inv_one = lax.rsqrt(jnp.mean(inputs * inputs, axis=-1, keepdims=True) + epsilon)
    normed = (inputs * inv_one * norm1_gain).astype(jnp.bfloat16)
    queries = project(normed, w_query).astype(jnp.bfloat16)
    key_rows = project(normed, w_key).astype(jnp.bfloat16)
    value_rows = project(normed, w_value).astype(jnp.bfloat16)
    out_gate = project(normed, w_outgate)
    rank_act = project(normed, w_rank_down).astype(jnp.bfloat16)
    gate_pre = project(rank_act, w_rank_up) + decay_bias
    log_decay = jax.nn.log_sigmoid(gate_pre) / 16.0
    split_k = (row_count, seg_len, HEADS, head_k)
    split_v = (row_count, seg_len, HEADS, head_v)
    q_heads = queries.astype(jnp.float32).reshape(split_k)
    k_heads = key_rows.astype(jnp.float32).reshape(split_k)
    v_heads = value_rows.astype(jnp.float32).reshape(split_v)
    decay_heads = log_decay.reshape(split_k)
    mixer = jax.vmap(run_spans)
    empty = jnp.zeros((row_count, HEADS, head_k, head_v), jnp.float32)
    local_out, local_state = mixer(q_heads, k_heads, v_heads, decay_heads, resets, empty)
    running_sum = jnp.cumsum(decay_heads, axis=1)
    alive = (jnp.cumsum(resets, axis=1) == 0).astype(jnp.float32)
    decay_total = jnp.exp(running_sum[:, -1]) * alive[:, -1][:, None, None]
    reach = q_heads * jnp.exp(running_sum) * alive[:, :, None, None]
    carried = prefix(
        (decay_total, local_state), "seq", chain, (jnp.ones_like(decay_total), empty), False
    )
    state_in = carried[1]
    mixed = local_out + head_scale * jnp.einsum(
        "rthc,rhce->rthe", reach, state_in, precision=highest
    )
    inv_head = lax.rsqrt(jnp.mean(mixed * mixed, axis=-1, keepdims=True) + epsilon)
    flat_heads = (mixed * inv_head * group_gain).reshape(tokens, value_width)
    gate_sig = jax.nn.sigmoid(out_gate)
    gated = (flat_heads * out_gate * gate_sig).astype(jnp.bfloat16)
    middle = inputs + project(gated, w_output)
    inv_two = lax.rsqrt(jnp.mean(middle * middle, axis=-1, keepdims=True) + epsilon)
    normed2 = (middle * inv_two * norm2_gain).astype(jnp.bfloat16)
    ff_gate = project(normed2, w_ffgate)
    ff_up = project(normed2, w_ffup)
    ff_sig = jax.nn.sigmoid(ff_gate)
    hidden = (ff_gate * ff_sig * ff_up).astype(jnp.bfloat16)
    block_out = (
        (middle + project(hidden, w_ffdown)).astype(jnp.bfloat16).reshape(row_count, seg_len, width)
    )
    d_down = cotangent.reshape(tokens, width)
    grad_ffdown = outer_sum(hidden, d_down)
    d_hidden = back_project(d_down, w_ffdown)
    d_ffgate = (d_hidden * ff_up * ff_sig * (1.0 + ff_gate * (1.0 - ff_sig))).astype(jnp.bfloat16)
    d_ffup = (d_hidden * ff_gate * ff_sig).astype(jnp.bfloat16)
    grad_ffgate = outer_sum(normed2, d_ffgate)
    grad_ffup = outer_sum(normed2, d_ffup)
    d_normed2 = back_project(d_ffgate, w_ffgate) + back_project(d_ffup, w_ffup)
    grad_norm2 = jnp.sum(d_normed2 * middle * inv_two, axis=0)
    scaled_two = d_normed2 * norm2_gain
    d_middle = (
        d_down.astype(jnp.float32)
        + inv_two * scaled_two
        - middle * inv_two**3 * jnp.mean(scaled_two * middle, axis=-1, keepdims=True)
    )
    d_out = d_middle.astype(jnp.bfloat16)
    grad_output = outer_sum(gated, d_out)
    d_gated = back_project(d_out, w_output)
    d_heads = (d_gated * out_gate * gate_sig).reshape(split_v)
    d_outgate = (d_gated * flat_heads * gate_sig * (1.0 + out_gate * (1.0 - gate_sig))).astype(
        jnp.bfloat16
    )
    grad_outgate = outer_sum(normed, d_outgate)
    grad_group = jnp.sum(d_heads * mixed * inv_head, axis=(0, 1, 2))
    scaled_head = d_heads * group_gain
    d_mixed = inv_head * scaled_head - mixed * inv_head**3 * jnp.mean(
        scaled_head * mixed, axis=-1, keepdims=True
    )
    state_grad = head_scale * jnp.einsum("rthc,rthe->rhce", reach, d_mixed, precision=highest)
    returned = prefix(
        (decay_total, state_grad), "seq", chain, (jnp.ones_like(decay_total), empty), True
    )
    state_out_grad = returned[1]

    def mix_inputs(q_in, k_in, v_in, decay_in, state_start):
        return mixer(q_in, k_in, v_in, decay_in, resets, state_start)

    recomputed, pull_back = jax.vjp(mix_inputs, q_heads, k_heads, v_heads, decay_heads, state_in)
    d_q, d_k, d_v, d_decay, d_start = pull_back((d_mixed, state_out_grad))
    d_queries = d_q.reshape(tokens, key_width).astype(jnp.bfloat16)
    d_keys = d_k.reshape(tokens, key_width).astype(jnp.bfloat16)
    d_values = d_v.reshape(tokens, value_width).astype(jnp.bfloat16)
    d_gate = (d_decay.reshape(tokens, key_width) * jax.nn.sigmoid(-gate_pre) / 16.0).astype(
        jnp.bfloat16
    )
    grad_rank_up = outer_sum(rank_act, d_gate)
    grad_bias = jnp.sum(d_gate.astype(jnp.float32), axis=0)
    d_rank = back_project(d_gate, w_rank_up).astype(jnp.bfloat16)
    grad_rank_down = outer_sum(normed, d_rank)
    grad_query = outer_sum(normed, d_queries)
    grad_key = outer_sum(normed, d_keys)
    grad_value = outer_sum(normed, d_values)
    d_normed = (
        back_project(d_queries, w_query)
        + back_project(d_keys, w_key)
        + back_project(d_values, w_value)
    )
    d_normed = d_normed + back_project(d_outgate, w_outgate) + back_project(d_rank, w_rank_down)
    grad_norm1 = jnp.sum(d_normed * inputs * inv_one, axis=0)
    scaled_one = d_normed * norm1_gain
    grad_in = (
        d_middle
        + inv_one * scaled_one
        - inputs * inv_one**3 * jnp.mean(scaled_one * inputs, axis=-1, keepdims=True)
    )
    grad_in = grad_in.reshape(row_count, seg_len, width)
    partial_grads = (
        grad_norm1,
        grad_query,
        grad_key,
        grad_value,
        grad_outgate,
        grad_rank_down,
        grad_rank_up,
        grad_bias,
        grad_group,
        grad_output,
        grad_norm2,
        grad_ffgate,
        grad_ffup,
        grad_ffdown,
    )
    summed = (
        lax.psum_scatter(partial_grads[0], ("dp", "seq"), scatter_dimension=0, tiled=True),
        lax.psum_scatter(partial_grads[1], ("dp", "seq"), scatter_dimension=0, tiled=True),
        lax.psum_scatter(partial_grads[2], ("dp", "seq"), scatter_dimension=0, tiled=True),
        lax.psum_scatter(partial_grads[3], ("dp", "seq"), scatter_dimension=0, tiled=True),
        lax.psum_scatter(partial_grads[4], ("dp", "seq"), scatter_dimension=0, tiled=True),
        lax.psum_scatter(partial_grads[5], ("dp", "seq"), scatter_dimension=0, tiled=True),
        lax.psum_scatter(partial_grads[6], ("dp", "seq"), scatter_dimension=1, tiled=True),
        lax.psum_scatter(partial_grads[7], ("dp", "seq"), scatter_dimension=0, tiled=True),
        lax.psum_scatter(partial_grads[8], ("dp", "seq"), scatter_dimension=0, tiled=True),
        lax.psum_scatter(partial_grads[9], ("dp", "seq"), scatter_dimension=0, tiled=True),
        lax.psum_scatter(partial_grads[10], ("dp", "seq"), scatter_dimension=0, tiled=True),
        lax.psum_scatter(partial_grads[11], ("dp", "seq"), scatter_dimension=0, tiled=True),
        lax.psum_scatter(partial_grads[12], ("dp", "seq"), scatter_dimension=0, tiled=True),
        lax.psum_scatter(partial_grads[13], ("dp", "seq"), scatter_dimension=0, tiled=True),
    )
    return (
        block_out,
        grad_in,
        summed[0],
        summed[1],
        summed[2],
        summed[3],
        summed[4],
        summed[5],
        summed[6],
        summed[7],
        summed[8],
        summed[9],
        summed[10],
        summed[11],
        summed[12],
        summed[13],
    )


def solution(mesh):
    placed = (
        P("dp", "seq", None),
        P("dp", None),
        P("dp", "seq", None),
        P(),
        P(),
        P(),
        P(),
        P(),
        P(),
        P(),
        P(),
        P(),
        P(),
        P(),
        P(),
        P(),
        P(),
    )
    return jax.shard_map(
        local,
        mesh=mesh,
        in_specs=placed,
        out_specs=(
            P("dp", "seq", None),
            P("dp", "seq", None),
            P(("dp", "seq")),
            P(("dp", "seq"), None),
            P(("dp", "seq"), None),
            P(("dp", "seq"), None),
            P(("dp", "seq"), None),
            P(("dp", "seq"), None),
            P(None, ("dp", "seq")),
            P(("dp", "seq")),
            P(("dp", "seq")),
            P(("dp", "seq"), None),
            P(("dp", "seq")),
            P(("dp", "seq"), None),
            P(("dp", "seq"), None),
            P(("dp", "seq"), None),
        ),
        check_vma=False,
    )
```

profile of v0, /device:TPU:0, one launch (start us, length us, event | category | flops | bytes accessed | tf_op | source)
XLA Modules:
  0.0 2336.0 jit_solution(11575210034722930738)
XLA Ops:
  34.2 5.5 fusion.95
  51.1 40.4 %while.84 = (s32[]{:T(128)}, f32[6,4,128,256]{3,2,1,0:T(8,128)}, f32[2,6,64,4,256]{4,2,3,1,0:T(8,128)}, f32[2,6,64,4,128]{4,3,2,1,0:T(4,128)}, f32[2,6,64]{2,1,0...) while((s32[]{:T(128)}, f32[6,4,128,256]{3,2,1,0:T(8,128)}, ...), condition=%wide.region_5.6_spmd.clone.clone, body=%wide.region_2.5_spmd.clone.sunk.clone | while | flops 1678819456 | bytes 82328992 | solution.py:58
  80.1 5.9 bitcast_dynamic-update-slice_fusion.16
  109.7 24.8 %all_gather.18 = f32[16,6,4,128]{3,2,1,0:T(4,128)S(1)} all-gather(f32[1,6,4,128]{3,2,1,0:T(4,128)S(1)} %fusion.119), channel_id=1, replica_groups=mesh['dp'=2,'seq'=16] {'seq'}, dimensions={0}, use_global_device_ids=true | all-gather | bytes 208896 | tf_op jit(solution)/shard_map/all_gather | solution.py:16
  134.5 208.3 %all-gather.5.cloned.1.call-done = f32[96,4,128,256]{3,2,1,0:T(8,128)} async-done(((f32[6,4,128,256]{3,2,1,0:T(8,128)}), f32[96,4,128,256]{3,2,1,0:T(8,128)}) %all-gather.5.cloned.1.call-update) | async-done | bytes 50331664 | tf_op jit(solution)/shard_map/all_gather | solution.py:16
  342.8 80.0 %while.85 = (s32[]{:T(128)}, f32[6,4,128,256]{3,2,1,0:T(8,128)}, s32[]{:T(128)}, f32[16,6,4,128]{3,2,1,0:T(4,128)S(1)}, f32[16,6,4,128,256]{4,3,2,1,0:T(8,128)}) while((s32[]{:T(128)}, f32[6,4,128,256]{3,2,1,0:T(8,128)}, s32[]{:T(128)}, f32[16,6,4,128]{3,2,1,0:T(4,128)S(1)}, f32[16,6,4,128,256]{4,3,2,1,0:T(8,128)}) %tuple.264), condition=%wide.region_9.10_spmd.clone.clone, body=%wide.region_8.9_spmd.clone.sunk.clone | while | flops 3145732 | bytes 9474145 | solution.py:27
  422.8 7.3 multiply_reduce_fusion.6
  444.4 7.2 fusion.124
  451.6 6.8 fusion.125
  458.4 17.4 multiply_convert_fusion
  475.8 8.1 fusion.126
  484.0 8.1 multiply_reduce_fusion.1
  501.0 5.3 reshape.378
  523.4 30.0 %while.82 = (s32[]{:T(128)}, f32[6,4,128,256]{3,2,1,0:T(8,128)}, f32[2,6,4,128,256]{4,3,2,1,0:T(8,128)}, f32[2,6,64,4,128]{4,3,2,1,0:T(4,128)}, f32[2,6,64]{2,1,...) while((s32[]{:T(128)}, f32[6,4,128,256]{3,2,1,0:T(8,128)}, ...), condition=%wide.region_19.20_spmd.clone, body=%wide.region_16.19_spmd.sunk.clone | while | flops 618557184 | bytes 44125348 | solution.py:58
  553.4 212.4 %all-gather.7.cloned.1.call-done = f32[96,4,128,256]{3,2,1,0:T(8,128)} async-done(((f32[6,4,128,256]{3,2,1,0:T(8,128)}), f32[96,4,128,256]{3,2,1,0:T(8,128)}) %all-gather.7.cloned.1.call-update) | async-done | bytes 50331664 | tf_op jit(solution)/shard_map/all_gather | solution.py:16
  765.8 49.6 %while.86 = (s32[]{:T(128)}, f32[6,4,128,256]{3,2,1,0:T(8,128)S(1)}, s32[]{:T(128)}, f32[16,6,4,128]{3,2,1,0:T(4,128)S(1)}, f32[16,6,4,128,256]{4,3,2,1,0:T(8,128)}) while((s32[]{:T(128)}, f32[6,4,128,256]{3,2,1,0:T(8,128)S(1)}, s32[]{:T(128)}, f32[16,6,4,128]{3,2,1,0:T(4,128)S(1)}, ...), condition=%wide.region_15.16_spmd.clone.clone, body=%wide.region_14.15_spmd.clone.sunk.clone | while | flops 3145736 | bytes 9474191 | solution.py:27
  819.0 80.0 %while.83 = (s32[]{:T(128)}, f32[6,4,128,256]{3,2,1,0:T(8,128)S(1)}, bf16[2,6,64,4,128]{4,2,3,1,0:T(8,128)(2,1)}, bf16[2,6,64,4,128]{4,2,3,1,0:T(8,128)(2,1)}, b...) while((s32[]{:T(128)}, ...), condition=%wide.region_26.27_spmd.clone, body=%wide.region_20.26_spmd.sunk.clone | while | flops 3510324224 | bytes 213423504 | solution.py:58
  918.3 9.7 fusion.131
  928.0 9.7 fusion.132
  939.1 9.8 fusion.133
  970.3 9.9 add_convert_fusion
  988.8 39.8 %all-reduce.5 = (f32[1024]{0:T(1024)S(1)}, f32[512]{0:T(512)S(1)}, f32[256]{0:T(256)S(1)}, f32[1024]{0:T(1024)S(1)}) all-reduce(f32[1024]{0:T(1024)S(1)} %get-tuple-element.761, f32[512]{0:T(512)S(1)} %get-tuple-element.845, f32[256]{0:T(256)S(1)} %copy-done.83, ...), channel_id=4, replica_groups=mesh['dp'=2,'seq'=16] {'dp','seq'}, use_global_device_ids=true, to_apply=%region_29.30.clone | all-reduce | flops 2816 | bytes 22528
  1031.0 5.9 fusion.91
  1038.3 131.1 %reduce-scatter.31.cloned.1.call-done = f32[32,16]{1,0:T(8,128)} async-done(((f32[1024,16]{1,0:T(8,128)}), f32[32,16]{1,0:T(8,128)}) %reduce-scatter.31.cloned.1.call-update) | async-done | bytes 2064
  1170.8 138.9 %reduce-scatter.21.cloned.1.call-done = f32[32,1024]{1,0:T(8,128)} async-done(((f32[1024,1024]{1,0:T(8,128)}), f32[32,1024]{1,0:T(8,128)}) %reduce-scatter.21.cloned.1.call-update) | async-done | bytes 131088 | tf_op jit(solution)/shard_map/reduce_scatter | solution.py:251
  1309.7 140.8 %reduce-scatter.23.cloned.1.call-done = f32[32,1024]{1,0:T(8,128)} async-done(((f32[1024,1024]{1,0:T(8,128)}), f32[32,1024]{1,0:T(8,128)}) %reduce-scatter.23.cloned.1.call-update) | async-done | bytes 131088 | tf_op jit(solution)/shard_map/reduce_scatter | solution.py:256
  1450.5 153.6 %reduce-scatter.25.cloned.1.call-done = f32[32,2816]{1,0:T(8,128)} async-done(((f32[1024,2816]{1,0:T(8,128)}), f32[32,2816]{1,0:T(8,128)}) %reduce-scatter.25.cloned.1.call-update) | async-done | bytes 360464 | tf_op jit(solution)/shard_map/reduce_scatter | solution.py:258
  1604.1 155.7 %reduce-scatter.27.cloned.1.call-done = f32[32,2816]{1,0:T(8,128)} async-done(((f32[1024,2816]{1,0:T(8,128)}), f32[32,2816]{1,0:T(8,128)}) %reduce-scatter.27.cloned.1.call-update) | async-done | bytes 360464 | tf_op jit(solution)/shard_map/reduce_scatter | solution.py:259
  1759.8 155.9 %reduce-scatter.29.cloned.1.call-done = f32[88,1024]{1,0:T(8,128)} async-done(((f32[2816,1024]{1,0:T(8,128)}), f32[88,1024]{1,0:T(8,128)}) %reduce-scatter.29.cloned.1.call-update) | async-done | bytes 360464 | tf_op jit(solution)/shard_map/reduce_scatter | solution.py:260
  1915.7 137.6 %reduce-scatter.15.cloned.1.call-done = f32[32,512]{1,0:T(8,128)} async-done(((f32[1024,512]{1,0:T(8,128)}), f32[32,512]{1,0:T(8,128)}) %reduce-scatter.15.cloned.1.call-update) | async-done | bytes 65552 | tf_op jit(solution)/shard_map/reduce_scatter | solution.py:248
  2053.3 135.8 %reduce-scatter.17.cloned.1.call-done = f32[32,512]{1,0:T(8,128)} async-done(((f32[1024,512]{1,0:T(8,128)}), f32[32,512]{1,0:T(8,128)}) %reduce-scatter.17.cloned.1.call-update) | async-done | bytes 65552 | tf_op jit(solution)/shard_map/reduce_scatter | solution.py:249
  2189.1 139.9 %reduce-scatter.19.cloned.1.call-done = f32[32,1024]{1,0:T(8,128)} async-done(((f32[1024,1024]{1,0:T(8,128)}), f32[32,1024]{1,0:T(8,128)}) %reduce-scatter.19.cloned.1.call-update) | async-done | bytes 131088 | tf_op jit(solution)/shard_map/reduce_scatter | solution.py:250
  (527 shorter events, 426.9 us)
Async XLA Ops:
  7.2 433.2 %copy-start = (bf16[1024,1024]{1,0:T(8,128)(2,1)S(1)}, bf16[1024,1024]{1,0:T(8,128)(2,1)}, u32[]{:S(2)}) copy-start(bf16[1024,1024]{1,0:T(8,128)(2,1)} %param.39) | copy-start | bytes 6291460
  7.2 335.6 %all-gather.5.cloned.1.call-start = ((), (), s32[]{:S(2)}) async-start(), calls=%async_computation.18 | async-start | bytes 53477376 | tf_op jit(solution)/shard_map/all_gather | solution.py:16
  7.3 5.8 copy-start.80
  7.3 5.8 copy-start.87
  80.1 6.1 copy-start.10
  80.1 6.1 copy-start.12
  80.1 6.2 copy-start.16
  91.6 674.2 %all-gather.7.cloned.1.call-start = ((), (), s32[]{:S(2)}) async-start(), calls=%async_computation.19 | async-start | bytes 53477376 | tf_op jit(solution)/shard_map/all_gather | solution.py:16
  422.8 7.3 copy-start.82
  434.6 5.8 copy-start.50
  442.4 49.7 %copy-start.34 = (f32[768,1024]{1,0:T(8,128)}, f32[768,1024]{1,0:T(8,128)S(1)}, u32[]{:S(2)}) copy-start(f32[768,1024]{1,0:T(8,128)S(1)} %get-tuple-element.884) | copy-start | bytes 9437188
  442.4 9.2 slice-start.2
  444.4 7.2 copy-start.28
  444.4 7.2 slice-start.3
  451.6 6.8 copy-start.63
  475.8 8.1 copy-start.45
  493.0 8.0 copy-start.36
  518.0 518.9 %reduce-scatter.33.cloned.1.call-start = ((), (), s32[]{:S(2)}) async-start(), calls=%async_computation.21 | async-start | bytes 270336
  821.5 7.4 copy-start.5
  861.2 7.4 copy-start.5
  902.9 266.5 %reduce-scatter.31.cloned.1.call-start = ((), (), s32[]{:S(2)}) async-start(), calls=%async_computation.20 | async-start | bytes 540672
  904.5 405.2 %reduce-scatter.21.cloned.1.call-start = ((), (), s32[]{:S(2)}) async-start(), calls=%async_computation.13 | async-start | bytes 4325376 | tf_op jit(solution)/shard_map/reduce_scatter | solution.py:251
  909.8 540.7 %reduce-scatter.23.cloned.1.call-start = ((), (), s32[]{:S(2)}) async-start(), calls=%async_computation.14 | async-start | bytes 4325376 | tf_op jit(solution)/shard_map/reduce_scatter | solution.py:256
  916.9 687.2 %reduce-scatter.25.cloned.1.call-start = ((), (), s32[]{:S(2)}) async-start(), calls=%async_computation.15 | async-start | bytes 11894784 | tf_op jit(solution)/shard_map/reduce_scatter | solution.py:258
  928.0 831.8 %reduce-scatter.27.cloned.1.call-start = ((), (), s32[]{:S(2)}) async-start(), calls=%async_computation.16 | async-start | bytes 11894784 | tf_op jit(solution)/shard_map/reduce_scatter | solution.py:259
  937.7 978.0 %reduce-scatter.29.cloned.1.call-start = ((), (), s32[]{:S(2)}) async-start(), calls=%async_computation.17 | async-start | bytes 11894784 | tf_op jit(solution)/shard_map/reduce_scatter | solution.py:260
  949.0 1104.3 %reduce-scatter.15.cloned.1.call-start = ((), (), s32[]{:S(2)}) async-start(), calls=%async_computation.10 | async-start | bytes 2162688 | tf_op jit(solution)/shard_map/reduce_scatter | solution.py:248
  954.3 1234.8 %reduce-scatter.17.cloned.1.call-start = ((), (), s32[]{:S(2)}) async-start(), calls=%async_computation.11 | async-start | bytes 2162688 | tf_op jit(solution)/shard_map/reduce_scatter | solution.py:249
  959.7 1369.3 %reduce-scatter.19.cloned.1.call-start = ((), (), s32[]{:S(2)}) async-start(), calls=%async_computation.12 | async-start | bytes 4325376 | tf_op jit(solution)/shard_map/reduce_scatter | solution.py:250
  970.3 9.9 copy-start.47
  970.3 9.9 copy-start.66
  1031.0 1298.0 %copy-start.1 = (bf16[1024,1024]{1,0:T(8,128)(2,1)S(1)}, bf16[1024,1024]{1,0:T(8,128)(2,1)}, u32[]{:S(2)}) copy-start(bf16[1024,1024]{1,0:T(8,128)(2,1)} %param.39) | copy-start | bytes 6291460
  (101 other events, 278.0 us)
Sparse Core Ops, SparseCore 0:
  91.7 251.1 all-gather.4
  518.2 247.5 all-gather.6
  903.0 133.8 reduce-scatter.32
  1039.1 130.2 reduce-scatter.30
  1172.1 137.5 reduce-scatter.20
  1312.4 138.0 reduce-scatter.22
  1453.4 150.6 reduce-scatter.24
  1607.0 152.7 reduce-scatter.26
  1762.7 152.9 reduce-scatter.28
  1918.4 134.8 reduce-scatter.14
  2056.2 132.7 reduce-scatter.16
  2191.8 137.1 reduce-scatter.18
where the time goes:
time: 2340 us
  waiting for transfers between devices  1710 us (73%)
  matrix products  238 us (10%)
  other arithmetic  181 us (8%)
  local copies, waits for them, and re-layouts  123 us (5%)
  blocking collectives  64.6 us (3%)
    all_gather x2, waiting for transfers between devices, prefix(): everything = jax.tree.map(lambda part: lax.all_gather(part, axis), x)  421 us
    reduce_scatter x1, waiting for transfers between devices, local(): lax.psum_scatter(partial_grads[13], ('dp', 'seq'), scatter_dimension=0, t...  156 us
    reduce_scatter x1, waiting for transfers between devices, local(): lax.psum_scatter(partial_grads[12], ('dp', 'seq'), scatter_dimension=0, t...  156 us
    reduce_scatter x1, waiting for transfers between devices, local(): lax.psum_scatter(partial_grads[11], ('dp', 'seq'), scatter_dimension=0, t...  154 us
    reduce_scatter x1, waiting for transfers between devices, local(): lax.psum_scatter(partial_grads[9], ('dp', 'seq'), scatter_dimension=0, ti...  141 us
    reduce_scatter x1, waiting for transfers between devices, local(): lax.psum_scatter(partial_grads[3], ('dp', 'seq'), scatter_dimension=0, ti...  140 us
    reduce_scatter x1, waiting for transfers between devices, local(): lax.psum_scatter(partial_grads[4], ('dp', 'seq'), scatter_dimension=0, ti...  139 us
    reduce_scatter x1, waiting for transfers between devices, local(): lax.psum_scatter(partial_grads[1], ('dp', 'seq'), scatter_dimension=0, ti...  138 us
  transfers between devices with their start and end apart: 12, of which 11 were waited for; matrix products, arithmetic and copies ran while one was open for 6% of the time, Pallas kernels for 0%

commit v1 on v0

v1 whole, which is shorter than its diff:
```python
import functools

import jax
import jax.numpy as jnp
from jax import lax
from jax.experimental import pallas as pl
from jax.experimental.pallas import tpu as pltpu
from jax.sharding import PartitionSpec as P

HEADS = 4
EPS = 1e-06
MIB = 1 << 20
BF = jnp.bfloat16
F32 = jnp.float32
HIGHEST = lax.Precision.HIGHEST


def nn(a, b, precision=None):
    return lax.dot_general(
        a, b, (((1,), (0,)), ((), ())), precision=precision, preferred_element_type=F32
    )


def nt(a, b):
    return lax.dot_general(a, b, (((1,), (1,)), ((), ())), preferred_element_type=F32)


def tn(a, b):
    return lax.dot_general(a, b, (((0,), (0,)), ((), ())), preferred_element_type=F32)


def shape(dims, dtype):
    return jax.ShapeDtypeStruct(dims, dtype)


def call(body, out_shape, grid, in_specs, out_specs, prefetch=0, scratch=(), flops=0, moved=0):
    return pl.pallas_call(
        body,
        out_shape=out_shape,
        grid_spec=pltpu.PrefetchScalarGridSpec(
            num_scalar_prefetch=prefetch,
            grid=grid,
            in_specs=in_specs,
            out_specs=out_specs,
            scratch_shapes=list(scratch),
        ),
        compiler_params=pltpu.CompilerParams(vmem_limit_bytes=56 * MIB),
        cost_estimate=pl.CostEstimate(flops=flops, bytes_accessed=moved, transcendentals=0),
    )


def block(dims, index):
    return pl.BlockSpec(dims, index)


def whole(dims):
    zero = (0,) * len(dims)
    return pl.BlockSpec(dims, lambda *_: zero)


def reset_masks(docs_ref, row, docs, length):
    at_i = lax.broadcasted_iota(jnp.int32, (length, length), 0)
    at_j = lax.broadcasted_iota(jnp.int32, (length, length), 1)
    token = lax.broadcasted_iota(jnp.int32, (length, 1), 0)
    visible = at_i >= at_j
    alive = token >= 0
    tail = token >= 0
    whole_alive = jnp.float32(1.0)
    for n in range(docs):
        start = docs_ref[row * docs + n]
        visible = visible & jnp.logical_not((at_j < start) & (start <= at_i))
        inside = (start >= 0) & (start < length)
        first = jnp.where(start >= 0, start, length)
        alive = alive & (token < first)
        last = jnp.where(start < length, start, -1)
        tail = tail & (token >= last)
        whole_alive = whole_alive * jnp.where(inside, 0.0, 1.0)
    return visible, alive.astype(F32), tail.astype(F32), whole_alive


def lower_ones(length, strict=False):
    at_i = lax.broadcasted_iota(jnp.int32, (length, length), 0)
    at_j = lax.broadcasted_iota(jnp.int32, (length, length), 1)
    return (at_i > at_j if strict else at_i >= at_j).astype(F32)


def project_body(
    rows, docs, length, hk, hv, parts,
    docs_ref, table_ref, x_ref, gain_ref, wq_ref, wk_ref, wv_ref, wog_ref, wrd_ref, wru_ref, bias_ref,
    normed_ref, q_ref, k_ref, v_ref, og_ref, ra_ref, gp_ref, cum_ref, keep_ref, send_ref, decay_ref,
    hold,
):
    x = x_ref[...].astype(F32)
    inv = lax.rsqrt(jnp.mean(x * x, axis=-1, keepdims=True) + EPS)
    normed = (x * inv * gain_ref[...]).astype(BF)
    normed_ref[...] = normed
    rank = nn(normed, wrd_ref[...]).astype(BF)
    ra_ref[...] = rank
    gate = nn(rank, wru_ref[...]) + bias_ref[...]
    gp_ref[...] = gate
    q_ref[...] = nn(normed, wq_ref[...]).astype(BF)
    key = nn(normed, wk_ref[...]).astype(BF)
    k_ref[...] = key
    value = nn(normed, wv_ref[...]).astype(BF)
    v_ref[...] = value
    og_ref[...] = nn(normed, wog_ref[...])
    log_decay = (jnp.minimum(gate, 0.0) - jnp.log1p(jnp.exp(-jnp.abs(gate)))) * (1.0 / 16.0)
    tri = lower_ones(length)
    size = hv // parts
    for r in range(rows):
        at = slice(r * length, (r + 1) * length)
        row = pl.program_id(0) * rows + r
        cum = nn(tri, log_decay[at], HIGHEST)
        cum_ref[at, :] = cum
        _, _, tail, whole_alive = reset_masks(docs_ref, row, docs, length)
        last = cum[length - 1 :, :]
        decay_ref[r] = jnp.exp(last) * whole_alive
        weighted = (key[at].astype(F32) * jnp.exp(last - cum) * tail).astype(BF)
        for h in range(HEADS):
            hold[...] = tn(value[at, h * hv : (h + 1) * hv], weighted[:, h * hk : (h + 1) * hk])
            for j in range(parts // 2):
                first = pl.multiple_of(table_ref[j] * size, size)
                keep_ref[j, r, h] = hold[pl.ds(first, size), :]
                second = pl.multiple_of(table_ref[parts // 2 + j] * size, size)
                send_ref[j, r, h] = hold[pl.ds(second, size), :]


def project_all(x, docs, table, gain, wq, wk, wv, wog, wrd, wru, bias, dims):
    row_count, length, width, kw, vw, ndocs, parts = dims
    tokens = row_count * length
    rows = 2 if row_count % 2 == 0 else 1
    tm = rows * length
    hk, hv = kw // HEADS, vw // HEADS
    rank = wrd.shape[1]
    size = hv // parts
    tile = lambda n: block((tm, n), lambda i, *_: (i, 0))
    half = (parts // 2, row_count, HEADS, size, hk)
    half_block = block((parts // 2, rows, HEADS, size, hk), lambda i, *_: (0, i, 0, 0, 0))
    body = functools.partial(project_body, rows, ndocs, length, hk, hv, parts)
    return call(
        body,
        (
            shape((tokens, width), BF),
            shape((tokens, kw), BF),
            shape((tokens, kw), BF),
            shape((tokens, vw), BF),
            shape((tokens, vw), F32),
            shape((tokens, rank), BF),
            shape((tokens, kw), F32),
            shape((tokens, kw), F32),
            shape(half, F32),
            shape(half, F32),
            shape((row_count, 1, kw), F32),
        ),
        (row_count // rows,),
        [
            tile(width), whole((1, width)), whole(wq.shape), whole(wk.shape), whole(wv.shape),
            whole(wog.shape), whole(wrd.shape), whole(wru.shape), whole((1, kw)),
        ],
        (
            tile(width), tile(kw), tile(kw), tile(vw), tile(vw), tile(rank), tile(kw), tile(kw),
            half_block, half_block, block((rows, 1, kw), lambda i, *_: (i, 0, 0)),
        ),
        prefetch=2,
        scratch=[pltpu.VMEM((hv, hk), F32)],
        flops=2 * tokens * width * (2 * kw + 2 * vw),
        moved=20 * MIB,
    )(docs, table, x, gain.reshape(1, -1), wq, wk, wv, wog, wrd, wru, bias.reshape(1, -1))


def span_factors(cum, length):
    middle = cum[length // 2 - 1 : length // 2, :]
    return jnp.exp(cum - middle), jnp.exp(middle - cum)


def inner_body(docs, length, hk, hv, docs_ref, q_ref, k_ref, v_ref, cum_ref, inner_ref):
    visible, _, _, _ = reset_masks(docs_ref, pl.program_id(0), docs, length)
    up, down = span_factors(cum_ref[...], length)
    q = (q_ref[...].astype(F32) * up).astype(BF)
    k = (k_ref[...].astype(F32) * down).astype(BF)
    for h in range(HEADS):
        kk = slice(h * hk, (h + 1) * hk)
        vv = slice(h * hv, (h + 1) * hv)
        scores = jnp.where(visible, nt(q[:, kk], k[:, kk]), 0.0).astype(BF)
        inner_ref[:, vv] = nn(scores, v_ref[:, vv])


def inner_all(q, k, v, cum, docs, dims):
    row_count, length, width, kw, vw, ndocs, parts = dims
    tokens = row_count * length
    tile = lambda n: block((length, n), lambda i, *_: (i, 0))
    return call(
        functools.partial(inner_body, ndocs, length, kw // HEADS, vw // HEADS),
        shape((tokens, vw), F32),
        (row_count,),
        [tile(kw), tile(kw), tile(vw), tile(kw)],
        tile(vw),
        prefetch=1,
        flops=2 * tokens * length * (kw + vw),
        moved=8 * MIB,
    )(docs, q, k, v, cum)


def gather_state(state_ref, table_ref, h, parts):
    return jnp.concatenate([state_ref[table_ref[parts + p], 0, h] for p in range(parts)], axis=0)


def mix_body(
    docs, length, hk, hv, parts,
    docs_ref, table_ref, q_ref, cum_ref, inner_ref, og_ref, state_ref, gain_ref,
    mixed_ref, gated_ref, kept_ref,
):
    _, alive, _, _ = reset_masks(docs_ref, pl.program_id(0), docs, length)
    reach = (q_ref[...].astype(F32) * jnp.exp(cum_ref[...]) * alive).astype(BF)
    scale = hk ** (-0.5)
    for h in range(HEADS):
        kk = slice(h * hk, (h + 1) * hk)
        vv = slice(h * hv, (h + 1) * hv)
        state = gather_state(state_ref, table_ref, h, parts).astype(BF)
        kept_ref[0, h] = state
        mixed = scale * (inner_ref[:, vv] + nt(reach[:, kk], state))
        mixed_ref[:, vv] = mixed
        inv = lax.rsqrt(jnp.mean(mixed * mixed, axis=-1, keepdims=True) + EPS)
        og = og_ref[:, vv]
        gated_ref[:, vv] = (mixed * inv * gain_ref[...] * og * jax.nn.sigmoid(og)).astype(BF)


def mix_all(q, cum, inner, og, state, gain, docs, table, dims):
    row_count, length, width, kw, vw, ndocs, parts = dims
    tokens = row_count * length
    hk, hv = kw // HEADS, vw // HEADS
    tile = lambda n: block((length, n), lambda i, *_: (i, 0))
    return call(
        functools.partial(mix_body, ndocs, length, hk, hv, parts),
        (
            shape((tokens, vw), F32),
            shape((tokens, vw), BF),
            shape((row_count, HEADS, hv, hk), BF),
        ),
        (row_count,),
        [
            tile(kw), tile(kw), tile(vw), tile(vw),
            block((parts, 1, HEADS, hv // parts, hk), lambda i, *_: (0, i, 0, 0, 0)),
            whole((1, hv)),
        ],
        (tile(vw), tile(vw), block((1, HEADS, hv, hk), lambda i, *_: (i, 0, 0, 0))),
        prefetch=2,
        flops=2 * tokens * hk * vw,
        moved=18 * MIB,
    )(docs, table, q, cum, inner, og, state, gain.reshape(1, -1))


def ff_body(
    steps,
    x_ref, cot_ref, gated_ref, wo_ref, gain_ref, wg_ref, wu_ref, wd_ref,
    hidden_ref, dg_ref, du_ref, normed2_ref, out_ref, dmid_ref, dout_ref, dgated_ref, gnorm_ref,
    middle, total, back,
):
    step = pl.program_id(0)

    @pl.when(step == 0)
    def _():
        mid = x_ref[...].astype(F32) + nn(gated_ref[...], wo_ref[...])
        middle[...] = mid
        inv = lax.rsqrt(jnp.mean(mid * mid, axis=-1, keepdims=True) + EPS)
        normed2_ref[...] = (mid * inv * gain_ref[...]).astype(BF)

    normed2 = normed2_ref[...]
    gate = nn(normed2, wg_ref[...])
    up = nn(normed2, wu_ref[...])
    d_hidden = nt(cot_ref[...], wd_ref[...])
    sig = jax.nn.sigmoid(gate)
    act = gate * sig
    hidden = (act * up).astype(BF)
    dg = (d_hidden * up * sig * (1.0 + gate * (1.0 - sig))).astype(BF)
    du = (d_hidden * act).astype(BF)
    hidden_ref[...] = hidden
    dg_ref[...] = dg
    du_ref[...] = du
    more = nn(hidden, wd_ref[...])
    more_back = nt(dg, wg_ref[...]) + nt(du, wu_ref[...])

    @pl.when(step == 0)
    def _():
        total[...] = more
        back[...] = more_back

    @pl.when(step > 0)
    def _():
        total[...] += more
        back[...] += more_back

    @pl.when(step == steps - 1)
    def _():
        mid = middle[...]
        out_ref[...] = (mid + total[...]).astype(BF)
        inv = lax.rsqrt(jnp.mean(mid * mid, axis=-1, keepdims=True) + EPS)
        d_normed2 = back[...]
        gnorm_ref[...] = jnp.sum(d_normed2 * mid * inv, axis=0, keepdims=True)
        scaled = d_normed2 * gain_ref[...]
        d_middle = (
            cot_ref[...].astype(F32)
            + inv * scaled
            - mid * (inv * inv * inv) * jnp.mean(scaled * mid, axis=-1, keepdims=True)
        )
        dmid_ref[...] = d_middle
        d_out = d_middle.astype(BF)
        dout_ref[...] = d_out
        dgated_ref[...] = nt(d_out, wo_ref[...])


def ff_all(x, cot, gated, wo, gain, wg, wu, wd):
    tokens, width = x.shape
    vw = gated.shape[1]
    ff = wg.shape[1]
    tile = 256
    steps = ff // tile
    col = lambda n: block((n, tile), lambda i: (0, i))
    once = lambda dims: pl.BlockSpec(dims, lambda i: (0, 0), pipeline_mode=pl.Buffered(1))
    return call(
        functools.partial(ff_body, steps),
        (
            shape((tokens, ff), BF), shape((tokens, ff), BF), shape((tokens, ff), BF),
            shape((tokens, width), BF), shape((tokens, width), BF), shape((tokens, width), F32),
            shape((tokens, width), BF), shape((tokens, vw), F32), shape((1, width), F32),
        ),
        (steps,),
        [
            once((tokens, width)), once((tokens, width)), once((tokens, vw)), once(wo.shape),
            once((1, width)), col(width), col(width), block((tile, width), lambda i: (i, 0)),
        ],
        (
            col(tokens), col(tokens), col(tokens),
            whole((tokens, width)), whole((tokens, width)), whole((tokens, width)),
            whole((tokens, width)), whole((tokens, vw)), whole((1, width)),
        ),
        scratch=[pltpu.VMEM((tokens, width), F32)] * 3,
        flops=12 * tokens * width * ff,
        moved=45 * MIB,
    )(x, cot, gated, wo, gain.reshape(1, -1), wg, wu, wd)


def head_back_body(
    docs, length, hk, hv, parts,
    docs_ref, table_ref, dgated_ref, og_ref, mixed_ref, q_ref, cum_ref, gain_ref,
    dmix_ref, dog_ref, keep_ref, send_ref, ggroup_ref,
    hold,
):
    row = pl.program_id(0)
    _, alive, _, _ = reset_masks(docs_ref, row, docs, length)
    reach = (q_ref[...].astype(F32) * jnp.exp(cum_ref[...]) * alive).astype(BF)
    scale = hk ** (-0.5)
    size = hv // parts
    ggroup = jnp.zeros((1, hv), F32)
    for h in range(HEADS):
        kk = slice(h * hk, (h + 1) * hk)
        vv = slice(h * hv, (h + 1) * hv)
        mixed = mixed_ref[:, vv]
        inv = lax.rsqrt(jnp.mean(mixed * mixed, axis=-1, keepdims=True) + EPS)
        og = og_ref[:, vv]
        sig = jax.nn.sigmoid(og)
        dgated = dgated_ref[:, vv]
        unit = mixed * inv
        dog_ref[:, vv] = (
            dgated * unit * gain_ref[...] * sig * (1.0 + og * (1.0 - sig))
        ).astype(BF)
        d_heads = dgated * og * sig
        ggroup = ggroup + jnp.sum(d_heads * unit, axis=0, keepdims=True)
        scaled = d_heads * gain_ref[...]
        d_mixed = inv * scaled - mixed * (inv * inv * inv) * jnp.mean(
            scaled * mixed, axis=-1, keepdims=True
        )
        d_mixed = (scale * d_mixed).astype(BF)
        dmix_ref[:, vv] = d_mixed
        hold[...] = tn(d_mixed, reach[:, kk])
        for j in range(parts // 2):
            first = pl.multiple_of(table_ref[j] * size, size)
            keep_ref[j, 0, h] = hold[pl.ds(first, size), :]
            second = pl.multiple_of(table_ref[parts // 2 + j] * size, size)
            send_ref[j, 0, h] = hold[pl.ds(second, size), :]

    @pl.when(row == 0)
    def _():
        ggroup_ref[...] = ggroup

    @pl.when(row > 0)
    def _():
        ggroup_ref[...] += ggroup


def head_back_all(dgated, og, mixed, q, cum, gain, docs, table, dims):
    row_count, length, width, kw, vw, ndocs, parts = dims
    tokens = row_count * length
    hk, hv = kw // HEADS, vw // HEADS
    size = hv // parts
    tile = lambda n: block((length, n), lambda i, *_: (i, 0))
    half = (parts // 2, row_count, HEADS, size, hk)
    half_block = block((parts // 2, 1, HEADS, size, hk), lambda i, *_: (0, i, 0, 0, 0))
    return call(
        functools.partial(head_back_body, ndocs, length, hk, hv, parts),
        (
            shape((tokens, vw), BF), shape((tokens, vw), BF),
            shape(half, F32), shape(half, F32), shape((1, hv), F32),
        ),
        (row_count,),
        [tile(vw), tile(vw), tile(vw), tile(kw), tile(kw), whole((1, hv))],
        (tile(vw), tile(vw), half_block, half_block, whole((1, hv))),
        prefetch=2,
        scratch=[pltpu.VMEM((hv, hk), F32)],
        flops=2 * tokens * hk * vw,
        moved=20 * MIB,
    )(docs, table, dgated, og, mixed, q, cum, gain.reshape(1, -1))


def mix_back_body(
    docs, length, hk, hv, parts,
    docs_ref, table_ref, q_ref, k_ref, v_ref, cum_ref, gp_ref, ra_ref, dmix_ref, state_ref, grad_ref,
    wru_ref,
    dqkv_ref, drank_ref, grup_ref, gbias_ref,
):
    row = pl.program_id(0)
    kw = HEADS * hk
    visible, alive, tail, whole_alive = reset_masks(docs_ref, row, docs, length)
    cum = cum_ref[...]
    last = cum[length - 1 :, :]
    up, down = span_factors(cum, length)
    from_start = jnp.exp(cum) * alive
    to_end = jnp.exp(last - cum) * tail
    total = jnp.exp(last) * whole_alive
    q = q_ref[...].astype(F32)
    k = k_ref[...].astype(F32)
    q_span = (q * up).astype(BF)
    k_span = (k * down).astype(BF)
    reach = (q * from_start).astype(BF)
    weighted = (k * to_end).astype(BF)
    later, earlier, crossing = [], [], []
    for h in range(HEADS):
        kk = slice(h * hk, (h + 1) * hk)
        vv = slice(h * hv, (h + 1) * hv)
        qs, ks = q_span[:, kk], k_span[:, kk]
        d_mix = dmix_ref[:, vv]
        value = v_ref[:, vv]
        state = state_ref[0, h]
        grad32 = gather_state(grad_ref, table_ref, h, parts)
        grad = grad32.astype(BF)
        scores = jnp.where(visible, nt(qs, ks), 0.0).astype(BF)
        d_scores = jnp.where(visible, nt(d_mix, value), 0.0).astype(BF)
        dq_in = nn(d_scores, ks)
        dk_in = tn(d_scores, qs)
        dq_out = nn(d_mix, state)
        dk_out = nn(value, grad)
        dqkv_ref[:, kk] = (dq_in * up[:, kk] + dq_out * from_start[:, kk]).astype(BF)
        dqkv_ref[:, kw + h * hk : kw + (h + 1) * hk] = (
            dk_in * down[:, kk] + dk_out * to_end[:, kk]
        ).astype(BF)
        dqkv_ref[:, 2 * kw + h * hv : 2 * kw + (h + 1) * hv] = (
            tn(scores, d_mix) + nt(weighted[:, kk], grad)
        ).astype(BF)
        later.append(
            qs.astype(F32) * dq_in - ks.astype(F32) * dk_in + reach[:, kk].astype(F32) * dq_out
        )
        earlier.append(weighted[:, kk].astype(F32) * dk_out)
        crossing.append(jnp.sum(state.astype(F32) * grad32, axis=0, keepdims=True))
    later = jnp.concatenate(later, axis=1)
    earlier = jnp.concatenate(earlier, axis=1)
    crossing = jnp.concatenate(crossing, axis=1)
    at_i = lax.broadcasted_iota(jnp.int32, (length, length), 0)
    at_j = lax.broadcasted_iota(jnp.int32, (length, length), 1)
    after = (at_i <= at_j).astype(F32)
    before = (at_i > at_j).astype(F32)
    d_decay = nn(after, later, HIGHEST) + nn(before, earlier, HIGHEST) + total * crossing
    d_gate = (d_decay * jax.nn.sigmoid(-gp_ref[...]) * (1.0 / 16.0)).astype(BF)
    drank_ref[...] = nt(d_gate, wru_ref[...]).astype(BF)
    grup = tn(ra_ref[...], d_gate)
    gbias = jnp.sum(d_gate.astype(F32), axis=0, keepdims=True)

    @pl.when(row == 0)
    def _():
        grup_ref[...] = grup
        gbias_ref[...] = gbias

    @pl.when(row > 0)
    def _():
        grup_ref[...] += grup
        gbias_ref[...] += gbias


def mix_back_all(q, k, v, cum, gp, ra, dmix, state, grad, wru, docs, table, dims):
    row_count, length, width, kw, vw, ndocs, parts = dims
    tokens = row_count * length
    hk, hv = kw // HEADS, vw // HEADS
    rank = wru.shape[0]
    tile = lambda n: block((length, n), lambda i, *_: (i, 0))
    return call(
        functools.partial(mix_back_body, ndocs, length, hk, hv, parts),
        (
            shape((tokens, 2 * kw + vw), BF), shape((tokens, rank), BF),
            shape((rank, kw), F32), shape((1, kw), F32),
        ),
        (row_count,),
        [
            tile(kw), tile(kw), tile(vw), tile(kw), tile(kw), tile(rank), tile(vw),
            block((1, HEADS, hv, hk), lambda i, *_: (i, 0, 0, 0)),
            block((parts, 1, HEADS, hv // parts, hk), lambda i, *_: (0, i, 0, 0, 0)),
            whole((rank, kw)),
        ],
        (tile(2 * kw + vw), tile(rank), whole((rank, kw)), whole((1, kw))),
        prefetch=2,
        flops=16 * tokens * length * vw,
        moved=16 * MIB,
    )(docs, table, q, k, v, cum, gp, ra, dmix, state, grad, wru)


def input_back_body(
    kw, vw,
    x_ref, dmid_ref, dqkv_ref, dog_ref, drank_ref, gain_ref, wq_ref, wk_ref, wv_ref, wog_ref, wrd_ref,
    gin_ref, gnorm_ref,
):
    step = pl.program_id(0)
    d_normed = (
        nt(dqkv_ref[:, :kw], wq_ref[...])
        + nt(dqkv_ref[:, kw : 2 * kw], wk_ref[...])
        + nt(dqkv_ref[:, 2 * kw :], wv_ref[...])
        + nt(dog_ref[...], wog_ref[...])
        + nt(drank_ref[...], wrd_ref[...])
    )
    x = x_ref[...].astype(F32)
    inv = lax.rsqrt(jnp.mean(x * x, axis=-1, keepdims=True) + EPS)
    gnorm = jnp.sum(d_normed * x * inv, axis=0, keepdims=True)
    scaled = d_normed * gain_ref[...]
    gin_ref[...] = (
        dmid_ref[...]
        + inv * scaled
        - x * (inv * inv * inv) * jnp.mean(scaled * x, axis=-1, keepdims=True)
    )

    @pl.when(step == 0)
    def _():
        gnorm_ref[...] = gnorm

    @pl.when(step > 0)
    def _():
        gnorm_ref[...] += gnorm


def input_back_all(x, dmid, dqkv, dog, drank, gain, wq, wk, wv, wog, wrd):
    tokens, width = x.shape
    kw, vw = wq.shape[1], wv.shape[1]
    tm = 256 if tokens % 256 == 0 else 128
    tile = lambda n: block((tm, n), lambda i: (i, 0))
    return call(
        functools.partial(input_back_body, kw, vw),
        (shape((tokens, width), F32), shape((1, width), F32)),
        (tokens // tm,),
        [
            tile(width), tile(width), tile(2 * kw + vw), tile(vw), tile(drank.shape[1]),
            whole((1, width)), whole(wq.shape), whole(wk.shape), whole(wv.shape), whole(wog.shape),
            whole(wrd.shape),
        ],
        (tile(width), whole((1, width))),
        flops=2 * tokens * width * (2 * kw + 2 * vw),
        moved=20 * MIB,
    )(x, dmid, dqkv, dog, drank, gain.reshape(1, -1), wq, wk, wv, wog, wrd)


def weight_body(count, pieces, per, *refs):
    table_ref, left_ref = refs[:2]
    rights = refs[2 : 2 + count]
    outs = refs[2 + count : 2 + 3 * count]
    turned, hold = refs[2 + 3 * count :]

    @pl.when(pl.program_id(0) == 0)
    def _():
        turned[...] = left_ref[...].T

    for n in range(count):
        hold[...] = nn(turned[...], rights[n][...])
        keep_ref, send_ref = outs[2 * n], outs[2 * n + 1]
        for j in range(pieces // 2):
            first = pl.multiple_of(table_ref[j] * per, per)
            keep_ref[j] = hold[pl.ds(first, per), :]
            second = pl.multiple_of(table_ref[pieces // 2 + j] * per, per)
            send_ref[j] = hold[pl.ds(second, per), :]


def weight_grads(left, rights, table, tile=256):
    tokens, rows = left.shape
    pieces = table.shape[0]
    per = rows // pieces
    cols = rights[0].shape[1]
    if per % 8:
        out = []
        for right in rights:
            parts = tn(left, right).reshape(pieces, per, cols)[table]
            out.append((parts[: pieces // 2], parts[pieces // 2 :]))
        return out
    count = len(rights)
    half = shape((pieces // 2, per, cols), F32)
    half_block = block((pieces // 2, per, tile), lambda i, *_: (0, 0, i))
    flat = call(
        functools.partial(weight_body, count, pieces, per),
        (half,) * (2 * count),
        (cols // tile,),
        [whole((tokens, rows))] + [block((tokens, tile), lambda i, *_: (0, i))] * count,
        (half_block,) * (2 * count),
        prefetch=1,
        scratch=[pltpu.VMEM((rows, tokens), BF), pltpu.VMEM((rows, tile), F32)],
        flops=2 * tokens * rows * cols * count,
        moved=4 * rows * cols * count,
    )(table, left, *rights)
    return [(flat[2 * n], flat[2 * n + 1]) for n in range(count)]


def bits_of(n):
    return n.bit_length() - 1


class Links:
    def __init__(self):
        self.n_dp, self.n_seq = lax.axis_size("dp"), lax.axis_size("seq")
        self.seq_bits, self.dp_bits = bits_of(self.n_seq), bits_of(self.n_dp)
        self.at_seq = lax.axis_index("seq")
        self.me = lax.axis_index("dp") * self.n_seq + self.at_seq

    def swap(self, value, bit):
        name, n, flip = "seq", self.n_seq, 1 << bit
        if bit >= self.seq_bits:
            name, n, flip = "dp", self.n_dp, 1 << (bit - self.seq_bits)
        return lax.ppermute(value, name, [(i, i ^ flip) for i in range(n)])

    def table(self, order):
        n = 1 << len(order)
        places = [
            sum(((at >> (len(order) - 1 - k)) & 1) << bit for k, bit in enumerate(order))
            for at in range(n)
        ]
        here = self.me if n == self.n_dp * self.n_seq else self.at_seq
        return jnp.array(places, jnp.int32) ^ here

    def order(self, *seq_bits, across):
        dp = tuple(range(self.seq_bits, self.seq_bits + self.dp_bits))
        rest = [bit for bit in range(self.seq_bits) if bit not in seq_bits]
        order = list(seq_bits) + rest
        return tuple(order[:across]) + dp + tuple(order[across:])

    def reduce(self, pair, order):
        keep, send = pair
        for k, bit in enumerate(order):
            got = self.swap(send, bit)
            if k == len(order) - 1:
                return keep + got
            half = keep.shape[0] // 2
            send = keep[half:] + got[half:]
            keep = keep[:half] + got[:half]


def scan_states(links, keep, send, decays, backwards):
    bits = links.seq_bits
    levels = []
    decay = None if backwards else decays
    kept = [] if not backwards else decays
    for bit in range(bits - 1):
        got = links.swap(send, bit)
        if backwards:
            mine_d, got_d = kept[bit]
        else:
            mine_d, got_d = decay, links.swap(decay, bit)
            kept.append((mine_d, got_d))
            decay = mine_d * got_d
        odd = (links.at_seq >> bit) & 1
        second = (odd == 0) if backwards else (odd == 1)
        levels.append((second, keep, got, mine_d, got_d))
        total = jnp.where(second, mine_d * got + keep, got_d * keep + got)
        half = total.shape[0] // 2
        if bit < bits - 2:
            keep, send = total[:half], total[half:]
        else:
            keep = total
    flip = 1 << (bits - 1)
    pairs = [(i, i ^ flip) for i in range(links.n_seq) if ((i >> (bits - 1)) & 1) == int(backwards)]
    state = lax.ppermute(keep, "seq", pairs)
    for bit in reversed(range(bits - 1)):
        second, keep, got, mine_d, got_d = levels[bit]
        theirs = jnp.where(second, state, mine_d * state + keep)
        mine = jnp.where(second, got_d * state + got, state)
        state = jnp.concatenate([mine, links.swap(theirs, bit)], axis=0)
    return state, kept


def local(
    block_in, doc_starts, cotangent, norm1_gain, w_query, w_key, w_value, w_outgate, w_rank_down,
    w_rank_up, decay_bias, group_gain, w_output, norm2_gain, w_ffgate, w_ffup, w_ffdown,
):
    row_count, length, width = block_in.shape
    tokens = row_count * length
    kw, vw = w_query.shape[1], w_value.shape[1]
    links = Links()
    parts = links.n_seq
    everyone = links.n_dp * links.n_seq
    dims = (row_count, length, width, kw, vw, doc_starts.shape[1], parts)
    x = block_in.reshape(tokens, width)
    cot = cotangent.reshape(tokens, width)
    docs = (doc_starts - links.at_seq * length).reshape(-1)

    levels = tuple(range(links.seq_bits - 1))
    step = 1 << len(levels)
    source = links.table(tuple(levels))
    size = parts // step
    low = links.at_seq & (step - 1)
    reverse = jnp.array(
        [sum(((p >> b) & 1) << (len(levels) - 1 - b) for b in levels) for p in range(step)], jnp.int32
    )
    source = reverse ^ low
    place = reverse[jnp.arange(step) ^ low]
    spread = jnp.arange(size)
    to_piece = (source[:, None] * size + spread).reshape(-1)
    to_place = (place[:, None] * size + spread).reshape(-1)
    state_table = jnp.concatenate([to_piece, to_place]).astype(jnp.int32)

    normed, q, k, v, og, ra, gp, cum, keep, send, decay = project_all(
        x, docs, state_table, norm1_gain, w_query, w_key, w_value, w_outgate, w_rank_down, w_rank_up,
        decay_bias, dims,
    )
    decay = decay.reshape(1, row_count, HEADS, 1, kw // HEADS)
    state_in, decays = scan_states(links, keep, send, decay, False)
    inner = inner_all(q, k, v, cum, docs, dims)
    mixed, gated, state_kept = mix_all(q, cum, inner, og, state_in, group_gain, docs, state_table, dims)

    hidden, dg, du, normed2, block_out, d_middle, d_out, d_gated, gnorm2 = ff_all(
        x, cot, gated, w_output, norm2_gain, w_ffgate, w_ffup, w_ffdown
    )
    d_mix, d_og, keep, send, ggroup = head_back_all(
        d_gated, og, mixed, q, cum, group_gain, docs, state_table, dims
    )
    state_grad, _ = scan_states(links, keep, send, decays, True)

    order_a = links.order(0, across=1)
    order_b = links.order(0, 1, across=2)
    table_a, table_b = links.table(order_a), links.table(order_b)
    (gate_pair,) = weight_grads(normed2, [dg], table_a)
    (up_pair,) = weight_grads(normed2, [du], table_b)
    (down_pair,) = weight_grads(hidden, [cot], table_a)
    (output_pair,) = weight_grads(gated, [d_out], table_b)
    (og_pair,) = weight_grads(normed, [d_og], table_b)
    g_ffgate = links.reduce(gate_pair, order_a)
    g_ffup = links.reduce(up_pair, order_b)
    g_ffdown = links.reduce(down_pair, order_a)
    g_output = links.reduce(output_pair, order_b)
    g_outgate = links.reduce(og_pair, order_b)

    d_qkv, d_rank, grup, gbias = mix_back_all(
        q, k, v, cum, gp, ra, d_mix, state_kept, state_grad, w_rank_up, docs, state_table, dims
    )
    (qkv_pair,) = weight_grads(normed, [d_qkv], table_a)
    g_qkv = links.reduce(qkv_pair, order_a)
    grad_in, gnorm1 = input_back_all(
        x, d_middle, d_qkv, d_og, d_rank, norm1_gain, w_query, w_key, w_value, w_outgate, w_rank_down
    )
    g_rank_down = tn(normed, d_rank)

    rank = w_rank_up.shape[0]
    by_device = lambda value: value.reshape(everyone, -1)
    small = [
        by_device(g_rank_down),
        grup.reshape(rank, everyone, kw // everyone).transpose(1, 0, 2).reshape(everyone, -1),
        by_device(gnorm1), by_device(gnorm2), by_device(gbias), by_device(ggroup),
    ]
    widths = [part.shape[1] for part in small]
    packed = jnp.concatenate(small, axis=1)
    packed = jnp.pad(packed, ((0, 0), (0, -packed.shape[1] % 128)))[table_a]
    packed = packed.reshape(everyone, 1, -1)
    packed = links.reduce((packed[: everyone // 2], packed[everyone // 2 :]), order_a).reshape(-1)
    out_small, at = [], 0
    for n in widths:
        out_small.append(packed[at : at + n])
        at += n
    s_down, s_up, s_norm1, s_norm2, s_bias, s_group = out_small
    g_qkv = g_qkv[0]
    return (
        block_out.reshape(row_count, length, width),
        grad_in.reshape(row_count, length, width),
        s_norm1,
        g_qkv[:, :kw],
        g_qkv[:, kw : 2 * kw],
        g_qkv[:, 2 * kw :],
        g_outgate[0],
        s_down.reshape(-1, rank),
        s_up.reshape(rank, -1),
        s_bias,
        s_group,
        g_output[0],
        s_norm2,
        g_ffgate[0],
        g_ffup[0],
        g_ffdown[0],
    )


def solution(mesh):
    tokens = P("dp", "seq", None)
    rows = P(("dp", "seq"), None)
    vector = P(("dp", "seq"))
    return jax.shard_map(
        local,
        mesh=mesh,
        in_specs=(tokens, P("dp", None), tokens) + (P(),) * 14,
        out_specs=(
            tokens, tokens, vector, rows, rows, rows, rows, rows, P(None, ("dp", "seq")), vector,
            vector, rows, vector, rows, rows, rows,
        ),
        check_vma=False,
    )
```

time: 2340 us -> 717 us (0.31)
  waiting for transfers between devices: 1710 us -> 355 us
  matrix products: 238 us -> 1.53 us
  Pallas kernels: 0 us -> 188 us
  local copies, waits for them, and re-layouts: 123 us -> 16.5 us
  other arithmetic: 181 us -> 81.5 us
  starting transfers between devices: 0.5 us -> 65.9 us
  blocking collectives: 64.6 us -> 0 us
    reduce_scatter x8 -> x0, waiting for transfers between devices: 1160 us -> none  [the longest x1 156 us: local(): lax.psum_scatter(partial_grads[13], ('dp', 'seq'), scatter_dimension=0, t...]
    all_gather x2 -> x0, waiting for transfers between devices: 421 us -> none  [prefix(): everything = jax.tree.map(lambda part: lax.all_gather(part, axis), x)]
    ppermute x0 -> x52, waiting for transfers between devices: none -> 355 us  [the longest x50 343 us: swap(): return lax.ppermute(value, name, [(i, i ^ flip) for i in range(n)])]
    dot_general x58 -> x1, matrix products: 236 us -> 1.53 us  [tn(): lax.dot_general(a, b, (((0,), (0,)), ((), ())), preferred_element_type=F32)]
    pallas_call x0 -> x13, Pallas kernels: none -> 188 us  [the longest x6 66.1 us: weight_grads(): call(functools.partial(weight_body, count, pieces, per), (half,) * (2 * c...]
    unnamed x14 -> x0, waiting for transfers between devices: 131 us -> none
    select_n x32 -> x13, other arithmetic: 129 us -> 16.4 us  [the longest x6 8.33 us: scan_states(): total = jnp.where(second, mine_d * got + keep, got_d * keep + got)]
    ppermute x0 -> x52, starting transfers between devices: none -> 65.9 us  [the longest x50 60.2 us: swap(): return lax.ppermute(value, name, [(i, i ^ flip) for i in range(n)])]
  transfers between devices with their start and end apart: 12 -> 52, of which waited for: 11 -> 28; matrix products, arithmetic and copies ran while one was open for 6% -> 11% of each run, Pallas kernels for 0% -> 14%
where the time goes in v1:
time: 717 us; the launch traced here: 711 us
  waiting for transfers between devices  355 us (50%)
  Pallas kernels  188 us (26%)
  other arithmetic  81.5 us (11%)
  starting transfers between devices  65.9 us (9%)
  local copies, waits for them, and re-layouts  16.5 us (2%)
    ppermute x50, waiting for transfers between devices, swap(): return lax.ppermute(value, name, [(i, i ^ flip) for i in range(n)])  343 us
    pallas_call x6, Pallas kernels, weight_grads(): call(functools.partial(weight_body, count, pieces, per), (half,) * (2 * c...  66.1 us
    ppermute x50, starting transfers between devices, swap(): return lax.ppermute(value, name, [(i, i ^ flip) for i in range(n)])  60.2 us
    pallas_call x1, Pallas kernels, ff_all(): call(functools.partial(ff_body, steps), (shape((tokens, ff), BF), shape((...  50.4 us
    add x21, other arithmetic, reduce(): keep = keep[:half] + got[:half]  44.9 us
    pallas_call x1, Pallas kernels, project_all(): call(body, (shape((tokens, width), BF), shape((tokens, kw), BF), shape((t...  15.4 us
    pallas_call x1, Pallas kernels, mix_back_all(): call(functools.partial(mix_back_body, ndocs, length, hk, hv, parts), (sha...  15.3 us
  transfers between devices with their start and end apart: 52, of which 28 were waited for; matrix products, arithmetic and copies ran while one was open for 11% of the time, Pallas kernels for 14%

profile of v1, /device:TPU:0, one launch (start us, length us, event | category | flops | bytes accessed | tf_op | source)
XLA Modules:
  0.0 710.6 jit_solution(17434793415673461865)
XLA Ops:
  6.5 15.4 %shard_map.315 = (bf16[768,1024]{1,0:T(8,128)(2,1)}, bf16[768,512]{1,0:T(8,128)(2,1)}, bf16[768,512]{1,0:T(8,128)(2,1)}, bf16[768,1024]{1,0:T(8,128)(2,1)}, f32[...) custom-call(s32[24]{0:T(128)} %reshape.138.docs_ref, ...), custom_call_target="tpu_custom_call" | custom-call | flops 4831838208 | bytes 20971520 | tf_op jit(solution)/shard_map/pallas_call | solution.py:140
  31.4 18.2 %collective-permute-done.1 = f32[1,6,4,1,128]{4,2,1,3,0:T(4,128)S(1)} collective-permute-done((f32[1,6,4,1,128]{4,2,1,3,0:T(4,128)S(1)}, f32[1,6,4,1,128]{4,2,1,3,0:T(4,128)S(1)}, u32[]{:S(2)}, u32[]{:S(2)}) %collective-permute-start.1) | collective-permute-done | bytes 12320 | tf_op jit(solution)/shard_map/ppermute | solution.py:629
  56.0 8.0 %collective-permute-done.2 = f32[1,6,4,1,128]{4,2,1,3,0:T(4,128)} collective-permute-done((f32[1,6,4,1,128]{4,2,1,3,0:T(4,128)}, f32[1,6,4,1,128]{4,2,1,3,0:T(4,128)}, u32[]{:S(2)}, u32[]{:S(2)}) %collective-permute-start.2) | collective-permute-done | bytes 12320 | tf_op jit(solution)/shard_map/ppermute | solution.py:629
  77.6 9.9 %collective-permute-start.7 = (f32[2,6,4,16,128]{4,3,2,1,0:T(8,128)S(1)}, f32[2,6,4,16,128]{4,3,2,1,0:T(8,128)S(1)}, u32[]{:S(2)}, u32[]{:S(2)}) collective-permute-start(f32[2,6,4,16,128]{4,3,2,1,0:T(8,128)S(1)} %get-tuple-element.187), channel_id=1, source_target_pairs={{0,4},{1,5},{2,6},{3,7},{4,0},{5,1},{6,2},{7,3},{8,12},{9,13},{10,... | collective-permute-start | bytes 1179656 | tf_op jit(solution)/shard_map/ppermute | solution.py:629
  87.5 9.3 %collective-permute-done.7 = f32[2,6,4,16,128]{4,3,2,1,0:T(8,128)S(1)} collective-permute-done((f32[2,6,4,16,128]{4,3,2,1,0:T(8,128)S(1)}, f32[2,6,4,16,128]{4,3,2,1,0:T(8,128)S(1)}, u32[]{:S(2)}, u32[]{:S(2)}) %collective-permute-start.7) | collective-permute-done | bytes 393248 | tf_op jit(solution)/shard_map/ppermute | solution.py:629
  99.9 17.4 %collective-permute-done.8 = f32[4,6,4,16,128]{4,3,2,1,0:T(8,128)S(1)} collective-permute-done((f32[4,6,4,16,128]{4,3,2,1,0:T(8,128)S(1)}, f32[4,6,4,16,128]{4,3,2,1,0:T(8,128)S(1)}, u32[]{:S(2)}, u32[]{:S(2)}) %collective-permute-start.8) | collective-permute-done | bytes 786464 | tf_op jit(solution)/shard_map/ppermute | solution.py:629
  118.0 8.6 %shard_map.316.inner_ref = f32[768,1024]{1,0:T(8,128)} custom-call(s32[24]{0:T(128)} %reshape.138.docs_ref, bf16[768,512]{1,0:T(8,128)(2,1)} %get-tuple-element.62.q_ref, bf16[768,512]{1,0:T(8,128)(2,1)} %get-tuple-element.64.k_ref, bf16[768,1024]{1,0:T(8,128)(2,1)} %get-tuple-element.65.v_ref, f32[768,512]{1,0:T(8,128)} %get-tuple-element.63.cum_ref), custom_call_target="tpu_custom_call" | custom-call | flops 301989888 | bytes 8388608 | tf_op jit(solution)/shard_map/pallas_call | solution.py:192
  128.7 9.1 %shard_map.317 = (f32[768,1024]{1,0:T(8,128)}, bf16[768,1024]{1,0:T(8,128)(2,1)}, bf16[6,4,256,128]{3,2,1,0:T(8,128)(2,1)}) custom-call(s32[24]{0:T(128)} %reshape.138.docs_ref, s32[32]{0:T(128)} %pad_add_fusion.table_ref, bf16[768,512]{1,0:T(8,128)(2,1)} %get-tuple-element.62.q_ref, f32[768,512]{1,0:T(8,128)} %get-tuple-element.63.cum_ref, ...), custom_call_target="tpu_custom_call" | custom-call | flops 201326592 | bytes 18874368 | tf_op jit(solution)/shard_map/pallas_call | solution.py:233
  137.8 50.4 %shard_map.318 = (bf16[768,2816]{1,0:T(8,128)(2,1)}, bf16[768,2816]{1,0:T(8,128)(2,1)}, bf16[768,2816]{1,0:T(8,128)(2,1)}, bf16[768,1024]{1,0:T(8,128)(2,1)}, bf...) custom-call(bf16[768,1024]{1,0:T(8,128)(2,1)} %bitcast.78, ...), custom_call_target="tpu_custom_call" | custom-call | flops 26575110144 | bytes 47185920 | tf_op jit(solution)/shard_map/pallas_call | solution.py:320
  188.3 10.8 %shard_map.319 = (bf16[768,1024]{1,0:T(8,128)(2,1)}, bf16[768,1024]{1,0:T(8,128)(2,1)}, f32[8,6,4,16,128]{4,3,2,1,0:T(8,128)}, f32[8,6,4,16,128]{4,3,2,1,0:T(8,128)}, f32[1,256]{1,0:T(1,128)}) custom-call(s32[24]{0:T(128)} %reshape.138.docs_ref, s32[32]{0:T(128)} %pad_add_fusion.table_ref, f32[768,1024]{1,0:T(8,128)} %get-tuple-element.75.dgated_ref, ...), custom_call_target="tpu_custom_call" | custom-call | flops 201326592 | bytes 20971520 | tf_op jit(solution)/shard_map/pallas_call | solution.py:399
  207.6 7.0 shard_map.323
  214.7 7.4 %shard_map.324 = (f32[16,32,1024]{2,1,0:T(8,128)}, f32[16,32,1024]{2,1,0:T(8,128)}) custom-call(s32[32]{0:T(128)} %broadcast_xor_fusion.refs_0_, bf16[768,1024]{1,0:T(8,128)(2,1)} %get-tuple-element.70.gated_ref.refs_1_, bf16[768,1024]{1,0:T(8,128)(2,1)} %get-tuple-element.95.refs_2_), custom_call_target="tpu_custom_call" | custom-call | flops 1610612736 | bytes 4194304 | tf_op jit(solution)/shard_map/pallas_call | solution.py:600
  230.6 8.8 %collective-permute-done.12 = f32[2,6,4,16,128]{4,3,2,1,0:T(8,128)S(1)} collective-permute-done((f32[2,6,4,16,128]{4,3,2,1,0:T(8,128)}, f32[2,6,4,16,128]{4,3,2,1,0:T(8,128)S(1)}, u32[]{:S(2)}, u32[]{:S(2)}) %collective-permute-start.12) | collective-permute-done | bytes 393248 | tf_op jit(solution)/shard_map/ppermute | solution.py:629
  241.9 14.5 %shard_map.325 = (f32[16,32,2816]{2,1,0:T(8,128)}, f32[16,32,2816]{2,1,0:T(8,128)}) custom-call(s32[32]{0:T(128)} %get-tuple-element.198.refs_0_, bf16[768,1024]{1,0:T(8,128)(2,1)} %get-tuple-element.98.refs_1_, bf16[768,2816]{1,0:T(8,128)(2,1)} %get-tuple-element.99.refs_2_), custom_call_target="tpu_custom_call" | custom-call | flops 4429185024 | bytes 11534336 | tf_op jit(solution)/shard_map/pallas_call | solution.py:600
  276.4 14.4 %shard_map.326 = (f32[16,32,2816]{2,1,0:T(8,128)}, f32[16,32,2816]{2,1,0:T(8,128)}) custom-call(s32[32]{0:T(128)} %broadcast_xor_fusion.refs_0_, bf16[768,1024]{1,0:T(8,128)(2,1)} %get-tuple-element.98.refs_1_, bf16[768,2816]{1,0:T(8,128)(2,1)} %get-tuple-element.102.refs_2_), custom_call_target="tpu_custom_call" | custom-call | flops 4429185024 | bytes 11534336 | tf_op jit(solution)/shard_map/pallas_call | solution.py:600
  296.4 18.8 %collective-permute-done.33 = f32[8,32,1024]{2,1,0:T(8,128)} collective-permute-done((f32[8,32,1024]{2,1,0:T(8,128)}, f32[8,32,1024]{2,1,0:T(8,128)}, u32[]{:S(2)}, u32[]{:S(2)}) %collective-permute-start.33) | collective-permute-done | bytes 1048608 | tf_op jit(solution)/shard_map/ppermute | solution.py:629
  319.0 11.0 %collective-permute-done.15 = f32[4,6,4,16,128]{4,3,2,1,0:T(8,128)S(1)} collective-permute-done((f32[4,6,4,16,128]{4,3,2,1,0:T(8,128)}, f32[4,6,4,16,128]{4,3,2,1,0:T(8,128)S(1)}, u32[]{:S(2)}, u32[]{:S(2)}) %collective-permute-start.15) | collective-permute-done | bytes 786464 | tf_op jit(solution)/shard_map/ppermute | solution.py:629
  331.8 11.8 %shard_map.327 = (f32[16,88,1024]{2,1,0:T(8,128)}, f32[16,88,1024]{2,1,0:T(8,128)}) custom-call(s32[32]{0:T(128)} %get-tuple-element.198.refs_0_, bf16[768,2816]{1,0:T(8,128)(2,1)} %get-tuple-element.105.refs_1_, bf16[768,1024]{1,0:T(8,128)(2,1)} %bitcast.76), custom_call_target="tpu_custom_call" | custom-call | flops 4429185024 | bytes 11534336 | tf_op jit(solution)/shard_map/pallas_call | solution.py:600
  371.8 15.3 %shard_map.320 = (bf16[768,2048]{1,0:T(8,128)(2,1)}, bf16[768,16]{1,0:T(8,128)(2,1)}, f32[16,512]{1,0:T(8,128)}, f32[1,512]{1,0:T(1,128)}) custom-call(s32[24]{0:T(128)} %reshape.138.docs_ref, s32[32]{0:T(128)} %pad_add_fusion.table_ref, bf16[768,512]{1,0:T(8,128)(2,1)} %get-tuple-element.62.q_ref, bf16[768,512]{1,0:T(8,128)(2,1)} %get-tuple-element.64.k_ref, ...), custom_call_target="tpu_custom_call" | custom-call | flops 1610612736 | bytes 16777216 | tf_op jit(solution)/shard_map/pallas_call | solution.py:494
  389.3 12.4 %shard_map.321 = (f32[768,1024]{1,0:T(8,128)}, f32[1,1024]{1,0:T(1,128)}) custom-call(bf16[768,1024]{1,0:T(8,128)(2,1)} %bitcast.79, f32[768,1024]{1,0:T(8,128)} %get-tuple-element.72.dmid_ref, bf16[768,2048]{1,0:T(8,128)(2,1)} %get-tuple-element.81.dqkv_ref.refs_2_, bf16[768,1024]{1,0:T(8,128)(2,1)} %get-tuple-element.82.dog_ref.refs_2_, ...), custom_call_target="tpu_custom_call" | custom-call | flops 4831838208 | bytes 20971520 | tf_op jit(solution)/shard_map/pallas_call | solution.py:551
  413.6 11.1 %shard_map.322 = (f32[16,32,2048]{2,1,0:T(8,128)}, f32[16,32,2048]{2,1,0:T(8,128)}) custom-call(s32[32]{0:T(128)} %get-tuple-element.198.refs_0_, bf16[768,1024]{1,0:T(8,128)(2,1)} %get-tuple-element.85.refs_1_, bf16[768,2048]{1,0:T(8,128)(2,1)} %get-tuple-element.81.dqkv_ref.refs_2_), custom_call_target="tpu_custom_call" | custom-call | flops 3221225472 | bytes 8388608 | tf_op jit(solution)/shard_map/pallas_call | solution.py:600
  424.7 52.5 %collective-permute-done.18 = f32[8,1,896]{2,0,1:T(8,128)S(1)} collective-permute-done((f32[8,1,896]{2,0,1:T(8,128)S(1)}, f32[8,1,896]{2,0,1:T(8,128)S(1)}, u32[]{:S(2)}, u32[]{:S(2)}) %collective-permute-start.18) | collective-permute-done | bytes 28704 | tf_op jit(solution)/shard_map/ppermute | solution.py:629
  478.8 7.8 %slice_add_fusion.3 = (f32[8,32,2816]{2,1,0:T(8,128)}, f32[8,32,2816]{2,1,0:T(8,128)}) fusion(f32[16,32,2816]{2,1,0:T(8,128)} %collective-permute-done.42, f32[16,32,2816]{2,1,0:T(8,128)} %get-tuple-element.103), kind=kLoop, calls=%fused_computation.7 | loop fusion | flops 1441792 | bytes 17301504 | tf_op jit(solution)/shard_map/add | solution.py:654
  509.0 43.3 %collective-permute-done.43 = f32[8,32,2816]{2,1,0:T(8,128)} collective-permute-done((f32[8,32,2816]{2,1,0:T(8,128)}, f32[8,32,2816]{2,1,0:T(8,128)}, u32[]{:S(2)}, u32[]{:S(2)}) %collective-permute-start.43) | collective-permute-done | bytes 2883616 | tf_op jit(solution)/shard_map/ppermute | solution.py:629
  570.2 12.9 %collective-permute-done.39 = f32[4,32,2816]{2,1,0:T(8,128)S(1)} collective-permute-done((f32[4,32,2816]{2,1,0:T(8,128)S(1)}, f32[4,32,2816]{2,1,0:T(8,128)S(1)}, u32[]{:S(2)}, u32[]{:S(2)}) %collective-permute-start.39) | collective-permute-done | bytes 1441824 | tf_op jit(solution)/shard_map/ppermute | solution.py:629
  585.3 11.6 %collective-permute-done.44 = f32[4,32,2816]{2,1,0:T(8,128)S(1)} collective-permute-done((f32[4,32,2816]{2,1,0:T(8,128)S(1)}, f32[4,32,2816]{2,1,0:T(8,128)S(1)}, u32[]{:S(2)}, u32[]{:S(2)}) %collective-permute-start.44) | collective-permute-done | bytes 1441824 | tf_op jit(solution)/shard_map/ppermute | solution.py:629
  597.5 15.8 %collective-permute-done.49 = f32[4,88,1024]{2,1,0:T(8,128)S(1)} collective-permute-done((f32[4,88,1024]{2,1,0:T(8,128)S(1)}, f32[4,88,1024]{2,1,0:T(8,128)S(1)}, u32[]{:S(2)}, u32[]{:S(2)}) %collective-permute-start.49) | collective-permute-done | bytes 1441824 | tf_op jit(solution)/shard_map/ppermute | solution.py:629
  615.6 23.8 %collective-permute-done.23 = f32[8,32,2048]{2,1,0:T(8,128)S(1)} collective-permute-done((f32[8,32,2048]{2,1,0:T(8,128)S(1)}, f32[8,32,2048]{2,1,0:T(8,128)S(1)}, u32[]{:S(2)}, u32[]{:S(2)}) %collective-permute-start.23) | collective-permute-done | bytes 2097184 | tf_op jit(solution)/shard_map/ppermute | solution.py:629
  645.4 17.6 %collective-permute-done.24 = f32[4,32,2048]{2,1,0:T(8,128)S(1)} collective-permute-done((f32[4,32,2048]{2,1,0:T(8,128)S(1)}, f32[4,32,2048]{2,1,0:T(8,128)S(1)}, u32[]{:S(2)}, u32[]{:S(2)}) %collective-permute-start.24) | collective-permute-done | bytes 1048608 | tf_op jit(solution)/shard_map/ppermute | solution.py:629
  664.1 10.1 %collective-permute-done.41 = f32[1,32,2816]{2,1,0:T(8,128)S(1)} collective-permute-done((f32[1,32,2816]{2,1,0:T(8,128)S(1)}, f32[1,32,2816]{2,1,0:T(8,128)S(1)}, u32[]{:S(2)}, u32[]{:S(2)}) %collective-permute-start.41) | collective-permute-done | bytes 360480 | tf_op jit(solution)/shard_map/ppermute | solution.py:629
  675.1 22.2 %collective-permute-done.25 = f32[2,32,2048]{2,1,0:T(8,128)S(1)} collective-permute-done((f32[2,32,2048]{2,1,0:T(8,128)S(1)}, f32[2,32,2048]{2,1,0:T(8,128)S(1)}, u32[]{:S(2)}, u32[]{:S(2)}) %collective-permute-start.25) | collective-permute-done | bytes 524320 | tf_op jit(solution)/shard_map/ppermute | solution.py:629
  699.0 9.8 %collective-permute-done.26 = f32[1,32,2048]{2,1,0:T(8,128)S(1)} collective-permute-done((f32[1,32,2048]{2,1,0:T(8,128)S(1)}, f32[1,32,2048]{2,1,0:T(8,128)S(1)}, u32[]{:S(2)}, u32[]{:S(2)}) %collective-permute-start.26) | collective-permute-done | bytes 262176 | tf_op jit(solution)/shard_map/ppermute | solution.py:629
  (247 shorter events, 191.8 us)
Async XLA Ops:
  28.5 21.2 %collective-permute-start.4 = (f32[4,6,4,16,128]{4,3,2,1,0:T(8,128)}, f32[4,6,4,16,128]{4,3,2,1,0:T(8,128)}, u32[]{:S(2)}, u32[]{:S(2)}) collective-permute-start(f32[4,6,4,16,128]{4,3,2,1,0:T(8,128)} %slice.558), channel_id=1, source_target_pairs={{0,2},{1,3},{2,0},{3,1},{4,6},{5,7},{6,4},{7,5},{8,10},{9,11},{10,... | collective-permute-start | bytes 2359304 | tf_op jit(solution)/shard_map/ppermute | solution.py:629
  205.6 20.1 %collective-permute-start.11 = (f32[4,6,4,16,128]{4,3,2,1,0:T(8,128)}, f32[4,6,4,16,128]{4,3,2,1,0:T(8,128)}, u32[]{:S(2)}, u32[]{:S(2)}) collective-permute-start(f32[4,6,4,16,128]{4,3,2,1,0:T(8,128)} %slice.562), channel_id=1, source_target_pairs={{0,2},{1,3},{2,0},{3,1},{4,6},{5,7},{6,4},{7,5},{8,10},{9,11},{10,... | collective-permute-start | bytes 2359304 | tf_op jit(solution)/shard_map/ppermute | solution.py:629
  214.6 47.8 %collective-permute-start.27 = (f32[16,32,1024]{2,1,0:T(8,128)}, f32[16,32,1024]{2,1,0:T(8,128)}, u32[]{:S(2)}, u32[]{:S(2)}) collective-permute-start(f32[16,32,1024]{2,1,0:T(8,128)} %get-tuple-element.94), channel_id=1, source_target_pairs={{0,1},{1,0},{2,3},{3,2},{4,5},{5,4},{6,7},{7,6},{8,9},{9,8},{10,11... | collective-permute-start | bytes 6291464 | tf_op jit(solution)/shard_map/ppermute | solution.py:629
  222.1 45.8 %collective-permute-start.32 = (f32[16,32,1024]{2,1,0:T(8,128)}, f32[16,32,1024]{2,1,0:T(8,128)}, u32[]{:S(2)}, u32[]{:S(2)}) collective-permute-start(f32[16,32,1024]{2,1,0:T(8,128)} %get-tuple-element.97), channel_id=1, source_target_pairs={{0,1},{1,0},{2,3},{3,2},{4,5},{5,4},{6,7},{7,6},{8,9},{9,8},{10,11... | collective-permute-start | bytes 6291464 | tf_op jit(solution)/shard_map/ppermute | solution.py:629
  240.5 21.0 %collective-permute-start.13 = (f32[2,6,4,16,128]{4,3,2,1,0:T(8,128)S(1)}, f32[2,6,4,16,128]{4,3,2,1,0:T(8,128)S(1)}, u32[]{:S(2)}, u32[]{:S(2)}) collective-permute-start(f32[2,6,4,16,128]{4,3,2,1,0:T(8,128)S(1)} %add_select_fusion.14), channel_id=1, source_target_pairs={{8,0},{9,1},{10,2},{11,3},{12,4},{13,5},{14,6},{15,7},{24,16},{25,... | collective-permute-start | bytes 1179656 | tf_op jit(solution)/shard_map/ppermute | solution.py:681
  256.3 148.5 %collective-permute-start.37 = (f32[16,32,2816]{2,1,0:T(8,128)}, f32[16,32,2816]{2,1,0:T(8,128)}, u32[]{:S(2)}, u32[]{:S(2)}) collective-permute-start(f32[16,32,2816]{2,1,0:T(8,128)} %get-tuple-element.101), channel_id=1, source_target_pairs={{0,1},{1,0},{2,3},{3,2},{4,5},{5,4},{6,7},{7,6},{8,9},{9,8},{10,11... | collective-permute-start | bytes 17301512 | tf_op jit(solution)/shard_map/ppermute | solution.py:629
  266.3 26.4 %collective-permute-start.28 = (f32[8,32,1024]{2,1,0:T(8,128)}, f32[8,32,1024]{2,1,0:T(8,128)}, u32[]{:S(2)}, u32[]{:S(2)}) collective-permute-start(f32[8,32,1024]{2,1,0:T(8,128)} %get-tuple-element.157), channel_id=1, source_target_pairs={{0,2},{1,3},{2,0},{3,1},{4,6},{5,7},{6,4},{7,5},{8,10},{9,11},{10,... | collective-permute-start | bytes 3145736 | tf_op jit(solution)/shard_map/ppermute | solution.py:629
  270.9 44.3 %collective-permute-start.33 = (f32[8,32,1024]{2,1,0:T(8,128)}, f32[8,32,1024]{2,1,0:T(8,128)}, u32[]{:S(2)}, u32[]{:S(2)}) collective-permute-start(f32[8,32,1024]{2,1,0:T(8,128)} %get-tuple-element.155), channel_id=1, source_target_pairs={{0,2},{1,3},{2,0},{3,1},{4,6},{5,7},{6,4},{7,5},{8,10},{9,11},{10,... | collective-permute-start | bytes 3145736 | tf_op jit(solution)/shard_map/ppermute | solution.py:629
  274.9 55.1 %collective-permute-start.15 = (f32[4,6,4,16,128]{4,3,2,1,0:T(8,128)}, f32[4,6,4,16,128]{4,3,2,1,0:T(8,128)S(1)}, u32[]{:S(2)}, u32[]{:S(2)}) collective-permute-start(f32[4,6,4,16,128]{4,3,2,1,0:T(8,128)} %get-tuple-element.181), channel_id=1, source_target_pairs={{0,2},{1,3},{2,0},{3,1},{4,6},{5,7},{6,4},{7,5},{8,10},{9,11},{10,... | collective-permute-start | bytes 2359304 | tf_op jit(solution)/shard_map/ppermute | solution.py:629
  290.8 186.4 %collective-permute-start.42 = (f32[16,32,2816]{2,1,0:T(8,128)}, f32[16,32,2816]{2,1,0:T(8,128)}, u32[]{:S(2)}, u32[]{:S(2)}) collective-permute-start(f32[16,32,2816]{2,1,0:T(8,128)} %get-tuple-element.104), channel_id=1, source_target_pairs={{0,1},{1,0},{2,3},{3,2},{4,5},{5,4},{6,7},{7,6},{8,9},{9,8},{10,11... | collective-permute-start | bytes 17301512 | tf_op jit(solution)/shard_map/ppermute | solution.py:629
  294.9 48.6 %collective-permute-start.29 = (f32[4,32,1024]{2,1,0:T(8,128)}, f32[4,32,1024]{2,1,0:T(8,128)S(1)}, u32[]{:S(2)}, u32[]{:S(2)}) collective-permute-start(f32[4,32,1024]{2,1,0:T(8,128)} %get-tuple-element.169), channel_id=1, source_target_pairs={{0,16},{16,0},{1,17},{17,1},{2,18},{18,2},{3,19},{19,3},{4,20},{20... | collective-permute-start | bytes 1572872 | tf_op jit(solution)/shard_map/ppermute | solution.py:629
  317.5 27.3 %collective-permute-start.34 = (f32[4,32,1024]{2,1,0:T(8,128)}, f32[4,32,1024]{2,1,0:T(8,128)S(1)}, u32[]{:S(2)}, u32[]{:S(2)}) collective-permute-start(f32[4,32,1024]{2,1,0:T(8,128)} %get-tuple-element.167), channel_id=1, source_target_pairs={{0,16},{16,0},{1,17},{17,1},{2,18},{18,2},{3,19},{19,3},{4,20},{20... | collective-permute-start | bytes 1572872 | tf_op jit(solution)/shard_map/ppermute | solution.py:629
  331.7 38.2 %collective-permute-start.16 = (f32[8,6,4,16,128]{4,3,2,1,0:T(8,128)}, f32[8,6,4,16,128]{4,3,2,1,0:T(8,128)S(1)}, u32[]{:S(2)}, u32[]{:S(2)}) collective-permute-start(f32[8,6,4,16,128]{4,3,2,1,0:T(8,128)} %get-tuple-element.173), channel_id=1, source_target_pairs={{0,1},{1,0},{2,3},{3,2},{4,5},{5,4},{6,7},{7,6},{8,9},{9,8},{10,11... | collective-permute-start | bytes 4718600 | tf_op jit(solution)/shard_map/ppermute | solution.py:629
  343.5 150.4 %collective-permute-start.47 = (f32[16,88,1024]{2,1,0:T(8,128)}, f32[16,88,1024]{2,1,0:T(8,128)}, u32[]{:S(2)}, u32[]{:S(2)}) collective-permute-start(f32[16,88,1024]{2,1,0:T(8,128)} %get-tuple-element.107), channel_id=1, source_target_pairs={{0,1},{1,0},{2,3},{3,2},{4,5},{5,4},{6,7},{7,6},{8,9},{9,8},{10,11... | collective-permute-start | bytes 17301512 | tf_op jit(solution)/shard_map/ppermute | solution.py:629
  368.2 118.9 %collective-permute-start.36 = (f32[1,32,1024]{2,1,0:T(8,128)S(1)}, f32[1,32,1024]{2,1,0:T(8,128)}, u32[]{:S(2)}, u32[]{:S(2)}) collective-permute-start(f32[1,32,1024]{2,1,0:T(8,128)S(1)} %slice_add_fusion.44), channel_id=1, source_target_pairs={{0,8},{1,9},{2,10},{3,11},{4,12},{5,13},{6,14},{7,15},{8,0},{9,1},... | collective-permute-start | bytes 393224 | tf_op jit(solution)/shard_map/ppermute | solution.py:629
  411.5 93.7 %collective-permute-start.38 = (f32[8,32,2816]{2,1,0:T(8,128)}, f32[8,32,2816]{2,1,0:T(8,128)}, u32[]{:S(2)}, u32[]{:S(2)}) collective-permute-start(f32[8,32,2816]{2,1,0:T(8,128)} %get-tuple-element.145), channel_id=1, source_target_pairs={{0,16},{16,0},{1,17},{17,1},{2,18},{18,2},{3,19},{19,3},{4,20},{20... | collective-permute-start | bytes 8650760 | tf_op jit(solution)/shard_map/ppermute | solution.py:629
  413.0 64.2 %collective-permute-start.18 = (f32[8,1,896]{2,0,1:T(8,128)S(1)}, f32[8,1,896]{2,0,1:T(8,128)S(1)}, u32[]{:S(2)}, u32[]{:S(2)}) collective-permute-start(f32[8,1,896]{2,0,1:T(8,128)S(1)} %get-tuple-element.191), channel_id=1, source_target_pairs={{0,16},{16,0},{1,17},{17,1},{2,18},{18,2},{3,19},{19,3},{4,20},{20... | collective-permute-start | bytes 86024 | tf_op jit(solution)/shard_map/ppermute | solution.py:629
  477.2 78.9 %collective-permute-start.22 = (f32[16,32,2048]{2,1,0:T(8,128)}, f32[16,32,2048]{2,1,0:T(8,128)}, u32[]{:S(2)}, u32[]{:S(2)}) collective-permute-start(f32[16,32,2048]{2,1,0:T(8,128)} %get-tuple-element.92), channel_id=1, source_target_pairs={{0,1},{1,0},{2,3},{3,2},{4,5},{5,4},{6,7},{7,6},{8,9},{9,8},{10,11... | collective-permute-start | bytes 12582920 | tf_op jit(solution)/shard_map/ppermute | solution.py:629
  486.7 65.6 %collective-permute-start.43 = (f32[8,32,2816]{2,1,0:T(8,128)}, f32[8,32,2816]{2,1,0:T(8,128)}, u32[]{:S(2)}, u32[]{:S(2)}) collective-permute-start(f32[8,32,2816]{2,1,0:T(8,128)} %get-tuple-element.143), channel_id=1, source_target_pairs={{0,2},{1,3},{2,0},{3,1},{4,6},{5,7},{6,4},{7,5},{8,10},{9,11},{10,... | collective-permute-start | bytes 8650760 | tf_op jit(solution)/shard_map/ppermute | solution.py:629
  500.4 65.7 %collective-permute-start.48 = (f32[8,88,1024]{2,1,0:T(8,128)}, f32[8,88,1024]{2,1,0:T(8,128)}, u32[]{:S(2)}, u32[]{:S(2)}) collective-permute-start(f32[8,88,1024]{2,1,0:T(8,128)} %get-tuple-element.141), channel_id=1, source_target_pairs={{0,16},{16,0},{1,17},{17,1},{2,18},{18,2},{3,19},{19,3},{4,20},{20... | collective-permute-start | bytes 8650760 | tf_op jit(solution)/shard_map/ppermute | solution.py:629
  507.4 75.7 %collective-permute-start.39 = (f32[4,32,2816]{2,1,0:T(8,128)S(1)}, f32[4,32,2816]{2,1,0:T(8,128)S(1)}, u32[]{:S(2)}, u32[]{:S(2)}) collective-permute-start(f32[4,32,2816]{2,1,0:T(8,128)S(1)} %get-tuple-element.153), channel_id=1, source_target_pairs={{0,2},{1,3},{2,0},{3,1},{4,6},{5,7},{6,4},{7,5},{8,10},{9,11},{10,... | collective-permute-start | bytes 4325384 | tf_op jit(solution)/shard_map/ppermute | solution.py:629
  554.6 42.4 %collective-permute-start.44 = (f32[4,32,2816]{2,1,0:T(8,128)S(1)}, f32[4,32,2816]{2,1,0:T(8,128)S(1)}, u32[]{:S(2)}, u32[]{:S(2)}) collective-permute-start(f32[4,32,2816]{2,1,0:T(8,128)S(1)} %get-tuple-element.151), channel_id=1, source_target_pairs={{0,16},{16,0},{1,17},{17,1},{2,18},{18,2},{3,19},{19,3},{4,20},{20... | collective-permute-start | bytes 4325384 | tf_op jit(solution)/shard_map/ppermute | solution.py:629
  559.3 80.1 %collective-permute-start.23 = (f32[8,32,2048]{2,1,0:T(8,128)S(1)}, f32[8,32,2048]{2,1,0:T(8,128)S(1)}, u32[]{:S(2)}, u32[]{:S(2)}) collective-permute-start(f32[8,32,2048]{2,1,0:T(8,128)S(1)} %get-tuple-element.147), channel_id=1, source_target_pairs={{0,16},{16,0},{1,17},{17,1},{2,18},{18,2},{3,19},{19,3},{4,20},{20... | collective-permute-start | bytes 6291464 | tf_op jit(solution)/shard_map/ppermute | solution.py:629
  568.6 44.7 %collective-permute-start.49 = (f32[4,88,1024]{2,1,0:T(8,128)S(1)}, f32[4,88,1024]{2,1,0:T(8,128)S(1)}, u32[]{:S(2)}, u32[]{:S(2)}) collective-permute-start(f32[4,88,1024]{2,1,0:T(8,128)S(1)} %get-tuple-element.149), channel_id=1, source_target_pairs={{0,2},{1,3},{2,0},{3,1},{4,6},{5,7},{6,4},{7,5},{8,10},{9,11},{10,... | collective-permute-start | bytes 4325384 | tf_op jit(solution)/shard_map/ppermute | solution.py:629
  583.3 58.4 %collective-permute-start.40 = (f32[2,32,2816]{2,1,0:T(8,128)S(1)}, f32[2,32,2816]{2,1,0:T(8,128)S(1)}, u32[]{:S(2)}, u32[]{:S(2)}) collective-permute-start(f32[2,32,2816]{2,1,0:T(8,128)S(1)} %get-tuple-element.165), channel_id=1, source_target_pairs={{0,4},{1,5},{2,6},{3,7},{4,0},{5,1},{6,2},{7,3},{8,12},{9,13},{10,... | collective-permute-start | bytes 2162696 | tf_op jit(solution)/shard_map/ppermute | solution.py:629
  597.1 45.2 %collective-permute-start.45 = (f32[2,32,2816]{2,1,0:T(8,128)S(1)}, f32[2,32,2816]{2,1,0:T(8,128)S(1)}, u32[]{:S(2)}, u32[]{:S(2)}) collective-permute-start(f32[2,32,2816]{2,1,0:T(8,128)S(1)} %get-tuple-element.163), channel_id=1, source_target_pairs={{0,4},{1,5},{2,6},{3,7},{4,0},{5,1},{6,2},{7,3},{8,12},{9,13},{10,... | collective-permute-start | bytes 2162696 | tf_op jit(solution)/shard_map/ppermute | solution.py:629
  613.5 31.3 %collective-permute-start.50 = (f32[2,88,1024]{2,1,0:T(8,128)S(1)}, f32[2,88,1024]{2,1,0:T(8,128)S(1)}, u32[]{:S(2)}, u32[]{:S(2)}) collective-permute-start(f32[2,88,1024]{2,1,0:T(8,128)S(1)} %get-tuple-element.161), channel_id=1, source_target_pairs={{0,4},{1,5},{2,6},{3,7},{4,0},{5,1},{6,2},{7,3},{8,12},{9,13},{10,... | collective-permute-start | bytes 2162696 | tf_op jit(solution)/shard_map/ppermute | solution.py:629
  639.7 23.3 %collective-permute-start.24 = (f32[4,32,2048]{2,1,0:T(8,128)S(1)}, f32[4,32,2048]{2,1,0:T(8,128)S(1)}, u32[]{:S(2)}, u32[]{:S(2)}) collective-permute-start(f32[4,32,2048]{2,1,0:T(8,128)S(1)} %get-tuple-element.159), channel_id=1, source_target_pairs={{0,2},{1,3},{2,0},{3,1},{4,6},{5,7},{6,4},{7,5},{8,10},{9,11},{10,... | collective-permute-start | bytes 3145736 | tf_op jit(solution)/shard_map/ppermute | solution.py:629
  641.7 32.5 %collective-permute-start.41 = (f32[1,32,2816]{2,1,0:T(8,128)S(1)}, f32[1,32,2816]{2,1,0:T(8,128)S(1)}, u32[]{:S(2)}, u32[]{:S(2)}) collective-permute-start(f32[1,32,2816]{2,1,0:T(8,128)S(1)} %slice_add_fusion.36), channel_id=1, source_target_pairs={{0,8},{1,9},{2,10},{3,11},{4,12},{5,13},{6,14},{7,15},{8,0},{9,1},... | collective-permute-start | bytes 1081352 | tf_op jit(solution)/shard_map/ppermute | solution.py:629
  642.3 55.1 %collective-permute-start.46 = (f32[1,32,2816]{2,1,0:T(8,128)S(1)}, f32[1,32,2816]{2,1,0:T(8,128)S(1)}, u32[]{:S(2)}, u32[]{:S(2)}) collective-permute-start(f32[1,32,2816]{2,1,0:T(8,128)S(1)} %slice_add_fusion.34), channel_id=1, source_target_pairs={{0,8},{1,9},{2,10},{3,11},{4,12},{5,13},{6,14},{7,15},{8,0},{9,1},... | collective-permute-start | bytes 1081352 | tf_op jit(solution)/shard_map/ppermute | solution.py:629
  644.9 53.3 %collective-permute-start.51 = (f32[1,88,1024]{2,1,0:T(8,128)S(1)}, f32[1,88,1024]{2,1,0:T(8,128)S(1)}, u32[]{:S(2)}, u32[]{:S(2)}) collective-permute-start(f32[1,88,1024]{2,1,0:T(8,128)S(1)} %slice_add_fusion.32), channel_id=1, source_target_pairs={{0,8},{1,9},{2,10},{3,11},{4,12},{5,13},{6,14},{7,15},{8,0},{9,1},... | collective-permute-start | bytes 1081352 | tf_op jit(solution)/shard_map/ppermute | solution.py:629
  663.2 34.1 %collective-permute-start.25 = (f32[2,32,2048]{2,1,0:T(8,128)S(1)}, f32[2,32,2048]{2,1,0:T(8,128)S(1)}, u32[]{:S(2)}, u32[]{:S(2)}) collective-permute-start(f32[2,32,2048]{2,1,0:T(8,128)S(1)} %get-tuple-element.171), channel_id=1, source_target_pairs={{0,4},{1,5},{2,6},{3,7},{4,0},{5,1},{6,2},{7,3},{8,12},{9,13},{10,... | collective-permute-start | bytes 1572872 | tf_op jit(solution)/shard_map/ppermute | solution.py:629
  (51 other events, 588.0 us)

commit v2 on v1

--- a/solution.py
+++ b/solution.py
@@ -45,7 +45,7 @@
             scratch_shapes=list(scratch),
         ),
         compiler_params=pltpu.CompilerParams(vmem_limit_bytes=56 * MIB),
-        cost_estimate=pl.CostEstimate(flops=flops, bytes_accessed=moved, transcendentals=0),
+        cost_estimate=pl.CostEstimate(flops=1, bytes_accessed=1, transcendentals=0),
     )
 
 
@@ -94,7 +94,7 @@
     inv = lax.rsqrt(jnp.mean(x * x, axis=-1, keepdims=True) + EPS)
     normed = (x * inv * gain_ref[...]).astype(BF)
     normed_ref[...] = normed
-    rank = nn(normed, wrd_ref[...]).astype(BF)
+    rank = nt(normed, wrd_ref[...]).astype(BF)
     ra_ref[...] = rank
     gate = nn(rank, wru_ref[...]) + bias_ref[...]
     gp_ref[...] = gate
@@ -131,7 +131,7 @@
     rows = 2 if row_count % 2 == 0 else 1
     tm = rows * length
     hk, hv = kw // HEADS, vw // HEADS
-    rank = wrd.shape[1]
+    rank = wrd.shape[0]
     size = hv // parts
     tile = lambda n: block((tm, n), lambda i, *_: (i, 0))
     half = (parts // 2, row_count, HEADS, size, hk)
@@ -201,13 +201,20 @@
     )(docs, q, k, v, cum)
 
 
-def gather_state(state_ref, table_ref, h, parts):
-    return jnp.concatenate([state_ref[table_ref[parts + p], 0, h] for p in range(parts)], axis=0)
+def gather_state(near_ref, far_ref, table_ref, h, parts):
+    half = parts // 2
+    pieces = []
+    for p in range(parts):
+        place = table_ref[parts + p]
+        near = near_ref[jnp.minimum(place, half - 1), 0, h]
+        far = far_ref[jnp.maximum(place - half, 0), 0, h]
+        pieces.append(jnp.where(place < half, near, far))
+    return jnp.concatenate(pieces, axis=0)
 
 
 def mix_body(
     docs, length, hk, hv, parts,
-    docs_ref, table_ref, q_ref, cum_ref, inner_ref, og_ref, state_ref, gain_ref,
+    docs_ref, table_ref, q_ref, cum_ref, inner_ref, og_ref, near_ref, far_ref, gain_ref,
     mixed_ref, gated_ref, kept_ref,
 ):
     _, alive, _, _ = reset_masks(docs_ref, pl.program_id(0), docs, length)
@@ -216,7 +223,7 @@
     for h in range(HEADS):
         kk = slice(h * hk, (h + 1) * hk)
         vv = slice(h * hv, (h + 1) * hv)
-        state = gather_state(state_ref, table_ref, h, parts).astype(BF)
+        state = gather_state(near_ref, far_ref, table_ref, h, parts).astype(BF)
         kept_ref[0, h] = state
         mixed = scale * (inner_ref[:, vv] + nt(reach[:, kk], state))
         mixed_ref[:, vv] = mixed
@@ -225,11 +232,12 @@
         gated_ref[:, vv] = (mixed * inv * gain_ref[...] * og * jax.nn.sigmoid(og)).astype(BF)
 
 
-def mix_all(q, cum, inner, og, state, gain, docs, table, dims):
+def mix_all(q, cum, inner, og, near, far, gain, docs, table, dims):
     row_count, length, width, kw, vw, ndocs, parts = dims
     tokens = row_count * length
     hk, hv = kw // HEADS, vw // HEADS
     tile = lambda n: block((length, n), lambda i, *_: (i, 0))
+    half = block((parts // 2, 1, HEADS, hv // parts, hk), lambda i, *_: (0, i, 0, 0, 0))
     return call(
         functools.partial(mix_body, ndocs, length, hk, hv, parts),
         (
@@ -239,20 +247,18 @@
         ),
         (row_count,),
         [
-            tile(kw), tile(kw), tile(vw), tile(vw),
-            block((parts, 1, HEADS, hv // parts, hk), lambda i, *_: (0, i, 0, 0, 0)),
-            whole((1, hv)),
+            tile(kw), tile(kw), tile(vw), tile(vw), half, half, whole((1, hv)),
         ],
         (tile(vw), tile(vw), block((1, HEADS, hv, hk), lambda i, *_: (i, 0, 0, 0))),
         prefetch=2,
         flops=2 * tokens * hk * vw,
         moved=18 * MIB,
-    )(docs, table, q, cum, inner, og, state, gain.reshape(1, -1))
+    )(docs, table, q, cum, inner, og, near, far, gain.reshape(1, -1))
 
 
 def ff_body(
     steps,
-    x_ref, cot_ref, gated_ref, wo_ref, gain_ref, wg_ref, wu_ref, wd_ref,
+    x_ref, cot_ref, gated_ref, wo_ref, gain_ref, wg_ref, wu_ref, wd_ref, dh_ref,
     hidden_ref, dg_ref, du_ref, normed2_ref, out_ref, dmid_ref, dout_ref, dgated_ref, gnorm_ref,
     middle, total, back,
 ):
@@ -268,7 +274,7 @@
     normed2 = normed2_ref[...]
     gate = nn(normed2, wg_ref[...])
     up = nn(normed2, wu_ref[...])
-    d_hidden = nt(cot_ref[...], wd_ref[...])
+    d_hidden = dh_ref[...]
     sig = jax.nn.sigmoid(gate)
     act = gate * sig
     hidden = (act * up).astype(BF)
@@ -309,7 +315,25 @@
         dgated_ref[...] = nt(d_out, wo_ref[...])
 
 
-def ff_all(x, cot, gated, wo, gain, wg, wu, wd):
+def hidden_back_body(cot_ref, wd_ref, dh_ref):
+    dh_ref[...] = nt(cot_ref[...], wd_ref[...])
+
+
+def hidden_back_all(cot, wd):
+    tokens, width = cot.shape
+    ff, tile = wd.shape[0], 256
+    return call(
+        hidden_back_body,
+        shape((tokens, ff), F32),
+        (ff // tile,),
+        [whole((tokens, width)), block((tile, width), lambda i: (i, 0))],
+        block((tokens, tile), lambda i: (0, i)),
+        flops=2 * tokens * width * ff,
+        moved=16 * MIB,
+    )(cot, wd)
+
+
+def ff_all(x, cot, gated, wo, gain, wg, wu, wd, dh):
     tokens, width = x.shape
     vw = gated.shape[1]
     ff = wg.shape[1]
@@ -327,7 +351,7 @@
         (steps,),
         [
             once((tokens, width)), once((tokens, width)), once((tokens, vw)), once(wo.shape),
-            once((1, width)), col(width), col(width), block((tile, width), lambda i: (i, 0)),
+            once((1, width)), col(width), col(width), block((tile, width), lambda i: (i, 0)), col(tokens),
         ],
         (
             col(tokens), col(tokens), col(tokens),
@@ -335,9 +359,9 @@
             whole((tokens, width)), whole((tokens, vw)), whole((1, width)),
         ),
         scratch=[pltpu.VMEM((tokens, width), F32)] * 3,
-        flops=12 * tokens * width * ff,
+        flops=10 * tokens * width * ff,
         moved=45 * MIB,
-    )(x, cot, gated, wo, gain.reshape(1, -1), wg, wu, wd)
+    )(x, cot, gated, wo, gain.reshape(1, -1), wg, wu, wd, dh)
 
 
 def head_back_body(
@@ -414,8 +438,8 @@
 
 def mix_back_body(
     docs, length, hk, hv, parts,
-    docs_ref, table_ref, q_ref, k_ref, v_ref, cum_ref, gp_ref, ra_ref, dmix_ref, state_ref, grad_ref,
-    wru_ref,
+    docs_ref, table_ref, q_ref, k_ref, v_ref, cum_ref, gp_ref, ra_ref, dmix_ref, state_ref, near_ref,
+    far_ref, wru_ref,
     dqkv_ref, drank_ref, grup_ref, gbias_ref,
 ):
     row = pl.program_id(0)
@@ -441,7 +465,7 @@
         d_mix = dmix_ref[:, vv]
         value = v_ref[:, vv]
         state = state_ref[0, h]
-        grad32 = gather_state(grad_ref, table_ref, h, parts)
+        grad32 = gather_state(near_ref, far_ref, table_ref, h, parts)
         grad = grad32.astype(BF)
         scores = jnp.where(visible, nt(qs, ks), 0.0).astype(BF)
         d_scores = jnp.where(visible, nt(d_mix, value), 0.0).astype(BF)
@@ -485,12 +509,13 @@
         gbias_ref[...] += gbias
 
 
-def mix_back_all(q, k, v, cum, gp, ra, dmix, state, grad, wru, docs, table, dims):
+def mix_back_all(q, k, v, cum, gp, ra, dmix, state, near, far, wru, docs, table, dims):
     row_count, length, width, kw, vw, ndocs, parts = dims
     tokens = row_count * length
     hk, hv = kw // HEADS, vw // HEADS
     rank = wru.shape[0]
     tile = lambda n: block((length, n), lambda i, *_: (i, 0))
+    half = block((parts // 2, 1, HEADS, hv // parts, hk), lambda i, *_: (0, i, 0, 0, 0))
     return call(
         functools.partial(mix_back_body, ndocs, length, hk, hv, parts),
         (
@@ -501,14 +526,13 @@
         [
             tile(kw), tile(kw), tile(vw), tile(kw), tile(kw), tile(rank), tile(vw),
             block((1, HEADS, hv, hk), lambda i, *_: (i, 0, 0, 0)),
-            block((parts, 1, HEADS, hv // parts, hk), lambda i, *_: (0, i, 0, 0, 0)),
-            whole((rank, kw)),
+            half, half, whole((rank, kw)),
         ],
         (tile(2 * kw + vw), tile(rank), whole((rank, kw)), whole((1, kw))),
         prefetch=2,
         flops=16 * tokens * length * vw,
         moved=16 * MIB,
-    )(docs, table, q, k, v, cum, gp, ra, dmix, state, grad, wru)
+    )(docs, table, q, k, v, cum, gp, ra, dmix, state, near, far, wru)
 
 
 def input_back_body(
@@ -522,7 +546,7 @@
         + nt(dqkv_ref[:, kw : 2 * kw], wk_ref[...])
         + nt(dqkv_ref[:, 2 * kw :], wv_ref[...])
         + nt(dog_ref[...], wog_ref[...])
-        + nt(drank_ref[...], wrd_ref[...])
+        + nn(drank_ref[...], wrd_ref[...])
     )
     x = x_ref[...].astype(F32)
     inv = lax.rsqrt(jnp.mean(x * x, axis=-1, keepdims=True) + EPS)
@@ -563,52 +587,50 @@
     )(x, dmid, dqkv, dog, drank, gain.reshape(1, -1), wq, wk, wv, wog, wrd)
 
 
-def weight_body(count, pieces, per, *refs):
-    table_ref, left_ref = refs[:2]
-    rights = refs[2 : 2 + count]
-    outs = refs[2 + count : 2 + 3 * count]
-    turned, hold = refs[2 + 3 * count :]
+def weight_body(count, pieces, per, table_ref, *refs):
+    lefts, rights = refs[:count], refs[count : 2 * count]
+    keep_ref, send_ref, hold = refs[2 * count : 2 * count + 3]
+    turned = refs[2 * count + 3 :]
 
     @pl.when(pl.program_id(0) == 0)
     def _():
-        turned[...] = left_ref[...].T
+        for n in range(count):
+            turned[n][...] = lefts[n][...].T
 
     for n in range(count):
-        hold[...] = nn(turned[...], rights[n][...])
-        keep_ref, send_ref = outs[2 * n], outs[2 * n + 1]
+        hold[...] = nn(turned[n][...], rights[n][...])
+        at = slice(n * per, (n + 1) * per)
         for j in range(pieces // 2):
             first = pl.multiple_of(table_ref[j] * per, per)
-            keep_ref[j] = hold[pl.ds(first, per), :]
+            keep_ref[j, at, :] = hold[pl.ds(first, per), :]
             second = pl.multiple_of(table_ref[pieces // 2 + j] * per, per)
-            send_ref[j] = hold[pl.ds(second, per), :]
-
-
-def weight_grads(left, rights, table, tile=256):
-    tokens, rows = left.shape
-    pieces = table.shape[0]
+            send_ref[j, at, :] = hold[pl.ds(second, per), :]
+
+
+def weight_grads(pairs, table):
+    count, pieces = len(pairs), table.shape[0]
+    tokens, rows = pairs[0][0].shape
     per = rows // pieces
-    cols = rights[0].shape[1]
+    cols = pairs[0][1].shape[1]
     if per % 8:
-        out = []
-        for right in rights:
-            parts = tn(left, right).reshape(pieces, per, cols)[table]
-            out.append((parts[: pieces // 2], parts[pieces // 2 :]))
-        return out
-    count = len(rights)
-    half = shape((pieces // 2, per, cols), F32)
-    half_block = block((pieces // 2, per, tile), lambda i, *_: (0, 0, i))
-    flat = call(
+        both = [tn(left, right) for left, right in pairs]
+        parts = jnp.concatenate([part.reshape(pieces, per, cols) for part in both], axis=1)[table]
+        return parts[: pieces // 2], parts[pieces // 2 :]
+    tile = next(n for n in (1408, 512, 256, 128) if cols % n == 0)
+    half = shape((pieces // 2, count * per, cols), F32)
+    half_block = block((pieces // 2, count * per, tile), lambda i, *_: (0, 0, i))
+    return call(
         functools.partial(weight_body, count, pieces, per),
-        (half,) * (2 * count),
+        (half, half),
         (cols // tile,),
-        [whole((tokens, rows))] + [block((tokens, tile), lambda i, *_: (0, i))] * count,
-        (half_block,) * (2 * count),
+        [whole((tokens, rows))] * count
+        + [block((tokens, tile), lambda i, *_: (0, i))] * count,
+        (half_block, half_block),
         prefetch=1,
-        scratch=[pltpu.VMEM((rows, tokens), BF), pltpu.VMEM((rows, tile), F32)],
+        scratch=[pltpu.VMEM((rows, tile), F32)] + [pltpu.VMEM((rows, tokens), BF)] * count,
         flops=2 * tokens * rows * cols * count,
         moved=4 * rows * cols * count,
-    )(table, left, *rights)
-    return [(flat[2 * n], flat[2 * n + 1]) for n in range(count)]
+    )(table, *[left for left, _ in pairs], *[right for _, right in pairs])
 
 
 def bits_of(n):
@@ -637,36 +659,95 @@
         here = self.me if n == self.n_dp * self.n_seq else self.at_seq
         return jnp.array(places, jnp.int32) ^ here
 
-    def order(self, *seq_bits, across):
-        dp = tuple(range(self.seq_bits, self.seq_bits + self.dp_bits))
-        rest = [bit for bit in range(self.seq_bits) if bit not in seq_bits]
-        order = list(seq_bits) + rest
-        return tuple(order[:across]) + dp + tuple(order[across:])
-
-    def reduce(self, pair, order):
-        keep, send = pair
-        for k, bit in enumerate(order):
-            got = self.swap(send, bit)
-            if k == len(order) - 1:
-                return keep + got
-            half = keep.shape[0] // 2
-            send = keep[half:] + got[half:]
-            keep = keep[:half] + got[:half]
-
-
-def scan_states(links, keep, send, decays, backwards):
+    def order(self, *names):
+        across = tuple(range(self.seq_bits, self.seq_bits + self.dp_bits))
+        bits = [0]
+        for name in names:
+            bits.extend(across if name == "x" else [{"y": 1, "z0": 2, "z1": 3}[name]])
+        return tuple(bits) + tuple(b for b in range(self.seq_bits) if b not in bits)
+
+
+class Turns:
+    def __init__(self):
+        self.last = ()
+
+    def after(self, value):
+        return lax.optimization_barrier((value,) + self.last)[0]
+
+    def done(self, *values):
+        self.last = values
+
+
+class Task:
+    def __init__(self, steps):
+        self.steps, self.wanted, self.got, self.begun, self.over = steps, [], None, False, False
+
+    def advance(self, turns):
+        if self.over:
+            return
+        if self.wanted:
+            start([self], turns)
+        try:
+            self.wanted = self.steps.send(self.got) if self.begun else next(self.steps)
+            self.begun = True
+        except StopIteration:
+            self.wanted, self.over = [], True
+
+    def finish(self, turns):
+        while not self.over:
+            self.advance(turns)
+
+
+def start(tasks, turns):
+    tasks = [task for task in tasks if task.wanted]
+    values = [value for task in tasks for value, _ in task.wanted]
+    if not values:
+        return
+    tied = lax.optimization_barrier(tuple(values) + turns.last)[: len(values)]
+    turns.done(tied[0])
+    tied = iter(tied)
+    for task in tasks:
+        task.got = [move(next(tied)) for _, move in task.wanted]
+        task.wanted = []
+
+
+def reduce_steps(links, turns, make, order, out, name, halves=False):
+    keep, send = make()
+    turns.done(keep, send)
+    for k, bit in enumerate(order):
+        swap = functools.partial(links.swap, bit=bit)
+        half = keep.shape[0] // 2
+        if halves and k == 0:
+            near, far = yield [(send[:half], swap), (send[half:], swap)]
+        else:
+            (got,) = yield [(send, swap)]
+            near, far = got[:half], got[half:]
+        keep = turns.after(keep)
+        if k == len(order) - 1:
+            out[name] = keep + got
+            turns.done(out[name])
+            return
+        send = keep[half:] + far
+        keep = keep[:half] + near
+        turns.done(keep, send)
+
+
+def scan_steps(links, turns, make, decays, backwards, out):
+    keep, send, decay = make()
     bits = links.seq_bits
     levels = []
-    decay = None if backwards else decays
-    kept = [] if not backwards else decays
+    kept = [] if decays is None else decays
+    turns.done(keep, send)
     for bit in range(bits - 1):
-        got = links.swap(send, bit)
-        if backwards:
-            mine_d, got_d = kept[bit]
+        swap = functools.partial(links.swap, bit=bit)
+        if decays is None:
+            got, got_d = yield [(send, swap), (decay, swap)]
+            kept.append((decay, got_d))
+            decay = decay * got_d
         else:
-            mine_d, got_d = decay, links.swap(decay, bit)
-            kept.append((mine_d, got_d))
-            decay = mine_d * got_d
+            (got,) = yield [(send, swap)]
+        mine_d, got_d = kept[bit]
+        keep = turns.after(keep)
         odd = (links.at_seq >> bit) & 1
         second = (odd == 0) if backwards else (odd == 1)
         levels.append((second, keep, got, mine_d, got_d))
@@ -674,17 +755,45 @@
         half = total.shape[0] // 2
         if bit < bits - 2:
             keep, send = total[:half], total[half:]
+            turns.done(keep, send)
         else:
-            keep = total
+            send = total
+            turns.done(send)
     flip = 1 << (bits - 1)
     pairs = [(i, i ^ flip) for i in range(links.n_seq) if ((i >> (bits - 1)) & 1) == int(backwards)]
-    state = lax.ppermute(keep, "seq", pairs)
+    (state,) = yield [(send, lambda value: lax.ppermute(value, "seq", pairs))]
     for bit in reversed(range(bits - 1)):
         second, keep, got, mine_d, got_d = levels[bit]
+        keep = turns.after(keep)
         theirs = jnp.where(second, state, mine_d * state + keep)
         mine = jnp.where(second, got_d * state + got, state)
-        state = jnp.concatenate([mine, links.swap(theirs, bit)], axis=0)
-    return state, kept
+        turns.done(theirs, mine)
+        (far,) = yield [(theirs, functools.partial(links.swap, bit=bit))]
+        if bit == 0:
+            out["near"], out["far"], out["decays"] = mine, far, kept
+        else:
+            mine = turns.after(mine)
+            state = jnp.concatenate([mine, far], axis=0)
+
+
+ROUTES = {
+    "gate": ("x", "y", "z0", "z1"),
+    "up": ("y", "z0", "x", "z1"),
+    "down": ("z0", "x", "y", "z1"),
+    "mid": ("x", "y", "z0", "z1"),
+    "qkv": ("y", "x", "z0", "z1"),
+    "small": ("x", "y", "z0", "z1"),
+}
+SCHEDULE = (
+    "scan", ("scan",), "gate", "scan", ("scan", "gate"), "up", "gate", "scan", ("scan", "up"),
+    "down", "up", "scan", ("scan", "down"), "mid", "down", "scan", ("scan", "mid", "gate"),
+    "mid", "scan", ("scan", "down"), "scan", ("scan", "up"), "scan", "qkv", "gate", ("qkv",
+    "mid"), "up", "down", "qkv", ("up", "qkv", "down"), "small", ("small",), "mid", "small",
+    ("small", "gate"), "up", ("up",), "small", ("small",), "down", ("mid",), "qkv", ("down",),
+    "small", ("small",), "gate", ("qkv",), "up", ("gate",), "small", ("small",), "mid", ("up",),
+    "down", ("mid",), "small", "qkv", ("down",), "gate", ("qkv",), "up", ("gate",), "mid",
+    ("mid",), "down", "qkv", ("qkv",), "gate", "mid", "qkv",
+)
 
 
 def local(
@@ -694,105 +803,139 @@
     row_count, length, width = block_in.shape
     tokens = row_count * length
     kw, vw = w_query.shape[1], w_value.shape[1]
-    links = Links()
+    links, turns = Links(), Turns()
     parts = links.n_seq
     everyone = links.n_dp * links.n_seq
     dims = (row_count, length, width, kw, vw, doc_starts.shape[1], parts)
     x = block_in.reshape(tokens, width)
     cot = cotangent.reshape(tokens, width)
     docs = (doc_starts - links.at_seq * length).reshape(-1)
-
-    levels = tuple(range(links.seq_bits - 1))
+    rank_down_t = w_rank_down.T
+
+    levels = range(links.seq_bits - 1)
     step = 1 << len(levels)
-    source = links.table(tuple(levels))
     size = parts // step
     low = links.at_seq & (step - 1)
     reverse = jnp.array(
         [sum(((p >> b) & 1) << (len(levels) - 1 - b) for b in levels) for p in range(step)], jnp.int32
     )
-    source = reverse ^ low
-    place = reverse[jnp.arange(step) ^ low]
     spread = jnp.arange(size)
-    to_piece = (source[:, None] * size + spread).reshape(-1)
-    to_place = (place[:, None] * size + spread).reshape(-1)
+    to_piece = ((reverse ^ low)[:, None] * size + spread).reshape(-1)
+    to_place = (reverse[jnp.arange(step) ^ low][:, None] * size + spread).reshape(-1)
     state_table = jnp.concatenate([to_piece, to_place]).astype(jnp.int32)
 
     normed, q, k, v, og, ra, gp, cum, keep, send, decay = project_all(
-        x, docs, state_table, norm1_gain, w_query, w_key, w_value, w_outgate, w_rank_down, w_rank_up,
+        x, docs, state_table, norm1_gain, w_query, w_key, w_value, w_outgate, rank_down_t, w_rank_up,
         decay_bias, dims,
     )
     decay = decay.reshape(1, row_count, HEADS, 1, kw // HEADS)
-    state_in, decays = scan_states(links, keep, send, decay, False)
-    inner = inner_all(q, k, v, cum, docs, dims)
-    mixed, gated, state_kept = mix_all(q, cum, inner, og, state_in, group_gain, docs, state_table, dims)
-
+    fwd = {}
+    scan = Task(scan_steps(links, turns, lambda: (keep, send, decay), None, False, fwd))
+    scan.advance(turns)
+    scan.advance(turns)
+    start([scan], turns)
+    dh = hidden_back_all(turns.after(cot), w_ffdown)
+    turns.done(dh)
+    scan.advance(turns)
+    start([scan], turns)
+    inner = inner_all(q, k, v, cum, turns.after(docs), dims)
+    turns.done(inner)
+    scan.finish(turns)
+    mixed, gated, state_kept = mix_all(
+        q, cum, inner, og, fwd["near"], fwd["far"], group_gain, turns.after(docs), state_table, dims
+    )
     hidden, dg, du, normed2, block_out, d_middle, d_out, d_gated, gnorm2 = ff_all(
-        x, cot, gated, w_output, norm2_gain, w_ffgate, w_ffup, w_ffdown
+        x, cot, gated, w_output, norm2_gain, w_ffgate, w_ffup, w_ffdown, dh
     )
-    d_mix, d_og, keep, send, ggroup = head_back_all(
-        d_gated, og, mixed, q, cum, group_gain, docs, state_table, dims
-    )
-    state_grad, _ = scan_states(links, keep, send, decays, True)
-
-    order_a = links.order(0, across=1)
-    order_b = links.order(0, 1, across=2)
-    table_a, table_b = links.table(order_a), links.table(order_b)
-    (gate_pair,) = weight_grads(normed2, [dg], table_a)
-    (up_pair,) = weight_grads(normed2, [du], table_b)
-    (down_pair,) = weight_grads(hidden, [cot], table_a)
-    (output_pair,) = weight_grads(gated, [d_out], table_b)
-    (og_pair,) = weight_grads(normed, [d_og], table_b)
-    g_ffgate = links.reduce(gate_pair, order_a)
-    g_ffup = links.reduce(up_pair, order_b)
-    g_ffdown = links.reduce(down_pair, order_a)
-    g_output = links.reduce(output_pair, order_b)
-    g_outgate = links.reduce(og_pair, order_b)
-
-    d_qkv, d_rank, grup, gbias = mix_back_all(
-        q, k, v, cum, gp, ra, d_mix, state_kept, state_grad, w_rank_up, docs, state_table, dims
-    )
-    (qkv_pair,) = weight_grads(normed, [d_qkv], table_a)
-    g_qkv = links.reduce(qkv_pair, order_a)
-    grad_in, gnorm1 = input_back_all(
-        x, d_middle, d_qkv, d_og, d_rank, norm1_gain, w_query, w_key, w_value, w_outgate, w_rank_down
-    )
-    g_rank_down = tn(normed, d_rank)
+
+    routes = {name: links.order(*route) for name, route in ROUTES.items()}
+    tables = {route: links.table(route) for route in set(routes.values())}
+    back, grads, held = {}, {}, {}
+    ff = w_ffgate.shape[1]
+
+    def head_back():
+        d_mix, d_og, keep, send, ggroup = head_back_all(
+            d_gated, og, mixed, q, cum, group_gain, turns.after(docs), state_table, dims
+        )
+        held.update(d_mix=d_mix, d_og=d_og, ggroup=ggroup)
+        return keep, send, None
+
+    def all_back():
+        yield from scan_steps(links, turns, head_back, fwd["decays"], True, back)
+        held["d_qkv"], held["d_rank"], held["grup"], held["gbias"] = mix_back_all(
+            q, k, v, cum, gp, ra, held["d_mix"], state_kept, back["near"], back["far"], w_rank_up,
+            turns.after(docs), state_table, dims,
+        )
+        turns.done(held["d_rank"])
+
+    def weights(name, pairs, halves=False):
+        order = routes[name]
+        make = lambda: weight_grads(pairs(), turns.after(tables[order]))
+        return reduce_steps(links, turns, make, order, grads, name, halves)
+
+    def small_steps():
+        grad_in, gnorm1 = input_back_all(
+            x, d_middle, held["d_qkv"], held["d_og"], held["d_rank"], turns.after(norm1_gain), w_query,
+            w_key, w_value, w_outgate, rank_down_t,
+        )
+        held["grad_in"] = grad_in
+        by_device = lambda value: value.reshape(everyone, -1)
+        small = [
+            by_device(tn(normed, held["d_rank"])),
+            held["grup"].reshape(rank, everyone, -1).transpose(1, 0, 2).reshape(everyone, -1),
+            by_device(gnorm1), by_device(gnorm2), by_device(held["gbias"]), by_device(held["ggroup"]),
+        ]
+        held["widths"] = [part.shape[1] for part in small]
+        packed = jnp.concatenate(small, axis=1)
+        packed = jnp.pad(packed, ((0, 0), (0, -packed.shape[1] % 128)))[tables[routes["small"]]]
+        packed = packed.reshape(everyone, 1, -1)
+        make = lambda: (packed[: everyone // 2], packed[everyone // 2 :])
+        yield from reduce_steps(links, turns, make, routes["small"], grads, "small")
 
     rank = w_rank_up.shape[0]
-    by_device = lambda value: value.reshape(everyone, -1)
-    small = [
-        by_device(g_rank_down),
-        grup.reshape(rank, everyone, kw // everyone).transpose(1, 0, 2).reshape(everyone, -1),
-        by_device(gnorm1), by_device(gnorm2), by_device(gbias), by_device(ggroup),
-    ]
-    widths = [part.shape[1] for part in small]
-    packed = jnp.concatenate(small, axis=1)
-    packed = jnp.pad(packed, ((0, 0), (0, -packed.shape[1] % 128)))[table_a]
-    packed = packed.reshape(everyone, 1, -1)
-    packed = links.reduce((packed[: everyone // 2], packed[everyone // 2 :]), order_a).reshape(-1)
+    work = {
+        "scan": all_back(),
+        "gate": weights("gate", lambda: [(normed2, dg)]),
+        "up": weights("up", lambda: [(normed2, du)]),
+        "down": weights("down", lambda: [(hidden, cot)]),
+        "mid": weights("mid", lambda: [(gated, d_out), (normed, held["d_og"])]),
+        "qkv": weights("qkv", lambda: [(normed, held["d_qkv"])], True),
+        "small": small_steps(),
+    }
+    work = {name: Task(steps) for name, steps in work.items()}
+    for name in SCHEDULE + tuple(work) * (2 * len(routes["gate"])):
+        if isinstance(name, tuple):
+            start([work[each] for each in name], turns)
+            continue
+        if name in ("qkv", "small"):
+            work["scan"].finish(turns)
+        work[name].advance(turns)
+
+    packed = grads["small"].reshape(-1)
     out_small, at = [], 0
-    for n in widths:
+    for n in held["widths"]:
         out_small.append(packed[at : at + n])
         at += n
     s_down, s_up, s_norm1, s_norm2, s_bias, s_group = out_small
-    g_qkv = g_qkv[0]
+    per = width // everyone
+    mid, qkv = grads["mid"][0], grads["qkv"][0]
     return (
         block_out.reshape(row_count, length, width),
-        grad_in.reshape(row_count, length, width),
+        held["grad_in"].reshape(row_count, length, width),
         s_norm1,
-        g_qkv[:, :kw],
-        g_qkv[:, kw : 2 * kw],
-        g_qkv[:, 2 * kw :],
-        g_outgate[0],
+        qkv[:, :kw],
+        qkv[:, kw : 2 * kw],
+        qkv[:, 2 * kw :],
+        mid[per:],
         s_down.reshape(-1, rank),
         s_up.reshape(rank, -1),
         s_bias,
         s_group,
-        g_output[0],
+        mid[:per],
         s_norm2,
-        g_ffgate[0],
-        g_ffup[0],
-        g_ffdown[0],
+        grads["gate"][0],
+        grads["up"][0],
+        grads["down"][0],
     )
 
 

time: 717 us -> 570 us (0.79)
  waiting for transfers between devices: 355 us -> 229 us
  other arithmetic: 81.5 us -> 67.3 us
  starting transfers between devices: 65.9 us -> 56.7 us
    ppermute x50 -> x46, waiting for transfers between devices: 343 us -> 220 us  [swap(): return lax.ppermute(value, name, [(i, i ^ flip) for i in range(n)])]
    ppermute x50 -> x46, starting transfers between devices: 60.2 us -> 51 us  [swap(): return lax.ppermute(value, name, [(i, i ^ flip) for i in range(n)])]
    select_n x13 -> x14, other arithmetic: 16.4 us -> 10.9 us  [the longest x6 4.43 us: scan_steps(): total = jnp.where(second, mine_d * got + keep, got_d * keep + got)]
  transfers between devices with their start and end apart: 52 -> 48, of which waited for: 28 -> 24; matrix products, arithmetic and copies ran while one was open for 11% -> 12% of each run, Pallas kernels for 14% -> 19%
where the time goes in v2:
time: 570 us; the launch traced here: 563 us
  waiting for transfers between devices  229 us (40%)
  Pallas kernels  188 us (33%)
  other arithmetic  67.3 us (12%)
  starting transfers between devices  56.7 us (10%)
  local copies, waits for them, and re-layouts  19.7 us (3%)
    ppermute x46, waiting for transfers between devices, swap(): return lax.ppermute(value, name, [(i, i ^ flip) for i in range(n)])  220 us
    pallas_call x5, Pallas kernels, weight_grads(): call(functools.partial(weight_body, count, pieces, per), (half, half), (c...  55.4 us
    ppermute x46, starting transfers between devices, swap(): return lax.ppermute(value, name, [(i, i ^ flip) for i in range(n)])  51 us
    pallas_call x1, Pallas kernels, ff_all(): call(functools.partial(ff_body, steps), (shape((tokens, ff), BF), shape((...  47.5 us
    add x13, other arithmetic, reduce_steps(): send = keep[half:] + far  37.3 us
    pallas_call x1, Pallas kernels, project_all(): call(body, (shape((tokens, width), BF), shape((tokens, kw), BF), shape((t...  15.8 us
    pallas_call x1, Pallas kernels, mix_back_all(): call(functools.partial(mix_back_body, ndocs, length, hk, hv, parts), (sha...  15.3 us
    pallas_call x1, Pallas kernels, hidden_back_all(): call(hidden_back_body, shape((tokens, ff), F32), (ff // tile,), [whole((t...  12.9 us
  transfers between devices with their start and end apart: 48, of which 24 were waited for; matrix products, arithmetic and copies ran while one was open for 12% of the time, Pallas kernels for 19%

profile of v2, /device:TPU:0, one launch (start us, length us, event | category | flops | bytes accessed | tf_op | source)
XLA Modules:
  0.0 562.7 jit_solution(9241077023125632758)
XLA Ops:
  4.9 15.8 %shard_map.333 = (bf16[768,1024]{1,0:T(8,128)(2,1)}, bf16[768,512]{1,0:T(8,128)(2,1)}, bf16[768,512]{1,0:T(8,128)(2,1)}, bf16[768,1024]{1,0:T(8,128)(2,1)}, f32[...) custom-call(s32[24]{0:T(128)} %reshape.140.docs_ref, ...), custom_call_target="tpu_custom_call" | custom-call | flops 1 | bytes 1 | tf_op jit(solution)/shard_map/pallas_call | solution.py:140
  31.0 12.9 %shard_map.334.dh_ref = f32[768,2816]{1,0:T(8,128)} custom-call(bf16[768,1024]{1,0:T(8,128)(2,1)} %bitcast.47, bf16[2816,1024]{1,0:T(8,128)(2,1)} %wd_ref.3), custom_call_target="tpu_custom_call" | custom-call | flops 1 | bytes 1 | tf_op jit(solution)/shard_map/pallas_call | solution.py:325
  53.0 8.5 %shard_map.335.inner_ref = f32[768,1024]{1,0:T(8,128)} custom-call(s32[24]{0:T(128)} %reshape.140.docs_ref, bf16[768,512]{1,0:T(8,128)(2,1)} %get-tuple-element.176.q_ref, bf16[768,512]{1,0:T(8,128)(2,1)} %get-tuple-element.177.k_ref, bf16[768,1024]{1,0:T(8,128)(2,1)} %get-tuple-element.178.v_ref, f32[768,512]{1,0:T(8,128)} %get-tuple-element.179.cum_ref), custom_call_target="tpu_custom_call" | custom-call | flops 1 | bytes 1 | tf_op jit(solution)/shard_map/pallas_call | solution.py:192
  67.7 6.9 %collective-permute-done.6 = f32[2,6,4,16,128]{4,3,2,1,0:T(8,128)S(1)} collective-permute-done((f32[2,6,4,16,128]{4,3,2,1,0:T(8,128)S(1)}, f32[2,6,4,16,128]{4,3,2,1,0:T(8,128)S(1)}, u32[]{:S(2)}, u32[]{:S(2)}) %collective-permute-start.6) | collective-permute-done | bytes 393248 | tf_op jit(solution)/shard_map/ppermute | solution.py:764
  75.8 9.9 %collective-permute-start.7 = (f32[2,6,4,16,128]{4,3,2,1,0:T(8,128)S(1)}, f32[2,6,4,16,128]{4,3,2,1,0:T(8,128)S(1)}, u32[]{:S(2)}, u32[]{:S(2)}) collective-permute-start(f32[2,6,4,16,128]{4,3,2,1,0:T(8,128)S(1)} %get-tuple-element.182), channel_id=1, source_target_pairs={{0,4},{1,5},{2,6},{3,7},{4,0},{5,1},{6,2},{7,3},{8,12},{9,13},{10,... | collective-permute-start | bytes 1179656 | tf_op jit(solution)/shard_map/ppermute | solution.py:651
  85.7 9.3 %collective-permute-done.7 = f32[2,6,4,16,128]{4,3,2,1,0:T(8,128)S(1)} collective-permute-done((f32[2,6,4,16,128]{4,3,2,1,0:T(8,128)S(1)}, f32[2,6,4,16,128]{4,3,2,1,0:T(8,128)S(1)}, u32[]{:S(2)}, u32[]{:S(2)}) %collective-permute-start.7) | collective-permute-done | bytes 393248 | tf_op jit(solution)/shard_map/ppermute | solution.py:651
  96.9 17.4 %collective-permute-done.8 = f32[4,6,4,16,128]{4,3,2,1,0:T(8,128)S(1)} collective-permute-done((f32[4,6,4,16,128]{4,3,2,1,0:T(8,128)S(1)}, f32[4,6,4,16,128]{4,3,2,1,0:T(8,128)S(1)}, u32[]{:S(2)}, u32[]{:S(2)}) %collective-permute-start.8) | collective-permute-done | bytes 786464 | tf_op jit(solution)/shard_map/ppermute | solution.py:651
  120.7 9.4 %shard_map.336 = (f32[768,1024]{1,0:T(8,128)}, bf16[768,1024]{1,0:T(8,128)(2,1)}, bf16[6,4,256,128]{3,2,1,0:T(8,128)(2,1)}) custom-call(s32[24]{0:T(128)} %reshape.140.docs_ref, s32[32]{0:T(128)} %pad_add_fusion.table_ref, bf16[768,512]{1,0:T(8,128)(2,1)} %get-tuple-element.176.q_ref, f32[768,512]{1,0:T(8,128)} %get-tuple-element.179.cum_ref, ...), custom_call_target="tpu_custom_call" | custom-call | flops 1 | bytes 1 | tf_op jit(solution)/shard_map/pallas_call | solution.py:241
  130.1 47.5 %shard_map.337 = (bf16[768,2816]{1,0:T(8,128)(2,1)}, bf16[768,2816]{1,0:T(8,128)(2,1)}, bf16[768,2816]{1,0:T(8,128)(2,1)}, bf16[768,1024]{1,0:T(8,128)(2,1)}, bf...) custom-call(bf16[768,1024]{1,0:T(8,128)(2,1)} %bitcast.45, ...), custom_call_target="tpu_custom_call" | custom-call | flops 1 | bytes 1 | tf_op jit(solution)/shard_map/pallas_call | solution.py:344
  177.7 10.8 %shard_map.338 = (bf16[768,1024]{1,0:T(8,128)(2,1)}, bf16[768,1024]{1,0:T(8,128)(2,1)}, f32[8,6,4,16,128]{4,3,2,1,0:T(8,128)}, f32[8,6,4,16,128]{4,3,2,1,0:T(8,128)}, f32[1,256]{1,0:T(1,128)}) custom-call(s32[24]{0:T(128)} %reshape.140.docs_ref, s32[32]{0:T(128)} %pad_add_fusion.table_ref, f32[768,1024]{1,0:T(8,128)} %get-tuple-element.194.dgated_ref, ...), custom_call_target="tpu_custom_call" | custom-call | flops 1 | bytes 1 | tf_op jit(solution)/shard_map/pallas_call | solution.py:423
  189.1 11.6 %shard_map.339 = (f32[16,32,2816]{2,1,0:T(8,128)}, f32[16,32,2816]{2,1,0:T(8,128)}) custom-call(s32[32]{0:T(128)} %get-tuple-element.222.table_ref, bf16[768,1024]{1,0:T(8,128)(2,1)} %get-tuple-element.200.refs_0_, bf16[768,2816]{1,0:T(8,128)(2,1)} %get-tuple-element.201.refs_1_), custom_call_target="tpu_custom_call" | custom-call | flops 1 | bytes 1 | tf_op jit(solution)/shard_map/pallas_call | solution.py:622
  205.6 11.8 %shard_map.340 = (f32[16,32,2816]{2,1,0:T(8,128)}, f32[16,32,2816]{2,1,0:T(8,128)}) custom-call(s32[32]{0:T(128)} %broadcast_xor_fusion.2.table_ref, bf16[768,1024]{1,0:T(8,128)(2,1)} %get-tuple-element.200.refs_0_, bf16[768,2816]{1,0:T(8,128)(2,1)} %get-tuple-element.207.refs_1_), custom_call_target="tpu_custom_call" | custom-call | flops 1 | bytes 1 | tf_op jit(solution)/shard_map/pallas_call | solution.py:622
  217.4 6.8 %slice_add_fusion.4 = (f32[8,32,2816]{2,1,0:T(8,128)}, f32[8,32,2816]{2,1,0:T(8,128)S(1)}) fusion(f32[16,32,2816]{2,1,0:T(8,128)} %collective-permute-done.12, f32[16,32,2816]{2,1,0:T(8,128)} %get-tuple-element.210), kind=kLoop, calls=%fused_computation.6 | loop fusion | flops 1441792 | bytes 17301504 | tf_op jit(solution)/shard_map/add | solution.py:730
  226.7 12.2 %shard_map.341 = (f32[16,88,1024]{2,1,0:T(8,128)}, f32[16,88,1024]{2,1,0:T(8,128)}) custom-call(s32[32]{0:T(128)} %get-tuple-element.214.table_ref, bf16[768,2816]{1,0:T(8,128)(2,1)} %get-tuple-element.215.refs_0_, bf16[768,1024]{1,0:T(8,128)(2,1)} %bitcast.49), custom_call_target="tpu_custom_call" | custom-call | flops 1 | bytes 1 | tf_op jit(solution)/shard_map/pallas_call | solution.py:622
  239.0 6.7 %slice_add_fusion.2 = (f32[8,32,2816]{2,1,0:T(8,128)}, f32[8,32,2816]{2,1,0:T(8,128)S(1)}) fusion(f32[16,32,2816]{2,1,0:T(8,128)} %collective-permute-done.14, f32[16,32,2816]{2,1,0:T(8,128)} %get-tuple-element.218), kind=kLoop, calls=%fused_computation.4 | loop fusion | flops 1441792 | bytes 17301504 | tf_op jit(solution)/shard_map/add | solution.py:730
  248.0 10.3 %shard_map.342 = (f32[16,64,1024]{2,1,0:T(8,128)}, f32[16,64,1024]{2,1,0:T(8,128)}) custom-call(s32[32]{0:T(128)} %get-tuple-element.222.table_ref, bf16[768,1024]{1,0:T(8,128)(2,1)} %get-tuple-element.191.gated_ref.refs_0_, bf16[768,1024]{1,0:T(8,128)(2,1)} %get-tuple-element.223.refs_1_.refs_0_, bf16[768,1024]{1,0:T(8,128)(2,1)} %get-tuple-element.224.refs_2_, ...), custom_call_target="tpu_custom_call" | custom-call | flops 1 | bytes 1 | tf_op jit(solution)/shard_map/pallas_call | solution.py:622
  258.3 9.0 %slice_add_fusion = (f32[8,88,1024]{2,1,0:T(8,128)}, f32[8,88,1024]{2,1,0:T(8,128)}) fusion(f32[16,88,1024]{2,1,0:T(8,128)} %collective-permute-done.16, f32[16,88,1024]{2,1,0:T(8,128)} %get-tuple-element.228), kind=kLoop, calls=%fused_computation.2 | loop fusion | flops 1441792 | bytes 17301504 | tf_op jit(solution)/shard_map/add | solution.py:730
  270.4 7.1 %collective-permute-done.17 = f32[16,64,1024]{2,1,0:T(8,128)S(1)} collective-permute-done((f32[16,64,1024]{2,1,0:T(8,128)S(1)}, f32[16,64,1024]{2,1,0:T(8,128)S(1)}, u32[]{:S(2)}, u32[]{:S(2)}) %collective-permute-start.17) | collective-permute-done | bytes 4194336 | tf_op jit(solution)/shard_map/ppermute | solution.py:651
  285.1 16.6 %collective-permute-done.19 = f32[4,6,4,16,128]{4,3,2,1,0:T(8,128)S(1)} collective-permute-done((f32[4,6,4,16,128]{4,3,2,1,0:T(8,128)S(1)}, f32[4,6,4,16,128]{4,3,2,1,0:T(8,128)S(1)}, u32[]{:S(2)}, u32[]{:S(2)}) %collective-permute-start.19) | collective-permute-done | bytes 786464 | tf_op jit(solution)/shard_map/ppermute | solution.py:651
  308.1 15.3 %shard_map.343 = (bf16[768,2048]{1,0:T(8,128)(2,1)}, bf16[768,16]{1,0:T(8,128)(2,1)}, f32[16,512]{1,0:T(8,128)}, f32[1,512]{1,0:T(1,128)}) custom-call(s32[24]{0:T(128)} %reshape.140.docs_ref, s32[32]{0:T(128)} %pad_add_fusion.table_ref, bf16[768,512]{1,0:T(8,128)(2,1)} %get-tuple-element.176.q_ref, bf16[768,512]{1,0:T(8,128)(2,1)} %get-tuple-element.177.k_ref, ...), custom_call_target="tpu_custom_call" | custom-call | flops 1 | bytes 1 | tf_op jit(solution)/shard_map/pallas_call | solution.py:519
  323.4 9.5 %shard_map.344 = (f32[16,32,2048]{2,1,0:T(8,128)}, f32[16,32,2048]{2,1,0:T(8,128)}) custom-call(s32[32]{0:T(128)} %broadcast_xor_fusion.table_ref, bf16[768,1024]{1,0:T(8,128)(2,1)} %get-tuple-element.223.refs_1_.refs_0_, bf16[768,2048]{1,0:T(8,128)(2,1)} %get-tuple-element.245.refs_1_.dqkv_ref), custom_call_target="tpu_custom_call" | custom-call | flops 1 | bytes 1 | tf_op jit(solution)/shard_map/pallas_call | solution.py:622
  335.5 12.5 %collective-permute-done.21 = f32[8,32,2816]{2,1,0:T(8,128)} collective-permute-done((f32[8,32,2816]{2,1,0:T(8,128)}, f32[8,32,2816]{2,1,0:T(8,128)}, u32[]{:S(2)}, u32[]{:S(2)}) %collective-permute-start.21) | collective-permute-done | bytes 2883616 | tf_op jit(solution)/shard_map/ppermute | solution.py:651
  353.7 15.1 %collective-permute-done.22 = f32[8,32,2816]{2,1,0:T(8,128)} collective-permute-done((f32[8,32,2816]{2,1,0:T(8,128)}, f32[8,32,2816]{2,1,0:T(8,128)}, u32[]{:S(2)}, u32[]{:S(2)}) %collective-permute-start.22) | collective-permute-done | bytes 2883616 | tf_op jit(solution)/shard_map/ppermute | solution.py:651
  384.9 12.2 %shard_map.345 = (f32[768,1024]{1,0:T(8,128)}, f32[1,1024]{1,0:T(1,128)}) custom-call(bf16[768,1024]{1,0:T(8,128)(2,1)} %bitcast.46, f32[768,1024]{1,0:T(8,128)} %get-tuple-element.193.dmid_ref, bf16[768,2048]{1,0:T(8,128)(2,1)} %get-tuple-element.245.refs_1_.dqkv_ref, bf16[768,1024]{1,0:T(8,128)(2,1)} %get-tuple-element.225.refs_3_.dog_ref, ...), custom_call_target="tpu_custom_call" | custom-call | flops 1 | bytes 1 | tf_op jit(solution)/shard_map/pallas_call | solution.py:575
  404.5 8.5 %collective-permute-done.28 = f32[4,32,2816]{2,1,0:T(8,128)} collective-permute-done((f32[4,32,2816]{2,1,0:T(8,128)}, f32[4,32,2816]{2,1,0:T(8,128)}, u32[]{:S(2)}, u32[]{:S(2)}) %collective-permute-start.28) | collective-permute-done | bytes 1441824 | tf_op jit(solution)/shard_map/ppermute | solution.py:651
  414.6 19.6 %collective-permute-done.29 = f32[8,1,896]{2,0,1:T(8,128)S(1)} collective-permute-done((f32[8,1,896]{2,0,1:T(8,128)S(1)}, f32[8,1,896]{2,0,1:T(8,128)S(1)}, u32[]{:S(2)}, u32[]{:S(2)}) %collective-permute-start.29) | collective-permute-done | bytes 28704 | tf_op jit(solution)/shard_map/ppermute | solution.py:651
  440.1 21.6 %collective-permute-done.32 = f32[4,1,896]{2,0,1:T(4,128)S(1)} collective-permute-done((f32[4,1,896]{2,0,1:T(4,128)S(1)}, f32[4,1,896]{2,0,1:T(4,128)S(1)}, u32[]{:S(2)}, u32[]{:S(2)}) %collective-permute-start.32) | collective-permute-done | bytes 14368 | tf_op jit(solution)/shard_map/ppermute | solution.py:651
  468.9 15.2 %collective-permute-done.36 = f32[4,64,1024]{2,1,0:T(8,128)S(1)} collective-permute-done((f32[4,64,1024]{2,1,0:T(8,128)S(1)}, f32[4,64,1024]{2,1,0:T(8,128)S(1)}, u32[]{:S(2)}, u32[]{:S(2)}) %collective-permute-start.36) | collective-permute-done | bytes 1048608 | tf_op jit(solution)/shard_map/ppermute | solution.py:651
  486.4 11.8 %collective-permute-done.37 = f32[2,88,1024]{2,1,0:T(8,128)S(1)} collective-permute-done((f32[2,88,1024]{2,1,0:T(8,128)S(1)}, f32[2,88,1024]{2,1,0:T(8,128)S(1)}, u32[]{:S(2)}, u32[]{:S(2)}) %collective-permute-start.37) | collective-permute-done | bytes 720928 | tf_op jit(solution)/shard_map/ppermute | solution.py:651
  506.2 22.5 %collective-permute-done.42 = f32[2,64,1024]{2,1,0:T(8,128)S(1)} collective-permute-done((f32[2,64,1024]{2,1,0:T(8,128)S(1)}, f32[2,64,1024]{2,1,0:T(8,128)S(1)}, u32[]{:S(2)}, u32[]{:S(2)}) %collective-permute-start.42) | collective-permute-done | bytes 524320 | tf_op jit(solution)/shard_map/ppermute | solution.py:651
  532.3 6.4 %collective-permute-done.44 = f32[2,32,2048]{2,1,0:T(8,128)S(1)} collective-permute-done((f32[2,32,2048]{2,1,0:T(8,128)S(1)}, f32[2,32,2048]{2,1,0:T(8,128)S(1)}, u32[]{:S(2)}, u32[]{:S(2)}) %collective-permute-start.44) | collective-permute-done | bytes 524320 | tf_op jit(solution)/shard_map/ppermute | solution.py:651
  541.6 14.0 %collective-permute-done.46 = f32[1,64,1024]{2,1,0:T(8,128)S(1)} collective-permute-done((f32[1,64,1024]{2,1,0:T(8,128)S(1)}, f32[1,64,1024]{2,1,0:T(8,128)S(1)}, u32[]{:S(2)}, u32[]{:S(2)}) %collective-permute-start.46) | collective-permute-done | bytes 262176 | tf_op jit(solution)/shard_map/ppermute | solution.py:651
  (253 shorter events, 136.4 us)
Async XLA Ops:
  28.1 21.8 %collective-permute-start.3 = (f32[4,6,4,16,128]{4,3,2,1,0:T(8,128)}, f32[4,6,4,16,128]{4,3,2,1,0:T(8,128)S(1)}, u32[]{:S(2)}, u32[]{:S(2)}) collective-permute-start(f32[4,6,4,16,128]{4,3,2,1,0:T(8,128)} %get-tuple-element.170), channel_id=1, source_target_pairs={{0,2},{1,3},{2,0},{3,1},{4,6},{5,7},{6,4},{7,5},{8,10},{9,11},{10,... | collective-permute-start | bytes 2359304 | tf_op jit(solution)/shard_map/ppermute | solution.py:651
  75.8 19.2 %collective-permute-start.7 = (f32[2,6,4,16,128]{4,3,2,1,0:T(8,128)S(1)}, f32[2,6,4,16,128]{4,3,2,1,0:T(8,128)S(1)}, u32[]{:S(2)}, u32[]{:S(2)}) collective-permute-start(f32[2,6,4,16,128]{4,3,2,1,0:T(8,128)S(1)} %get-tuple-element.182), channel_id=1, source_target_pairs={{0,4},{1,5},{2,6},{3,7},{4,0},{5,1},{6,2},{7,3},{8,12},{9,13},{10,... | collective-permute-start | bytes 1179656 | tf_op jit(solution)/shard_map/ppermute | solution.py:651
  95.3 19.0 %collective-permute-start.8 = (f32[4,6,4,16,128]{4,3,2,1,0:T(8,128)S(1)}, f32[4,6,4,16,128]{4,3,2,1,0:T(8,128)S(1)}, u32[]{:S(2)}, u32[]{:S(2)}) collective-permute-start(f32[4,6,4,16,128]{4,3,2,1,0:T(8,128)S(1)} %get-tuple-element.185), channel_id=1, source_target_pairs={{0,2},{1,3},{2,0},{3,1},{4,6},{5,7},{6,4},{7,5},{8,10},{9,11},{10,... | collective-permute-start | bytes 2359304 | tf_op jit(solution)/shard_map/ppermute | solution.py:651
  204.1 20.1 %collective-permute-start.11 = (f32[4,6,4,16,128]{4,3,2,1,0:T(8,128)}, f32[4,6,4,16,128]{4,3,2,1,0:T(8,128)S(1)}, u32[]{:S(2)}, u32[]{:S(2)}) collective-permute-start(f32[4,6,4,16,128]{4,3,2,1,0:T(8,128)} %get-tuple-element.205), channel_id=1, source_target_pairs={{0,2},{1,3},{2,0},{3,1},{4,6},{5,7},{6,4},{7,5},{8,10},{9,11},{10,... | collective-permute-start | bytes 2359304 | tf_op jit(solution)/shard_map/ppermute | solution.py:651
  225.3 20.3 %collective-permute-start.13 = (f32[2,6,4,16,128]{4,3,2,1,0:T(8,128)}, f32[2,6,4,16,128]{4,3,2,1,0:T(8,128)S(1)}, u32[]{:S(2)}, u32[]{:S(2)}) collective-permute-start(f32[2,6,4,16,128]{4,3,2,1,0:T(8,128)} %get-tuple-element.213), channel_id=1, source_target_pairs={{0,4},{1,5},{2,6},{3,7},{4,0},{5,1},{6,2},{7,3},{8,12},{9,13},{10,... | collective-permute-start | bytes 1179656 | tf_op jit(solution)/shard_map/ppermute | solution.py:651
  246.7 22.6 %collective-permute-start.15 = (f32[2,6,4,16,128]{4,3,2,1,0:T(8,128)S(1)}, f32[2,6,4,16,128]{4,3,2,1,0:T(8,128)S(1)}, u32[]{:S(2)}, u32[]{:S(2)}) collective-permute-start(f32[2,6,4,16,128]{4,3,2,1,0:T(8,128)S(1)} %add_select_fusion.14), channel_id=1, source_target_pairs={{8,0},{9,1},{10,2},{11,3},{12,4},{13,5},{14,6},{15,7},{24,16},{25,... | collective-permute-start | bytes 1179656 | tf_op jit(solution)/shard_map/ppermute | solution.py:764
  282.2 19.5 %collective-permute-start.19 = (f32[4,6,4,16,128]{4,3,2,1,0:T(8,128)S(1)}, f32[4,6,4,16,128]{4,3,2,1,0:T(8,128)S(1)}, u32[]{:S(2)}, u32[]{:S(2)}) collective-permute-start(f32[4,6,4,16,128]{4,3,2,1,0:T(8,128)S(1)} %get-tuple-element.236), channel_id=1, source_target_pairs={{0,2},{1,3},{2,0},{3,1},{4,6},{5,7},{6,4},{7,5},{8,10},{9,11},{10,... | collective-permute-start | bytes 2359304 | tf_op jit(solution)/shard_map/ppermute | solution.py:651
  283.5 64.4 %collective-permute-start.21 = (f32[8,32,2816]{2,1,0:T(8,128)}, f32[8,32,2816]{2,1,0:T(8,128)}, u32[]{:S(2)}, u32[]{:S(2)}) collective-permute-start(f32[8,32,2816]{2,1,0:T(8,128)} %get-tuple-element.251), channel_id=1, source_target_pairs={{0,16},{16,0},{1,17},{17,1},{2,18},{18,2},{3,19},{19,3},{4,20},{20... | collective-permute-start | bytes 8650760 | tf_op jit(solution)/shard_map/ppermute | solution.py:651
  303.5 65.2 %collective-permute-start.22 = (f32[8,32,2816]{2,1,0:T(8,128)}, f32[8,32,2816]{2,1,0:T(8,128)}, u32[]{:S(2)}, u32[]{:S(2)}) collective-permute-start(f32[8,32,2816]{2,1,0:T(8,128)} %get-tuple-element.254), channel_id=1, source_target_pairs={{0,2},{1,3},{2,0},{3,1},{4,6},{5,7},{6,4},{7,5},{8,10},{9,11},{10,... | collective-permute-start | bytes 8650760 | tf_op jit(solution)/shard_map/ppermute | solution.py:651
  305.3 67.3 %collective-permute-start.23 = (f32[8,88,1024]{2,1,0:T(8,128)}, f32[8,88,1024]{2,1,0:T(8,128)}, u32[]{:S(2)}, u32[]{:S(2)}) collective-permute-start(f32[8,88,1024]{2,1,0:T(8,128)} %get-tuple-element.256), channel_id=1, source_target_pairs={{0,4},{1,5},{2,6},{3,7},{4,0},{5,1},{6,2},{7,3},{8,12},{9,13},{10,... | collective-permute-start | bytes 8650760 | tf_op jit(solution)/shard_map/ppermute | solution.py:651
  351.6 25.1 %collective-permute-start.25 = (f32[8,32,2048]{2,1,0:T(8,128)S(1)}, f32[8,32,2048]{2,1,0:T(8,128)S(1)}, u32[]{:S(2)}, u32[]{:S(2)}) collective-permute-start(f32[8,32,2048]{2,1,0:T(8,128)S(1)} %get-tuple-element.252), channel_id=1, source_target_pairs={{0,1},{1,0},{2,3},{3,2},{4,5},{5,4},{6,7},{7,6},{8,9},{9,8},{10,11... | collective-permute-start | bytes 6291464 | tf_op jit(solution)/shard_map/ppermute | solution.py:651
  351.6 25.1 %collective-permute-start.24 = (f32[8,32,2048]{2,1,0:T(8,128)S(1)}, f32[8,32,2048]{2,1,0:T(8,128)S(1)}, u32[]{:S(2)}, u32[]{:S(2)}) collective-permute-start(f32[8,32,2048]{2,1,0:T(8,128)S(1)} %get-tuple-element.258), channel_id=1, source_target_pairs={{0,1},{1,0},{2,3},{3,2},{4,5},{5,4},{6,7},{7,6},{8,9},{9,8},{10,11... | collective-permute-start | bytes 6291464 | tf_op jit(solution)/shard_map/ppermute | solution.py:651
  352.1 48.9 %collective-permute-start.26 = (f32[8,64,1024]{2,1,0:T(8,128)}, f32[8,64,1024]{2,1,0:T(8,128)}, u32[]{:S(2)}, u32[]{:S(2)}) collective-permute-start(f32[8,64,1024]{2,1,0:T(8,128)} %get-tuple-element.269), channel_id=1, source_target_pairs={{0,16},{16,0},{1,17},{17,1},{2,18},{18,2},{3,19},{19,3},{4,20},{20... | collective-permute-start | bytes 6291464 | tf_op jit(solution)/shard_map/ppermute | solution.py:651
  379.5 33.5 %collective-permute-start.28 = (f32[4,32,2816]{2,1,0:T(8,128)}, f32[4,32,2816]{2,1,0:T(8,128)}, u32[]{:S(2)}, u32[]{:S(2)}) collective-permute-start(f32[4,32,2816]{2,1,0:T(8,128)} %get-tuple-element.259), channel_id=1, source_target_pairs={{0,4},{1,5},{2,6},{3,7},{4,0},{5,1},{6,2},{7,3},{8,12},{9,13},{10,... | collective-permute-start | bytes 4325384 | tf_op jit(solution)/shard_map/ppermute | solution.py:651
  381.6 56.6 %collective-permute-start.31 = (f32[8,32,2048]{2,1,0:T(8,128)}, f32[8,32,2048]{2,1,0:T(8,128)}, u32[]{:S(2)}, u32[]{:S(2)}) collective-permute-start(f32[8,32,2048]{2,1,0:T(8,128)} %get-tuple-element.280), channel_id=1, source_target_pairs={{0,2},{1,3},{2,0},{3,1},{4,6},{5,7},{6,4},{7,5},{8,10},{9,11},{10,... | collective-permute-start | bytes 6291464 | tf_op jit(solution)/shard_map/ppermute | solution.py:651
  399.4 37.2 %collective-permute-start.30 = (f32[4,88,1024]{2,1,0:T(8,128)}, f32[4,88,1024]{2,1,0:T(8,128)S(1)}, u32[]{:S(2)}, u32[]{:S(2)}) collective-permute-start(f32[4,88,1024]{2,1,0:T(8,128)} %get-tuple-element.277), channel_id=1, source_target_pairs={{0,16},{16,0},{1,17},{17,1},{2,18},{18,2},{3,19},{19,3},{4,20},{20... | collective-permute-start | bytes 4325384 | tf_op jit(solution)/shard_map/ppermute | solution.py:651
  403.0 31.3 %collective-permute-start.29 = (f32[8,1,896]{2,0,1:T(8,128)S(1)}, f32[8,1,896]{2,0,1:T(8,128)S(1)}, u32[]{:S(2)}, u32[]{:S(2)}) collective-permute-start(f32[8,1,896]{2,0,1:T(8,128)S(1)} %get-tuple-element.271), channel_id=1, source_target_pairs={{0,16},{16,0},{1,17},{17,1},{2,18},{18,2},{3,19},{19,3},{4,20},{20... | collective-permute-start | bytes 86024 | tf_op jit(solution)/shard_map/ppermute | solution.py:651
  403.7 61.2 %collective-permute-start.33 = (f32[4,32,2816]{2,1,0:T(8,128)S(1)}, f32[4,32,2816]{2,1,0:T(8,128)S(1)}, u32[]{:S(2)}, u32[]{:S(2)}) collective-permute-start(f32[4,32,2816]{2,1,0:T(8,128)S(1)} %copy-done.20), channel_id=1, source_target_pairs={{0,2},{1,3},{2,0},{3,1},{4,6},{5,7},{6,4},{7,5},{8,10},{9,11},{10,... | collective-permute-start | bytes 4325384 | tf_op jit(solution)/shard_map/ppermute | solution.py:651
  434.2 27.4 %collective-permute-start.32 = (f32[4,1,896]{2,0,1:T(4,128)S(1)}, f32[4,1,896]{2,0,1:T(4,128)S(1)}, u32[]{:S(2)}, u32[]{:S(2)}) collective-permute-start(f32[4,1,896]{2,0,1:T(4,128)S(1)} %get-tuple-element.275), channel_id=1, source_target_pairs={{0,2},{1,3},{2,0},{3,1},{4,6},{5,7},{6,4},{7,5},{8,10},{9,11},{10,... | collective-permute-start | bytes 43016 | tf_op jit(solution)/shard_map/ppermute | solution.py:651
  435.1 31.6 %collective-permute-start.34 = (f32[2,32,2816]{2,1,0:T(8,128)S(1)}, f32[2,32,2816]{2,1,0:T(8,128)S(1)}, u32[]{:S(2)}, u32[]{:S(2)}) collective-permute-start(f32[2,32,2816]{2,1,0:T(8,128)S(1)} %get-tuple-element.273), channel_id=1, source_target_pairs={{0,16},{16,0},{1,17},{17,1},{2,18},{18,2},{3,19},{19,3},{4,20},{20... | collective-permute-start | bytes 2162696 | tf_op jit(solution)/shard_map/ppermute | solution.py:651
  436.9 47.2 %collective-permute-start.36 = (f32[4,64,1024]{2,1,0:T(8,128)S(1)}, f32[4,64,1024]{2,1,0:T(8,128)S(1)}, u32[]{:S(2)}, u32[]{:S(2)}) collective-permute-start(f32[4,64,1024]{2,1,0:T(8,128)S(1)} %get-tuple-element.278), channel_id=1, source_target_pairs={{0,2},{1,3},{2,0},{3,1},{4,6},{5,7},{6,4},{7,5},{8,10},{9,11},{10,... | collective-permute-start | bytes 3145736 | tf_op jit(solution)/shard_map/ppermute | solution.py:651
  463.7 34.5 %collective-permute-start.37 = (f32[2,88,1024]{2,1,0:T(8,128)S(1)}, f32[2,88,1024]{2,1,0:T(8,128)S(1)}, u32[]{:S(2)}, u32[]{:S(2)}) collective-permute-start(f32[2,88,1024]{2,1,0:T(8,128)S(1)} %get-tuple-element.281), channel_id=1, source_target_pairs={{0,2},{1,3},{2,0},{3,1},{4,6},{5,7},{6,4},{7,5},{8,10},{9,11},{10,... | collective-permute-start | bytes 2162696 | tf_op jit(solution)/shard_map/ppermute | solution.py:651
  465.1 36.2 %collective-permute-start.39 = (f32[4,32,2048]{2,1,0:T(8,128)S(1)}, f32[4,32,2048]{2,1,0:T(8,128)S(1)}, u32[]{:S(2)}, u32[]{:S(2)}) collective-permute-start(f32[4,32,2048]{2,1,0:T(8,128)S(1)} %get-tuple-element.286), channel_id=1, source_target_pairs={{0,16},{16,0},{1,17},{17,1},{2,18},{18,2},{3,19},{19,3},{4,20},{20... | collective-permute-start | bytes 3145736 | tf_op jit(solution)/shard_map/ppermute | solution.py:651
  466.8 33.3 %collective-permute-start.38 = (f32[1,1,896]{2,0,1:T(1,128)S(1)}, f32[1,1,896]{2,0,1:T(1,128)S(1)}, u32[]{:S(2)}, u32[]{:S(2)}) collective-permute-start(f32[1,1,896]{2,0,1:T(1,128)S(1)} %get-tuple-element.290), channel_id=1, source_target_pairs={{0,8},{1,9},{2,10},{3,11},{4,12},{5,13},{6,14},{7,15},{8,0},{9,1},... | collective-permute-start | bytes 10760 | tf_op jit(solution)/shard_map/ppermute | solution.py:651
  468.3 33.1 %collective-permute-start.40 = (f32[2,32,2816]{2,1,0:T(8,128)S(1)}, f32[2,32,2816]{2,1,0:T(8,128)S(1)}, u32[]{:S(2)}, u32[]{:S(2)}) collective-permute-start(f32[2,32,2816]{2,1,0:T(8,128)S(1)} %get-tuple-element.288), channel_id=1, source_target_pairs={{0,4},{1,5},{2,6},{3,7},{4,0},{5,1},{6,2},{7,3},{8,12},{9,13},{10,... | collective-permute-start | bytes 2162696 | tf_op jit(solution)/shard_map/ppermute | solution.py:651
  484.3 20.0 %collective-permute-start.41 = (f32[1,32,2816]{2,1,0:T(8,128)S(1)}, f32[1,32,2816]{2,1,0:T(8,128)S(1)}, u32[]{:S(2)}, u32[]{:S(2)}) collective-permute-start(f32[1,32,2816]{2,1,0:T(8,128)S(1)} %get-tuple-element.292), channel_id=1, source_target_pairs={{0,8},{1,9},{2,10},{3,11},{4,12},{5,13},{6,14},{7,15},{8,0},{9,1},... | collective-permute-start | bytes 1081352 | tf_op jit(solution)/shard_map/ppermute | solution.py:651
  498.3 30.4 %collective-permute-start.42 = (f32[2,64,1024]{2,1,0:T(8,128)S(1)}, f32[2,64,1024]{2,1,0:T(8,128)S(1)}, u32[]{:S(2)}, u32[]{:S(2)}) collective-permute-start(f32[2,64,1024]{2,1,0:T(8,128)S(1)} %get-tuple-element.294), channel_id=1, source_target_pairs={{0,4},{1,5},{2,6},{3,7},{4,0},{5,1},{6,2},{7,3},{8,12},{9,13},{10,... | collective-permute-start | bytes 1572872 | tf_op jit(solution)/shard_map/ppermute | solution.py:651
  501.5 37.1 %collective-permute-start.44 = (f32[2,32,2048]{2,1,0:T(8,128)S(1)}, f32[2,32,2048]{2,1,0:T(8,128)S(1)}, u32[]{:S(2)}, u32[]{:S(2)}) collective-permute-start(f32[2,32,2048]{2,1,0:T(8,128)S(1)} %get-tuple-element.299), channel_id=1, source_target_pairs={{0,4},{1,5},{2,6},{3,7},{4,0},{5,1},{6,2},{7,3},{8,12},{9,13},{10,... | collective-permute-start | bytes 1572872 | tf_op jit(solution)/shard_map/ppermute | solution.py:651
  502.5 29.0 %collective-permute-start.43 = (f32[1,88,1024]{2,1,0:T(8,128)S(1)}, f32[1,88,1024]{2,1,0:T(8,128)S(1)}, u32[]{:S(2)}, u32[]{:S(2)}) collective-permute-start(f32[1,88,1024]{2,1,0:T(8,128)S(1)} %get-tuple-element.297), channel_id=1, source_target_pairs={{0,8},{1,9},{2,10},{3,11},{4,12},{5,13},{6,14},{7,15},{8,0},{9,1},... | collective-permute-start | bytes 1081352 | tf_op jit(solution)/shard_map/ppermute | solution.py:651
  505.1 35.7 %collective-permute-start.45 = (f32[1,32,2816]{2,1,0:T(8,128)S(1)}, f32[1,32,2816]{2,1,0:T(8,128)S(1)}, u32[]{:S(2)}, u32[]{:S(2)}) collective-permute-start(f32[1,32,2816]{2,1,0:T(8,128)S(1)} %get-tuple-element.301), channel_id=1, source_target_pairs={{0,8},{1,9},{2,10},{3,11},{4,12},{5,13},{6,14},{7,15},{8,0},{9,1},... | collective-permute-start | bytes 1081352 | tf_op jit(solution)/shard_map/ppermute | solution.py:651
  528.7 26.9 %collective-permute-start.46 = (f32[1,64,1024]{2,1,0:T(8,128)S(1)}, f32[1,64,1024]{2,1,0:T(8,128)S(1)}, u32[]{:S(2)}, u32[]{:S(2)}) collective-permute-start(f32[1,64,1024]{2,1,0:T(8,128)S(1)} %get-tuple-element.303), channel_id=1, source_target_pairs={{0,8},{1,9},{2,10},{3,11},{4,12},{5,13},{6,14},{7,15},{8,0},{9,1},... | collective-permute-start | bytes 786440 | tf_op jit(solution)/shard_map/ppermute | solution.py:651
  538.8 22.4 %collective-permute-start.47 = (f32[1,32,2048]{2,1,0:T(8,128)S(1)}, f32[1,32,2048]{2,1,0:T(8,128)S(1)}, u32[]{:S(2)}, u32[]{:S(2)}) collective-permute-start(f32[1,32,2048]{2,1,0:T(8,128)S(1)} %get-tuple-element.306), channel_id=1, source_target_pairs={{0,8},{1,9},{2,10},{3,11},{4,12},{5,13},{6,14},{7,15},{8,0},{9,1},... | collective-permute-start | bytes 786440 | tf_op jit(solution)/shard_map/ppermute | solution.py:651
  (53 other events, 494.3 us)

commit v3 on v2

--- a/solution.py
+++ b/solution.py
@@ -33,7 +33,7 @@
     return jax.ShapeDtypeStruct(dims, dtype)
 
 
-def call(body, out_shape, grid, in_specs, out_specs, prefetch=0, scratch=(), flops=0, moved=0):
+def call(body, out_shape, grid, in_specs, out_specs, prefetch=0, scratch=()):
     return pl.pallas_call(
         body,
         out_shape=out_shape,
@@ -44,7 +44,7 @@
             out_specs=out_specs,
             scratch_shapes=list(scratch),
         ),
-        compiler_params=pltpu.CompilerParams(vmem_limit_bytes=56 * MIB),
+        compiler_params=pltpu.CompilerParams(vmem_limit_bytes=60 * MIB),
         cost_estimate=pl.CostEstimate(flops=1, bytes_accessed=1, transcendentals=0),
     )
 
@@ -87,7 +87,8 @@
 def project_body(
     rows, docs, length, hk, hv, parts,
     docs_ref, table_ref, x_ref, gain_ref, wq_ref, wk_ref, wv_ref, wog_ref, wrd_ref, wru_ref, bias_ref,
-    normed_ref, q_ref, k_ref, v_ref, og_ref, ra_ref, gp_ref, cum_ref, keep_ref, send_ref, decay_ref,
+    normed_ref, q_ref, k_ref, v_ref, og_ref, ra_ref, gp_ref, cum_ref, keep_a_ref, send_a_ref, keep_b_ref,
+    send_b_ref, decay_ref,
     hold,
 ):
     x = x_ref[...].astype(F32)
@@ -118,11 +119,12 @@
         weighted = (key[at].astype(F32) * jnp.exp(last - cum) * tail).astype(BF)
         for h in range(HEADS):
             hold[...] = tn(value[at, h * hv : (h + 1) * hv], weighted[:, h * hk : (h + 1) * hk])
+            keep_ref, send_ref = (keep_a_ref, send_a_ref) if h < HEADS // 2 else (keep_b_ref, send_b_ref)
             for j in range(parts // 2):
                 first = pl.multiple_of(table_ref[j] * size, size)
-                keep_ref[j, r, h] = hold[pl.ds(first, size), :]
+                keep_ref[j, r, h % (HEADS // 2)] = hold[pl.ds(first, size), :]
                 second = pl.multiple_of(table_ref[parts // 2 + j] * size, size)
-                send_ref[j, r, h] = hold[pl.ds(second, size), :]
+                send_ref[j, r, h % (HEADS // 2)] = hold[pl.ds(second, size), :]
 
 
 def project_all(x, docs, table, gain, wq, wk, wv, wog, wrd, wru, bias, dims):
@@ -134,8 +136,8 @@
     rank = wrd.shape[0]
     size = hv // parts
     tile = lambda n: block((tm, n), lambda i, *_: (i, 0))
-    half = (parts // 2, row_count, HEADS, size, hk)
-    half_block = block((parts // 2, rows, HEADS, size, hk), lambda i, *_: (0, i, 0, 0, 0))
+    half = (parts // 2, row_count, HEADS // 2, size, hk)
+    half_block = block((parts // 2, rows, HEADS // 2, size, hk), lambda i, *_: (0, i, 0, 0, 0))
     body = functools.partial(project_body, rows, ndocs, length, hk, hv, parts)
     return call(
         body,
@@ -150,6 +152,8 @@
             shape((tokens, kw), F32),
             shape(half, F32),
             shape(half, F32),
+            shape(half, F32),
+            shape(half, F32),
             shape((row_count, 1, kw), F32),
         ),
         (row_count // rows,),
@@ -159,12 +163,11 @@
         ],
         (
             tile(width), tile(kw), tile(kw), tile(vw), tile(vw), tile(rank), tile(kw), tile(kw),
-            half_block, half_block, block((rows, 1, kw), lambda i, *_: (i, 0, 0)),
+            half_block, half_block, half_block, half_block,
+            block((rows, 1, kw), lambda i, *_: (i, 0, 0)),
         ),
         prefetch=2,
         scratch=[pltpu.VMEM((hv, hk), F32)],
-        flops=2 * tokens * width * (2 * kw + 2 * vw),
-        moved=20 * MIB,
     )(docs, table, x, gain.reshape(1, -1), wq, wk, wv, wog, wrd, wru, bias.reshape(1, -1))
 
 
@@ -196,8 +199,6 @@
         [tile(kw), tile(kw), tile(vw), tile(kw)],
         tile(vw),
         prefetch=1,
-        flops=2 * tokens * length * (kw + vw),
-        moved=8 * MIB,
     )(docs, q, k, v, cum)
 
 
@@ -214,7 +215,8 @@
 
 def mix_body(
     docs, length, hk, hv, parts,
-    docs_ref, table_ref, q_ref, cum_ref, inner_ref, og_ref, near_ref, far_ref, gain_ref,
+    docs_ref, table_ref, q_ref, cum_ref, inner_ref, og_ref, near_a_ref, far_a_ref, near_b_ref, far_b_ref,
+    gain_ref,
     mixed_ref, gated_ref, kept_ref,
 ):
     _, alive, _, _ = reset_masks(docs_ref, pl.program_id(0), docs, length)
@@ -223,7 +225,8 @@
     for h in range(HEADS):
         kk = slice(h * hk, (h + 1) * hk)
         vv = slice(h * hv, (h + 1) * hv)
-        state = gather_state(near_ref, far_ref, table_ref, h, parts).astype(BF)
+        near_ref, far_ref = (near_a_ref, far_a_ref) if h < HEADS // 2 else (near_b_ref, far_b_ref)
+        state = gather_state(near_ref, far_ref, table_ref, h % (HEADS // 2), parts).astype(BF)
         kept_ref[0, h] = state
         mixed = scale * (inner_ref[:, vv] + nt(reach[:, kk], state))
         mixed_ref[:, vv] = mixed
@@ -232,12 +235,12 @@
         gated_ref[:, vv] = (mixed * inv * gain_ref[...] * og * jax.nn.sigmoid(og)).astype(BF)
 
 
-def mix_all(q, cum, inner, og, near, far, gain, docs, table, dims):
+def mix_all(q, cum, inner, og, states, gain, docs, table, dims):
     row_count, length, width, kw, vw, ndocs, parts = dims
     tokens = row_count * length
     hk, hv = kw // HEADS, vw // HEADS
     tile = lambda n: block((length, n), lambda i, *_: (i, 0))
-    half = block((parts // 2, 1, HEADS, hv // parts, hk), lambda i, *_: (0, i, 0, 0, 0))
+    half = block((parts // 2, 1, HEADS // 2, hv // parts, hk), lambda i, *_: (0, i, 0, 0, 0))
     return call(
         functools.partial(mix_body, ndocs, length, hk, hv, parts),
         (
@@ -247,72 +250,11 @@
         ),
         (row_count,),
         [
-            tile(kw), tile(kw), tile(vw), tile(vw), half, half, whole((1, hv)),
+            tile(kw), tile(kw), tile(vw), tile(vw), half, half, half, half, whole((1, hv)),
         ],
         (tile(vw), tile(vw), block((1, HEADS, hv, hk), lambda i, *_: (i, 0, 0, 0))),
         prefetch=2,
-        flops=2 * tokens * hk * vw,
-        moved=18 * MIB,
-    )(docs, table, q, cum, inner, og, near, far, gain.reshape(1, -1))
-
-
-def ff_body(
-    steps,
-    x_ref, cot_ref, gated_ref, wo_ref, gain_ref, wg_ref, wu_ref, wd_ref, dh_ref,
-    hidden_ref, dg_ref, du_ref, normed2_ref, out_ref, dmid_ref, dout_ref, dgated_ref, gnorm_ref,
-    middle, total, back,
-):
-    step = pl.program_id(0)
-
-    @pl.when(step == 0)
-    def _():
-        mid = x_ref[...].astype(F32) + nn(gated_ref[...], wo_ref[...])
-        middle[...] = mid
-        inv = lax.rsqrt(jnp.mean(mid * mid, axis=-1, keepdims=True) + EPS)
-        normed2_ref[...] = (mid * inv * gain_ref[...]).astype(BF)
-
-    normed2 = normed2_ref[...]
-    gate = nn(normed2, wg_ref[...])
-    up = nn(normed2, wu_ref[...])
-    d_hidden = dh_ref[...]
-    sig = jax.nn.sigmoid(gate)
-    act = gate * sig
-    hidden = (act * up).astype(BF)
-    dg = (d_hidden * up * sig * (1.0 + gate * (1.0 - sig))).astype(BF)
-    du = (d_hidden * act).astype(BF)
-    hidden_ref[...] = hidden
-    dg_ref[...] = dg
-    du_ref[...] = du
-    more = nn(hidden, wd_ref[...])
-    more_back = nt(dg, wg_ref[...]) + nt(du, wu_ref[...])
-
-    @pl.when(step == 0)
-    def _():
-        total[...] = more
-        back[...] = more_back
-
-    @pl.when(step > 0)
-    def _():
-        total[...] += more
-        back[...] += more_back
-
-    @pl.when(step == steps - 1)
-    def _():
-        mid = middle[...]
-        out_ref[...] = (mid + total[...]).astype(BF)
-        inv = lax.rsqrt(jnp.mean(mid * mid, axis=-1, keepdims=True) + EPS)
-        d_normed2 = back[...]
-        gnorm_ref[...] = jnp.sum(d_normed2 * mid * inv, axis=0, keepdims=True)
-        scaled = d_normed2 * gain_ref[...]
-        d_middle = (
-            cot_ref[...].astype(F32)
-            + inv * scaled
-            - mid * (inv * inv * inv) * jnp.mean(scaled * mid, axis=-1, keepdims=True)
-        )
-        dmid_ref[...] = d_middle
-        d_out = d_middle.astype(BF)
-        dout_ref[...] = d_out
-        dgated_ref[...] = nt(d_out, wo_ref[...])
+    )(docs, table, q, cum, inner, og, *states, gain.reshape(1, -1))
 
 
 def hidden_back_body(cot_ref, wd_ref, dh_ref):
@@ -328,40 +270,125 @@
         (ff // tile,),
         [whole((tokens, width)), block((tile, width), lambda i: (i, 0))],
         block((tokens, tile), lambda i: (0, i)),
-        flops=2 * tokens * width * ff,
-        moved=16 * MIB,
     )(cot, wd)
 
 
-def ff_all(x, cot, gated, wo, gain, wg, wu, wd, dh):
+def ff_body(
+    x_ref, gated_ref, wo_ref, gain_ref, wg_ref, wu_ref, dh_ref,
+    hidden_ref, dg_ref, du_ref, normed2_ref, middle_ref,
+):
+    @pl.when(pl.program_id(0) == 0)
+    def _():
+        mid = x_ref[...].astype(F32) + nn(gated_ref[...], wo_ref[...])
+        middle_ref[...] = mid
+        inv = lax.rsqrt(jnp.mean(mid * mid, axis=-1, keepdims=True) + EPS)
+        normed2_ref[...] = (mid * inv * gain_ref[...]).astype(BF)
+
+    normed2 = normed2_ref[...]
+    gate = nn(normed2, wg_ref[...])
+    up = nn(normed2, wu_ref[...])
+    d_hidden = dh_ref[...]
+    sig = jax.nn.sigmoid(gate)
+    act = gate * sig
+    hidden_ref[...] = (act * up).astype(BF)
+    dg_ref[...] = (d_hidden * up * sig * (1.0 + gate * (1.0 - sig))).astype(BF)
+    du_ref[...] = (d_hidden * act).astype(BF)
+
+
+def ff_all(x, gated, wo, gain, wg, wu, dh):
     tokens, width = x.shape
-    vw = gated.shape[1]
     ff = wg.shape[1]
     tile = 256
+    col = lambda n: block((n, tile), lambda i: (0, i))
+    once = lambda dims: pl.BlockSpec(dims, lambda i: (0, 0), pipeline_mode=pl.Buffered(1))
+    return call(
+        ff_body,
+        (
+            shape((tokens, ff), BF), shape((tokens, ff), BF), shape((tokens, ff), BF),
+            shape((tokens, width), BF), shape((tokens, width), F32),
+        ),
+        (ff // tile,),
+        [
+            once((tokens, width)), once(gated.shape), once(wo.shape), once((1, width)),
+            col(width), col(width), col(tokens),
+        ],
+        (
+            col(tokens), col(tokens), col(tokens), whole((tokens, width)), whole((tokens, width)),
+        ),
+    )(x, gated, wo, gain.reshape(1, -1), wg, wu, dh)
+
+
+def ff_back_body(
+    steps,
+    hidden_ref, dg_ref, du_ref, wd_ref, wg_ref, wu_ref, middle_ref, cot_ref, wo_ref, gain_ref,
+    out_ref, dmid_ref, dout_ref, dgated_ref, gnorm_ref,
+):
+    total, back = dgated_ref, dmid_ref
+    step = pl.program_id(0)
+    tokens = middle_ref.shape[0]
+    rows = 256 if tokens % 256 == 0 else tokens
+    for first in range(0, tokens, rows):
+        at = slice(first, first + rows)
+        more = nn(hidden_ref[at, :], wd_ref[...])
+        more_back = nt(dg_ref[at, :], wg_ref[...]) + nt(du_ref[at, :], wu_ref[...])
+
+        @pl.when(step == 0)
+        def _(at=at, more=more, more_back=more_back):
+            total[at, :] = more
+            back[at, :] = more_back
+
+        @pl.when(step > 0)
+        def _(at=at, more=more, more_back=more_back):
+            total[at, :] += more
+            back[at, :] += more_back
+
+    @pl.when(step == steps - 1)
+    def _():
+        gnorm = jnp.zeros((1, middle_ref.shape[1]), F32)
+        for first in range(0, tokens, rows):
+            at = slice(first, first + rows)
+            mid = middle_ref[at, :]
+            out_ref[at, :] = (mid + total[at, :]).astype(BF)
+            inv = lax.rsqrt(jnp.mean(mid * mid, axis=-1, keepdims=True) + EPS)
+            d_normed2 = back[at, :]
+            gnorm = gnorm + jnp.sum(d_normed2 * mid * inv, axis=0, keepdims=True)
+            scaled = d_normed2 * gain_ref[...]
+            d_middle = (
+                cot_ref[at, :].astype(F32)
+                + inv * scaled
+                - mid * (inv * inv * inv) * jnp.mean(scaled * mid, axis=-1, keepdims=True)
+            )
+            dmid_ref[at, :] = d_middle
+            d_out = d_middle.astype(BF)
+            dout_ref[at, :] = d_out
+            dgated_ref[at, :] = nt(d_out, wo_ref[...])
+        gnorm_ref[...] = gnorm
+
+
+def ff_back_all(hidden, dg, du, wd, wg, wu, middle, cot, wo, gain):
+    tokens, width = middle.shape
+    vw, ff = wo.shape[0], wg.shape[1]
+    tile = 1408 if ff % 1408 == 0 else 256
     steps = ff // tile
     col = lambda n: block((n, tile), lambda i: (0, i))
     once = lambda dims: pl.BlockSpec(dims, lambda i: (0, 0), pipeline_mode=pl.Buffered(1))
     return call(
-        functools.partial(ff_body, steps),
+        functools.partial(ff_back_body, steps),
         (
-            shape((tokens, ff), BF), shape((tokens, ff), BF), shape((tokens, ff), BF),
-            shape((tokens, width), BF), shape((tokens, width), BF), shape((tokens, width), F32),
-            shape((tokens, width), BF), shape((tokens, vw), F32), shape((1, width), F32),
+            shape((tokens, width), BF), shape((tokens, width), F32), shape((tokens, width), BF),
+            shape((tokens, vw), F32), shape((1, width), F32),
         ),
         (steps,),
         [
-            once((tokens, width)), once((tokens, width)), once((tokens, vw)), once(wo.shape),
-            once((1, width)), col(width), col(width), block((tile, width), lambda i: (i, 0)), col(tokens),
+            col(tokens), col(tokens), col(tokens), block((tile, width), lambda i: (i, 0)),
+            col(width), col(width), once((tokens, width)), once((tokens, width)), once(wo.shape),
+            once((1, width)),
         ],
         (
-            col(tokens), col(tokens), col(tokens),
             whole((tokens, width)), whole((tokens, width)), whole((tokens, width)),
-            whole((tokens, width)), whole((tokens, vw)), whole((1, width)),
+            whole((tokens, vw)), whole((1, width)),
         ),
-        scratch=[pltpu.VMEM((tokens, width), F32)] * 3,
-        flops=10 * tokens * width * ff,
-        moved=45 * MIB,
-    )(x, cot, gated, wo, gain.reshape(1, -1), wg, wu, wd, dh)
+    )(hidden, dg, du, wd, wg, wu, middle, cot, wo, gain.reshape(1, -1))
 
 
 def head_back_body(
@@ -431,8 +458,6 @@
         (tile(vw), tile(vw), half_block, half_block, whole((1, hv))),
         prefetch=2,
         scratch=[pltpu.VMEM((hv, hk), F32)],
-        flops=2 * tokens * hk * vw,
-        moved=20 * MIB,
     )(docs, table, dgated, og, mixed, q, cum, gain.reshape(1, -1))
 
 
@@ -530,8 +555,6 @@
         ],
         (tile(2 * kw + vw), tile(rank), whole((rank, kw)), whole((1, kw))),
         prefetch=2,
-        flops=16 * tokens * length * vw,
-        moved=16 * MIB,
     )(docs, table, q, k, v, cum, gp, ra, dmix, state, near, far, wru)
 
 
@@ -582,8 +605,6 @@
             whole(wrd.shape),
         ],
         (tile(width), whole((1, width))),
-        flops=2 * tokens * width * (2 * kw + 2 * vw),
-        moved=20 * MIB,
     )(x, dmid, dqkv, dog, drank, gain.reshape(1, -1), wq, wk, wv, wog, wrd)
 
 
@@ -607,16 +628,17 @@
             send_ref[j, at, :] = hold[pl.ds(second, per), :]
 
 
-def weight_grads(pairs, table):
+def weight_grads(pairs, table, columns=None):
     count, pieces = len(pairs), table.shape[0]
     tokens, rows = pairs[0][0].shape
     per = rows // pieces
-    cols = pairs[0][1].shape[1]
+    start, cols = columns or (0, pairs[0][1].shape[1])
     if per % 8:
-        both = [tn(left, right) for left, right in pairs]
+        both = [tn(left, right[:, start : start + cols]) for left, right in pairs]
         parts = jnp.concatenate([part.reshape(pieces, per, cols) for part in both], axis=1)[table]
         return parts[: pieces // 2], parts[pieces // 2 :]
-    tile = next(n for n in (1408, 512, 256, 128) if cols % n == 0)
+    tile = next(n for n in (1408, 512, 256, 128) if cols % n == 0 and start % n == 0)
+    skip = start // tile
     half = shape((pieces // 2, count * per, cols), F32)
     half_block = block((pieces // 2, count * per, tile), lambda i, *_: (0, 0, i))
     return call(
@@ -624,13 +646,70 @@
         (half, half),
         (cols // tile,),
         [whole((tokens, rows))] * count
-        + [block((tokens, tile), lambda i, *_: (0, i))] * count,
+        + [block((tokens, tile), lambda i, *_: (0, i + skip))] * count,
         (half_block, half_block),
         prefetch=1,
         scratch=[pltpu.VMEM((rows, tile), F32)] + [pltpu.VMEM((rows, tokens), BF)] * count,
-        flops=2 * tokens * rows * cols * count,
-        moved=4 * rows * cols * count,
     )(table, *[left for left, _ in pairs], *[right for _, right in pairs])
+
+
+def small_body(
+    pieces,
+    table_ref, normed_ref, drank_ref, gnorm1_ref, gnorm2_ref, grup_ref, gbias_ref, ggroup_ref,
+    keep_ref, send_ref,
+    hold,
+):
+    width, kw, hv = gnorm1_ref.shape[1], gbias_ref.shape[1], ggroup_ref.shape[1]
+    rank = grup_ref.shape[0]
+
+    def stand(rows):
+        have = sum(row.shape[0] for row in rows)
+        return jnp.concatenate(rows + [jnp.zeros((128 - have, rows[0].shape[1]), F32)], axis=0).T
+
+    spread = jnp.zeros((normed_ref.shape[0], 128 - rank), BF)
+    hold[:width, :] = tn(normed_ref[...], jnp.concatenate([drank_ref[...], spread], axis=1)) + stand(
+        [jnp.zeros((rank, width), F32), gnorm1_ref[...], gnorm2_ref[...]]
+    )
+    hold[width : width + kw, :] = stand([grup_ref[...], gbias_ref[...]])
+    hold[width + kw :, :] = stand([ggroup_ref[...]])
+    first, place = 0, 0
+    for rows in (width, kw, hv):
+        per = rows // pieces
+        for j in range(pieces // 2):
+            keep = pl.multiple_of(first + table_ref[j] * per, per)
+            keep_ref[j, place : place + per, :] = hold[pl.ds(keep, per), :]
+            send = pl.multiple_of(first + table_ref[pieces // 2 + j] * per, per)
+            send_ref[j, place : place + per, :] = hold[pl.ds(send, per), :]
+        first, place = first + rows, place + per
+
+
+def small_grads(normed, drank, gnorm1, gnorm2, grup, gbias, ggroup, table):
+    pieces, rank = table.shape[0], grup.shape[0]
+    width, kw, hv = gnorm1.shape[1], gbias.shape[1], ggroup.shape[1]
+    rows = (width + kw + hv) // pieces
+    if hv // pieces % 8:
+        wide = lambda value: jnp.pad(value, ((0, 0), (0, 128 - value.shape[1])))
+        cut = lambda value: wide(value).reshape(pieces, -1, 128)
+        both = jnp.concatenate(
+            [
+                cut(jnp.concatenate([tn(normed, drank), gnorm1.T, gnorm2.T], axis=1)),
+                cut(jnp.concatenate([grup.T, gbias.T], axis=1)),
+                cut(ggroup.T),
+            ],
+            axis=1,
+        )[table]
+        return both[: pieces // 2], both[pieces // 2 :]
+    half = shape((pieces // 2, rows, 128), F32)
+    operands = (normed, drank, gnorm1, gnorm2, grup, gbias, ggroup)
+    return call(
+        functools.partial(small_body, pieces),
+        (half, half),
+        (1,),
+        [whole(value.shape) for value in operands],
+        (whole(half.shape), whole(half.shape)),
+        prefetch=1,
+        scratch=[pltpu.VMEM((width + kw + hv, 128), F32)],
+    )(table, *operands)
 
 
 def bits_of(n):
@@ -711,24 +790,19 @@
         task.wanted = []
 
 
-def reduce_steps(links, turns, make, order, out, name, halves=False):
+def reduce_steps(links, turns, make, order, out, name):
     keep, send = make()
     turns.done(keep, send)
     for k, bit in enumerate(order):
-        swap = functools.partial(links.swap, bit=bit)
-        half = keep.shape[0] // 2
-        if halves and k == 0:
-            near, far = yield [(send[:half], swap), (send[half:], swap)]
-        else:
-            (got,) = yield [(send, swap)]
-            near, far = got[:half], got[half:]
+        (got,) = yield [(send, functools.partial(links.swap, bit=bit))]
         keep = turns.after(keep)
         if k == len(order) - 1:
             out[name] = keep + got
             turns.done(out[name])
             return
-        send = keep[half:] + far
-        keep = keep[:half] + near
+        half = keep.shape[0] // 2
+        send = keep[half:] + got[half:]
+        keep = keep[:half] + got[:half]
         turns.done(keep, send)
 
 
@@ -778,21 +852,23 @@
 
 ROUTES = {
     "gate": ("x", "y", "z0", "z1"),
-    "up": ("y", "z0", "x", "z1"),
-    "down": ("z0", "x", "y", "z1"),
+    "up": ("y", "x", "z0", "z1"),
+    "down": ("z0", "y", "x", "z1"),
     "mid": ("x", "y", "z0", "z1"),
-    "qkv": ("y", "x", "z0", "z1"),
+    "qk": ("x", "y", "z0", "z1"),
+    "v": ("y", "x", "z0", "z1"),
     "small": ("x", "y", "z0", "z1"),
 }
 SCHEDULE = (
-    "scan", ("scan",), "gate", "scan", ("scan", "gate"), "up", "gate", "scan", ("scan", "up"),
-    "down", "up", "scan", ("scan", "down"), "mid", "down", "scan", ("scan", "mid", "gate"),
-    "mid", "scan", ("scan", "down"), "scan", ("scan", "up"), "scan", "qkv", "gate", ("qkv",
-    "mid"), "up", "down", "qkv", ("up", "qkv", "down"), "small", ("small",), "mid", "small",
-    ("small", "gate"), "up", ("up",), "small", ("small",), "down", ("mid",), "qkv", ("down",),
-    "small", ("small",), "gate", ("qkv",), "up", ("gate",), "small", ("small",), "mid", ("up",),
-    "down", ("mid",), "small", "qkv", ("down",), "gate", ("qkv",), "up", ("gate",), "mid",
-    ("mid",), "down", "qkv", ("qkv",), "gate", "mid", "qkv",
+    "gate", ("gate",), "up", ("up",), "down", ("down",), "gate", ("gate",), "up", ("up",),
+    "down", ("down",), "ff", "scan", ("scan",), "gate", "up", "down", "scan", ("scan", "up"),
+    "mid", "scan", ("scan", "gate", "mid"), "mid", "scan", ("scan", "mid", "down"), "up",
+    "gate", "scan", ("scan",), "scan", ("scan",), "down", "mid", "scan", ("scan", "gate", "up",
+    "down", "mid"), "scan", "qk", "v", "gate", "up", "down", "mid", ("qk", "v", "gate", "up",
+    "mid"), "qk", "v", ("qk", "v"), "small", "small", "qk", "v", ("qk", "v"), "gate", "up",
+    ("small", "down"), "mid", "qk", "v", "small", ("qk", "v", "small"), "small", ("mid",),
+    "down", "qk", "v", ("small", "qk", "v"), "small", ("small",), "small", ("small",), "mid",
+    "qk", "v", "small",
 )
 
 
@@ -824,82 +900,110 @@
     to_place = (reverse[jnp.arange(step) ^ low][:, None] * size + spread).reshape(-1)
     state_table = jnp.concatenate([to_piece, to_place]).astype(jnp.int32)
 
-    normed, q, k, v, og, ra, gp, cum, keep, send, decay = project_all(
+    normed, q, k, v, og, ra, gp, cum, keep_a, send_a, keep_b, send_b, decay = project_all(
         x, docs, state_table, norm1_gain, w_query, w_key, w_value, w_outgate, rank_down_t, w_rank_up,
         decay_bias, dims,
     )
     decay = decay.reshape(1, row_count, HEADS, 1, kw // HEADS)
-    fwd = {}
-    scan = Task(scan_steps(links, turns, lambda: (keep, send, decay), None, False, fwd))
-    scan.advance(turns)
-    scan.advance(turns)
-    start([scan], turns)
+    fwd_a, fwd_b = {}, {}
+    one = Task(scan_steps(
+        links, turns, lambda: (keep_a, send_a, decay[:, :, : HEADS // 2]), None, False, fwd_a
+    ))
+    two = Task(scan_steps(
+        links, turns, lambda: (keep_b, send_b, decay[:, :, HEADS // 2 :]), None, False, fwd_b
+    ))
+    one.advance(turns)
+    start([one], turns)
+    two.advance(turns)
+    start([two], turns)
+    one.advance(turns)
+    start([one], turns)
+    two.advance(turns)
+    start([two], turns)
     dh = hidden_back_all(turns.after(cot), w_ffdown)
     turns.done(dh)
-    scan.advance(turns)
-    start([scan], turns)
+    one.advance(turns)
+    start([one], turns)
+    two.advance(turns)
+    start([two], turns)
     inner = inner_all(q, k, v, cum, turns.after(docs), dims)
     turns.done(inner)
-    scan.finish(turns)
+    while not two.over:
+        one.advance(turns)
+        start([one], turns)
+        two.advance(turns)
+        start([two], turns)
+    decays = [
+        tuple(jnp.concatenate(pair, axis=2) for pair in zip(*both))
+        for both in zip(fwd_a["decays"], fwd_b["decays"])
+    ]
+    states = (fwd_a["near"], fwd_a["far"], fwd_b["near"], fwd_b["far"])
     mixed, gated, state_kept = mix_all(
-        q, cum, inner, og, fwd["near"], fwd["far"], group_gain, turns.after(docs), state_table, dims
+        q, cum, inner, og, states, group_gain, turns.after(docs), state_table, dims
     )
-    hidden, dg, du, normed2, block_out, d_middle, d_out, d_gated, gnorm2 = ff_all(
-        x, cot, gated, w_output, norm2_gain, w_ffgate, w_ffup, w_ffdown, dh
+    hidden, dg, du, normed2, middle = ff_all(
+        x, gated, w_output, norm2_gain, w_ffgate, w_ffup, dh
     )
+    turns.done(normed2)
 
     routes = {name: links.order(*route) for name, route in ROUTES.items()}
     tables = {route: links.table(route) for route in set(routes.values())}
     back, grads, held = {}, {}, {}
     ff = w_ffgate.shape[1]
 
+    def ff_steps():
+        out, d_middle, d_out, d_gated, gnorm2 = ff_back_all(
+            hidden, dg, du, w_ffdown, w_ffgate, w_ffup, middle, turns.after(cot), w_output, norm2_gain
+        )
+        held.update(out=out, d_middle=d_middle, d_out=d_out, d_gated=d_gated, gnorm2=gnorm2)
+        turns.done(d_out)
+        return
+        yield
+
     def head_back():
         d_mix, d_og, keep, send, ggroup = head_back_all(
-            d_gated, og, mixed, q, cum, group_gain, turns.after(docs), state_table, dims
+            held["d_gated"], og, mixed, q, cum, group_gain, turns.after(docs), state_table, dims
         )
         held.update(d_mix=d_mix, d_og=d_og, ggroup=ggroup)
         return keep, send, None
 
     def all_back():
-        yield from scan_steps(links, turns, head_back, fwd["decays"], True, back)
+        yield from scan_steps(links, turns, head_back, decays, True, back)
         held["d_qkv"], held["d_rank"], held["grup"], held["gbias"] = mix_back_all(
             q, k, v, cum, gp, ra, held["d_mix"], state_kept, back["near"], back["far"], w_rank_up,
             turns.after(docs), state_table, dims,
         )
         turns.done(held["d_rank"])
 
-    def weights(name, pairs, halves=False):
+    def weights(name, pairs, columns=None):
         order = routes[name]
-        make = lambda: weight_grads(pairs(), turns.after(tables[order]))
-        return reduce_steps(links, turns, make, order, grads, name, halves)
+        make = lambda: weight_grads(pairs(), turns.after(tables[order]), columns)
+        return reduce_steps(links, turns, make, order, grads, name)
 
     def small_steps():
         grad_in, gnorm1 = input_back_all(
-            x, d_middle, held["d_qkv"], held["d_og"], held["d_rank"], turns.after(norm1_gain), w_query,
-            w_key, w_value, w_outgate, rank_down_t,
+            x, held["d_middle"], held["d_qkv"], held["d_og"], held["d_rank"], turns.after(norm1_gain),
+            w_query, w_key, w_value, w_outgate, rank_down_t,
         )
         held["grad_in"] = grad_in
-        by_device = lambda value: value.reshape(everyone, -1)
-        small = [
-            by_device(tn(normed, held["d_rank"])),
-            held["grup"].reshape(rank, everyone, -1).transpose(1, 0, 2).reshape(everyone, -1),
-            by_device(gnorm1), by_device(gnorm2), by_device(held["gbias"]), by_device(held["ggroup"]),
-        ]
-        held["widths"] = [part.shape[1] for part in small]
-        packed = jnp.concatenate(small, axis=1)
-        packed = jnp.pad(packed, ((0, 0), (0, -packed.shape[1] % 128)))[tables[routes["small"]]]
-        packed = packed.reshape(everyone, 1, -1)
-        make = lambda: (packed[: everyone // 2], packed[everyone // 2 :])
+        turns.done(gnorm1)
+        yield []
+        make = lambda: small_grads(
+            normed, held["d_rank"], gnorm1, held["gnorm2"], held["grup"], held["gbias"],
+            held["ggroup"], turns.after(tables[routes["small"]]),
+        )
         yield from reduce_steps(links, turns, make, routes["small"], grads, "small")
 
     rank = w_rank_up.shape[0]
     work = {
+        "ff": ff_steps(),
         "scan": all_back(),
         "gate": weights("gate", lambda: [(normed2, dg)]),
         "up": weights("up", lambda: [(normed2, du)]),
         "down": weights("down", lambda: [(hidden, cot)]),
-        "mid": weights("mid", lambda: [(gated, d_out), (normed, held["d_og"])]),
-        "qkv": weights("qkv", lambda: [(normed, held["d_qkv"])], True),
+        "mid": weights("mid", lambda: [(gated, held["d_out"]), (normed, held["d_og"])]),
+        "qk": weights("qk", lambda: [(normed, held["d_qkv"])], (0, 2 * kw)),
+        "v": weights("v", lambda: [(normed, held["d_qkv"])], (2 * kw, vw)),
         "small": small_steps(),
     }
     work = {name: Task(steps) for name, steps in work.items()}
@@ -907,32 +1011,30 @@
         if isinstance(name, tuple):
             start([work[each] for each in name], turns)
             continue
-        if name in ("qkv", "small"):
+        if name in ("scan", "mid"):
+            work["ff"].finish(turns)
+        if name in ("qk", "v", "small"):
             work["scan"].finish(turns)
         work[name].advance(turns)
 
-    packed = grads["small"].reshape(-1)
-    out_small, at = [], 0
-    for n in held["widths"]:
-        out_small.append(packed[at : at + n])
-        at += n
-    s_down, s_up, s_norm1, s_norm2, s_bias, s_group = out_small
-    per = width // everyone
-    mid, qkv = grads["mid"][0], grads["qkv"][0]
+    per, per_k = width // everyone, kw // everyone
+    small = grads["small"][0]
+    first, second, third = small[:per], small[per : per + per_k], small[per + per_k :]
+    mid, qk = grads["mid"][0], grads["qk"][0]
     return (
-        block_out.reshape(row_count, length, width),
+        held["out"].reshape(row_count, length, width),
         held["grad_in"].reshape(row_count, length, width),
-        s_norm1,
-        qkv[:, :kw],
-        qkv[:, kw : 2 * kw],
-        qkv[:, 2 * kw :],
+        first[:, rank],
+        qk[:, :kw],
+        qk[:, kw:],
+        grads["v"][0],
         mid[per:],
-        s_down.reshape(-1, rank),
-        s_up.reshape(rank, -1),
-        s_bias,
-        s_group,
+        first[:, :rank],
+        second[:, :rank].T,
+        second[:, rank],
+        third[:, 0],
         mid[:per],
-        s_norm2,
+        first[:, rank + 1],
         grads["gate"][0],
         grads["up"][0],
         grads["down"][0],

time: 570 us -> 543 us (0.953)
  waiting for transfers between devices: 229 us -> 157 us
  starting transfers between devices: 56.7 us -> 75.8 us
  Pallas kernels: 188 us -> 203 us
  other arithmetic: 67.3 us -> 80.3 us
    ppermute x46 -> x59, waiting for transfers between devices: 220 us -> 155 us  [swap(): return lax.ppermute(value, name, [(i, i ^ flip) for i in range(n)])]
    ppermute x46 -> x59, starting transfers between devices: 51 us -> 68.1 us  [swap(): return lax.ppermute(value, name, [(i, i ^ flip) for i in range(n)])]
    pallas_call x1 -> x3, Pallas kernels: 47.5 us -> 59.5 us  [the longest x1 32 us: ff_back_all(): call(functools.partial(ff_back_body, steps), (shape((tokens, width), BF),...]
    add x24 -> x28, other arithmetic: 46.2 us -> 53.9 us  [the longest x17 28.2 us: reduce_steps(): keep = keep[:half] + got[:half]]
    ppermute x2 -> x3, waiting for transfers between devices: 9.01 us -> 2.19 us  [scan_steps(): state, = (yield [(send, lambda value: lax.ppermute(value, 'seq', pairs))])]
    pallas_call x5 -> x6, Pallas kernels: 55.4 us -> 58.3 us  [weight_grads(): call(functools.partial(weight_body, count, pieces, per), (half, half), (c...]
  transfers between devices with their start and end apart: 48 -> 62, of which waited for: 24 -> 34; matrix products, arithmetic and copies ran while one was open for 12% -> 14% of each run, Pallas kernels for 19% -> 27%
where the time goes in v3:
time: 543 us; the launch traced here: 535 us
  Pallas kernels  203 us (37%)
  waiting for transfers between devices  157 us (29%)
  other arithmetic  80.3 us (15%)
  starting transfers between devices  75.8 us (14%)
  local copies, waits for them, and re-layouts  16.2 us (3%)
    ppermute x59, waiting for transfers between devices, swap(): return lax.ppermute(value, name, [(i, i ^ flip) for i in range(n)])  155 us
    ppermute x59, starting transfers between devices, swap(): return lax.ppermute(value, name, [(i, i ^ flip) for i in range(n)])  68.1 us
    pallas_call x6, Pallas kernels, weight_grads(): call(functools.partial(weight_body, count, pieces, per), (half, half), (c...  58.3 us
    pallas_call x1, Pallas kernels, ff_back_all(): call(functools.partial(ff_back_body, steps), (shape((tokens, width), BF),...  32 us
    add x17, other arithmetic, reduce_steps(): keep = keep[:half] + got[:half]  28.2 us
    add x11, other arithmetic, reduce_steps(): send = keep[half:] + got[half:]  25.7 us
    pallas_call x1, Pallas kernels, ff_all(): call(ff_body, (shape((tokens, ff), BF), shape((tokens, ff), BF), shape((t...  23.5 us
    pallas_call x1, Pallas kernels, project_all(): call(body, (shape((tokens, width), BF), shape((tokens, kw), BF), shape((t...  16 us
  transfers between devices with their start and end apart: 62, of which 34 were waited for; matrix products, arithmetic and copies ran while one was open for 14% of the time, Pallas kernels for 27%

profile of v3, /device:TPU:0, one launch (start us, length us, event | category | flops | bytes accessed | tf_op | source)
XLA Modules:
  0.0 534.9 jit_solution(3182459921626074734)
XLA Ops:
  4.9 16.0 %shard_map.324 = (bf16[768,1024]{1,0:T(8,128)(2,1)}, bf16[768,512]{1,0:T(8,128)(2,1)}, bf16[768,512]{1,0:T(8,128)(2,1)}, bf16[768,1024]{1,0:T(8,128)(2,1)}, f32[...) custom-call(s32[24]{0:T(128)} %reshape.104.docs_ref, ...), custom_call_target="tpu_custom_call" | custom-call | flops 1 | bytes 1 | tf_op jit(solution)/shard_map/pallas_call | solution.py:142
  33.3 12.9 %shard_map.325.dh_ref = f32[768,2816]{1,0:T(8,128)} custom-call(bf16[768,1024]{1,0:T(8,128)(2,1)} %bitcast.56, bf16[2816,1024]{1,0:T(8,128)(2,1)} %wd_ref.3), custom_call_target="tpu_custom_call" | custom-call | flops 1 | bytes 1 | tf_op jit(solution)/shard_map/pallas_call | solution.py:267
  55.0 8.5 %shard_map.326.inner_ref = f32[768,1024]{1,0:T(8,128)} custom-call(s32[24]{0:T(128)} %reshape.104.docs_ref, bf16[768,512]{1,0:T(8,128)(2,1)} %get-tuple-element.222.q_ref, bf16[768,512]{1,0:T(8,128)(2,1)} %get-tuple-element.223.k_ref, bf16[768,1024]{1,0:T(8,128)(2,1)} %get-tuple-element.224.v_ref, f32[768,512]{1,0:T(8,128)} %get-tuple-element.225.cum_ref), custom_call_target="tpu_custom_call" | custom-call | flops 1 | bytes 1 | tf_op jit(solution)/shard_map/pallas_call | solution.py:195
  64.4 4.9 collective-permute-start.13
  74.8 7.8 %collective-permute-start.14 = (f32[2,6,2,16,128]{4,3,2,1,0:T(8,128)S(1)}, f32[2,6,2,16,128]{4,3,2,1,0:T(8,128)S(1)}, u32[]{:S(2)}, u32[]{:S(2)}) collective-permute-start(f32[2,6,2,16,128]{4,3,2,1,0:T(8,128)S(1)} %get-tuple-element.230), channel_id=1, source_target_pairs={{0,4},{1,5},{2,6},{3,7},{4,0},{5,1},{6,2},{7,3},{8,12},{9,13},{10,... | collective-permute-start | bytes 589832 | tf_op jit(solution)/shard_map/ppermute | solution.py:730
  94.5 6.0 %collective-permute-done.16 = f32[4,6,2,16,128]{4,3,2,1,0:T(8,128)S(1)} collective-permute-done((f32[4,6,2,16,128]{4,3,2,1,0:T(8,128)S(1)}, f32[4,6,2,16,128]{4,3,2,1,0:T(8,128)S(1)}, u32[]{:S(2)}, u32[]{:S(2)}) %collective-permute-start.16) | collective-permute-done | bytes 393248 | tf_op jit(solution)/shard_map/ppermute | solution.py:730
  102.0 5.0 collective-permute-done.17
  112.8 9.7 %shard_map.327 = (f32[768,1024]{1,0:T(8,128)}, bf16[768,1024]{1,0:T(8,128)(2,1)}, bf16[6,4,256,128]{3,2,1,0:T(8,128)(2,1)}) custom-call(s32[24]{0:T(128)} %reshape.104.docs_ref, s32[32]{0:T(128)} %pad_add_fusion.table_ref, bf16[768,512]{1,0:T(8,128)(2,1)} %get-tuple-element.222.q_ref, f32[768,512]{1,0:T(8,128)} %get-tuple-element.225.cum_ref, ...), custom_call_target="tpu_custom_call" | custom-call | flops 1 | bytes 1 | tf_op jit(solution)/shard_map/pallas_call | solution.py:244
  122.4 23.5 %shard_map.328 = (bf16[768,2816]{1,0:T(8,128)(2,1)}, bf16[768,2816]{1,0:T(8,128)(2,1)}, bf16[768,2816]{1,0:T(8,128)(2,1)}, bf16[768,1024]{1,0:T(8,128)(2,1)}, f32[768,1024]{1,0:T(8,128)}) custom-call(bf16[768,1024]{1,0:T(8,128)(2,1)} %bitcast.60, bf16[768,1024]{1,0:T(8,128)(2,1)} %get-tuple-element.247.gated_ref.refs_0_, bf16[1024,1024]{1,0:T(8,128)(2,1)} %wo_ref.3, ...), custom_call_target="tpu_custom_call" | custom-call | flops 1 | bytes 1 | tf_op jit(solution)/shard_map/pallas_call | solution.py:304
  145.9 11.5 %shard_map.329 = (f32[16,32,2816]{2,1,0:T(8,128)}, f32[16,32,2816]{2,1,0:T(8,128)}) custom-call(s32[32]{0:T(128)} %get-tuple-element.342.table_ref, bf16[768,1024]{1,0:T(8,128)(2,1)} %get-tuple-element.252.refs_0_, bf16[768,2816]{1,0:T(8,128)(2,1)} %get-tuple-element.249.refs_1_.dg_ref), custom_call_target="tpu_custom_call" | custom-call | flops 1 | bytes 1 | tf_op jit(solution)/shard_map/pallas_call | solution.py:644
  157.6 11.7 %shard_map.330 = (f32[16,32,2816]{2,1,0:T(8,128)}, f32[16,32,2816]{2,1,0:T(8,128)}) custom-call(s32[32]{0:T(128)} %get-tuple-element.323.table_ref, bf16[768,1024]{1,0:T(8,128)(2,1)} %get-tuple-element.252.refs_0_, bf16[768,2816]{1,0:T(8,128)(2,1)} %get-tuple-element.250.refs_1_.du_ref), custom_call_target="tpu_custom_call" | custom-call | flops 1 | bytes 1 | tf_op jit(solution)/shard_map/pallas_call | solution.py:644
  170.1 12.4 %shard_map.331 = (f32[16,88,1024]{2,1,0:T(8,128)}, f32[16,88,1024]{2,1,0:T(8,128)}) custom-call(s32[32]{0:T(128)} %broadcast_xor_fusion.2.table_ref, bf16[768,2816]{1,0:T(8,128)(2,1)} %get-tuple-element.248.refs_0_.hidden_ref, bf16[768,1024]{1,0:T(8,128)(2,1)} %bitcast.57), custom_call_target="tpu_custom_call" | custom-call | flops 1 | bytes 1 | tf_op jit(solution)/shard_map/pallas_call | solution.py:644
  182.8 6.8 %slice_add_fusion.4 = (f32[8,32,2816]{2,1,0:T(8,128)S(1)}, f32[8,32,2816]{2,1,0:T(8,128)}) fusion(f32[16,32,2816]{2,1,0:T(8,128)} %collective-permute-done.20, f32[16,32,2816]{2,1,0:T(8,128)} %get-tuple-element.265), kind=kLoop, calls=%fused_computation.5 | loop fusion | flops 1441792 | bytes 17301504 | tf_op jit(solution)/shard_map/add | solution.py:805
  191.1 6.1 %slice_add_fusion.2 = (f32[8,32,2816]{2,1,0:T(8,128)}, f32[8,32,2816]{2,1,0:T(8,128)}) fusion(f32[16,32,2816]{2,1,0:T(8,128)} %collective-permute-done.21, f32[16,32,2816]{2,1,0:T(8,128)S(1)} %bitcast.65), kind=kLoop, calls=%fused_computation.3 | loop fusion | flops 1441792 | bytes 17301504 | tf_op jit(solution)/shard_map/add | solution.py:805
  204.1 32.0 %shard_map.332 = (bf16[768,1024]{1,0:T(8,128)(2,1)}, f32[768,1024]{1,0:T(8,128)}, bf16[768,1024]{1,0:T(8,128)(2,1)}, f32[768,1024]{1,0:T(8,128)}, f32[1,1024]{1,0:T(1,128)}) custom-call(bf16[768,2816]{1,0:T(8,128)(2,1)} %get-tuple-element.248.refs_0_.hidden_ref, bf16[768,2816]{1,0:T(8,128)(2,1)} %get-tuple-element.249.refs_1_.dg_ref, ...), custom_call_target="tpu_custom_call" | custom-call | flops 1 | bytes 1 | tf_op jit(solution)/shard_map/pallas_call | solution.py:375
  236.1 10.9 %shard_map.333 = (bf16[768,1024]{1,0:T(8,128)(2,1)}, bf16[768,1024]{1,0:T(8,128)(2,1)}, f32[8,6,4,16,128]{4,3,2,1,0:T(8,128)}, f32[8,6,4,16,128]{4,3,2,1,0:T(8,128)}, f32[1,256]{1,0:T(1,128)}) custom-call(s32[24]{0:T(128)} %reshape.104.docs_ref, s32[32]{0:T(128)} %pad_add_fusion.table_ref, f32[768,1024]{1,0:T(8,128)} %get-tuple-element.276.dgated_ref, ...), custom_call_target="tpu_custom_call" | custom-call | flops 1 | bytes 1 | tf_op jit(solution)/shard_map/pallas_call | solution.py:450
  247.1 7.6 %collective-permute-done.24 = f32[8,32,2816]{2,1,0:T(8,128)} collective-permute-done((f32[8,32,2816]{2,1,0:T(8,128)}, f32[8,32,2816]{2,1,0:T(8,128)}, u32[]{:S(2)}, u32[]{:S(2)}) %collective-permute-start.24) | collective-permute-done | bytes 2883616 | tf_op jit(solution)/shard_map/ppermute | solution.py:730
  275.0 9.9 %shard_map.334 = (f32[16,64,1024]{2,1,0:T(8,128)}, f32[16,64,1024]{2,1,0:T(8,128)}) custom-call(s32[32]{0:T(128)} %get-tuple-element.342.table_ref, bf16[768,1024]{1,0:T(8,128)(2,1)} %get-tuple-element.247.gated_ref.refs_0_, bf16[768,1024]{1,0:T(8,128)(2,1)} %get-tuple-element.287.refs_1_.refs_0_.normed_ref, bf16[768,1024]{1,0:T(8,128)(2,1)} %get-tuple-element.274.refs_2_, ...), custom_call_target="tpu_custom_call" | custom-call | flops 1 | bytes 1 | tf_op jit(solution)/shard_map/pallas_call | solution.py:644
  284.9 7.8 %collective-permute-done.27 = f32[4,6,4,16,128]{4,3,2,1,0:T(8,128)S(1)} collective-permute-done((f32[4,6,4,16,128]{4,3,2,1,0:T(8,128)}, f32[4,6,4,16,128]{4,3,2,1,0:T(8,128)S(1)}, u32[]{:S(2)}, u32[]{:S(2)}) %collective-permute-start.27) | collective-permute-done | bytes 786464 | tf_op jit(solution)/shard_map/ppermute | solution.py:730
  308.6 19.4 %collective-permute-done.31 = f32[4,32,2816]{2,1,0:T(8,128)} collective-permute-done((f32[4,32,2816]{2,1,0:T(8,128)}, f32[4,32,2816]{2,1,0:T(8,128)}, u32[]{:S(2)}, u32[]{:S(2)}) %collective-permute-start.31) | collective-permute-done | bytes 1441824 | tf_op jit(solution)/shard_map/ppermute | solution.py:730
  334.5 8.9 %collective-permute-done.33 = f32[2,6,4,16,128]{4,3,2,1,0:T(8,128)S(1)} collective-permute-done((f32[2,6,4,16,128]{4,3,2,1,0:T(8,128)S(1)}, f32[2,6,4,16,128]{4,3,2,1,0:T(8,128)S(1)}, u32[]{:S(2)}, u32[]{:S(2)}) %collective-permute-start.33) | collective-permute-done | bytes 393248 | tf_op jit(solution)/shard_map/ppermute | solution.py:730
  345.3 19.9 %collective-permute-done.34 = f32[4,88,1024]{2,1,0:T(8,128)S(1)} collective-permute-done((f32[4,88,1024]{2,1,0:T(8,128)S(1)}, f32[4,88,1024]{2,1,0:T(8,128)S(1)}, u32[]{:S(2)}, u32[]{:S(2)}) %collective-permute-start.34) | collective-permute-done | bytes 1441824 | tf_op jit(solution)/shard_map/ppermute | solution.py:730
  366.3 11.9 %collective-permute-done.35 = f32[8,64,1024]{2,1,0:T(8,128)S(1)} collective-permute-done((f32[8,64,1024]{2,1,0:T(8,128)S(1)}, f32[8,64,1024]{2,1,0:T(8,128)S(1)}, u32[]{:S(2)}, u32[]{:S(2)}) %collective-permute-start.35) | collective-permute-done | bytes 2097184 | tf_op jit(solution)/shard_map/ppermute | solution.py:730
  388.1 15.6 %shard_map.335 = (bf16[768,2048]{1,0:T(8,128)(2,1)}, bf16[768,16]{1,0:T(8,128)(2,1)}, f32[16,512]{1,0:T(8,128)}, f32[1,512]{1,0:T(1,128)}) custom-call(s32[24]{0:T(128)} %reshape.104.docs_ref, s32[32]{0:T(128)} %pad_add_fusion.table_ref, bf16[768,512]{1,0:T(8,128)(2,1)} %get-tuple-element.222.q_ref, bf16[768,512]{1,0:T(8,128)(2,1)} %get-tuple-element.223.k_ref, ...), custom_call_target="tpu_custom_call" | custom-call | flops 1 | bytes 1 | tf_op jit(solution)/shard_map/pallas_call | solution.py:544
  403.6 6.4 %shard_map.336 = (f32[16,32,1024]{2,1,0:T(8,128)}, f32[16,32,1024]{2,1,0:T(8,128)}) custom-call(s32[32]{0:T(128)} %get-tuple-element.342.table_ref, bf16[768,1024]{1,0:T(8,128)(2,1)} %get-tuple-element.287.refs_1_.refs_0_.normed_ref, bf16[768,2048]{1,0:T(8,128)(2,1)} %get-tuple-element.318.refs_1_.dqkv_ref), custom_call_target="tpu_custom_call" | custom-call | flops 1 | bytes 1 | tf_op jit(solution)/shard_map/pallas_call | solution.py:644
  410.0 6.5 %shard_map.337 = (f32[16,32,1024]{2,1,0:T(8,128)}, f32[16,32,1024]{2,1,0:T(8,128)}) custom-call(s32[32]{0:T(128)} %get-tuple-element.323.table_ref, bf16[768,1024]{1,0:T(8,128)(2,1)} %get-tuple-element.287.refs_1_.refs_0_.normed_ref, bf16[768,2048]{1,0:T(8,128)(2,1)} %get-tuple-element.318.refs_1_.dqkv_ref), custom_call_target="tpu_custom_call" | custom-call | flops 1 | bytes 1 | tf_op jit(solution)/shard_map/pallas_call | solution.py:644
  435.9 4.6 collective-permute-start.46
  442.1 12.1 %shard_map.338 = (f32[768,1024]{1,0:T(8,128)}, f32[1,1024]{1,0:T(1,128)}) custom-call(bf16[768,1024]{1,0:T(8,128)(2,1)} %bitcast.61, f32[768,1024]{1,0:T(8,128)} %get-tuple-element.273.dmid_ref, bf16[768,2048]{1,0:T(8,128)(2,1)} %get-tuple-element.318.refs_1_.dqkv_ref, bf16[768,1024]{1,0:T(8,128)(2,1)} %get-tuple-element.288.refs_3_.dog_ref, ...), custom_call_target="tpu_custom_call" | custom-call | flops 1 | bytes 1 | tf_op jit(solution)/shard_map/pallas_call | solution.py:598
  467.3 4.8 collective-permute-done.47
  477.2 4.6 collective-permute-start.53
  483.9 12.4 %collective-permute-done.53 = f32[1,88,1024]{2,1,0:T(8,128)S(1)} collective-permute-done((f32[1,88,1024]{2,1,0:T(8,128)S(1)}, f32[1,88,1024]{2,1,0:T(8,128)S(1)}, u32[]{:S(2)}, u32[]{:S(2)}) %collective-permute-start.53) | collective-permute-done | bytes 360480 | tf_op jit(solution)/shard_map/ppermute | solution.py:730
  512.4 11.6 %collective-permute-done.58 = f32[1,64,1024]{2,1,0:T(8,128)S(1)} collective-permute-done((f32[1,64,1024]{2,1,0:T(8,128)S(1)}, f32[1,64,1024]{2,1,0:T(8,128)S(1)}, u32[]{:S(2)}, u32[]{:S(2)}) %collective-permute-start.58) | collective-permute-done | bytes 262176 | tf_op jit(solution)/shard_map/ppermute | solution.py:730
  (328 shorter events, 183.4 us)
Async XLA Ops:
  27.3 20.3 %collective-permute-start.6 = (f32[4,6,2,16,128]{4,3,2,1,0:T(8,128)}, f32[4,6,2,16,128]{4,3,2,1,0:T(8,128)S(1)}, u32[]{:S(2)}, u32[]{:S(2)}) collective-permute-start(f32[4,6,2,16,128]{4,3,2,1,0:T(8,128)} %get-tuple-element.209), channel_id=1, source_target_pairs={{0,2},{1,3},{2,0},{3,1},{4,6},{5,7},{6,4},{7,5},{8,10},{9,11},{10,... | collective-permute-start | bytes 1179656 | tf_op jit(solution)/shard_map/ppermute | solution.py:730
  33.2 17.9 %collective-permute-start.5 = (f32[4,6,2,16,128]{4,3,2,1,0:T(8,128)}, f32[4,6,2,16,128]{4,3,2,1,0:T(8,128)}, u32[]{:S(2)}, u32[]{:S(2)}) collective-permute-start(f32[4,6,2,16,128]{4,3,2,1,0:T(8,128)} %get-tuple-element.213), channel_id=1, source_target_pairs={{0,2},{1,3},{2,0},{3,1},{4,6},{5,7},{6,4},{7,5},{8,10},{9,11},{10,... | collective-permute-start | bytes 1179656 | tf_op jit(solution)/shard_map/ppermute | solution.py:730
  52.9 16.4 %collective-permute-start.9 = (f32[2,6,2,16,128]{4,3,2,1,0:T(8,128)}, f32[2,6,2,16,128]{4,3,2,1,0:T(8,128)}, u32[]{:S(2)}, u32[]{:S(2)}) collective-permute-start(f32[2,6,2,16,128]{4,3,2,1,0:T(8,128)} %get-tuple-element.220), channel_id=1, source_target_pairs={{0,4},{1,5},{2,6},{3,7},{4,0},{5,1},{6,2},{7,3},{8,12},{9,13},{10,... | collective-permute-start | bytes 589832 | tf_op jit(solution)/shard_map/ppermute | solution.py:730
  157.4 25.3 %collective-permute-start.20 = (f32[16,32,2816]{2,1,0:T(8,128)}, f32[16,32,2816]{2,1,0:T(8,128)}, u32[]{:S(2)}, u32[]{:S(2)}) collective-permute-start(f32[16,32,2816]{2,1,0:T(8,128)} %get-tuple-element.256), channel_id=1, source_target_pairs={{0,1},{1,0},{2,3},{3,2},{4,5},{5,4},{6,7},{7,6},{8,9},{9,8},{10,11... | collective-permute-start | bytes 17301512 | tf_op jit(solution)/shard_map/ppermute | solution.py:730
  169.2 21.8 %collective-permute-start.21 = (f32[16,32,2816]{2,1,0:T(8,128)}, f32[16,32,2816]{2,1,0:T(8,128)}, u32[]{:S(2)}, u32[]{:S(2)}) collective-permute-start(f32[16,32,2816]{2,1,0:T(8,128)} %get-tuple-element.260), channel_id=1, source_target_pairs={{0,1},{1,0},{2,3},{3,2},{4,5},{5,4},{6,7},{7,6},{8,9},{9,8},{10,11... | collective-permute-start | bytes 17301512 | tf_op jit(solution)/shard_map/ppermute | solution.py:730
  182.5 16.2 %collective-permute-start.22 = (f32[16,88,1024]{2,1,0:T(8,128)}, f32[16,88,1024]{2,1,0:T(8,128)S(1)}, u32[]{:S(2)}, u32[]{:S(2)}) collective-permute-start(f32[16,88,1024]{2,1,0:T(8,128)} %get-tuple-element.264), channel_id=1, source_target_pairs={{0,1},{1,0},{2,3},{3,2},{4,5},{5,4},{6,7},{7,6},{8,9},{9,8},{10,11... | collective-permute-start | bytes 17301512 | tf_op jit(solution)/shard_map/ppermute | solution.py:730
  189.5 65.1 %collective-permute-start.24 = (f32[8,32,2816]{2,1,0:T(8,128)}, f32[8,32,2816]{2,1,0:T(8,128)}, u32[]{:S(2)}, u32[]{:S(2)}) collective-permute-start(f32[8,32,2816]{2,1,0:T(8,128)} %get-tuple-element.266), channel_id=1, source_target_pairs={{0,16},{16,0},{1,17},{17,1},{2,18},{18,2},{3,19},{19,3},{4,20},{20... | collective-permute-start | bytes 8650760 | tf_op jit(solution)/shard_map/ppermute | solution.py:730
  197.2 65.1 %collective-permute-start.25 = (f32[8,32,2816]{2,1,0:T(8,128)}, f32[8,32,2816]{2,1,0:T(8,128)}, u32[]{:S(2)}, u32[]{:S(2)}) collective-permute-start(f32[8,32,2816]{2,1,0:T(8,128)} %get-tuple-element.268), channel_id=1, source_target_pairs={{0,2},{1,3},{2,0},{3,1},{4,6},{5,7},{6,4},{7,5},{8,10},{9,11},{10,... | collective-permute-start | bytes 8650760 | tf_op jit(solution)/shard_map/ppermute | solution.py:730
  202.7 64.9 %collective-permute-start.26 = (f32[8,88,1024]{2,1,0:T(8,128)}, f32[8,88,1024]{2,1,0:T(8,128)}, u32[]{:S(2)}, u32[]{:S(2)}) collective-permute-start(f32[8,88,1024]{2,1,0:T(8,128)} %get-tuple-element.270), channel_id=1, source_target_pairs={{0,4},{1,5},{2,6},{3,7},{4,0},{5,1},{6,2},{7,3},{8,12},{9,13},{10,... | collective-permute-start | bytes 8650760 | tf_op jit(solution)/shard_map/ppermute | solution.py:730
  247.0 24.5 %collective-permute-start.23 = (f32[8,6,4,16,128]{4,3,2,1,0:T(8,128)}, f32[8,6,4,16,128]{4,3,2,1,0:T(8,128)S(1)}, u32[]{:S(2)}, u32[]{:S(2)}) collective-permute-start(f32[8,6,4,16,128]{4,3,2,1,0:T(8,128)} %get-tuple-element.280), channel_id=1, source_target_pairs={{0,1},{1,0},{2,3},{3,2},{4,5},{5,4},{6,7},{7,6},{8,9},{9,8},{10,11... | collective-permute-start | bytes 4718600 | tf_op jit(solution)/shard_map/ppermute | solution.py:730
  273.6 19.0 %collective-permute-start.27 = (f32[4,6,4,16,128]{4,3,2,1,0:T(8,128)}, f32[4,6,4,16,128]{4,3,2,1,0:T(8,128)S(1)}, u32[]{:S(2)}, u32[]{:S(2)}) collective-permute-start(f32[4,6,4,16,128]{4,3,2,1,0:T(8,128)} %get-tuple-element.285), channel_id=1, source_target_pairs={{0,2},{1,3},{2,0},{3,1},{4,6},{5,7},{6,4},{7,5},{8,10},{9,11},{10,... | collective-permute-start | bytes 2359304 | tf_op jit(solution)/shard_map/ppermute | solution.py:730
  293.7 34.3 %collective-permute-start.31 = (f32[4,32,2816]{2,1,0:T(8,128)}, f32[4,32,2816]{2,1,0:T(8,128)}, u32[]{:S(2)}, u32[]{:S(2)}) collective-permute-start(f32[4,32,2816]{2,1,0:T(8,128)} %get-tuple-element.298), channel_id=1, source_target_pairs={{0,16},{16,0},{1,17},{17,1},{2,18},{18,2},{3,19},{19,3},{4,20},{20... | collective-permute-start | bytes 4325384 | tf_op jit(solution)/shard_map/ppermute | solution.py:730
  296.7 34.9 %collective-permute-start.32 = (f32[4,32,2816]{2,1,0:T(8,128)}, f32[4,32,2816]{2,1,0:T(8,128)S(1)}, u32[]{:S(2)}, u32[]{:S(2)}) collective-permute-start(f32[4,32,2816]{2,1,0:T(8,128)} %get-tuple-element.300), channel_id=1, source_target_pairs={{0,2},{1,3},{2,0},{3,1},{4,6},{5,7},{6,4},{7,5},{8,10},{9,11},{10,... | collective-permute-start | bytes 4325384 | tf_op jit(solution)/shard_map/ppermute | solution.py:730
  307.1 25.8 %collective-permute-start.30 = (f32[2,6,4,16,128]{4,3,2,1,0:T(8,128)S(1)}, f32[2,6,4,16,128]{4,3,2,1,0:T(8,128)S(1)}, u32[]{:S(2)}, u32[]{:S(2)}) collective-permute-start(f32[2,6,4,16,128]{4,3,2,1,0:T(8,128)S(1)} %add_select_fusion.14), channel_id=1, source_target_pairs={{8,0},{9,1},{10,2},{11,3},{12,4},{13,5},{14,6},{15,7},{24,16},{25,... | collective-permute-start | bytes 1179656 | tf_op jit(solution)/shard_map/ppermute | solution.py:838
  330.7 34.5 %collective-permute-start.34 = (f32[4,88,1024]{2,1,0:T(8,128)S(1)}, f32[4,88,1024]{2,1,0:T(8,128)S(1)}, u32[]{:S(2)}, u32[]{:S(2)}) collective-permute-start(f32[4,88,1024]{2,1,0:T(8,128)S(1)} %copy-done.18), channel_id=1, source_target_pairs={{0,2},{1,3},{2,0},{3,1},{4,6},{5,7},{6,4},{7,5},{8,10},{9,11},{10,... | collective-permute-start | bytes 4325384 | tf_op jit(solution)/shard_map/ppermute | solution.py:730
  331.3 47.0 %collective-permute-start.35 = (f32[8,64,1024]{2,1,0:T(8,128)S(1)}, f32[8,64,1024]{2,1,0:T(8,128)S(1)}, u32[]{:S(2)}, u32[]{:S(2)}) collective-permute-start(f32[8,64,1024]{2,1,0:T(8,128)S(1)} %get-tuple-element.309), channel_id=1, source_target_pairs={{0,16},{16,0},{1,17},{17,1},{2,18},{18,2},{3,19},{19,3},{4,20},{20... | collective-permute-start | bytes 6291464 | tf_op jit(solution)/shard_map/ppermute | solution.py:730
  343.8 37.0 %collective-permute-start.36 = (f32[4,6,4,16,128]{4,3,2,1,0:T(8,128)S(1)}, f32[4,6,4,16,128]{4,3,2,1,0:T(8,128)S(1)}, u32[]{:S(2)}, u32[]{:S(2)}) collective-permute-start(f32[4,6,4,16,128]{4,3,2,1,0:T(8,128)S(1)} %get-tuple-element.305), channel_id=1, source_target_pairs={{0,2},{1,3},{2,0},{3,1},{4,6},{5,7},{6,4},{7,5},{8,10},{9,11},{10,... | collective-permute-start | bytes 2359304 | tf_op jit(solution)/shard_map/ppermute | solution.py:730
  382.9 33.6 %collective-permute-start.38 = (f32[2,32,2816]{2,1,0:T(8,128)}, f32[2,32,2816]{2,1,0:T(8,128)}, u32[]{:S(2)}, u32[]{:S(2)}) collective-permute-start(f32[2,32,2816]{2,1,0:T(8,128)} %get-tuple-element.327), channel_id=1, source_target_pairs={{0,4},{1,5},{2,6},{3,7},{4,0},{5,1},{6,2},{7,3},{8,12},{9,13},{10,... | collective-permute-start | bytes 2162696 | tf_op jit(solution)/shard_map/ppermute | solution.py:730
  384.4 34.2 %collective-permute-start.39 = (f32[2,32,2816]{2,1,0:T(8,128)}, f32[2,32,2816]{2,1,0:T(8,128)}, u32[]{:S(2)}, u32[]{:S(2)}) collective-permute-start(f32[2,32,2816]{2,1,0:T(8,128)} %get-tuple-element.329), channel_id=1, source_target_pairs={{0,4},{1,5},{2,6},{3,7},{4,0},{5,1},{6,2},{7,3},{8,12},{9,13},{10,... | collective-permute-start | bytes 2162696 | tf_op jit(solution)/shard_map/ppermute | solution.py:730
  385.0 35.8 %collective-permute-start.40 = (f32[2,88,1024]{2,1,0:T(8,128)}, f32[2,88,1024]{2,1,0:T(8,128)}, u32[]{:S(2)}, u32[]{:S(2)}) collective-permute-start(f32[2,88,1024]{2,1,0:T(8,128)} %get-tuple-element.331), channel_id=1, source_target_pairs={{0,16},{16,0},{1,17},{17,1},{2,18},{18,2},{3,19},{19,3},{4,20},{20... | collective-permute-start | bytes 2162696 | tf_op jit(solution)/shard_map/ppermute | solution.py:730
  385.4 37.5 %collective-permute-start.41 = (f32[4,64,1024]{2,1,0:T(8,128)}, f32[4,64,1024]{2,1,0:T(8,128)}, u32[]{:S(2)}, u32[]{:S(2)}) collective-permute-start(f32[4,64,1024]{2,1,0:T(8,128)} %get-tuple-element.333), channel_id=1, source_target_pairs={{0,2},{1,3},{2,0},{3,1},{4,6},{5,7},{6,4},{7,5},{8,10},{9,11},{10,... | collective-permute-start | bytes 3145736 | tf_op jit(solution)/shard_map/ppermute | solution.py:730
  433.8 25.3 %collective-permute-start.44 = (f32[8,32,1024]{2,1,0:T(8,128)S(1)}, f32[8,32,1024]{2,1,0:T(8,128)}, u32[]{:S(2)}, u32[]{:S(2)}) collective-permute-start(f32[8,32,1024]{2,1,0:T(8,128)S(1)} %get-tuple-element.338), channel_id=1, source_target_pairs={{0,16},{16,0},{1,17},{17,1},{2,18},{18,2},{3,19},{19,3},{4,20},{20... | collective-permute-start | bytes 3145736 | tf_op jit(solution)/shard_map/ppermute | solution.py:730
  435.3 25.2 %collective-permute-start.45 = (f32[8,32,1024]{2,1,0:T(8,128)}, f32[8,32,1024]{2,1,0:T(8,128)}, u32[]{:S(2)}, u32[]{:S(2)}) collective-permute-start(f32[8,32,1024]{2,1,0:T(8,128)} %get-tuple-element.351), channel_id=1, source_target_pairs={{0,2},{1,3},{2,0},{3,1},{4,6},{5,7},{6,4},{7,5},{8,10},{9,11},{10,... | collective-permute-start | bytes 3145736 | tf_op jit(solution)/shard_map/ppermute | solution.py:730
  435.9 29.6 %collective-permute-start.46 = (f32[1,32,2816]{2,1,0:T(8,128)}, f32[1,32,2816]{2,1,0:T(8,128)}, u32[]{:S(2)}, u32[]{:S(2)}) collective-permute-start(f32[1,32,2816]{2,1,0:T(8,128)} %get-tuple-element.354), channel_id=1, source_target_pairs={{0,8},{1,9},{2,10},{3,11},{4,12},{5,13},{6,14},{7,15},{8,0},{9,1},... | collective-permute-start | bytes 1081352 | tf_op jit(solution)/shard_map/ppermute | solution.py:730
  440.5 31.5 %collective-permute-start.47 = (f32[1,32,2816]{2,1,0:T(8,128)}, f32[1,32,2816]{2,1,0:T(8,128)S(1)}, u32[]{:S(2)}, u32[]{:S(2)}) collective-permute-start(f32[1,32,2816]{2,1,0:T(8,128)} %get-tuple-element.356), channel_id=1, source_target_pairs={{0,8},{1,9},{2,10},{3,11},{4,12},{5,13},{6,14},{7,15},{8,0},{9,1},... | collective-permute-start | bytes 1081352 | tf_op jit(solution)/shard_map/ppermute | solution.py:730
  440.6 32.3 %collective-permute-start.48 = (f32[2,64,1024]{2,1,0:T(8,128)}, f32[2,64,1024]{2,1,0:T(8,128)}, u32[]{:S(2)}, u32[]{:S(2)}) collective-permute-start(f32[2,64,1024]{2,1,0:T(8,128)} %get-tuple-element.359), channel_id=1, source_target_pairs={{0,4},{1,5},{2,6},{3,7},{4,0},{5,1},{6,2},{7,3},{8,12},{9,13},{10,... | collective-permute-start | bytes 1572872 | tf_op jit(solution)/shard_map/ppermute | solution.py:730
  477.2 19.0 %collective-permute-start.53 = (f32[1,88,1024]{2,1,0:T(8,128)S(1)}, f32[1,88,1024]{2,1,0:T(8,128)S(1)}, u32[]{:S(2)}, u32[]{:S(2)}) collective-permute-start(f32[1,88,1024]{2,1,0:T(8,128)S(1)} %copy-done.22), channel_id=1, source_target_pairs={{0,8},{1,9},{2,10},{3,11},{4,12},{5,13},{6,14},{7,15},{8,0},{9,1},... | collective-permute-start | bytes 1081352 | tf_op jit(solution)/shard_map/ppermute | solution.py:730
  483.4 16.8 %collective-permute-start.55 = (f32[2,32,1024]{2,1,0:T(8,128)S(1)}, f32[2,32,1024]{2,1,0:T(8,128)S(1)}, u32[]{:S(2)}, u32[]{:S(2)}) collective-permute-start(f32[2,32,1024]{2,1,0:T(8,128)S(1)} %get-tuple-element.372), channel_id=1, source_target_pairs={{0,4},{1,5},{2,6},{3,7},{4,0},{5,1},{6,2},{7,3},{8,12},{9,13},{10,... | collective-permute-start | bytes 786440 | tf_op jit(solution)/shard_map/ppermute | solution.py:730
  506.4 17.6 %collective-permute-start.58 = (f32[1,64,1024]{2,1,0:T(8,128)S(1)}, f32[1,64,1024]{2,1,0:T(8,128)S(1)}, u32[]{:S(2)}, u32[]{:S(2)}) collective-permute-start(f32[1,64,1024]{2,1,0:T(8,128)S(1)} %get-tuple-element.367), channel_id=1, source_target_pairs={{0,8},{1,9},{2,10},{3,11},{4,12},{5,13},{6,14},{7,15},{8,0},{9,1},... | collective-permute-start | bytes 786440 | tf_op jit(solution)/shard_map/ppermute | solution.py:730
  507.8 19.0 %collective-permute-start.59 = (f32[1,32,1024]{2,1,0:T(8,128)S(1)}, f32[1,32,1024]{2,1,0:T(8,128)S(1)}, u32[]{:S(2)}, u32[]{:S(2)}) collective-permute-start(f32[1,32,1024]{2,1,0:T(8,128)S(1)} %get-tuple-element.380), channel_id=1, source_target_pairs={{0,8},{1,9},{2,10},{3,11},{4,12},{5,13},{6,14},{7,15},{8,0},{9,1},... | collective-permute-start | bytes 393224 | tf_op jit(solution)/shard_map/ppermute | solution.py:730
  509.4 19.6 %collective-permute-start.60 = (f32[1,32,1024]{2,1,0:T(8,128)S(1)}, f32[1,32,1024]{2,1,0:T(8,128)S(1)}, u32[]{:S(2)}, u32[]{:S(2)}) collective-permute-start(f32[1,32,1024]{2,1,0:T(8,128)S(1)} %get-tuple-element.382), channel_id=1, source_target_pairs={{0,8},{1,9},{2,10},{3,11},{4,12},{5,13},{6,14},{7,15},{8,0},{9,1},... | collective-permute-start | bytes 393224 | tf_op jit(solution)/shard_map/ppermute | solution.py:730
  510.7 18.9 %collective-permute-start.61 = (f32[1,56,128]{2,1,0:T(8,128)S(1)}, f32[1,56,128]{2,1,0:T(8,128)S(1)}, u32[]{:S(2)}, u32[]{:S(2)}) collective-permute-start(f32[1,56,128]{2,1,0:T(8,128)S(1)} %get-tuple-element.377), channel_id=1, source_target_pairs={{0,8},{1,9},{2,10},{3,11},{4,12},{5,13},{6,14},{7,15},{8,0},{9,1},... | collective-permute-start | bytes 86024 | tf_op jit(solution)/shard_map/ppermute | solution.py:730
  (86 other events, 979.7 us)

commit v4 on v3

--- a/solution.py
+++ b/solution.py
@@ -86,8 +86,8 @@
 
 def project_body(
     rows, docs, length, hk, hv, parts,
-    docs_ref, table_ref, x_ref, gain_ref, wq_ref, wk_ref, wv_ref, wog_ref, wrd_ref, wru_ref, bias_ref,
-    normed_ref, q_ref, k_ref, v_ref, og_ref, ra_ref, gp_ref, cum_ref, keep_a_ref, send_a_ref, keep_b_ref,
+    docs_ref, table_ref, x_ref, gain_ref, wk_ref, wv_ref, wrd_ref, wru_ref, bias_ref,
+    normed_ref, k_ref, v_ref, ra_ref, gp_ref, cum_ref, keep_a_ref, send_a_ref, keep_b_ref,
     send_b_ref, decay_ref,
     hold,
 ):
@@ -99,12 +99,10 @@
     ra_ref[...] = rank
     gate = nn(rank, wru_ref[...]) + bias_ref[...]
     gp_ref[...] = gate
-    q_ref[...] = nn(normed, wq_ref[...]).astype(BF)
     key = nn(normed, wk_ref[...]).astype(BF)
     k_ref[...] = key
     value = nn(normed, wv_ref[...]).astype(BF)
     v_ref[...] = value
-    og_ref[...] = nn(normed, wog_ref[...])
     log_decay = (jnp.minimum(gate, 0.0) - jnp.log1p(jnp.exp(-jnp.abs(gate)))) * (1.0 / 16.0)
     tri = lower_ones(length)
     size = hv // parts
@@ -127,7 +125,7 @@
                 send_ref[j, r, h % (HEADS // 2)] = hold[pl.ds(second, size), :]
 
 
-def project_all(x, docs, table, gain, wq, wk, wv, wog, wrd, wru, bias, dims):
+def project_all(x, docs, table, gain, wk, wv, wrd, wru, bias, dims):
     row_count, length, width, kw, vw, ndocs, parts = dims
     tokens = row_count * length
     rows = 2 if row_count % 2 == 0 else 1
@@ -144,9 +142,7 @@
         (
             shape((tokens, width), BF),
             shape((tokens, kw), BF),
-            shape((tokens, kw), BF),
             shape((tokens, vw), BF),
-            shape((tokens, vw), F32),
             shape((tokens, rank), BF),
             shape((tokens, kw), F32),
             shape((tokens, kw), F32),
@@ -158,17 +154,35 @@
         ),
         (row_count // rows,),
         [
-            tile(width), whole((1, width)), whole(wq.shape), whole(wk.shape), whole(wv.shape),
-            whole(wog.shape), whole(wrd.shape), whole(wru.shape), whole((1, kw)),
+            tile(width), whole((1, width)), whole(wk.shape), whole(wv.shape), whole(wrd.shape),
+            whole(wru.shape), whole((1, kw)),
         ],
         (
-            tile(width), tile(kw), tile(kw), tile(vw), tile(vw), tile(rank), tile(kw), tile(kw),
+            tile(width), tile(kw), tile(vw), tile(rank), tile(kw), tile(kw),
             half_block, half_block, half_block, half_block,
             block((rows, 1, kw), lambda i, *_: (i, 0, 0)),
         ),
         prefetch=2,
         scratch=[pltpu.VMEM((hv, hk), F32)],
-    )(docs, table, x, gain.reshape(1, -1), wq, wk, wv, wog, wrd, wru, bias.reshape(1, -1))
+    )(docs, table, x, gain.reshape(1, -1), wk, wv, wrd, wru, bias.reshape(1, -1))
+
+
+def readers_body(normed_ref, wq_ref, wog_ref, q_ref, og_ref):
+    q_ref[...] = nn(normed_ref[...], wq_ref[...]).astype(BF)
+    og_ref[...] = nn(normed_ref[...], wog_ref[...])
+
+
+def readers_all(normed, wq, wog):
+    tokens, width = normed.shape
+    tm = 256 if tokens % 256 == 0 else 128
+    tile = lambda n: block((tm, n), lambda i: (i, 0))
+    return call(
+        readers_body,
+        (shape((tokens, wq.shape[1]), BF), shape((tokens, wog.shape[1]), F32)),
+        (tokens // tm,),
+        [tile(width), whole(wq.shape), whole(wog.shape)],
+        (tile(wq.shape[1]), tile(wog.shape[1])),
+    )(normed, wq, wog)
 
 
 def span_factors(cum, length):
@@ -461,63 +475,92 @@
     )(docs, table, dgated, og, mixed, q, cum, gain.reshape(1, -1))
 
 
-def mix_back_body(
-    docs, length, hk, hv, parts,
-    docs_ref, table_ref, q_ref, k_ref, v_ref, cum_ref, gp_ref, ra_ref, dmix_ref, state_ref, near_ref,
-    far_ref, wru_ref,
-    dqkv_ref, drank_ref, grup_ref, gbias_ref,
+def mix_local_body(
+    docs, length, hk, hv,
+    docs_ref, q_ref, k_ref, v_ref, cum_ref, dmix_ref, state_ref,
+    dq_ref, dk_ref, dv_ref, decay_ref,
 ):
-    row = pl.program_id(0)
-    kw = HEADS * hk
-    visible, alive, tail, whole_alive = reset_masks(docs_ref, row, docs, length)
+    visible, alive, _, _ = reset_masks(docs_ref, pl.program_id(0), docs, length)
     cum = cum_ref[...]
-    last = cum[length - 1 :, :]
     up, down = span_factors(cum, length)
     from_start = jnp.exp(cum) * alive
-    to_end = jnp.exp(last - cum) * tail
-    total = jnp.exp(last) * whole_alive
     q = q_ref[...].astype(F32)
-    k = k_ref[...].astype(F32)
     q_span = (q * up).astype(BF)
-    k_span = (k * down).astype(BF)
+    k_span = (k_ref[...].astype(F32) * down).astype(BF)
     reach = (q * from_start).astype(BF)
-    weighted = (k * to_end).astype(BF)
-    later, earlier, crossing = [], [], []
+    later = []
     for h in range(HEADS):
         kk = slice(h * hk, (h + 1) * hk)
         vv = slice(h * hv, (h + 1) * hv)
         qs, ks = q_span[:, kk], k_span[:, kk]
         d_mix = dmix_ref[:, vv]
-        value = v_ref[:, vv]
-        state = state_ref[0, h]
-        grad32 = gather_state(near_ref, far_ref, table_ref, h, parts)
-        grad = grad32.astype(BF)
         scores = jnp.where(visible, nt(qs, ks), 0.0).astype(BF)
-        d_scores = jnp.where(visible, nt(d_mix, value), 0.0).astype(BF)
+        d_scores = jnp.where(visible, nt(d_mix, v_ref[:, vv]), 0.0).astype(BF)
         dq_in = nn(d_scores, ks)
         dk_in = tn(d_scores, qs)
-        dq_out = nn(d_mix, state)
-        dk_out = nn(value, grad)
-        dqkv_ref[:, kk] = (dq_in * up[:, kk] + dq_out * from_start[:, kk]).astype(BF)
-        dqkv_ref[:, kw + h * hk : kw + (h + 1) * hk] = (
-            dk_in * down[:, kk] + dk_out * to_end[:, kk]
-        ).astype(BF)
-        dqkv_ref[:, 2 * kw + h * hv : 2 * kw + (h + 1) * hv] = (
-            tn(scores, d_mix) + nt(weighted[:, kk], grad)
-        ).astype(BF)
+        dq_out = nn(d_mix, state_ref[0, h])
+        dq_ref[:, kk] = (dq_in * up[:, kk] + dq_out * from_start[:, kk]).astype(BF)
+        dk_ref[:, kk] = dk_in * down[:, kk]
+        dv_ref[:, vv] = tn(scores, d_mix)
         later.append(
             qs.astype(F32) * dq_in - ks.astype(F32) * dk_in + reach[:, kk].astype(F32) * dq_out
         )
-        earlier.append(weighted[:, kk].astype(F32) * dk_out)
-        crossing.append(jnp.sum(state.astype(F32) * grad32, axis=0, keepdims=True))
-    later = jnp.concatenate(later, axis=1)
-    earlier = jnp.concatenate(earlier, axis=1)
-    crossing = jnp.concatenate(crossing, axis=1)
     at_i = lax.broadcasted_iota(jnp.int32, (length, length), 0)
     at_j = lax.broadcasted_iota(jnp.int32, (length, length), 1)
-    after = (at_i <= at_j).astype(F32)
-    before = (at_i > at_j).astype(F32)
-    d_decay = nn(after, later, HIGHEST) + nn(before, earlier, HIGHEST) + total * crossing
+    decay_ref[...] = nn((at_i <= at_j).astype(F32), jnp.concatenate(later, axis=1), HIGHEST)
+
+
+def mix_local_all(q, k, v, cum, dmix, state, docs, dims):
+    row_count, length, width, kw, vw, ndocs, parts = dims
+    tokens = row_count * length
+    hk, hv = kw // HEADS, vw // HEADS
+    tile = lambda n: block((length, n), lambda i, *_: (i, 0))
+    return call(
+        functools.partial(mix_local_body, ndocs, length, hk, hv),
+        (
+            shape((tokens, kw), BF), shape((tokens, kw), F32), shape((tokens, vw), F32),
+            shape((tokens, kw), F32),
+        ),
+        (row_count,),
+        [
+            tile(kw), tile(kw), tile(vw), tile(kw), tile(vw),
+            block((1, HEADS, hv, hk), lambda i, *_: (i, 0, 0, 0)),
+        ],
+        (tile(kw), tile(kw), tile(vw), tile(kw)),
+        prefetch=1,
+    )(docs, q, k, v, cum, dmix, state)
+
+
+def mix_back_body(
+    docs, length, hk, hv, parts,
+    docs_ref, table_ref, k_ref, v_ref, cum_ref, gp_ref, ra_ref, state_ref, dk_ref, dv_ref, decay_ref,
+    near_ref, far_ref, wru_ref,
+    dk_out_ref, dv_out_ref, drank_ref, grup_ref, gbias_ref,
+):
+    row = pl.program_id(0)
+    _, _, tail, whole_alive = reset_masks(docs_ref, row, docs, length)
+    cum = cum_ref[...]
+    last = cum[length - 1 :, :]
+    to_end = jnp.exp(last - cum) * tail
+    weighted = (k_ref[...].astype(F32) * to_end).astype(BF)
+    earlier, crossing = [], []
+    for h in range(HEADS):
+        kk = slice(h * hk, (h + 1) * hk)
+        vv = slice(h * hv, (h + 1) * hv)
+        grad32 = gather_state(near_ref, far_ref, table_ref, h, parts)
+        grad = grad32.astype(BF)
+        dk_out = nn(v_ref[:, vv], grad)
+        dk_out_ref[:, kk] = (dk_ref[:, kk] + dk_out * to_end[:, kk]).astype(BF)
+        dv_out_ref[:, vv] = (
+            dv_ref[:, vv] + nt(weighted[:, kk], grad)
+        ).astype(BF)
+        earlier.append(weighted[:, kk].astype(F32) * dk_out)
+        crossing.append(jnp.sum(state_ref[0, h].astype(F32) * grad32, axis=0, keepdims=True))
+    d_decay = (
+        decay_ref[...]
+        + nn(lower_ones(length, True), jnp.concatenate(earlier, axis=1), HIGHEST)
+        + jnp.exp(last) * whole_alive * jnp.concatenate(crossing, axis=1)
+    )
     d_gate = (d_decay * jax.nn.sigmoid(-gp_ref[...]) * (1.0 / 16.0)).astype(BF)
     drank_ref[...] = nt(d_gate, wru_ref[...]).astype(BF)
     grup = tn(ra_ref[...], d_gate)
@@ -534,7 +577,7 @@
         gbias_ref[...] += gbias
 
 
-def mix_back_all(q, k, v, cum, gp, ra, dmix, state, near, far, wru, docs, table, dims):
+def mix_back_all(k, v, cum, gp, ra, state, dk, dv, decay, near, far, wru, docs, table, dims):
     row_count, length, width, kw, vw, ndocs, parts = dims
     tokens = row_count * length
     hk, hv = kw // HEADS, vw // HEADS
@@ -544,30 +587,29 @@
     return call(
         functools.partial(mix_back_body, ndocs, length, hk, hv, parts),
         (
-            shape((tokens, 2 * kw + vw), BF), shape((tokens, rank), BF),
+            shape((tokens, kw), BF), shape((tokens, vw), BF), shape((tokens, rank), BF),
             shape((rank, kw), F32), shape((1, kw), F32),
         ),
         (row_count,),
         [
-            tile(kw), tile(kw), tile(vw), tile(kw), tile(kw), tile(rank), tile(vw),
+            tile(kw), tile(vw), tile(kw), tile(kw), tile(rank),
             block((1, HEADS, hv, hk), lambda i, *_: (i, 0, 0, 0)),
-            half, half, whole((rank, kw)),
+            tile(kw), tile(vw), tile(kw), half, half, whole((rank, kw)),
         ],
-        (tile(2 * kw + vw), tile(rank), whole((rank, kw)), whole((1, kw))),
+        (tile(kw), tile(vw), tile(rank), whole((rank, kw)), whole((1, kw))),
         prefetch=2,
-    )(docs, table, q, k, v, cum, gp, ra, dmix, state, near, far, wru)
+    )(docs, table, k, v, cum, gp, ra, state, dk, dv, decay, near, far, wru)
 
 
 def input_back_body(
-    kw, vw,
-    x_ref, dmid_ref, dqkv_ref, dog_ref, drank_ref, gain_ref, wq_ref, wk_ref, wv_ref, wog_ref, wrd_ref,
+    x_ref, dmid_ref, dq_ref, dk_ref, dv_ref, dog_ref, drank_ref, gain_ref, wq_ref, wk_ref, wv_ref, wog_ref, wrd_ref,
     gin_ref, gnorm_ref,
 ):
     step = pl.program_id(0)
     d_normed = (
-        nt(dqkv_ref[:, :kw], wq_ref[...])
-        + nt(dqkv_ref[:, kw : 2 * kw], wk_ref[...])
-        + nt(dqkv_ref[:, 2 * kw :], wv_ref[...])
+        nt(dq_ref[...], wq_ref[...])
+        + nt(dk_ref[...], wk_ref[...])
+        + nt(dv_ref[...], wv_ref[...])
         + nt(dog_ref[...], wog_ref[...])
         + nn(drank_ref[...], wrd_ref[...])
     )
@@ -590,67 +632,93 @@
         gnorm_ref[...] += gnorm
 
 
-def input_back_all(x, dmid, dqkv, dog, drank, gain, wq, wk, wv, wog, wrd):
+def input_back_all(x, dmid, dq, dk, dv, dog, drank, gain, wq, wk, wv, wog, wrd):
     tokens, width = x.shape
     kw, vw = wq.shape[1], wv.shape[1]
     tm = 256 if tokens % 256 == 0 else 128
     tile = lambda n: block((tm, n), lambda i: (i, 0))
     return call(
-        functools.partial(input_back_body, kw, vw),
+        input_back_body,
         (shape((tokens, width), F32), shape((1, width), F32)),
         (tokens // tm,),
         [
-            tile(width), tile(width), tile(2 * kw + vw), tile(vw), tile(drank.shape[1]),
+            tile(width), tile(width), tile(kw), tile(kw), tile(vw), tile(vw), tile(drank.shape[1]),
             whole((1, width)), whole(wq.shape), whole(wk.shape), whole(wv.shape), whole(wog.shape),
             whole(wrd.shape),
         ],
         (tile(width), whole((1, width))),
-    )(x, dmid, dqkv, dog, drank, gain.reshape(1, -1), wq, wk, wv, wog, wrd)
-
-
-def weight_body(count, pieces, per, table_ref, *refs):
-    lefts, rights = refs[:count], refs[count : 2 * count]
-    keep_ref, send_ref, hold = refs[2 * count : 2 * count + 3]
-    turned = refs[2 * count + 3 :]
+    )(x, dmid, dq, dk, dv, dog, drank, gain.reshape(1, -1), wq, wk, wv, wog, wrd)
+
+
+def weight_body(groups, lefts, pieces, *refs):
+    tables = refs[: len(groups)]
+    refs = refs[len(groups) :]
+    left_refs, refs = refs[:lefts], refs[lefts:]
+    count = sum(len(group) for group in groups)
+    rights, refs = refs[:count], refs[count:]
+    outs, refs = refs[: 2 * len(groups)], refs[2 * len(groups) :]
+    turned, holds = refs[:lefts], refs[lefts:]
 
     @pl.when(pl.program_id(0) == 0)
     def _():
-        for n in range(count):
-            turned[n][...] = lefts[n][...].T
-
-    for n in range(count):
-        hold[...] = nn(turned[n][...], rights[n][...])
-        at = slice(n * per, (n + 1) * per)
-        for j in range(pieces // 2):
-            first = pl.multiple_of(table_ref[j] * per, per)
-            keep_ref[j, at, :] = hold[pl.ds(first, per), :]
-            second = pl.multiple_of(table_ref[pieces // 2 + j] * per, per)
-            send_ref[j, at, :] = hold[pl.ds(second, per), :]
-
-
-def weight_grads(pairs, table, columns=None):
-    count, pieces = len(pairs), table.shape[0]
-    tokens, rows = pairs[0][0].shape
-    per = rows // pieces
-    start, cols = columns or (0, pairs[0][1].shape[1])
-    if per % 8:
-        both = [tn(left, right[:, start : start + cols]) for left, right in pairs]
-        parts = jnp.concatenate([part.reshape(pieces, per, cols) for part in both], axis=1)[table]
-        return parts[: pieces // 2], parts[pieces // 2 :]
-    tile = next(n for n in (1408, 512, 256, 128) if cols % n == 0 and start % n == 0)
-    skip = start // tile
-    half = shape((pieces // 2, count * per, cols), F32)
-    half_block = block((pieces // 2, count * per, tile), lambda i, *_: (0, 0, i))
-    return call(
-        functools.partial(weight_body, count, pieces, per),
-        (half, half),
-        (cols // tile,),
-        [whole((tokens, rows))] * count
-        + [block((tokens, tile), lambda i, *_: (0, i + skip))] * count,
-        (half_block, half_block),
-        prefetch=1,
-        scratch=[pltpu.VMEM((rows, tile), F32)] + [pltpu.VMEM((rows, tokens), BF)] * count,
-    )(table, *[left for left, _ in pairs], *[right for _, right in pairs])
+        for n in range(lefts):
+            turned[n][...] = left_refs[n][...].T
+
+    at = 0
+    for g, group in enumerate(groups):
+        keep_ref, send_ref = outs[2 * g], outs[2 * g + 1]
+        place = 0
+        for left in group:
+            hold = holds[g]
+            hold[...] = nn(turned[left][...], rights[at][...])
+            per = hold.shape[0] // pieces
+            rows = slice(place, place + per)
+            for j in range(pieces // 2):
+                first = pl.multiple_of(tables[g][j] * per, per)
+                keep_ref[j, rows, :] = hold[pl.ds(first, per), :]
+                second = pl.multiple_of(tables[g][pieces // 2 + j] * per, per)
+                send_ref[j, rows, :] = hold[pl.ds(second, per), :]
+            at, place = at + 1, place + per
+
+
+def weight_grads(groups, tables, steps=2):
+    pieces = tables[0].shape[0]
+    tokens = groups[0][0][0].shape[0]
+    out = []
+    if any(left.shape[1] // pieces % 8 for group in groups for left, _ in group):
+        for group, table in zip(groups, tables):
+            parts = [tn(left, right) for left, right in group]
+            parts = [part.reshape(pieces, -1, part.shape[1]) for part in parts]
+            parts = jnp.concatenate(parts, axis=1)[table]
+            out.append((parts[: pieces // 2], parts[pieces // 2 :]))
+        return out
+    lefts, index = [], []
+    for group in groups:
+        index.append([])
+        for left, _ in group:
+            known = [n for n, other in enumerate(lefts) if other is left]
+            if not known:
+                lefts.append(left)
+            index[-1].append(known[0] if known else len(lefts) - 1)
+    rights = [right for group in groups for _, right in group]
+    column = lambda n: block((tokens, n // steps), lambda i, *_: (0, i))
+    shapes, blocks, holds = [], [], []
+    for group in groups:
+        rows, cols = group[0][0].shape[1], group[0][1].shape[1]
+        dims = (pieces // 2, len(group) * rows // pieces, cols)
+        shapes += [shape(dims, F32)] * 2
+        blocks += [block(dims[:2] + (cols // steps,), lambda i, *_: (0, 0, i))] * 2
+        holds.append(pltpu.VMEM((rows, cols // steps), F32))
+    flat = call(
+        functools.partial(weight_body, index, len(lefts), pieces),
+        tuple(shapes),
+        (steps,),
+        [whole(left.shape) for left in lefts] + [column(right.shape[1]) for right in rights],
+        tuple(blocks),
+        prefetch=len(groups),
+        scratch=[pltpu.VMEM(left.shape[::-1], BF) for left in lefts] + holds,
+    )(*tables, *lefts, *rights)
+    return [(flat[2 * g], flat[2 * g + 1]) for g in range(len(groups))]
 
 
 def small_body(
@@ -853,22 +921,22 @@
 ROUTES = {
     "gate": ("x", "y", "z0", "z1"),
     "up": ("y", "x", "z0", "z1"),
-    "down": ("z0", "y", "x", "z1"),
+    "down": ("z0", "x", "y", "z1"),
     "mid": ("x", "y", "z0", "z1"),
     "qk": ("x", "y", "z0", "z1"),
     "v": ("y", "x", "z0", "z1"),
     "small": ("x", "y", "z0", "z1"),
 }
 SCHEDULE = (
-    "gate", ("gate",), "up", ("up",), "down", ("down",), "gate", ("gate",), "up", ("up",),
-    "down", ("down",), "ff", "scan", ("scan",), "gate", "up", "down", "scan", ("scan", "up"),
-    "mid", "scan", ("scan", "gate", "mid"), "mid", "scan", ("scan", "mid", "down"), "up",
-    "gate", "scan", ("scan",), "scan", ("scan",), "down", "mid", "scan", ("scan", "gate", "up",
-    "down", "mid"), "scan", "qk", "v", "gate", "up", "down", "mid", ("qk", "v", "gate", "up",
-    "mid"), "qk", "v", ("qk", "v"), "small", "small", "qk", "v", ("qk", "v"), "gate", "up",
-    ("small", "down"), "mid", "qk", "v", "small", ("qk", "v", "small"), "small", ("mid",),
-    "down", "qk", "v", ("small", "qk", "v"), "small", ("small",), "small", ("small",), "mid",
-    "qk", "v", "small",
+    "gate", "up", ("gate", "up"), "down", ("down",), "gate", ("gate",), "up", ("up",), "down",
+    ("down",), "ff", "scan", ("scan",), "mid", "gate", "up", "down", "scan", ("scan", "up",
+    "mid"), "mid", "scan", ("scan", "gate"), "up", "scan", ("scan", "mid"), "local", "gate",
+    "scan", ("scan",), "scan", ("scan",), "mid", "scan", ("scan", "gate", "up", "down", "mid"),
+    "scan", "qk", "v", "gate", "up", "down", "mid", ("qk", "v", "gate", "up", "mid"), "qk", "v",
+    ("qk", "v"), "small", "small", "qk", "v", ("qk", "v"), "gate", "up", ("small", "down"),
+    "mid", ("mid",), "qk", "v", ("qk", "v"), "small", ("small",), "qk", "v", ("qk", "v"),
+    "down", ("down",), "small", ("small",), "mid", "small", ("small",), "qk", "v", "small",
+    ("small",), "down", "small",
 )
 
 
@@ -892,17 +960,15 @@
     step = 1 << len(levels)
     size = parts // step
     low = links.at_seq & (step - 1)
-    reverse = jnp.array(
-        [sum(((p >> b) & 1) << (len(levels) - 1 - b) for b in levels) for p in range(step)], jnp.int32
-    )
+    turn = lambda p: sum(((p >> b) & 1) << (len(levels) - 1 - b) for b in levels)
+    reverse = jnp.array([turn(p) for p in range(step)], jnp.int32)
     spread = jnp.arange(size)
     to_piece = ((reverse ^ low)[:, None] * size + spread).reshape(-1)
-    to_place = (reverse[jnp.arange(step) ^ low][:, None] * size + spread).reshape(-1)
+    to_place = ((reverse ^ turn(low))[:, None] * size + spread).reshape(-1)
     state_table = jnp.concatenate([to_piece, to_place]).astype(jnp.int32)
 
-    normed, q, k, v, og, ra, gp, cum, keep_a, send_a, keep_b, send_b, decay = project_all(
-        x, docs, state_table, norm1_gain, w_query, w_key, w_value, w_outgate, rank_down_t, w_rank_up,
-        decay_bias, dims,
+    normed, k, v, ra, gp, cum, keep_a, send_a, keep_b, send_b, decay = project_all(
+        x, docs, state_table, norm1_gain, w_key, w_value, rank_down_t, w_rank_up, decay_bias, dims
     )
     decay = decay.reshape(1, row_count, HEADS, 1, kw // HEADS)
     fwd_a, fwd_b = {}, {}
@@ -926,6 +992,12 @@
     start([one], turns)
     two.advance(turns)
     start([two], turns)
+    q, og = readers_all(turns.after(normed), w_query, w_outgate)
+    turns.done(q)
+    one.advance(turns)
+    start([one], turns)
+    two.advance(turns)
+    start([two], turns)
     inner = inner_all(q, k, v, cum, turns.after(docs), dims)
     turns.done(inner)
     while not two.over:
@@ -967,23 +1039,47 @@
         held.update(d_mix=d_mix, d_og=d_og, ggroup=ggroup)
         return keep, send, None
 
+    def local_steps():
+        held["d_q"], held["own_k"], held["own_v"], held["decay"] = mix_local_all(
+            q, k, v, cum, held["d_mix"], state_kept, turns.after(docs), dims
+        )
+        turns.done(held["d_q"])
+        return
+        yield
+
     def all_back():
         yield from scan_steps(links, turns, head_back, decays, True, back)
-        held["d_qkv"], held["d_rank"], held["grup"], held["gbias"] = mix_back_all(
-            q, k, v, cum, gp, ra, held["d_mix"], state_kept, back["near"], back["far"], w_rank_up,
-            turns.after(docs), state_table, dims,
+        held["d_k"], held["d_v"], held["d_rank"], held["grup"], held["gbias"] = mix_back_all(
+            k, v, cum, gp, ra, state_kept, held["own_k"], held["own_v"], held["decay"], back["near"],
+            back["far"], w_rank_up, turns.after(docs), state_table, dims,
         )
         turns.done(held["d_rank"])
 
-    def weights(name, pairs, columns=None):
-        order = routes[name]
-        make = lambda: weight_grads(pairs(), turns.after(tables[order]), columns)
-        return reduce_steps(links, turns, make, order, grads, name)
+    operands = {
+        "gate": lambda: [(normed2, dg)],
+        "up": lambda: [(normed2, du)],
+        "down": lambda: [(hidden, cot)],
+        "mid": lambda: [(gated, held["d_out"]), (normed, held["d_og"])],
+        "qk": lambda: [(normed, held["d_q"]), (normed, held["d_k"])],
+        "v": lambda: [(normed, held["d_v"])],
+    }
+    made = {}
+
+    def weights(name, *names):
+        def make():
+            if name not in made:
+                ordered = [tables[routes[each]] for each in names]
+                ordered[0] = turns.after(ordered[0])
+                groups = weight_grads([operands[each]() for each in names], ordered)
+                made.update(zip(names, groups))
+            return made[name]
+
+        return reduce_steps(links, turns, make, routes[name], grads, name)
 
     def small_steps():
         grad_in, gnorm1 = input_back_all(
-            x, held["d_middle"], held["d_qkv"], held["d_og"], held["d_rank"], turns.after(norm1_gain),
-            w_query, w_key, w_value, w_outgate, rank_down_t,
+            x, held["d_middle"], held["d_q"], held["d_k"], held["d_v"], held["d_og"], held["d_rank"],
+            turns.after(norm1_gain), w_query, w_key, w_value, w_outgate, rank_down_t,
         )
         held["grad_in"] = grad_in
         turns.done(gnorm1)
@@ -998,12 +1094,13 @@
     work = {
         "ff": ff_steps(),
         "scan": all_back(),
-        "gate": weights("gate", lambda: [(normed2, dg)]),
-        "up": weights("up", lambda: [(normed2, du)]),
-        "down": weights("down", lambda: [(hidden, cot)]),
-        "mid": weights("mid", lambda: [(gated, held["d_out"]), (normed, held["d_og"])]),
-        "qk": weights("qk", lambda: [(normed, held["d_qkv"])], (0, 2 * kw)),
-        "v": weights("v", lambda: [(normed, held["d_qkv"])], (2 * kw, vw)),
+        "gate": weights("gate", "gate", "up"),
+        "up": weights("up", "gate", "up"),
+        "down": weights("down", "down"),
+        "mid": weights("mid", "mid"),
+        "local": local_steps(),
+        "qk": weights("qk", "qk", "v"),
+        "v": weights("v", "qk", "v"),
         "small": small_steps(),
     }
     work = {name: Task(steps) for name, steps in work.items()}
@@ -1011,9 +1108,10 @@
         if isinstance(name, tuple):
             start([work[each] for each in name], turns)
             continue
-        if name in ("scan", "mid"):
+        if name in ("scan", "mid", "local"):
             work["ff"].finish(turns)
         if name in ("qk", "v", "small"):
+            work["local"].finish(turns)
             work["scan"].finish(turns)
         work[name].advance(turns)
 
@@ -1025,8 +1123,8 @@
         held["out"].reshape(row_count, length, width),
         held["grad_in"].reshape(row_count, length, width),
         first[:, rank],
-        qk[:, :kw],
-        qk[:, kw:],
+        qk[:per],
+        qk[per:],
         grads["v"][0],
         mid[per:],
         first[:, :rank],

time: 543 us -> 510 us (0.939)
  waiting for transfers between devices: 157 us -> 128 us
  starting transfers between devices: 75.8 us -> 61.4 us
  other arithmetic: 80.3 us -> 92.3 us
    ppermute x59, waiting for transfers between devices: 155 us -> 127 us  [swap(): return lax.ppermute(value, name, [(i, i ^ flip) for i in range(n)])]
    ppermute x59, starting transfers between devices: 68.1 us -> 52.3 us  [swap(): return lax.ppermute(value, name, [(i, i ^ flip) for i in range(n)])]
    pallas_call x7, Pallas kernels: 70.4 us -> 80.3 us  [the longest x4 49.8 us: weight_grads(): call(functools.partial(weight_body, index, len(lefts), pieces), tuple(sha...]
    add x11 -> x9, other arithmetic: 25.7 us -> 29 us  [reduce_steps(): send = keep[half:] + got[half:]]
    add x17 -> x19, other arithmetic: 28.2 us -> 29.2 us  [reduce_steps(): keep = keep[:half] + got[:half]]
  transfers between devices with their start and end apart: 62 -> 62, of which waited for: 34 -> 31; matrix products, arithmetic and copies ran while one was open for 14% -> 17% of each run, Pallas kernels for 27% -> 28%
where the time goes in v4:
time: 510 us; the launch traced here: 503 us
  Pallas kernels  205 us (40%)
  waiting for transfers between devices  128 us (25%)
  other arithmetic  92.3 us (18%)
  starting transfers between devices  61.4 us (12%)
  local copies, waits for them, and re-layouts  15.1 us (3%)
    ppermute x59, waiting for transfers between devices, swap(): return lax.ppermute(value, name, [(i, i ^ flip) for i in range(n)])  127 us
    ppermute x59, starting transfers between devices, swap(): return lax.ppermute(value, name, [(i, i ^ flip) for i in range(n)])  52.3 us
    pallas_call x4, Pallas kernels, weight_grads(): call(functools.partial(weight_body, index, len(lefts), pieces), tuple(sha...  49.8 us
    pallas_call x1, Pallas kernels, ff_back_all(): call(functools.partial(ff_back_body, steps), (shape((tokens, width), BF),...  32.5 us
    add x19, other arithmetic, reduce_steps(): keep = keep[:half] + got[:half]  29.2 us
    add x9, other arithmetic, reduce_steps(): send = keep[half:] + got[half:]  29 us
    pallas_call x1, Pallas kernels, ff_all(): call(ff_body, (shape((tokens, ff), BF), shape((tokens, ff), BF), shape((t...  23.5 us
    pallas_call x1, Pallas kernels, hidden_back_all(): call(hidden_back_body, shape((tokens, ff), F32), (ff // tile,), [whole((t...  12.9 us
  transfers between devices with their start and end apart: 62, of which 31 were waited for; matrix products, arithmetic and copies ran while one was open for 17% of the time, Pallas kernels for 28%

profile of v4, /device:TPU:0, one launch (start us, length us, event | category | flops | bytes accessed | tf_op | source)
XLA Modules:
  0.0 503.4 jit_solution(11053961040943126784)
XLA Ops:
  3.5 12.3 %shard_map.324 = (bf16[768,1024]{1,0:T(8,128)(2,1)}, bf16[768,512]{1,0:T(8,128)(2,1)}, bf16[768,1024]{1,0:T(8,128)(2,1)}, bf16[768,16]{1,0:T(8,128)(2,1)}, f32[7...) custom-call(s32[24]{0:T(128)} %reshape.88.docs_ref, ...), custom_call_target="tpu_custom_call" | custom-call | flops 1 | bytes 1 | tf_op jit(solution)/shard_map/pallas_call | solution.py:140
  28.1 12.9 %shard_map.325.dh_ref = f32[768,2816]{1,0:T(8,128)} custom-call(bf16[768,1024]{1,0:T(8,128)(2,1)} %bitcast.57, bf16[2816,1024]{1,0:T(8,128)(2,1)} %wd_ref.3), custom_call_target="tpu_custom_call" | custom-call | flops 1 | bytes 1 | tf_op jit(solution)/shard_map/pallas_call | solution.py:281
  49.8 6.5 %shard_map.326 = (bf16[768,512]{1,0:T(8,128)(2,1)}, f32[768,1024]{1,0:T(8,128)}) custom-call(bf16[768,1024]{1,0:T(8,128)(2,1)} %get-tuple-element.227.normed_ref.refs_2_, bf16[1024,512]{1,0:T(8,128)(2,1)} %wq_ref.3, bf16[1024,1024]{1,0:T(8,128)(2,1)} %wog_ref.3), custom_call_target="tpu_custom_call" | custom-call | flops 1 | bytes 1 | tf_op jit(solution)/shard_map/pallas_call | solution.py:179
  57.9 5.6 %collective-permute-start.13 = (f32[2,6,2,16,128]{4,3,2,1,0:T(8,128)}, f32[2,6,2,16,128]{4,3,2,1,0:T(8,128)}, u32[]{:S(2)}, u32[]{:S(2)}) collective-permute-start(f32[2,6,2,16,128]{4,3,2,1,0:T(8,128)} %add_select_fusion.26), channel_id=1, source_target_pairs={{0,8},{1,9},{2,10},{3,11},{4,12},{5,13},{6,14},{7,15},{16,24},{17,... | collective-permute-start | bytes 589832 | tf_op jit(solution)/shard_map/ppermute | solution.py:906
  67.4 8.5 %shard_map.327.inner_ref = f32[768,1024]{1,0:T(8,128)} custom-call(s32[24]{0:T(128)} %reshape.88.docs_ref, bf16[768,512]{1,0:T(8,128)(2,1)} %get-tuple-element.228.q_ref, bf16[768,512]{1,0:T(8,128)(2,1)} %get-tuple-element.233.k_ref, bf16[768,1024]{1,0:T(8,128)(2,1)} %get-tuple-element.234.v_ref, f32[768,512]{1,0:T(8,128)} %get-tuple-element.235.cum_ref), custom_call_target="tpu_custom_call" | custom-call | flops 1 | bytes 1 | tf_op jit(solution)/shard_map/pallas_call | solution.py:209
  80.6 4.0 collective-permute-done.14
  89.5 7.4 %collective-permute-done.16 = f32[4,6,2,16,128]{4,3,2,1,0:T(8,128)S(1)} collective-permute-done((f32[4,6,2,16,128]{4,3,2,1,0:T(8,128)S(1)}, f32[4,6,2,16,128]{4,3,2,1,0:T(8,128)S(1)}, u32[]{:S(2)}, u32[]{:S(2)}) %collective-permute-start.16) | collective-permute-done | bytes 393248 | tf_op jit(solution)/shard_map/ppermute | solution.py:798
  106.9 9.2 %shard_map.328 = (f32[768,1024]{1,0:T(8,128)}, bf16[768,1024]{1,0:T(8,128)(2,1)}, bf16[6,4,256,128]{3,2,1,0:T(8,128)(2,1)}) custom-call(s32[24]{0:T(128)} %reshape.88.docs_ref, s32[32]{0:T(128)} %pad_add_fusion.table_ref, bf16[768,512]{1,0:T(8,128)(2,1)} %get-tuple-element.228.q_ref, f32[768,512]{1,0:T(8,128)} %get-tuple-element.235.cum_ref, ...), custom_call_target="tpu_custom_call" | custom-call | flops 1 | bytes 1 | tf_op jit(solution)/shard_map/pallas_call | solution.py:258
  116.1 23.5 %shard_map.329 = (bf16[768,2816]{1,0:T(8,128)(2,1)}, bf16[768,2816]{1,0:T(8,128)(2,1)}, bf16[768,2816]{1,0:T(8,128)(2,1)}, bf16[768,1024]{1,0:T(8,128)(2,1)}, f32[768,1024]{1,0:T(8,128)}) custom-call(bf16[768,1024]{1,0:T(8,128)(2,1)} %bitcast.61, bf16[768,1024]{1,0:T(8,128)(2,1)} %get-tuple-element.254.gated_ref.refs_1_, bf16[1024,1024]{1,0:T(8,128)(2,1)} %wo_ref.3, ...), custom_call_target="tpu_custom_call" | custom-call | flops 1 | bytes 1 | tf_op jit(solution)/shard_map/pallas_call | solution.py:318
  139.6 18.4 %shard_map.330 = (f32[16,32,2816]{2,1,0:T(8,128)}, f32[16,32,2816]{2,1,0:T(8,128)}, f32[16,32,2816]{2,1,0:T(8,128)}, f32[16,32,2816]{2,1,0:T(8,128)}) custom-call(s32[32]{0:T(128)} %get-tuple-element.350.refs_0_.table_ref, s32[32]{0:T(128)} %get-tuple-element.528.refs_1_, bf16[768,1024]{1,0:T(8,128)(2,1)} %get-tuple-element.259.refs_2_, ...), custom_call_target="tpu_custom_call" | custom-call | flops 1 | bytes 1 | tf_op jit(solution)/shard_map/pallas_call | solution.py:712
  159.1 12.5 %shard_map.331 = (f32[16,88,1024]{2,1,0:T(8,128)}, f32[16,88,1024]{2,1,0:T(8,128)}) custom-call(s32[32]{0:T(128)} %broadcast_xor_fusion.2.refs_0_, bf16[768,2816]{1,0:T(8,128)(2,1)} %get-tuple-element.255.refs_1_.hidden_ref, bf16[768,1024]{1,0:T(8,128)(2,1)} %bitcast.58), custom_call_target="tpu_custom_call" | custom-call | flops 1 | bytes 1 | tf_op jit(solution)/shard_map/pallas_call | solution.py:712
  171.7 6.8 %slice_add_fusion.4 = (f32[8,32,2816]{2,1,0:T(8,128)S(1)}, f32[8,32,2816]{2,1,0:T(8,128)}) fusion(f32[16,32,2816]{2,1,0:T(8,128)} %collective-permute-done.20, f32[16,32,2816]{2,1,0:T(8,128)} %get-tuple-element.270), kind=kLoop, calls=%fused_computation.4 | loop fusion | flops 1441792 | bytes 17301504 | tf_op jit(solution)/shard_map/add | solution.py:873
  180.1 6.0 %slice_add_fusion.2 = (f32[8,32,2816]{2,1,0:T(8,128)}, f32[8,32,2816]{2,1,0:T(8,128)}) fusion(f32[16,32,2816]{2,1,0:T(8,128)} %collective-permute-done.21, f32[16,32,2816]{2,1,0:T(8,128)S(1)} %bitcast.64), kind=kLoop, calls=%fused_computation.2 | loop fusion | flops 1441792 | bytes 17301504 | tf_op jit(solution)/shard_map/add | solution.py:873
  193.4 32.5 %shard_map.332 = (bf16[768,1024]{1,0:T(8,128)(2,1)}, f32[768,1024]{1,0:T(8,128)}, bf16[768,1024]{1,0:T(8,128)(2,1)}, f32[768,1024]{1,0:T(8,128)}, f32[1,1024]{1,0:T(1,128)}) custom-call(bf16[768,2816]{1,0:T(8,128)(2,1)} %get-tuple-element.255.refs_1_.hidden_ref, bf16[768,2816]{1,0:T(8,128)(2,1)} %get-tuple-element.256.refs_3_.dg_ref, ...), custom_call_target="tpu_custom_call" | custom-call | flops 1 | bytes 1 | tf_op jit(solution)/shard_map/pallas_call | solution.py:389
  225.8 10.7 %shard_map.333 = (bf16[768,1024]{1,0:T(8,128)(2,1)}, bf16[768,1024]{1,0:T(8,128)(2,1)}, f32[8,6,4,16,128]{4,3,2,1,0:T(8,128)}, f32[8,6,4,16,128]{4,3,2,1,0:T(8,128)}, f32[1,256]{1,0:T(1,128)}) custom-call(s32[24]{0:T(128)} %reshape.88.docs_ref, s32[32]{0:T(128)} %pad_add_fusion.table_ref, f32[768,1024]{1,0:T(8,128)} %get-tuple-element.282.dgated_ref, ...), custom_call_target="tpu_custom_call" | custom-call | flops 1 | bytes 1 | tf_op jit(solution)/shard_map/pallas_call | solution.py:464
  236.6 10.0 %shard_map.334 = (f32[16,64,1024]{2,1,0:T(8,128)}, f32[16,64,1024]{2,1,0:T(8,128)}) custom-call(s32[32]{0:T(128)} %get-tuple-element.350.refs_0_.table_ref, bf16[768,1024]{1,0:T(8,128)(2,1)} %get-tuple-element.254.gated_ref.refs_1_, bf16[768,1024]{1,0:T(8,128)(2,1)} %get-tuple-element.227.normed_ref.refs_2_, bf16[768,1024]{1,0:T(8,128)(2,1)} %get-tuple-element.280.refs_3_, ...), custom_call_target="tpu_custom_call" | custom-call | flops 1 | bytes 1 | tf_op jit(solution)/shard_map/pallas_call | solution.py:712
  264.8 5.9 %collective-permute-done.28 = f32[16,64,1024]{2,1,0:T(8,128)} collective-permute-done((f32[16,64,1024]{2,1,0:T(8,128)}, f32[16,64,1024]{2,1,0:T(8,128)}, u32[]{:S(2)}, u32[]{:S(2)}) %collective-permute-start.28) | collective-permute-done | bytes 4194336 | tf_op jit(solution)/shard_map/ppermute | solution.py:798
  270.7 6.0 %slice_add_fusion.6 = (f32[8,64,1024]{2,1,0:T(8,128)}, f32[8,64,1024]{2,1,0:T(8,128)S(1)}) fusion(f32[16,64,1024]{2,1,0:T(8,128)} %collective-permute-done.28, f32[16,64,1024]{2,1,0:T(8,128)} %get-tuple-element.296), kind=kLoop, calls=%fused_computation.6 | loop fusion | flops 1048576 | bytes 12582912 | tf_op jit(solution)/shard_map/add | solution.py:872
  276.7 6.7 %collective-permute-done.27 = f32[4,6,4,16,128]{4,3,2,1,0:T(8,128)} collective-permute-done((f32[4,6,4,16,128]{4,3,2,1,0:T(8,128)}, f32[4,6,4,16,128]{4,3,2,1,0:T(8,128)}, u32[]{:S(2)}, u32[]{:S(2)}) %collective-permute-start.27) | collective-permute-done | bytes 786464 | tf_op jit(solution)/shard_map/ppermute | solution.py:798
  288.1 9.8 %collective-permute-done.30 = f32[4,32,2816]{2,1,0:T(8,128)} collective-permute-done((f32[4,32,2816]{2,1,0:T(8,128)}, f32[4,32,2816]{2,1,0:T(8,128)}, u32[]{:S(2)}, u32[]{:S(2)}) %collective-permute-start.30) | collective-permute-done | bytes 1441824 | tf_op jit(solution)/shard_map/ppermute | solution.py:798
  303.4 11.6 %shard_map.335 = (bf16[768,512]{1,0:T(8,128)(2,1)}, f32[768,512]{1,0:T(8,128)}, f32[768,1024]{1,0:T(8,128)}, f32[768,512]{1,0:T(8,128)}) custom-call(s32[24]{0:T(128)} %reshape.88.docs_ref, bf16[768,512]{1,0:T(8,128)(2,1)} %get-tuple-element.228.q_ref, bf16[768,512]{1,0:T(8,128)(2,1)} %get-tuple-element.233.k_ref, ...), custom_call_target="tpu_custom_call" | custom-call | flops 1 | bytes 1 | tf_op jit(solution)/shard_map/pallas_call | solution.py:518
  315.0 4.2 collective-permute-done.32
  325.2 9.5 %collective-permute-done.33 = f32[2,6,4,16,128]{4,3,2,1,0:T(8,128)S(1)} collective-permute-done((f32[2,6,4,16,128]{4,3,2,1,0:T(8,128)S(1)}, f32[2,6,4,16,128]{4,3,2,1,0:T(8,128)S(1)}, u32[]{:S(2)}, u32[]{:S(2)}) %collective-permute-start.33) | collective-permute-done | bytes 393248 | tf_op jit(solution)/shard_map/ppermute | solution.py:798
  337.7 12.7 %collective-permute-done.34 = f32[8,64,1024]{2,1,0:T(8,128)} collective-permute-done((f32[8,64,1024]{2,1,0:T(8,128)}, f32[8,64,1024]{2,1,0:T(8,128)}, u32[]{:S(2)}, u32[]{:S(2)}) %collective-permute-start.34) | collective-permute-done | bytes 2097184 | tf_op jit(solution)/shard_map/ppermute | solution.py:798
  362.9 10.9 %shard_map.336 = (bf16[768,512]{1,0:T(8,128)(2,1)}, bf16[768,1024]{1,0:T(8,128)(2,1)}, bf16[768,16]{1,0:T(8,128)(2,1)}, f32[16,512]{1,0:T(8,128)}, f32[1,512]{1,0:T(1,128)}) custom-call(s32[24]{0:T(128)} %reshape.88.docs_ref, s32[32]{0:T(128)} %pad_add_fusion.table_ref, bf16[768,512]{1,0:T(8,128)(2,1)} %get-tuple-element.233.k_ref, ...), custom_call_target="tpu_custom_call" | custom-call | flops 1 | bytes 1 | tf_op jit(solution)/shard_map/pallas_call | solution.py:587
  373.7 8.9 %shard_map.337 = (f32[16,64,512]{2,1,0:T(8,128)}, f32[16,64,512]{2,1,0:T(8,128)}, f32[16,32,1024]{2,1,0:T(8,128)}, f32[16,32,1024]{2,1,0:T(8,128)}) custom-call(s32[32]{0:T(128)} %get-tuple-element.350.refs_0_.table_ref, s32[32]{0:T(128)} %get-tuple-element.528.refs_1_, bf16[768,1024]{1,0:T(8,128)(2,1)} %get-tuple-element.227.normed_ref.refs_2_, ...), custom_call_target="tpu_custom_call" | custom-call | flops 1 | bytes 1 | tf_op jit(solution)/shard_map/pallas_call | solution.py:712
  384.7 7.3 %collective-permute-done.38 = f32[2,32,2816]{2,1,0:T(8,128)S(1)} collective-permute-done((f32[2,32,2816]{2,1,0:T(8,128)}, f32[2,32,2816]{2,1,0:T(8,128)S(1)}, u32[]{:S(2)}, u32[]{:S(2)}) %collective-permute-start.38) | collective-permute-done | bytes 720928 | tf_op jit(solution)/shard_map/ppermute | solution.py:798
  413.9 12.4 %shard_map.338 = (f32[768,1024]{1,0:T(8,128)}, f32[1,1024]{1,0:T(1,128)}) custom-call(bf16[768,1024]{1,0:T(8,128)(2,1)} %bitcast.62, f32[768,1024]{1,0:T(8,128)} %get-tuple-element.279.dmid_ref, bf16[768,512]{1,0:T(8,128)(2,1)} %get-tuple-element.307.refs_3_.dq_ref, bf16[768,512]{1,0:T(8,128)(2,1)} %get-tuple-element.326.refs_4_.dk_ref, ...), custom_call_target="tpu_custom_call" | custom-call | flops 1 | bytes 1 | tf_op jit(solution)/shard_map/pallas_call | solution.py:640
  439.2 5.4 %collective-permute-done.46 = f32[1,32,2816]{2,1,0:T(8,128)} collective-permute-done((f32[1,32,2816]{2,1,0:T(8,128)}, f32[1,32,2816]{2,1,0:T(8,128)}, u32[]{:S(2)}, u32[]{:S(2)}) %collective-permute-start.46) | collective-permute-done | bytes 360480 | tf_op jit(solution)/shard_map/ppermute | solution.py:798
  457.1 7.6 %collective-permute-done.51 = f32[2,64,512]{2,1,0:T(8,128)S(1)} collective-permute-done((f32[2,64,512]{2,1,0:T(8,128)S(1)}, f32[2,64,512]{2,1,0:T(8,128)S(1)}, u32[]{:S(2)}, u32[]{:S(2)}) %collective-permute-start.51) | collective-permute-done | bytes 262176 | tf_op jit(solution)/shard_map/ppermute | solution.py:798
  478.4 11.4 %collective-permute-done.57 = f32[1,64,512]{2,1,0:T(8,128)S(1)} collective-permute-done((f32[1,64,512]{2,1,0:T(8,128)S(1)}, f32[1,64,512]{2,1,0:T(8,128)S(1)}, u32[]{:S(2)}, u32[]{:S(2)}) %collective-permute-start.57) | collective-permute-done | bytes 131104 | tf_op jit(solution)/shard_map/ppermute | solution.py:798
  494.0 5.0 collective-permute-done.60
  (297 shorter events, 179.8 us)
Async XLA Ops:
  22.1 20.4 %collective-permute-start.6 = (f32[4,6,2,16,128]{4,3,2,1,0:T(8,128)}, f32[4,6,2,16,128]{4,3,2,1,0:T(8,128)S(1)}, u32[]{:S(2)}, u32[]{:S(2)}) collective-permute-start(f32[4,6,2,16,128]{4,3,2,1,0:T(8,128)} %get-tuple-element.214), channel_id=1, source_target_pairs={{0,2},{1,3},{2,0},{3,1},{4,6},{5,7},{6,4},{7,5},{8,10},{9,11},{10,... | collective-permute-start | bytes 1179656 | tf_op jit(solution)/shard_map/ppermute | solution.py:798
  24.9 16.1 %collective-permute-start.7 = (f32[1,6,2,1,128]{4,2,1,3,0:T(2,128)S(1)}, f32[1,6,2,1,128]{4,2,1,3,0:T(2,128)}, u32[]{:S(2)}, u32[]{:S(2)}) collective-permute-start(f32[1,6,2,1,128]{4,2,1,3,0:T(2,128)S(1)} %get-tuple-element.221), channel_id=1, source_target_pairs={{0,2},{1,3},{2,0},{3,1},{4,6},{5,7},{6,4},{7,5},{8,10},{9,11},{10,... | collective-permute-start | bytes 18440 | tf_op jit(solution)/shard_map/ppermute | solution.py:798
  28.0 17.9 %collective-permute-start.5 = (f32[4,6,2,16,128]{4,3,2,1,0:T(8,128)}, f32[4,6,2,16,128]{4,3,2,1,0:T(8,128)}, u32[]{:S(2)}, u32[]{:S(2)}) collective-permute-start(f32[4,6,2,16,128]{4,3,2,1,0:T(8,128)} %get-tuple-element.218), channel_id=1, source_target_pairs={{0,2},{1,3},{2,0},{3,1},{4,6},{5,7},{6,4},{7,5},{8,10},{9,11},{10,... | collective-permute-start | bytes 1179656 | tf_op jit(solution)/shard_map/ppermute | solution.py:798
  47.8 15.8 %collective-permute-start.9 = (f32[2,6,2,16,128]{4,3,2,1,0:T(8,128)}, f32[2,6,2,16,128]{4,3,2,1,0:T(8,128)}, u32[]{:S(2)}, u32[]{:S(2)}) collective-permute-start(f32[2,6,2,16,128]{4,3,2,1,0:T(8,128)} %get-tuple-element.225), channel_id=1, source_target_pairs={{0,4},{1,5},{2,6},{3,7},{4,0},{5,1},{6,2},{7,3},{8,12},{9,13},{10,... | collective-permute-start | bytes 589832 | tf_op jit(solution)/shard_map/ppermute | solution.py:798
  57.9 17.9 %collective-permute-start.13 = (f32[2,6,2,16,128]{4,3,2,1,0:T(8,128)}, f32[2,6,2,16,128]{4,3,2,1,0:T(8,128)}, u32[]{:S(2)}, u32[]{:S(2)}) collective-permute-start(f32[2,6,2,16,128]{4,3,2,1,0:T(8,128)} %add_select_fusion.26), channel_id=1, source_target_pairs={{0,8},{1,9},{2,10},{3,11},{4,12},{5,13},{6,14},{7,15},{16,24},{17,... | collective-permute-start | bytes 589832 | tf_op jit(solution)/shard_map/ppermute | solution.py:906
  158.2 21.9 %collective-permute-start.21 = (f32[16,32,2816]{2,1,0:T(8,128)}, f32[16,32,2816]{2,1,0:T(8,128)}, u32[]{:S(2)}, u32[]{:S(2)}) collective-permute-start(f32[16,32,2816]{2,1,0:T(8,128)} %get-tuple-element.273), channel_id=1, source_target_pairs={{0,1},{1,0},{2,3},{3,2},{4,5},{5,4},{6,7},{7,6},{8,9},{9,8},{10,11... | collective-permute-start | bytes 17301512 | tf_op jit(solution)/shard_map/ppermute | solution.py:798
  171.6 16.1 %collective-permute-start.22 = (f32[16,88,1024]{2,1,0:T(8,128)}, f32[16,88,1024]{2,1,0:T(8,128)S(1)}, u32[]{:S(2)}, u32[]{:S(2)}) collective-permute-start(f32[16,88,1024]{2,1,0:T(8,128)} %get-tuple-element.269), channel_id=1, source_target_pairs={{0,1},{1,0},{2,3},{3,2},{4,5},{5,4},{6,7},{7,6},{8,9},{9,8},{10,11... | collective-permute-start | bytes 17301512 | tf_op jit(solution)/shard_map/ppermute | solution.py:798
  178.5 68.0 %collective-permute-start.24 = (f32[8,32,2816]{2,1,0:T(8,128)}, f32[8,32,2816]{2,1,0:T(8,128)}, u32[]{:S(2)}, u32[]{:S(2)}) collective-permute-start(f32[8,32,2816]{2,1,0:T(8,128)} %get-tuple-element.271), channel_id=1, source_target_pairs={{0,16},{16,0},{1,17},{17,1},{2,18},{18,2},{3,19},{19,3},{4,20},{20... | collective-permute-start | bytes 8650760 | tf_op jit(solution)/shard_map/ppermute | solution.py:798
  186.2 65.1 %collective-permute-start.25 = (f32[8,32,2816]{2,1,0:T(8,128)}, f32[8,32,2816]{2,1,0:T(8,128)}, u32[]{:S(2)}, u32[]{:S(2)}) collective-permute-start(f32[8,32,2816]{2,1,0:T(8,128)} %get-tuple-element.274), channel_id=1, source_target_pairs={{0,2},{1,3},{2,0},{3,1},{4,6},{5,7},{6,4},{7,5},{8,10},{9,11},{10,... | collective-permute-start | bytes 8650760 | tf_op jit(solution)/shard_map/ppermute | solution.py:798
  191.4 64.9 %collective-permute-start.26 = (f32[8,88,1024]{2,1,0:T(8,128)}, f32[8,88,1024]{2,1,0:T(8,128)}, u32[]{:S(2)}, u32[]{:S(2)}) collective-permute-start(f32[8,88,1024]{2,1,0:T(8,128)} %get-tuple-element.276), channel_id=1, source_target_pairs={{0,4},{1,5},{2,6},{3,7},{4,0},{5,1},{6,2},{7,3},{8,12},{9,13},{10,... | collective-permute-start | bytes 8650760 | tf_op jit(solution)/shard_map/ppermute | solution.py:798
  236.5 23.8 %collective-permute-start.23 = (f32[8,6,4,16,128]{4,3,2,1,0:T(8,128)}, f32[8,6,4,16,128]{4,3,2,1,0:T(8,128)}, u32[]{:S(2)}, u32[]{:S(2)}) collective-permute-start(f32[8,6,4,16,128]{4,3,2,1,0:T(8,128)} %get-tuple-element.286), channel_id=1, source_target_pairs={{0,1},{1,0},{2,3},{3,2},{4,5},{5,4},{6,7},{7,6},{8,9},{9,8},{10,11... | collective-permute-start | bytes 4718600 | tf_op jit(solution)/shard_map/ppermute | solution.py:798
  263.2 20.3 %collective-permute-start.27 = (f32[4,6,4,16,128]{4,3,2,1,0:T(8,128)}, f32[4,6,4,16,128]{4,3,2,1,0:T(8,128)}, u32[]{:S(2)}, u32[]{:S(2)}) collective-permute-start(f32[4,6,4,16,128]{4,3,2,1,0:T(8,128)} %get-tuple-element.295), channel_id=1, source_target_pairs={{0,2},{1,3},{2,0},{3,1},{4,6},{5,7},{6,4},{7,5},{8,10},{9,11},{10,... | collective-permute-start | bytes 2359304 | tf_op jit(solution)/shard_map/ppermute | solution.py:798
  263.8 34.1 %collective-permute-start.30 = (f32[4,32,2816]{2,1,0:T(8,128)}, f32[4,32,2816]{2,1,0:T(8,128)}, u32[]{:S(2)}, u32[]{:S(2)}) collective-permute-start(f32[4,32,2816]{2,1,0:T(8,128)} %get-tuple-element.301), channel_id=1, source_target_pairs={{0,16},{16,0},{1,17},{17,1},{2,18},{18,2},{3,19},{19,3},{4,20},{20... | collective-permute-start | bytes 4325384 | tf_op jit(solution)/shard_map/ppermute | solution.py:798
  285.7 33.5 %collective-permute-start.32 = (f32[4,32,2816]{2,1,0:T(8,128)}, f32[4,32,2816]{2,1,0:T(8,128)}, u32[]{:S(2)}, u32[]{:S(2)}) collective-permute-start(f32[4,32,2816]{2,1,0:T(8,128)} %get-tuple-element.309), channel_id=1, source_target_pairs={{0,2},{1,3},{2,0},{3,1},{4,6},{5,7},{6,4},{7,5},{8,10},{9,11},{10,... | collective-permute-start | bytes 4325384 | tf_op jit(solution)/shard_map/ppermute | solution.py:798
  301.8 22.0 %collective-permute-start.31 = (f32[2,6,4,16,128]{4,3,2,1,0:T(8,128)}, f32[2,6,4,16,128]{4,3,2,1,0:T(8,128)}, u32[]{:S(2)}, u32[]{:S(2)}) collective-permute-start(f32[2,6,4,16,128]{4,3,2,1,0:T(8,128)} %add_select_fusion.14), channel_id=1, source_target_pairs={{8,0},{9,1},{10,2},{11,3},{12,4},{13,5},{14,6},{15,7},{24,16},{25,... | collective-permute-start | bytes 1179656 | tf_op jit(solution)/shard_map/ppermute | solution.py:906
  303.0 47.3 %collective-permute-start.34 = (f32[8,64,1024]{2,1,0:T(8,128)}, f32[8,64,1024]{2,1,0:T(8,128)}, u32[]{:S(2)}, u32[]{:S(2)}) collective-permute-start(f32[8,64,1024]{2,1,0:T(8,128)} %get-tuple-element.316), channel_id=1, source_target_pairs={{0,16},{16,0},{1,17},{17,1},{2,18},{18,2},{3,19},{19,3},{4,20},{20... | collective-permute-start | bytes 6291464 | tf_op jit(solution)/shard_map/ppermute | solution.py:798
  336.1 17.4 %collective-permute-start.35 = (f32[4,6,4,16,128]{4,3,2,1,0:T(8,128)S(1)}, f32[4,6,4,16,128]{4,3,2,1,0:T(8,128)S(1)}, u32[]{:S(2)}, u32[]{:S(2)}) collective-permute-start(f32[4,6,4,16,128]{4,3,2,1,0:T(8,128)S(1)} %get-tuple-element.314), channel_id=1, source_target_pairs={{0,2},{1,3},{2,0},{3,1},{4,6},{5,7},{6,4},{7,5},{8,10},{9,11},{10,... | collective-permute-start | bytes 2359304 | tf_op jit(solution)/shard_map/ppermute | solution.py:798
  357.8 24.8 %collective-permute-start.37 = (f32[2,32,2816]{2,1,0:T(8,128)}, f32[2,32,2816]{2,1,0:T(8,128)}, u32[]{:S(2)}, u32[]{:S(2)}) collective-permute-start(f32[2,32,2816]{2,1,0:T(8,128)} %get-tuple-element.335), channel_id=1, source_target_pairs={{0,4},{1,5},{2,6},{3,7},{4,0},{5,1},{6,2},{7,3},{8,12},{9,13},{10,... | collective-permute-start | bytes 2162696 | tf_op jit(solution)/shard_map/ppermute | solution.py:798
  359.6 34.0 %collective-permute-start.39 = (f32[4,88,1024]{2,1,0:T(8,128)}, f32[4,88,1024]{2,1,0:T(8,128)}, u32[]{:S(2)}, u32[]{:S(2)}) collective-permute-start(f32[4,88,1024]{2,1,0:T(8,128)} %get-tuple-element.339), channel_id=1, source_target_pairs={{0,16},{16,0},{1,17},{17,1},{2,18},{18,2},{3,19},{19,3},{4,20},{20... | collective-permute-start | bytes 4325384 | tf_op jit(solution)/shard_map/ppermute | solution.py:798
  360.0 32.1 %collective-permute-start.38 = (f32[2,32,2816]{2,1,0:T(8,128)}, f32[2,32,2816]{2,1,0:T(8,128)S(1)}, u32[]{:S(2)}, u32[]{:S(2)}) collective-permute-start(f32[2,32,2816]{2,1,0:T(8,128)} %get-tuple-element.337), channel_id=1, source_target_pairs={{0,4},{1,5},{2,6},{3,7},{4,0},{5,1},{6,2},{7,3},{8,12},{9,13},{10,... | collective-permute-start | bytes 2162696 | tf_op jit(solution)/shard_map/ppermute | solution.py:798
  360.2 36.0 %collective-permute-start.40 = (f32[4,64,1024]{2,1,0:T(8,128)}, f32[4,64,1024]{2,1,0:T(8,128)}, u32[]{:S(2)}, u32[]{:S(2)}) collective-permute-start(f32[4,64,1024]{2,1,0:T(8,128)} %get-tuple-element.341), channel_id=1, source_target_pairs={{0,2},{1,3},{2,0},{3,1},{4,6},{5,7},{6,4},{7,5},{8,10},{9,11},{10,... | collective-permute-start | bytes 3145736 | tf_op jit(solution)/shard_map/ppermute | solution.py:798
  407.2 25.5 %collective-permute-start.43 = (f32[8,64,512]{2,1,0:T(8,128)}, f32[8,64,512]{2,1,0:T(8,128)}, u32[]{:S(2)}, u32[]{:S(2)}) collective-permute-start(f32[8,64,512]{2,1,0:T(8,128)} %get-tuple-element.346), channel_id=1, source_target_pairs={{0,16},{16,0},{1,17},{17,1},{2,18},{18,2},{3,19},{19,3},{4,20},{20... | collective-permute-start | bytes 3145736 | tf_op jit(solution)/shard_map/ppermute | solution.py:798
  407.5 26.6 %collective-permute-start.44 = (f32[8,32,1024]{2,1,0:T(8,128)}, f32[8,32,1024]{2,1,0:T(8,128)}, u32[]{:S(2)}, u32[]{:S(2)}) collective-permute-start(f32[8,32,1024]{2,1,0:T(8,128)} %get-tuple-element.359), channel_id=1, source_target_pairs={{0,2},{1,3},{2,0},{3,1},{4,6},{5,7},{6,4},{7,5},{8,10},{9,11},{10,... | collective-permute-start | bytes 3145736 | tf_op jit(solution)/shard_map/ppermute | solution.py:798
  409.0 28.5 %collective-permute-start.45 = (f32[1,32,2816]{2,1,0:T(8,128)}, f32[1,32,2816]{2,1,0:T(8,128)}, u32[]{:S(2)}, u32[]{:S(2)}) collective-permute-start(f32[1,32,2816]{2,1,0:T(8,128)} %get-tuple-element.362), channel_id=1, source_target_pairs={{0,8},{1,9},{2,10},{3,11},{4,12},{5,13},{6,14},{7,15},{8,0},{9,1},... | collective-permute-start | bytes 1081352 | tf_op jit(solution)/shard_map/ppermute | solution.py:798
  412.9 31.6 %collective-permute-start.46 = (f32[1,32,2816]{2,1,0:T(8,128)}, f32[1,32,2816]{2,1,0:T(8,128)}, u32[]{:S(2)}, u32[]{:S(2)}) collective-permute-start(f32[1,32,2816]{2,1,0:T(8,128)} %get-tuple-element.364), channel_id=1, source_target_pairs={{0,8},{1,9},{2,10},{3,11},{4,12},{5,13},{6,14},{7,15},{8,0},{9,1},... | collective-permute-start | bytes 1081352 | tf_op jit(solution)/shard_map/ppermute | solution.py:798
  412.9 33.4 %collective-permute-start.47 = (f32[2,64,1024]{2,1,0:T(8,128)}, f32[2,64,1024]{2,1,0:T(8,128)}, u32[]{:S(2)}, u32[]{:S(2)}) collective-permute-start(f32[2,64,1024]{2,1,0:T(8,128)} %get-tuple-element.367), channel_id=1, source_target_pairs={{0,4},{1,5},{2,6},{3,7},{4,0},{5,1},{6,2},{7,3},{8,12},{9,13},{10,... | collective-permute-start | bytes 1572872 | tf_op jit(solution)/shard_map/ppermute | solution.py:798
  451.0 23.8 %collective-permute-start.55 = (f32[1,64,1024]{2,1,0:T(8,128)S(1)}, f32[1,64,1024]{2,1,0:T(8,128)S(1)}, u32[]{:S(2)}, u32[]{:S(2)}) collective-permute-start(f32[1,64,1024]{2,1,0:T(8,128)S(1)} %get-tuple-element.368), channel_id=1, source_target_pairs={{0,8},{1,9},{2,10},{3,11},{4,12},{5,13},{6,14},{7,15},{8,0},{9,1},... | collective-permute-start | bytes 786440 | tf_op jit(solution)/shard_map/ppermute | solution.py:798
  455.0 16.1 %collective-permute-start.53 = (f32[2,88,1024]{2,1,0:T(8,128)S(1)}, f32[2,88,1024]{2,1,0:T(8,128)S(1)}, u32[]{:S(2)}, u32[]{:S(2)}) collective-permute-start(f32[2,88,1024]{2,1,0:T(8,128)S(1)} %copy-done.14), channel_id=1, source_target_pairs={{0,2},{1,3},{2,0},{3,1},{4,6},{5,7},{6,4},{7,5},{8,10},{9,11},{10,... | collective-permute-start | bytes 2162696 | tf_op jit(solution)/shard_map/ppermute | solution.py:798
  471.9 17.9 %collective-permute-start.57 = (f32[1,64,512]{2,1,0:T(8,128)S(1)}, f32[1,64,512]{2,1,0:T(8,128)S(1)}, u32[]{:S(2)}, u32[]{:S(2)}) collective-permute-start(f32[1,64,512]{2,1,0:T(8,128)S(1)} %get-tuple-element.378), channel_id=1, source_target_pairs={{0,8},{1,9},{2,10},{3,11},{4,12},{5,13},{6,14},{7,15},{8,0},{9,1},... | collective-permute-start | bytes 393224 | tf_op jit(solution)/shard_map/ppermute | solution.py:798
  472.5 20.1 %collective-permute-start.58 = (f32[1,32,1024]{2,1,0:T(8,128)S(1)}, f32[1,32,1024]{2,1,0:T(8,128)S(1)}, u32[]{:S(2)}, u32[]{:S(2)}) collective-permute-start(f32[1,32,1024]{2,1,0:T(8,128)S(1)} %get-tuple-element.389), channel_id=1, source_target_pairs={{0,8},{1,9},{2,10},{3,11},{4,12},{5,13},{6,14},{7,15},{8,0},{9,1},... | collective-permute-start | bytes 393224 | tf_op jit(solution)/shard_map/ppermute | solution.py:798
  476.1 17.1 %collective-permute-start.59 = (f32[2,56,128]{2,1,0:T(8,128)S(1)}, f32[2,56,128]{2,1,0:T(8,128)S(1)}, u32[]{:S(2)}, u32[]{:S(2)}) collective-permute-start(f32[2,56,128]{2,1,0:T(8,128)S(1)} %get-tuple-element.386), channel_id=1, source_target_pairs={{0,4},{1,5},{2,6},{3,7},{4,0},{5,1},{6,2},{7,3},{8,12},{9,13},{10,... | collective-permute-start | bytes 172040 | tf_op jit(solution)/shard_map/ppermute | solution.py:798
  477.9 21.0 %collective-permute-start.60 = (f32[1,88,1024]{2,1,0:T(8,128)S(1)}, f32[1,88,1024]{2,1,0:T(8,128)S(1)}, u32[]{:S(2)}, u32[]{:S(2)}) collective-permute-start(f32[1,88,1024]{2,1,0:T(8,128)S(1)} %get-tuple-element.381), channel_id=1, source_target_pairs={{0,8},{1,9},{2,10},{3,11},{4,12},{5,13},{6,14},{7,15},{8,0},{9,1},... | collective-permute-start | bytes 1081352 | tf_op jit(solution)/shard_map/ppermute | solution.py:798
  (73 other events, 649.3 us)

commit v5 on v4

--- a/solution.py
+++ b/solution.py
@@ -33,7 +33,7 @@
     return jax.ShapeDtypeStruct(dims, dtype)
 
 
-def call(body, out_shape, grid, in_specs, out_specs, prefetch=0, scratch=()):
+def call(body, out_shape, grid, in_specs, out_specs, prefetch=0, scratch=(), room=60):
     return pl.pallas_call(
         body,
         out_shape=out_shape,
@@ -44,7 +44,7 @@
             out_specs=out_specs,
             scratch_shapes=list(scratch),
         ),
-        compiler_params=pltpu.CompilerParams(vmem_limit_bytes=60 * MIB),
+        compiler_params=pltpu.CompilerParams(vmem_limit_bytes=room * MIB),
         cost_estimate=pl.CostEstimate(flops=1, bytes_accessed=1, transcendentals=0),
     )
 
@@ -528,6 +528,7 @@
         ],
         (tile(kw), tile(kw), tile(vw), tile(kw)),
         prefetch=1,
+        room=28,
     )(docs, q, k, v, cum, dmix, state)
 
 
@@ -598,6 +599,7 @@
         ],
         (tile(kw), tile(vw), tile(rank), whole((rank, kw)), whole((1, kw))),
         prefetch=2,
+        room=28,
     )(docs, table, k, v, cum, gp, ra, state, dk, dv, decay, near, far, wru)
 
 
@@ -647,6 +649,7 @@
             whole(wrd.shape),
         ],
         (tile(width), whole((1, width))),
+        room=28,
     )(x, dmid, dq, dk, dv, dog, drank, gain.reshape(1, -1), wq, wk, wv, wog, wrd)
 
 
@@ -681,7 +684,7 @@
             at, place = at + 1, place + per
 
 
-def weight_grads(groups, tables, steps=2):
+def weight_grads(groups, tables, room, steps=2):
     pieces = tables[0].shape[0]
     tokens = groups[0][0][0].shape[0]
     out = []
@@ -717,6 +720,7 @@
         tuple(blocks),
         prefetch=len(groups),
         scratch=[pltpu.VMEM(left.shape[::-1], BF) for left in lefts] + holds,
+        room=room,
     )(*tables, *lefts, *rights)
     return [(flat[2 * g], flat[2 * g + 1]) for g in range(len(groups))]
 
@@ -777,6 +781,7 @@
         (whole(half.shape), whole(half.shape)),
         prefetch=1,
         scratch=[pltpu.VMEM((width + kw + hv, 128), F32)],
+        room=16,
     )(table, *operands)
 
 
@@ -1070,7 +1075,8 @@
             if name not in made:
                 ordered = [tables[routes[each]] for each in names]
                 ordered[0] = turns.after(ordered[0])
-                groups = weight_grads([operands[each]() for each in names], ordered)
+                room = 60 if name in ("gate", "up", "down") else 32
+                groups = weight_grads([operands[each]() for each in names], ordered, room)
                 made.update(zip(names, groups))
             return made[name]
 

time: 510 us -> 494 us (0.969)
  other arithmetic: 92.3 us -> 72.2 us
  Pallas kernels: 205 us -> 186 us
  waiting for transfers between devices: 128 us -> 145 us
    ppermute x59, waiting for transfers between devices: 127 us -> 144 us  [swap(): return lax.ppermute(value, name, [(i, i ^ flip) for i in range(n)])]
    add x19, other arithmetic: 29.2 us -> 19.9 us  [reduce_steps(): keep = keep[:half] + got[:half]]
  transfers between devices with their start and end apart: 62 -> 62, of which waited for: 31 -> 30; matrix products, arithmetic and copies ran while one was open for 17% -> 15% of each run, Pallas kernels for 28% -> 25%
where the time goes in v5:
time: 494 us; the launch traced here: 488 us
  Pallas kernels  186 us (38%)
  waiting for transfers between devices  145 us (29%)
  other arithmetic  72.2 us (15%)
  starting transfers between devices  64.1 us (13%)
  local copies, waits for them, and re-layouts  19 us (4%)
    ppermute x59, waiting for transfers between devices, swap(): return lax.ppermute(value, name, [(i, i ^ flip) for i in range(n)])  144 us
    ppermute x59, starting transfers between devices, swap(): return lax.ppermute(value, name, [(i, i ^ flip) for i in range(n)])  55 us
    pallas_call x4, Pallas kernels, weight_grads(): call(functools.partial(weight_body, index, len(lefts), pieces), tuple(sha...  44.8 us
    pallas_call x1, Pallas kernels, ff_back_all(): call(functools.partial(ff_back_body, steps), (shape((tokens, width), BF),...  32.6 us
    add x9, other arithmetic, reduce_steps(): send = keep[half:] + got[half:]  24.3 us
    pallas_call x1, Pallas kernels, ff_all(): call(ff_body, (shape((tokens, ff), BF), shape((tokens, ff), BF), shape((t...  23.5 us
    add x19, other arithmetic, reduce_steps(): keep = keep[:half] + got[:half]  19.9 us
    pallas_call x1, Pallas kernels, hidden_back_all(): call(hidden_back_body, shape((tokens, ff), F32), (ff // tile,), [whole((t...  12.9 us
  transfers between devices with their start and end apart: 62, of which 30 were waited for; matrix products, arithmetic and copies ran while one was open for 15% of the time, Pallas kernels for 25%

profile of v5, /device:TPU:0, one launch (start us, length us, event | category | flops | bytes accessed | tf_op | source)
XLA Modules:
  0.0 488.2 jit_solution(18142767970131020998)
XLA Ops:
  3.5 12.2 %shard_map.324 = (bf16[768,1024]{1,0:T(8,128)(2,1)}, bf16[768,512]{1,0:T(8,128)(2,1)}, bf16[768,1024]{1,0:T(8,128)(2,1)}, bf16[768,16]{1,0:T(8,128)(2,1)}, f32[7...) custom-call(s32[24]{0:T(128)} %reshape.88.docs_ref, ...), custom_call_target="tpu_custom_call" | custom-call | flops 1 | bytes 1 | tf_op jit(solution)/shard_map/pallas_call | solution.py:140
  28.6 12.9 %shard_map.325.dh_ref = f32[768,2816]{1,0:T(8,128)} custom-call(bf16[768,1024]{1,0:T(8,128)(2,1)} %bitcast.64, bf16[2816,1024]{1,0:T(8,128)(2,1)} %wd_ref.3), custom_call_target="tpu_custom_call" | custom-call | flops 1 | bytes 1 | tf_op jit(solution)/shard_map/pallas_call | solution.py:281
  50.3 6.5 %shard_map.326 = (bf16[768,512]{1,0:T(8,128)(2,1)}, f32[768,1024]{1,0:T(8,128)}) custom-call(bf16[768,1024]{1,0:T(8,128)(2,1)} %get-tuple-element.227.normed_ref.refs_2_, bf16[1024,512]{1,0:T(8,128)(2,1)} %wq_ref.3, bf16[1024,1024]{1,0:T(8,128)(2,1)} %wog_ref.3), custom_call_target="tpu_custom_call" | custom-call | flops 1 | bytes 1 | tf_op jit(solution)/shard_map/pallas_call | solution.py:179
  58.4 5.6 %collective-permute-start.13 = (f32[2,6,2,16,128]{4,3,2,1,0:T(8,128)}, f32[2,6,2,16,128]{4,3,2,1,0:T(8,128)}, u32[]{:S(2)}, u32[]{:S(2)}) collective-permute-start(f32[2,6,2,16,128]{4,3,2,1,0:T(8,128)} %add_select_fusion.26), channel_id=1, source_target_pairs={{0,8},{1,9},{2,10},{3,11},{4,12},{5,13},{6,14},{7,15},{16,24},{17,... | collective-permute-start | bytes 589832 | tf_op jit(solution)/shard_map/ppermute | solution.py:911
  67.8 8.5 %shard_map.327.inner_ref = f32[768,1024]{1,0:T(8,128)} custom-call(s32[24]{0:T(128)} %reshape.88.docs_ref, bf16[768,512]{1,0:T(8,128)(2,1)} %get-tuple-element.228.q_ref, bf16[768,512]{1,0:T(8,128)(2,1)} %get-tuple-element.233.k_ref, bf16[768,1024]{1,0:T(8,128)(2,1)} %get-tuple-element.234.v_ref, f32[768,512]{1,0:T(8,128)} %get-tuple-element.235.cum_ref), custom_call_target="tpu_custom_call" | custom-call | flops 1 | bytes 1 | tf_op jit(solution)/shard_map/pallas_call | solution.py:209
  90.0 7.3 %collective-permute-done.16 = f32[4,6,2,16,128]{4,3,2,1,0:T(8,128)S(1)} collective-permute-done((f32[4,6,2,16,128]{4,3,2,1,0:T(8,128)S(1)}, f32[4,6,2,16,128]{4,3,2,1,0:T(8,128)S(1)}, u32[]{:S(2)}, u32[]{:S(2)}) %collective-permute-start.16) | collective-permute-done | bytes 393248 | tf_op jit(solution)/shard_map/ppermute | solution.py:803
  107.1 9.2 %shard_map.328 = (f32[768,1024]{1,0:T(8,128)}, bf16[768,1024]{1,0:T(8,128)(2,1)}, bf16[6,4,256,128]{3,2,1,0:T(8,128)(2,1)}) custom-call(s32[24]{0:T(128)} %reshape.88.docs_ref, s32[32]{0:T(128)} %pad_add_fusion.table_ref, bf16[768,512]{1,0:T(8,128)(2,1)} %get-tuple-element.228.q_ref, f32[768,512]{1,0:T(8,128)} %get-tuple-element.235.cum_ref, ...), custom_call_target="tpu_custom_call" | custom-call | flops 1 | bytes 1 | tf_op jit(solution)/shard_map/pallas_call | solution.py:258
  116.4 23.5 %shard_map.329 = (bf16[768,2816]{1,0:T(8,128)(2,1)}, bf16[768,2816]{1,0:T(8,128)(2,1)}, bf16[768,2816]{1,0:T(8,128)(2,1)}, bf16[768,1024]{1,0:T(8,128)(2,1)}, f32[768,1024]{1,0:T(8,128)}) custom-call(bf16[768,1024]{1,0:T(8,128)(2,1)} %bitcast.58, bf16[768,1024]{1,0:T(8,128)(2,1)} %get-tuple-element.254.gated_ref.refs_1_, bf16[1024,1024]{1,0:T(8,128)(2,1)} %wo_ref.3, ...), custom_call_target="tpu_custom_call" | custom-call | flops 1 | bytes 1 | tf_op jit(solution)/shard_map/pallas_call | solution.py:318
  139.8 18.4 %shard_map.330 = (f32[16,32,2816]{2,1,0:T(8,128)}, f32[16,32,2816]{2,1,0:T(8,128)}, f32[16,32,2816]{2,1,0:T(8,128)}, f32[16,32,2816]{2,1,0:T(8,128)}) custom-call(s32[32]{0:T(128)} %get-tuple-element.350.refs_0_.table_ref, s32[32]{0:T(128)} %get-tuple-element.528.refs_1_, bf16[768,1024]{1,0:T(8,128)(2,1)} %get-tuple-element.259.refs_2_, ...), custom_call_target="tpu_custom_call" | custom-call | flops 1 | bytes 1 | tf_op jit(solution)/shard_map/pallas_call | solution.py:715
  159.3 12.5 %shard_map.331 = (f32[16,88,1024]{2,1,0:T(8,128)}, f32[16,88,1024]{2,1,0:T(8,128)}) custom-call(s32[32]{0:T(128)} %broadcast_xor_fusion.2.refs_0_, bf16[768,2816]{1,0:T(8,128)(2,1)} %get-tuple-element.255.refs_1_.hidden_ref, bf16[768,1024]{1,0:T(8,128)(2,1)} %bitcast.65), custom_call_target="tpu_custom_call" | custom-call | flops 1 | bytes 1 | tf_op jit(solution)/shard_map/pallas_call | solution.py:715
  172.0 7.7 %slice_add_fusion.4 = (f32[8,32,2816]{2,1,0:T(8,128)}, f32[8,32,2816]{2,1,0:T(8,128)}) fusion(f32[16,32,2816]{2,1,0:T(8,128)} %collective-permute-done.20, f32[16,32,2816]{2,1,0:T(8,128)} %get-tuple-element.270), kind=kLoop, calls=%fused_computation.4 | loop fusion | flops 1441792 | bytes 17301504 | tf_op jit(solution)/shard_map/add | solution.py:878
  181.3 6.1 %slice_add_fusion.2 = (f32[8,32,2816]{2,1,0:T(8,128)}, f32[8,32,2816]{2,1,0:T(8,128)}) fusion(f32[16,32,2816]{2,1,0:T(8,128)} %collective-permute-done.21, f32[16,32,2816]{2,1,0:T(8,128)S(1)} %bitcast.68), kind=kLoop, calls=%fused_computation.2 | loop fusion | flops 1441792 | bytes 17301504 | tf_op jit(solution)/shard_map/add | solution.py:878
  194.6 32.6 %shard_map.332 = (bf16[768,1024]{1,0:T(8,128)(2,1)}, f32[768,1024]{1,0:T(8,128)}, bf16[768,1024]{1,0:T(8,128)(2,1)}, f32[768,1024]{1,0:T(8,128)}, f32[1,1024]{1,0:T(1,128)}) custom-call(bf16[768,2816]{1,0:T(8,128)(2,1)} %get-tuple-element.255.refs_1_.hidden_ref, bf16[768,2816]{1,0:T(8,128)(2,1)} %get-tuple-element.256.refs_3_.dg_ref, ...), custom_call_target="tpu_custom_call" | custom-call | flops 1 | bytes 1 | tf_op jit(solution)/shard_map/pallas_call | solution.py:389
  227.2 10.9 %shard_map.333 = (bf16[768,1024]{1,0:T(8,128)(2,1)}, bf16[768,1024]{1,0:T(8,128)(2,1)}, f32[8,6,4,16,128]{4,3,2,1,0:T(8,128)}, f32[8,6,4,16,128]{4,3,2,1,0:T(8,128)}, f32[1,256]{1,0:T(1,128)}) custom-call(s32[24]{0:T(128)} %reshape.88.docs_ref, s32[32]{0:T(128)} %pad_add_fusion.table_ref, f32[768,1024]{1,0:T(8,128)} %get-tuple-element.282.dgated_ref, ...), custom_call_target="tpu_custom_call" | custom-call | flops 1 | bytes 1 | tf_op jit(solution)/shard_map/pallas_call | solution.py:464
  241.0 7.6 %shard_map.334 = (f32[16,64,1024]{2,1,0:T(8,128)S(1)}, f32[16,64,1024]{2,1,0:T(8,128)}) custom-call(s32[32]{0:T(128)S(1)} %copy-done.24, bf16[768,1024]{1,0:T(8,128)(2,1)S(1)} %copy-done.11, bf16[768,1024]{1,0:T(8,128)(2,1)S(1)} %copy-done.1, bf16[768,1024]{1,0:T(8,128)(2,1)S(1)} %copy-done.17, bf16[768,1024]{1,0:T(8,128)(2,1)S(1)} %copy-done.8), custom_call_target="tpu_custom_call" | custom-call | flops 1 | bytes 1 | tf_op jit(solution)/shard_map/pallas_call | solution.py:715
  248.7 5.3 %slice_add_fusion.12 = (f32[4,32,2816]{2,1,0:T(8,128)}, f32[4,32,2816]{2,1,0:T(8,128)}) fusion(f32[8,32,2816]{2,1,0:T(8,128)} %collective-permute-done.24, f32[8,32,2816]{2,1,0:T(8,128)S(1)} %copy-done.29), kind=kLoop, calls=%fused_computation.15 | loop fusion | flops 720896 | bytes 8650752 | tf_op jit(solution)/shard_map/add | solution.py:877
  266.6 5.2 %collective-permute-done.28 = f32[16,64,1024]{2,1,0:T(8,128)} collective-permute-done((f32[16,64,1024]{2,1,0:T(8,128)}, f32[16,64,1024]{2,1,0:T(8,128)}, u32[]{:S(2)}, u32[]{:S(2)}) %collective-permute-start.28) | collective-permute-done | bytes 4194336 | tf_op jit(solution)/shard_map/ppermute | solution.py:803
  271.8 6.9 %slice_add_fusion.6 = (f32[8,64,1024]{2,1,0:T(8,128)}, f32[8,64,1024]{2,1,0:T(8,128)}) fusion(f32[16,64,1024]{2,1,0:T(8,128)} %collective-permute-done.28, f32[16,64,1024]{2,1,0:T(8,128)} %copy-done.12), kind=kLoop, calls=%fused_computation.6 | loop fusion | flops 1048576 | bytes 12582912 | tf_op jit(solution)/shard_map/add | solution.py:877
  278.7 5.5 %collective-permute-done.27 = f32[4,6,4,16,128]{4,3,2,1,0:T(8,128)} collective-permute-done((f32[4,6,4,16,128]{4,3,2,1,0:T(8,128)S(1)}, f32[4,6,4,16,128]{4,3,2,1,0:T(8,128)}, u32[]{:S(2)}, u32[]{:S(2)}) %collective-permute-start.27) | collective-permute-done | bytes 786464 | tf_op jit(solution)/shard_map/ppermute | solution.py:803
  290.1 8.8 %collective-permute-done.30 = f32[4,32,2816]{2,1,0:T(8,128)} collective-permute-done((f32[4,32,2816]{2,1,0:T(8,128)}, f32[4,32,2816]{2,1,0:T(8,128)}, u32[]{:S(2)}, u32[]{:S(2)}) %collective-permute-start.30) | collective-permute-done | bytes 1441824 | tf_op jit(solution)/shard_map/ppermute | solution.py:803
  304.3 9.3 %shard_map.335 = (bf16[768,512]{1,0:T(8,128)(2,1)S(1)}, f32[768,512]{1,0:T(8,128)S(1)}, f32[768,1024]{1,0:T(8,128)S(1)}, f32[768,512]{1,0:T(8,128)S(1)}) custom-call(s32[24]{0:T(128)S(1)} %copy-done.22, bf16[768,512]{1,0:T(8,128)(2,1)S(1)} %copy-done.4, bf16[768,512]{1,0:T(8,128)(2,1)S(1)} %copy-done.7, bf16[768,1024]{1,0:T(8,128)(2,1)S(1)} %copy-done.2, ...), custom_call_target="tpu_custom_call" | custom-call | flops 1 | bytes 1 | tf_op jit(solution)/shard_map/pallas_call | solution.py:518
  313.6 5.9 %collective-permute-done.32 = f32[4,32,2816]{2,1,0:T(8,128)} collective-permute-done((f32[4,32,2816]{2,1,0:T(8,128)}, f32[4,32,2816]{2,1,0:T(8,128)}, u32[]{:S(2)}, u32[]{:S(2)}) %collective-permute-start.32) | collective-permute-done | bytes 1441824 | tf_op jit(solution)/shard_map/ppermute | solution.py:803
  323.2 8.4 %collective-permute-done.33 = f32[2,6,4,16,128]{4,3,2,1,0:T(8,128)S(1)} collective-permute-done((f32[2,6,4,16,128]{4,3,2,1,0:T(8,128)S(1)}, f32[2,6,4,16,128]{4,3,2,1,0:T(8,128)S(1)}, u32[]{:S(2)}, u32[]{:S(2)}) %collective-permute-start.33) | collective-permute-done | bytes 393248 | tf_op jit(solution)/shard_map/ppermute | solution.py:803
  335.0 13.8 %collective-permute-done.34 = f32[8,64,1024]{2,1,0:T(8,128)S(1)} collective-permute-done((f32[8,64,1024]{2,1,0:T(8,128)}, f32[8,64,1024]{2,1,0:T(8,128)S(1)}, u32[]{:S(2)}, u32[]{:S(2)}) %collective-permute-start.34) | collective-permute-done | bytes 2097184 | tf_op jit(solution)/shard_map/ppermute | solution.py:803
  356.4 6.2 %shard_map.336 = (bf16[768,512]{1,0:T(8,128)(2,1)S(1)}, bf16[768,1024]{1,0:T(8,128)(2,1)S(1)}, bf16[768,16]{1,0:T(8,128)(2,1)S(1)}, f32[16,512]{1,0:T(8,128)S(1)}, f32[1,512]{1,0:T(1,128)S(1)}) custom-call(s32[24]{0:T(128)S(1)} %copy-done.22, s32[32]{0:T(128)S(1)} %copy-done.25, bf16[768,512]{1,0:T(8,128)(2,1)S(1)} %copy-done.7, ...), custom_call_target="tpu_custom_call" | custom-call | flops 1 | bytes 1 | tf_op jit(solution)/shard_map/pallas_call | solution.py:588
  362.6 6.2 %shard_map.337 = (f32[16,64,512]{2,1,0:T(8,128)S(1)}, f32[16,64,512]{2,1,0:T(8,128)S(1)}, f32[16,32,1024]{2,1,0:T(8,128)S(1)}, f32[16,32,1024]{2,1,0:T(8,128)S(1)}) custom-call(s32[32]{0:T(128)S(1)} %copy-done.24, s32[32]{0:T(128)S(1)} %copy-done.26, bf16[768,1024]{1,0:T(8,128)(2,1)S(1)} %copy-done.1, ...), custom_call_target="tpu_custom_call" | custom-call | flops 1 | bytes 1 | tf_op jit(solution)/shard_map/pallas_call | solution.py:715
  371.1 15.1 %collective-permute-done.38 = f32[2,32,2816]{2,1,0:T(8,128)S(1)} collective-permute-done((f32[2,32,2816]{2,1,0:T(8,128)S(1)}, f32[2,32,2816]{2,1,0:T(8,128)S(1)}, u32[]{:S(2)}, u32[]{:S(2)}) %collective-permute-start.38) | collective-permute-done | bytes 720928 | tf_op jit(solution)/shard_map/ppermute | solution.py:803
  401.6 8.0 %shard_map.338 = (f32[768,1024]{1,0:T(8,128)}, f32[1,1024]{1,0:T(1,128)S(1)}) custom-call(bf16[768,1024]{1,0:T(8,128)(2,1)S(1)} %bitcast.59, f32[768,1024]{1,0:T(8,128)S(1)} %copy-done.15, bf16[768,512]{1,0:T(8,128)(2,1)S(1)} %get-tuple-element.307.refs_3_.dq_ref, bf16[768,512]{1,0:T(8,128)(2,1)S(1)} %get-tuple-element.326.refs_4_.dk_ref, ...), custom_call_target="tpu_custom_call" | custom-call | flops 1 | bytes 1 | tf_op jit(solution)/shard_map/pallas_call | solution.py:642
  411.1 10.1 %collective-permute-done.43 = f32[8,64,512]{2,1,0:T(8,128)S(1)} collective-permute-done((f32[8,64,512]{2,1,0:T(8,128)S(1)}, f32[8,64,512]{2,1,0:T(8,128)S(1)}, u32[]{:S(2)}, u32[]{:S(2)}) %collective-permute-start.43) | collective-permute-done | bytes 1048608 | tf_op jit(solution)/shard_map/ppermute | solution.py:803
  425.4 6.8 %collective-permute-done.46 = f32[1,32,2816]{2,1,0:T(8,128)S(1)} collective-permute-done((f32[1,32,2816]{2,1,0:T(8,128)S(1)}, f32[1,32,2816]{2,1,0:T(8,128)S(1)}, u32[]{:S(2)}, u32[]{:S(2)}) %collective-permute-start.46) | collective-permute-done | bytes 360480 | tf_op jit(solution)/shard_map/ppermute | solution.py:803
  443.3 6.5 %collective-permute-done.51 = f32[2,64,512]{2,1,0:T(8,128)S(1)} collective-permute-done((f32[2,64,512]{2,1,0:T(8,128)S(1)}, f32[2,64,512]{2,1,0:T(8,128)S(1)}, u32[]{:S(2)}, u32[]{:S(2)}) %collective-permute-start.51) | collective-permute-done | bytes 262176 | tf_op jit(solution)/shard_map/ppermute | solution.py:803
  463.3 11.3 %collective-permute-done.57 = f32[1,64,512]{2,1,0:T(8,128)S(1)} collective-permute-done((f32[1,64,512]{2,1,0:T(8,128)S(1)}, f32[1,64,512]{2,1,0:T(8,128)S(1)}, u32[]{:S(2)}, u32[]{:S(2)}) %collective-permute-start.57) | collective-permute-done | bytes 131104 | tf_op jit(solution)/shard_map/ppermute | solution.py:803
  (363 shorter events, 164.9 us)
Async XLA Ops:
  22.5 20.3 %collective-permute-start.6 = (f32[4,6,2,16,128]{4,3,2,1,0:T(8,128)}, f32[4,6,2,16,128]{4,3,2,1,0:T(8,128)S(1)}, u32[]{:S(2)}, u32[]{:S(2)}) collective-permute-start(f32[4,6,2,16,128]{4,3,2,1,0:T(8,128)} %get-tuple-element.214), channel_id=1, source_target_pairs={{0,2},{1,3},{2,0},{3,1},{4,6},{5,7},{6,4},{7,5},{8,10},{9,11},{10,... | collective-permute-start | bytes 1179656 | tf_op jit(solution)/shard_map/ppermute | solution.py:803
  25.4 16.0 %collective-permute-start.7 = (f32[1,6,2,1,128]{4,2,1,3,0:T(2,128)S(1)}, f32[1,6,2,1,128]{4,2,1,3,0:T(2,128)}, u32[]{:S(2)}, u32[]{:S(2)}) collective-permute-start(f32[1,6,2,1,128]{4,2,1,3,0:T(2,128)S(1)} %get-tuple-element.221), channel_id=1, source_target_pairs={{0,2},{1,3},{2,0},{3,1},{4,6},{5,7},{6,4},{7,5},{8,10},{9,11},{10,... | collective-permute-start | bytes 18440 | tf_op jit(solution)/shard_map/ppermute | solution.py:803
  28.5 17.9 %collective-permute-start.5 = (f32[4,6,2,16,128]{4,3,2,1,0:T(8,128)}, f32[4,6,2,16,128]{4,3,2,1,0:T(8,128)}, u32[]{:S(2)}, u32[]{:S(2)}) collective-permute-start(f32[4,6,2,16,128]{4,3,2,1,0:T(8,128)} %get-tuple-element.218), channel_id=1, source_target_pairs={{0,2},{1,3},{2,0},{3,1},{4,6},{5,7},{6,4},{7,5},{8,10},{9,11},{10,... | collective-permute-start | bytes 1179656 | tf_op jit(solution)/shard_map/ppermute | solution.py:803
  48.2 15.8 %collective-permute-start.9 = (f32[2,6,2,16,128]{4,3,2,1,0:T(8,128)}, f32[2,6,2,16,128]{4,3,2,1,0:T(8,128)}, u32[]{:S(2)}, u32[]{:S(2)}) collective-permute-start(f32[2,6,2,16,128]{4,3,2,1,0:T(8,128)} %get-tuple-element.225), channel_id=1, source_target_pairs={{0,4},{1,5},{2,6},{3,7},{4,0},{5,1},{6,2},{7,3},{8,12},{9,13},{10,... | collective-permute-start | bytes 589832 | tf_op jit(solution)/shard_map/ppermute | solution.py:803
  58.4 17.9 %collective-permute-start.13 = (f32[2,6,2,16,128]{4,3,2,1,0:T(8,128)}, f32[2,6,2,16,128]{4,3,2,1,0:T(8,128)}, u32[]{:S(2)}, u32[]{:S(2)}) collective-permute-start(f32[2,6,2,16,128]{4,3,2,1,0:T(8,128)} %add_select_fusion.26), channel_id=1, source_target_pairs={{0,8},{1,9},{2,10},{3,11},{4,12},{5,13},{6,14},{7,15},{16,24},{17,... | collective-permute-start | bytes 589832 | tf_op jit(solution)/shard_map/ppermute | solution.py:911
  158.4 22.8 %collective-permute-start.21 = (f32[16,32,2816]{2,1,0:T(8,128)}, f32[16,32,2816]{2,1,0:T(8,128)}, u32[]{:S(2)}, u32[]{:S(2)}) collective-permute-start(f32[16,32,2816]{2,1,0:T(8,128)} %get-tuple-element.273), channel_id=1, source_target_pairs={{0,1},{1,0},{2,3},{3,2},{4,5},{5,4},{6,7},{7,6},{8,9},{9,8},{10,11... | collective-permute-start | bytes 17301512 | tf_op jit(solution)/shard_map/ppermute | solution.py:803
  171.8 17.1 %collective-permute-start.22 = (f32[16,88,1024]{2,1,0:T(8,128)}, f32[16,88,1024]{2,1,0:T(8,128)S(1)}, u32[]{:S(2)}, u32[]{:S(2)}) collective-permute-start(f32[16,88,1024]{2,1,0:T(8,128)} %get-tuple-element.269), channel_id=1, source_target_pairs={{0,1},{1,0},{2,3},{3,2},{4,5},{5,4},{6,7},{7,6},{8,9},{9,8},{10,11... | collective-permute-start | bytes 17301512 | tf_op jit(solution)/shard_map/ppermute | solution.py:803
  179.7 69.0 %collective-permute-start.24 = (f32[8,32,2816]{2,1,0:T(8,128)}, f32[8,32,2816]{2,1,0:T(8,128)}, u32[]{:S(2)}, u32[]{:S(2)}) collective-permute-start(f32[8,32,2816]{2,1,0:T(8,128)} %get-tuple-element.271), channel_id=1, source_target_pairs={{0,16},{16,0},{1,17},{17,1},{2,18},{18,2},{3,19},{19,3},{4,20},{20... | collective-permute-start | bytes 8650760 | tf_op jit(solution)/shard_map/ppermute | solution.py:803
  187.4 66.7 %collective-permute-start.25 = (f32[8,32,2816]{2,1,0:T(8,128)}, f32[8,32,2816]{2,1,0:T(8,128)}, u32[]{:S(2)}, u32[]{:S(2)}) collective-permute-start(f32[8,32,2816]{2,1,0:T(8,128)} %get-tuple-element.274), channel_id=1, source_target_pairs={{0,2},{1,3},{2,0},{3,1},{4,6},{5,7},{6,4},{7,5},{8,10},{9,11},{10,... | collective-permute-start | bytes 8650760 | tf_op jit(solution)/shard_map/ppermute | solution.py:803
  192.7 65.2 %collective-permute-start.26 = (f32[8,88,1024]{2,1,0:T(8,128)}, f32[8,88,1024]{2,1,0:T(8,128)}, u32[]{:S(2)}, u32[]{:S(2)}) collective-permute-start(f32[8,88,1024]{2,1,0:T(8,128)} %get-tuple-element.276), channel_id=1, source_target_pairs={{0,4},{1,5},{2,6},{3,7},{4,0},{5,1},{6,2},{7,3},{8,12},{9,13},{10,... | collective-permute-start | bytes 8650760 | tf_op jit(solution)/shard_map/ppermute | solution.py:803
  238.1 23.9 %collective-permute-start.23 = (f32[8,6,4,16,128]{4,3,2,1,0:T(8,128)}, f32[8,6,4,16,128]{4,3,2,1,0:T(8,128)S(1)}, u32[]{:S(2)}, u32[]{:S(2)}) collective-permute-start(f32[8,6,4,16,128]{4,3,2,1,0:T(8,128)} %get-tuple-element.286), channel_id=1, source_target_pairs={{0,1},{1,0},{2,3},{3,2},{4,5},{5,4},{6,7},{7,6},{8,9},{9,8},{10,11... | collective-permute-start | bytes 4718600 | tf_op jit(solution)/shard_map/ppermute | solution.py:803
  264.7 19.6 %collective-permute-start.27 = (f32[4,6,4,16,128]{4,3,2,1,0:T(8,128)S(1)}, f32[4,6,4,16,128]{4,3,2,1,0:T(8,128)}, u32[]{:S(2)}, u32[]{:S(2)}) collective-permute-start(f32[4,6,4,16,128]{4,3,2,1,0:T(8,128)S(1)} %get-tuple-element.295), channel_id=1, source_target_pairs={{0,2},{1,3},{2,0},{3,1},{4,6},{5,7},{6,4},{7,5},{8,10},{9,11},{10,... | collective-permute-start | bytes 2359304 | tf_op jit(solution)/shard_map/ppermute | solution.py:803
  265.2 33.6 %collective-permute-start.30 = (f32[4,32,2816]{2,1,0:T(8,128)}, f32[4,32,2816]{2,1,0:T(8,128)}, u32[]{:S(2)}, u32[]{:S(2)}) collective-permute-start(f32[4,32,2816]{2,1,0:T(8,128)} %get-tuple-element.301), channel_id=1, source_target_pairs={{0,16},{16,0},{1,17},{17,1},{2,18},{18,2},{3,19},{19,3},{4,20},{20... | collective-permute-start | bytes 4325384 | tf_op jit(solution)/shard_map/ppermute | solution.py:803
  286.5 33.0 %collective-permute-start.32 = (f32[4,32,2816]{2,1,0:T(8,128)}, f32[4,32,2816]{2,1,0:T(8,128)}, u32[]{:S(2)}, u32[]{:S(2)}) collective-permute-start(f32[4,32,2816]{2,1,0:T(8,128)} %get-tuple-element.309), channel_id=1, source_target_pairs={{0,2},{1,3},{2,0},{3,1},{4,6},{5,7},{6,4},{7,5},{8,10},{9,11},{10,... | collective-permute-start | bytes 4325384 | tf_op jit(solution)/shard_map/ppermute | solution.py:803
  300.8 21.1 %collective-permute-start.31 = (f32[2,6,4,16,128]{4,3,2,1,0:T(8,128)S(1)}, f32[2,6,4,16,128]{4,3,2,1,0:T(8,128)S(1)}, u32[]{:S(2)}, u32[]{:S(2)}) collective-permute-start(f32[2,6,4,16,128]{4,3,2,1,0:T(8,128)S(1)} %add_select_fusion.14), channel_id=1, source_target_pairs={{8,0},{9,1},{10,2},{11,3},{12,4},{13,5},{14,6},{15,7},{24,16},{25,... | collective-permute-start | bytes 1179656 | tf_op jit(solution)/shard_map/ppermute | solution.py:911
  302.1 46.7 %collective-permute-start.34 = (f32[8,64,1024]{2,1,0:T(8,128)}, f32[8,64,1024]{2,1,0:T(8,128)S(1)}, u32[]{:S(2)}, u32[]{:S(2)}) collective-permute-start(f32[8,64,1024]{2,1,0:T(8,128)} %get-tuple-element.316), channel_id=1, source_target_pairs={{0,16},{16,0},{1,17},{17,1},{2,18},{18,2},{3,19},{19,3},{4,20},{20... | collective-permute-start | bytes 6291464 | tf_op jit(solution)/shard_map/ppermute | solution.py:803
  333.3 17.1 %collective-permute-start.35 = (f32[4,6,4,16,128]{4,3,2,1,0:T(8,128)S(1)}, f32[4,6,4,16,128]{4,3,2,1,0:T(8,128)S(1)}, u32[]{:S(2)}, u32[]{:S(2)}) collective-permute-start(f32[4,6,4,16,128]{4,3,2,1,0:T(8,128)S(1)} %get-tuple-element.314), channel_id=1, source_target_pairs={{0,2},{1,3},{2,0},{3,1},{4,6},{5,7},{6,4},{7,5},{8,10},{9,11},{10,... | collective-permute-start | bytes 2359304 | tf_op jit(solution)/shard_map/ppermute | solution.py:803
  352.0 19.1 %collective-permute-start.37 = (f32[2,32,2816]{2,1,0:T(8,128)S(1)}, f32[2,32,2816]{2,1,0:T(8,128)S(1)}, u32[]{:S(2)}, u32[]{:S(2)}) collective-permute-start(f32[2,32,2816]{2,1,0:T(8,128)S(1)} %get-tuple-element.335), channel_id=1, source_target_pairs={{0,4},{1,5},{2,6},{3,7},{4,0},{5,1},{6,2},{7,3},{8,12},{9,13},{10,... | collective-permute-start | bytes 2162696 | tf_op jit(solution)/shard_map/ppermute | solution.py:803
  354.1 33.7 %collective-permute-start.39 = (f32[4,88,1024]{2,1,0:T(8,128)S(1)}, f32[4,88,1024]{2,1,0:T(8,128)S(1)}, u32[]{:S(2)}, u32[]{:S(2)}) collective-permute-start(f32[4,88,1024]{2,1,0:T(8,128)S(1)} %copy-done.43), channel_id=1, source_target_pairs={{0,16},{16,0},{1,17},{17,1},{2,18},{18,2},{3,19},{19,3},{4,20},{20... | collective-permute-start | bytes 4325384 | tf_op jit(solution)/shard_map/ppermute | solution.py:803
  354.4 31.9 %collective-permute-start.38 = (f32[2,32,2816]{2,1,0:T(8,128)S(1)}, f32[2,32,2816]{2,1,0:T(8,128)S(1)}, u32[]{:S(2)}, u32[]{:S(2)}) collective-permute-start(f32[2,32,2816]{2,1,0:T(8,128)S(1)} %get-tuple-element.337), channel_id=1, source_target_pairs={{0,4},{1,5},{2,6},{3,7},{4,0},{5,1},{6,2},{7,3},{8,12},{9,13},{10,... | collective-permute-start | bytes 2162696 | tf_op jit(solution)/shard_map/ppermute | solution.py:803
  354.9 33.2 %collective-permute-start.40 = (f32[4,64,1024]{2,1,0:T(8,128)S(1)}, f32[4,64,1024]{2,1,0:T(8,128)S(1)}, u32[]{:S(2)}, u32[]{:S(2)}) collective-permute-start(f32[4,64,1024]{2,1,0:T(8,128)S(1)} %get-tuple-element.341), channel_id=1, source_target_pairs={{0,2},{1,3},{2,0},{3,1},{4,6},{5,7},{6,4},{7,5},{8,10},{9,11},{10,... | collective-permute-start | bytes 3145736 | tf_op jit(solution)/shard_map/ppermute | solution.py:803
  396.0 25.3 %collective-permute-start.43 = (f32[8,64,512]{2,1,0:T(8,128)S(1)}, f32[8,64,512]{2,1,0:T(8,128)S(1)}, u32[]{:S(2)}, u32[]{:S(2)}) collective-permute-start(f32[8,64,512]{2,1,0:T(8,128)S(1)} %get-tuple-element.346), channel_id=1, source_target_pairs={{0,16},{16,0},{1,17},{17,1},{2,18},{18,2},{3,19},{19,3},{4,20},{20... | collective-permute-start | bytes 3145736 | tf_op jit(solution)/shard_map/ppermute | solution.py:803
  396.3 25.1 %collective-permute-start.44 = (f32[8,32,1024]{2,1,0:T(8,128)S(1)}, f32[8,32,1024]{2,1,0:T(8,128)S(1)}, u32[]{:S(2)}, u32[]{:S(2)}) collective-permute-start(f32[8,32,1024]{2,1,0:T(8,128)S(1)} %get-tuple-element.359), channel_id=1, source_target_pairs={{0,2},{1,3},{2,0},{3,1},{4,6},{5,7},{6,4},{7,5},{8,10},{9,11},{10,... | collective-permute-start | bytes 3145736 | tf_op jit(solution)/shard_map/ppermute | solution.py:803
  397.8 26.8 %collective-permute-start.45 = (f32[1,32,2816]{2,1,0:T(8,128)S(1)}, f32[1,32,2816]{2,1,0:T(8,128)S(1)}, u32[]{:S(2)}, u32[]{:S(2)}) collective-permute-start(f32[1,32,2816]{2,1,0:T(8,128)S(1)} %get-tuple-element.362), channel_id=1, source_target_pairs={{0,8},{1,9},{2,10},{3,11},{4,12},{5,13},{6,14},{7,15},{8,0},{9,1},... | collective-permute-start | bytes 1081352 | tf_op jit(solution)/shard_map/ppermute | solution.py:803
  401.1 31.2 %collective-permute-start.46 = (f32[1,32,2816]{2,1,0:T(8,128)S(1)}, f32[1,32,2816]{2,1,0:T(8,128)S(1)}, u32[]{:S(2)}, u32[]{:S(2)}) collective-permute-start(f32[1,32,2816]{2,1,0:T(8,128)S(1)} %get-tuple-element.364), channel_id=1, source_target_pairs={{0,8},{1,9},{2,10},{3,11},{4,12},{5,13},{6,14},{7,15},{8,0},{9,1},... | collective-permute-start | bytes 1081352 | tf_op jit(solution)/shard_map/ppermute | solution.py:803
  401.1 31.9 %collective-permute-start.47 = (f32[2,64,1024]{2,1,0:T(8,128)S(1)}, f32[2,64,1024]{2,1,0:T(8,128)S(1)}, u32[]{:S(2)}, u32[]{:S(2)}) collective-permute-start(f32[2,64,1024]{2,1,0:T(8,128)S(1)} %get-tuple-element.367), channel_id=1, source_target_pairs={{0,4},{1,5},{2,6},{3,7},{4,0},{5,1},{6,2},{7,3},{8,12},{9,13},{10,... | collective-permute-start | bytes 1572872 | tf_op jit(solution)/shard_map/ppermute | solution.py:803
  436.5 23.1 %collective-permute-start.55 = (f32[1,64,1024]{2,1,0:T(8,128)S(1)}, f32[1,64,1024]{2,1,0:T(8,128)S(1)}, u32[]{:S(2)}, u32[]{:S(2)}) collective-permute-start(f32[1,64,1024]{2,1,0:T(8,128)S(1)} %get-tuple-element.368), channel_id=1, source_target_pairs={{0,8},{1,9},{2,10},{3,11},{4,12},{5,13},{6,14},{7,15},{8,0},{9,1},... | collective-permute-start | bytes 786440 | tf_op jit(solution)/shard_map/ppermute | solution.py:803
  439.8 16.1 %collective-permute-start.53 = (f32[2,88,1024]{2,1,0:T(8,128)S(1)}, f32[2,88,1024]{2,1,0:T(8,128)S(1)}, u32[]{:S(2)}, u32[]{:S(2)}) collective-permute-start(f32[2,88,1024]{2,1,0:T(8,128)S(1)} %get-tuple-element.380), channel_id=1, source_target_pairs={{0,2},{1,3},{2,0},{3,1},{4,6},{5,7},{6,4},{7,5},{8,10},{9,11},{10,... | collective-permute-start | bytes 2162696 | tf_op jit(solution)/shard_map/ppermute | solution.py:803
  456.7 17.9 %collective-permute-start.57 = (f32[1,64,512]{2,1,0:T(8,128)S(1)}, f32[1,64,512]{2,1,0:T(8,128)S(1)}, u32[]{:S(2)}, u32[]{:S(2)}) collective-permute-start(f32[1,64,512]{2,1,0:T(8,128)S(1)} %get-tuple-element.378), channel_id=1, source_target_pairs={{0,8},{1,9},{2,10},{3,11},{4,12},{5,13},{6,14},{7,15},{8,0},{9,1},... | collective-permute-start | bytes 393224 | tf_op jit(solution)/shard_map/ppermute | solution.py:803
  457.9 19.5 %collective-permute-start.58 = (f32[1,32,1024]{2,1,0:T(8,128)S(1)}, f32[1,32,1024]{2,1,0:T(8,128)S(1)}, u32[]{:S(2)}, u32[]{:S(2)}) collective-permute-start(f32[1,32,1024]{2,1,0:T(8,128)S(1)} %get-tuple-element.389), channel_id=1, source_target_pairs={{0,8},{1,9},{2,10},{3,11},{4,12},{5,13},{6,14},{7,15},{8,0},{9,1},... | collective-permute-start | bytes 393224 | tf_op jit(solution)/shard_map/ppermute | solution.py:803
  460.9 17.2 %collective-permute-start.59 = (f32[2,56,128]{2,1,0:T(8,128)S(1)}, f32[2,56,128]{2,1,0:T(8,128)S(1)}, u32[]{:S(2)}, u32[]{:S(2)}) collective-permute-start(f32[2,56,128]{2,1,0:T(8,128)S(1)} %get-tuple-element.386), channel_id=1, source_target_pairs={{0,4},{1,5},{2,6},{3,7},{4,0},{5,1},{6,2},{7,3},{8,12},{9,13},{10,... | collective-permute-start | bytes 172040 | tf_op jit(solution)/shard_map/ppermute | solution.py:803
  463.3 20.4 %collective-permute-start.60 = (f32[1,88,1024]{2,1,0:T(8,128)S(1)}, f32[1,88,1024]{2,1,0:T(8,128)S(1)}, u32[]{:S(2)}, u32[]{:S(2)}) collective-permute-start(f32[1,88,1024]{2,1,0:T(8,128)S(1)} %get-tuple-element.381), channel_id=1, source_target_pairs={{0,8},{1,9},{2,10},{3,11},{4,12},{5,13},{6,14},{7,15},{8,0},{9,1},... | collective-permute-start | bytes 1081352 | tf_op jit(solution)/shard_map/ppermute | solution.py:803
  (106 other events, 1136.4 us)

commit v6 on v5

--- a/solution.py
+++ b/solution.py
@@ -182,6 +182,7 @@
         (tokens // tm,),
         [tile(width), whole(wq.shape), whole(wog.shape)],
         (tile(wq.shape[1]), tile(wog.shape[1])),
+        room=28,
     )(normed, wq, wog)
 
 
@@ -213,6 +214,7 @@
         [tile(kw), tile(kw), tile(vw), tile(kw)],
         tile(vw),
         prefetch=1,
+        room=28,
     )(docs, q, k, v, cum)
 
 

time: 494 us -> 493 us (level)
  starting transfers between devices: 64.1 us -> 73.2 us
  Pallas kernels: 186 us -> 179 us
  other arithmetic: 72.2 us -> 66.6 us
    ppermute x59, starting transfers between devices: 55 us -> 65.4 us  [swap(): return lax.ppermute(value, name, [(i, i ^ flip) for i in range(n)])]
    unnamed x160 -> x184, local copies, waits for them, and re-layouts: 8.92 us -> 11.3 us
  transfers between devices with their start and end apart: 62 -> 62, of which waited for: 30 -> 31; matrix products, arithmetic and copies ran while one was open for 15% -> 13% of each run, Pallas kernels for 25% -> 24%
where the time goes in v6:
time: 493 us; the launch traced here: 487 us
  Pallas kernels  179 us (36%)
  waiting for transfers between devices  146 us (30%)
  starting transfers between devices  73.2 us (15%)
  other arithmetic  66.6 us (14%)
  local copies, waits for them, and re-layouts  20 us (4%)
    ppermute x59, waiting for transfers between devices, swap(): return lax.ppermute(value, name, [(i, i ^ flip) for i in range(n)])  143 us
    ppermute x59, starting transfers between devices, swap(): return lax.ppermute(value, name, [(i, i ^ flip) for i in range(n)])  65.4 us
    pallas_call x4, Pallas kernels, weight_grads(): call(functools.partial(weight_body, index, len(lefts), pieces), tuple(sha...  44.7 us
    pallas_call x1, Pallas kernels, ff_back_all(): call(functools.partial(ff_back_body, steps), (shape((tokens, width), BF),...  32.5 us
    add x9, other arithmetic, reduce_steps(): send = keep[half:] + got[half:]  23.9 us
    pallas_call x1, Pallas kernels, ff_all(): call(ff_body, (shape((tokens, ff), BF), shape((tokens, ff), BF), shape((t...  23.5 us
    add x19, other arithmetic, reduce_steps(): keep = keep[:half] + got[:half]  19.9 us
    pallas_call x1, Pallas kernels, hidden_back_all(): call(hidden_back_body, shape((tokens, ff), F32), (ff // tile,), [whole((t...  12.9 us
  transfers between devices with their start and end apart: 62, of which 31 were waited for; matrix products, arithmetic and copies ran while one was open for 13% of the time, Pallas kernels for 24%

profile of v6, /device:TPU:0, one launch (start us, length us, event | category | flops | bytes accessed | tf_op | source)
XLA Modules:
  0.0 486.9 jit_solution(15351467699368013488)
XLA Ops:
  3.5 12.2 %shard_map.324 = (bf16[768,1024]{1,0:T(8,128)(2,1)}, bf16[768,512]{1,0:T(8,128)(2,1)}, bf16[768,1024]{1,0:T(8,128)(2,1)}, bf16[768,16]{1,0:T(8,128)(2,1)}, f32[7...) custom-call(s32[24]{0:T(128)} %reshape.88.docs_ref, ...), custom_call_target="tpu_custom_call" | custom-call | flops 1 | bytes 1 | tf_op jit(solution)/shard_map/pallas_call | solution.py:140
  28.6 12.9 %shard_map.325.dh_ref = f32[768,2816]{1,0:T(8,128)} custom-call(bf16[768,1024]{1,0:T(8,128)(2,1)} %bitcast.64, bf16[2816,1024]{1,0:T(8,128)(2,1)} %wd_ref.3), custom_call_target="tpu_custom_call" | custom-call | flops 1 | bytes 1 | tf_op jit(solution)/shard_map/pallas_call | solution.py:283
  67.2 5.3 %collective-permute-start.14 = (f32[2,6,2,16,128]{4,3,2,1,0:T(8,128)S(1)}, f32[2,6,2,16,128]{4,3,2,1,0:T(8,128)S(1)}, u32[]{:S(2)}, u32[]{:S(2)}) collective-permute-start(f32[2,6,2,16,128]{4,3,2,1,0:T(8,128)S(1)} %get-tuple-element.237), channel_id=1, source_target_pairs={{0,4},{1,5},{2,6},{3,7},{4,0},{5,1},{6,2},{7,3},{8,12},{9,13},{10,... | collective-permute-start | bytes 589832 | tf_op jit(solution)/shard_map/ppermute | solution.py:805
  84.1 6.3 %collective-permute-done.16 = f32[4,6,2,16,128]{4,3,2,1,0:T(8,128)S(1)} collective-permute-done((f32[4,6,2,16,128]{4,3,2,1,0:T(8,128)S(1)}, f32[4,6,2,16,128]{4,3,2,1,0:T(8,128)S(1)}, u32[]{:S(2)}, u32[]{:S(2)}) %collective-permute-start.16) | collective-permute-done | bytes 393248 | tf_op jit(solution)/shard_map/ppermute | solution.py:805
  91.7 5.4 %collective-permute-done.17 = f32[4,6,2,16,128]{4,3,2,1,0:T(8,128)S(1)} collective-permute-done((f32[4,6,2,16,128]{4,3,2,1,0:T(8,128)S(1)}, f32[4,6,2,16,128]{4,3,2,1,0:T(8,128)S(1)}, u32[]{:S(2)}, u32[]{:S(2)}) %collective-permute-start.17) | collective-permute-done | bytes 393248 | tf_op jit(solution)/shard_map/ppermute | solution.py:805
  103.1 9.3 %shard_map.328 = (f32[768,1024]{1,0:T(8,128)}, bf16[768,1024]{1,0:T(8,128)(2,1)}, bf16[6,4,256,128]{3,2,1,0:T(8,128)(2,1)}) custom-call(s32[24]{0:T(128)} %reshape.88.docs_ref, s32[32]{0:T(128)} %pad_add_fusion.table_ref, bf16[768,512]{1,0:T(8,128)(2,1)} %copy-done.8, f32[768,512]{1,0:T(8,128)} %get-tuple-element.235.cum_ref, f32[768,1024]{1,0:T(8,128)} %copy-done.7, ...), custom_call_target="tpu_custom_call" | custom-call | flops 1 | bytes 1 | tf_op jit(solution)/shard_map/pallas_call | solution.py:260
  112.4 23.5 %shard_map.329 = (bf16[768,2816]{1,0:T(8,128)(2,1)}, bf16[768,2816]{1,0:T(8,128)(2,1)}, bf16[768,2816]{1,0:T(8,128)(2,1)}, bf16[768,1024]{1,0:T(8,128)(2,1)}, f32[768,1024]{1,0:T(8,128)}) custom-call(bf16[768,1024]{1,0:T(8,128)(2,1)} %bitcast.58, bf16[768,1024]{1,0:T(8,128)(2,1)} %get-tuple-element.254.gated_ref.refs_1_, bf16[1024,1024]{1,0:T(8,128)(2,1)} %wo_ref.3, ...), custom_call_target="tpu_custom_call" | custom-call | flops 1 | bytes 1 | tf_op jit(solution)/shard_map/pallas_call | solution.py:320
  135.9 18.4 %shard_map.330 = (f32[16,32,2816]{2,1,0:T(8,128)}, f32[16,32,2816]{2,1,0:T(8,128)}, f32[16,32,2816]{2,1,0:T(8,128)}, f32[16,32,2816]{2,1,0:T(8,128)}) custom-call(s32[32]{0:T(128)} %get-tuple-element.350.refs_0_.table_ref, s32[32]{0:T(128)} %get-tuple-element.528.refs_1_, bf16[768,1024]{1,0:T(8,128)(2,1)} %get-tuple-element.259.refs_2_, ...), custom_call_target="tpu_custom_call" | custom-call | flops 1 | bytes 1 | tf_op jit(solution)/shard_map/pallas_call | solution.py:717
  155.3 12.5 %shard_map.331 = (f32[16,88,1024]{2,1,0:T(8,128)}, f32[16,88,1024]{2,1,0:T(8,128)}) custom-call(s32[32]{0:T(128)} %broadcast_xor_fusion.2.refs_0_, bf16[768,2816]{1,0:T(8,128)(2,1)} %get-tuple-element.255.refs_1_.hidden_ref, bf16[768,1024]{1,0:T(8,128)(2,1)} %bitcast.65), custom_call_target="tpu_custom_call" | custom-call | flops 1 | bytes 1 | tf_op jit(solution)/shard_map/pallas_call | solution.py:717
  167.9 7.7 %slice_add_fusion.4 = (f32[8,32,2816]{2,1,0:T(8,128)}, f32[8,32,2816]{2,1,0:T(8,128)}) fusion(f32[16,32,2816]{2,1,0:T(8,128)} %collective-permute-done.20, f32[16,32,2816]{2,1,0:T(8,128)} %get-tuple-element.270), kind=kLoop, calls=%fused_computation.4 | loop fusion | flops 1441792 | bytes 17301504 | tf_op jit(solution)/shard_map/add | solution.py:880
  177.2 6.1 %slice_add_fusion.2 = (f32[8,32,2816]{2,1,0:T(8,128)}, f32[8,32,2816]{2,1,0:T(8,128)}) fusion(f32[16,32,2816]{2,1,0:T(8,128)} %collective-permute-done.21, f32[16,32,2816]{2,1,0:T(8,128)S(1)} %bitcast.68), kind=kLoop, calls=%fused_computation.2 | loop fusion | flops 1441792 | bytes 17301504 | tf_op jit(solution)/shard_map/add | solution.py:880
  190.1 32.5 %shard_map.332 = (bf16[768,1024]{1,0:T(8,128)(2,1)}, f32[768,1024]{1,0:T(8,128)}, bf16[768,1024]{1,0:T(8,128)(2,1)}, f32[768,1024]{1,0:T(8,128)}, f32[1,1024]{1,0:T(1,128)}) custom-call(bf16[768,2816]{1,0:T(8,128)(2,1)} %get-tuple-element.255.refs_1_.hidden_ref, bf16[768,2816]{1,0:T(8,128)(2,1)} %get-tuple-element.256.refs_3_.dg_ref, ...), custom_call_target="tpu_custom_call" | custom-call | flops 1 | bytes 1 | tf_op jit(solution)/shard_map/pallas_call | solution.py:391
  222.6 10.8 %shard_map.333 = (bf16[768,1024]{1,0:T(8,128)(2,1)}, bf16[768,1024]{1,0:T(8,128)(2,1)}, f32[8,6,4,16,128]{4,3,2,1,0:T(8,128)}, f32[8,6,4,16,128]{4,3,2,1,0:T(8,128)}, f32[1,256]{1,0:T(1,128)}) custom-call(s32[24]{0:T(128)} %reshape.88.docs_ref, s32[32]{0:T(128)} %pad_add_fusion.table_ref, f32[768,1024]{1,0:T(8,128)} %get-tuple-element.282.dgated_ref, ...), custom_call_target="tpu_custom_call" | custom-call | flops 1 | bytes 1 | tf_op jit(solution)/shard_map/pallas_call | solution.py:466
  236.3 7.6 %shard_map.334 = (f32[16,64,1024]{2,1,0:T(8,128)S(1)}, f32[16,64,1024]{2,1,0:T(8,128)}) custom-call(s32[32]{0:T(128)S(1)} %copy-done.33, bf16[768,1024]{1,0:T(8,128)(2,1)S(1)} %copy-done.18, bf16[768,1024]{1,0:T(8,128)(2,1)S(1)} %copy-done.2, bf16[768,1024]{1,0:T(8,128)(2,1)S(1)} %copy-done.25, bf16[768,1024]{1,0:T(8,128)(2,1)S(1)} %copy-done.15), custom_call_target="tpu_custom_call" | custom-call | flops 1 | bytes 1 | tf_op jit(solution)/shard_map/pallas_call | solution.py:717
  261.6 5.4 %collective-permute-done.28 = f32[16,64,1024]{2,1,0:T(8,128)} collective-permute-done((f32[16,64,1024]{2,1,0:T(8,128)}, f32[16,64,1024]{2,1,0:T(8,128)}, u32[]{:S(2)}, u32[]{:S(2)}) %collective-permute-start.28) | collective-permute-done | bytes 4194336 | tf_op jit(solution)/shard_map/ppermute | solution.py:805
  267.1 6.9 %slice_add_fusion.6 = (f32[8,64,1024]{2,1,0:T(8,128)}, f32[8,64,1024]{2,1,0:T(8,128)}) fusion(f32[16,64,1024]{2,1,0:T(8,128)} %collective-permute-done.28, f32[16,64,1024]{2,1,0:T(8,128)} %copy-done.19), kind=kLoop, calls=%fused_computation.6 | loop fusion | flops 1048576 | bytes 12582912 | tf_op jit(solution)/shard_map/add | solution.py:879
  274.0 5.7 %collective-permute-done.27 = f32[4,6,4,16,128]{4,3,2,1,0:T(8,128)} collective-permute-done((f32[4,6,4,16,128]{4,3,2,1,0:T(8,128)S(1)}, f32[4,6,4,16,128]{4,3,2,1,0:T(8,128)}, u32[]{:S(2)}, u32[]{:S(2)}) %collective-permute-start.27) | collective-permute-done | bytes 786464 | tf_op jit(solution)/shard_map/ppermute | solution.py:805
  285.5 8.8 %collective-permute-done.30 = f32[4,32,2816]{2,1,0:T(8,128)} collective-permute-done((f32[4,32,2816]{2,1,0:T(8,128)}, f32[4,32,2816]{2,1,0:T(8,128)}, u32[]{:S(2)}, u32[]{:S(2)}) %collective-permute-start.30) | collective-permute-done | bytes 1441824 | tf_op jit(solution)/shard_map/ppermute | solution.py:805
  299.4 9.3 %shard_map.335 = (bf16[768,512]{1,0:T(8,128)(2,1)S(1)}, f32[768,512]{1,0:T(8,128)S(1)}, f32[768,1024]{1,0:T(8,128)S(1)}, f32[768,512]{1,0:T(8,128)S(1)}) custom-call(s32[24]{0:T(128)S(1)} %copy-done.31, bf16[768,512]{1,0:T(8,128)(2,1)S(1)} %copy-done.9, bf16[768,512]{1,0:T(8,128)(2,1)S(1)} %copy-done.14, bf16[768,1024]{1,0:T(8,128)(2,1)S(1)} %copy-done.4, ...), custom_call_target="tpu_custom_call" | custom-call | flops 1 | bytes 1 | tf_op jit(solution)/shard_map/pallas_call | solution.py:520
  308.7 6.7 %collective-permute-done.32 = f32[4,32,2816]{2,1,0:T(8,128)} collective-permute-done((f32[4,32,2816]{2,1,0:T(8,128)}, f32[4,32,2816]{2,1,0:T(8,128)}, u32[]{:S(2)}, u32[]{:S(2)}) %collective-permute-start.32) | collective-permute-done | bytes 1441824 | tf_op jit(solution)/shard_map/ppermute | solution.py:805
  320.1 9.3 %collective-permute-done.33 = f32[2,6,4,16,128]{4,3,2,1,0:T(8,128)S(1)} collective-permute-done((f32[2,6,4,16,128]{4,3,2,1,0:T(8,128)S(1)}, f32[2,6,4,16,128]{4,3,2,1,0:T(8,128)S(1)}, u32[]{:S(2)}, u32[]{:S(2)}) %collective-permute-start.33) | collective-permute-done | bytes 393248 | tf_op jit(solution)/shard_map/ppermute | solution.py:805
  332.8 12.0 %collective-permute-done.34 = f32[8,64,1024]{2,1,0:T(8,128)S(1)} collective-permute-done((f32[8,64,1024]{2,1,0:T(8,128)}, f32[8,64,1024]{2,1,0:T(8,128)S(1)}, u32[]{:S(2)}, u32[]{:S(2)}) %collective-permute-start.34) | collective-permute-done | bytes 2097184 | tf_op jit(solution)/shard_map/ppermute | solution.py:805
  353.1 6.2 %shard_map.336 = (bf16[768,512]{1,0:T(8,128)(2,1)S(1)}, bf16[768,1024]{1,0:T(8,128)(2,1)S(1)}, bf16[768,16]{1,0:T(8,128)(2,1)S(1)}, f32[16,512]{1,0:T(8,128)S(1)}, f32[1,512]{1,0:T(1,128)S(1)}) custom-call(s32[24]{0:T(128)S(1)} %copy-done.31, s32[32]{0:T(128)S(1)} %copy-done.34, bf16[768,512]{1,0:T(8,128)(2,1)S(1)} %copy-done.14, ...), custom_call_target="tpu_custom_call" | custom-call | flops 1 | bytes 1 | tf_op jit(solution)/shard_map/pallas_call | solution.py:590
  359.3 6.2 %shard_map.337 = (f32[16,64,512]{2,1,0:T(8,128)S(1)}, f32[16,64,512]{2,1,0:T(8,128)S(1)}, f32[16,32,1024]{2,1,0:T(8,128)S(1)}, f32[16,32,1024]{2,1,0:T(8,128)S(1)}) custom-call(s32[32]{0:T(128)S(1)} %copy-done.33, s32[32]{0:T(128)S(1)} %copy-done.35, bf16[768,1024]{1,0:T(8,128)(2,1)S(1)} %copy-done.2, ...), custom_call_target="tpu_custom_call" | custom-call | flops 1 | bytes 1 | tf_op jit(solution)/shard_map/pallas_call | solution.py:717
  368.1 14.9 %collective-permute-done.38 = f32[2,32,2816]{2,1,0:T(8,128)S(1)} collective-permute-done((f32[2,32,2816]{2,1,0:T(8,128)S(1)}, f32[2,32,2816]{2,1,0:T(8,128)S(1)}, u32[]{:S(2)}, u32[]{:S(2)}) %collective-permute-start.38) | collective-permute-done | bytes 720928 | tf_op jit(solution)/shard_map/ppermute | solution.py:805
  393.6 5.6 %collective-permute-start.45 = (f32[1,32,2816]{2,1,0:T(8,128)S(1)}, f32[1,32,2816]{2,1,0:T(8,128)S(1)}, u32[]{:S(2)}, u32[]{:S(2)}) collective-permute-start(f32[1,32,2816]{2,1,0:T(8,128)S(1)} %get-tuple-element.362), channel_id=1, source_target_pairs={{0,8},{1,9},{2,10},{3,11},{4,12},{5,13},{6,14},{7,15},{8,0},{9,1},... | collective-permute-start | bytes 1081352 | tf_op jit(solution)/shard_map/ppermute | solution.py:805
  399.7 8.0 %shard_map.338 = (f32[768,1024]{1,0:T(8,128)}, f32[1,1024]{1,0:T(1,128)S(1)}) custom-call(bf16[768,1024]{1,0:T(8,128)(2,1)S(1)} %bitcast.59, f32[768,1024]{1,0:T(8,128)S(1)} %copy-done.23, bf16[768,512]{1,0:T(8,128)(2,1)S(1)} %get-tuple-element.307.refs_3_.dq_ref, bf16[768,512]{1,0:T(8,128)(2,1)S(1)} %get-tuple-element.326.refs_4_.dk_ref, ...), custom_call_target="tpu_custom_call" | custom-call | flops 1 | bytes 1 | tf_op jit(solution)/shard_map/pallas_call | solution.py:644
  409.1 7.6 %collective-permute-done.43 = f32[8,64,512]{2,1,0:T(8,128)S(1)} collective-permute-done((f32[8,64,512]{2,1,0:T(8,128)S(1)}, f32[8,64,512]{2,1,0:T(8,128)S(1)}, u32[]{:S(2)}, u32[]{:S(2)}) %collective-permute-start.43) | collective-permute-done | bytes 1048608 | tf_op jit(solution)/shard_map/ppermute | solution.py:805
  423.5 6.8 %collective-permute-done.46 = f32[1,32,2816]{2,1,0:T(8,128)S(1)} collective-permute-done((f32[1,32,2816]{2,1,0:T(8,128)S(1)}, f32[1,32,2816]{2,1,0:T(8,128)S(1)}, u32[]{:S(2)}, u32[]{:S(2)}) %collective-permute-start.46) | collective-permute-done | bytes 360480 | tf_op jit(solution)/shard_map/ppermute | solution.py:805
  441.4 5.3 %collective-permute-done.51 = f32[2,64,512]{2,1,0:T(8,128)S(1)} collective-permute-done((f32[2,64,512]{2,1,0:T(8,128)S(1)}, f32[2,64,512]{2,1,0:T(8,128)S(1)}, u32[]{:S(2)}, u32[]{:S(2)}) %collective-permute-start.51) | collective-permute-done | bytes 262176 | tf_op jit(solution)/shard_map/ppermute | solution.py:805
  461.3 10.8 %collective-permute-done.57 = f32[1,64,512]{2,1,0:T(8,128)S(1)} collective-permute-done((f32[1,64,512]{2,1,0:T(8,128)S(1)}, f32[1,64,512]{2,1,0:T(8,128)S(1)}, u32[]{:S(2)}, u32[]{:S(2)}) %collective-permute-start.57) | collective-permute-done | bytes 131104 | tf_op jit(solution)/shard_map/ppermute | solution.py:805
  476.4 6.1 %collective-permute-done.60 = f32[1,88,1024]{2,1,0:T(8,128)S(1)} collective-permute-done((f32[1,88,1024]{2,1,0:T(8,128)S(1)}, f32[1,88,1024]{2,1,0:T(8,128)S(1)}, u32[]{:S(2)}, u32[]{:S(2)}) %collective-permute-start.60) | collective-permute-done | bytes 360480 | tf_op jit(solution)/shard_map/ppermute | solution.py:805
  (387 shorter events, 172.4 us)
Async XLA Ops:
  22.6 20.7 %collective-permute-start.6 = (f32[4,6,2,16,128]{4,3,2,1,0:T(8,128)}, f32[4,6,2,16,128]{4,3,2,1,0:T(8,128)S(1)}, u32[]{:S(2)}, u32[]{:S(2)}) collective-permute-start(f32[4,6,2,16,128]{4,3,2,1,0:T(8,128)} %get-tuple-element.214), channel_id=1, source_target_pairs={{0,2},{1,3},{2,0},{3,1},{4,6},{5,7},{6,4},{7,5},{8,10},{9,11},{10,... | collective-permute-start | bytes 1179656 | tf_op jit(solution)/shard_map/ppermute | solution.py:805
  25.5 16.0 %collective-permute-start.7 = (f32[1,6,2,1,128]{4,2,1,3,0:T(2,128)S(1)}, f32[1,6,2,1,128]{4,2,1,3,0:T(2,128)}, u32[]{:S(2)}, u32[]{:S(2)}) collective-permute-start(f32[1,6,2,1,128]{4,2,1,3,0:T(2,128)S(1)} %get-tuple-element.221), channel_id=1, source_target_pairs={{0,2},{1,3},{2,0},{3,1},{4,6},{5,7},{6,4},{7,5},{8,10},{9,11},{10,... | collective-permute-start | bytes 18440 | tf_op jit(solution)/shard_map/ppermute | solution.py:805
  26.6 15.8 %collective-permute-start.4 = (f32[1,6,2,1,128]{4,2,1,3,0:T(2,128)S(1)}, f32[1,6,2,1,128]{4,2,1,3,0:T(2,128)}, u32[]{:S(2)}, u32[]{:S(2)}) collective-permute-start(f32[1,6,2,1,128]{4,2,1,3,0:T(2,128)S(1)} %get-tuple-element.217), channel_id=1, source_target_pairs={{0,2},{1,3},{2,0},{3,1},{4,6},{5,7},{6,4},{7,5},{8,10},{9,11},{10,... | collective-permute-start | bytes 18440 | tf_op jit(solution)/shard_map/ppermute | solution.py:805
  28.6 17.8 %collective-permute-start.5 = (f32[4,6,2,16,128]{4,3,2,1,0:T(8,128)}, f32[4,6,2,16,128]{4,3,2,1,0:T(8,128)S(1)}, u32[]{:S(2)}, u32[]{:S(2)}) collective-permute-start(f32[4,6,2,16,128]{4,3,2,1,0:T(8,128)} %get-tuple-element.218), channel_id=1, source_target_pairs={{0,2},{1,3},{2,0},{3,1},{4,6},{5,7},{6,4},{7,5},{8,10},{9,11},{10,... | collective-permute-start | bytes 1179656 | tf_op jit(solution)/shard_map/ppermute | solution.py:805
  154.4 22.8 %collective-permute-start.21 = (f32[16,32,2816]{2,1,0:T(8,128)}, f32[16,32,2816]{2,1,0:T(8,128)}, u32[]{:S(2)}, u32[]{:S(2)}) collective-permute-start(f32[16,32,2816]{2,1,0:T(8,128)} %get-tuple-element.273), channel_id=1, source_target_pairs={{0,1},{1,0},{2,3},{3,2},{4,5},{5,4},{6,7},{7,6},{8,9},{9,8},{10,11... | collective-permute-start | bytes 17301512 | tf_op jit(solution)/shard_map/ppermute | solution.py:805
  167.8 17.0 %collective-permute-start.22 = (f32[16,88,1024]{2,1,0:T(8,128)}, f32[16,88,1024]{2,1,0:T(8,128)S(1)}, u32[]{:S(2)}, u32[]{:S(2)}) collective-permute-start(f32[16,88,1024]{2,1,0:T(8,128)} %get-tuple-element.269), channel_id=1, source_target_pairs={{0,1},{1,0},{2,3},{3,2},{4,5},{5,4},{6,7},{7,6},{8,9},{9,8},{10,11... | collective-permute-start | bytes 17301512 | tf_op jit(solution)/shard_map/ppermute | solution.py:805
  175.6 68.3 %collective-permute-start.24 = (f32[8,32,2816]{2,1,0:T(8,128)}, f32[8,32,2816]{2,1,0:T(8,128)}, u32[]{:S(2)}, u32[]{:S(2)}) collective-permute-start(f32[8,32,2816]{2,1,0:T(8,128)} %get-tuple-element.271), channel_id=1, source_target_pairs={{0,16},{16,0},{1,17},{17,1},{2,18},{18,2},{3,19},{19,3},{4,20},{20... | collective-permute-start | bytes 8650760 | tf_op jit(solution)/shard_map/ppermute | solution.py:805
  183.3 65.8 %collective-permute-start.25 = (f32[8,32,2816]{2,1,0:T(8,128)}, f32[8,32,2816]{2,1,0:T(8,128)}, u32[]{:S(2)}, u32[]{:S(2)}) collective-permute-start(f32[8,32,2816]{2,1,0:T(8,128)} %get-tuple-element.274), channel_id=1, source_target_pairs={{0,2},{1,3},{2,0},{3,1},{4,6},{5,7},{6,4},{7,5},{8,10},{9,11},{10,... | collective-permute-start | bytes 8650760 | tf_op jit(solution)/shard_map/ppermute | solution.py:805
  188.6 64.8 %collective-permute-start.26 = (f32[8,88,1024]{2,1,0:T(8,128)}, f32[8,88,1024]{2,1,0:T(8,128)}, u32[]{:S(2)}, u32[]{:S(2)}) collective-permute-start(f32[8,88,1024]{2,1,0:T(8,128)} %get-tuple-element.276), channel_id=1, source_target_pairs={{0,4},{1,5},{2,6},{3,7},{4,0},{5,1},{6,2},{7,3},{8,12},{9,13},{10,... | collective-permute-start | bytes 8650760 | tf_op jit(solution)/shard_map/ppermute | solution.py:805
  233.4 24.0 %collective-permute-start.23 = (f32[8,6,4,16,128]{4,3,2,1,0:T(8,128)}, f32[8,6,4,16,128]{4,3,2,1,0:T(8,128)S(1)}, u32[]{:S(2)}, u32[]{:S(2)}) collective-permute-start(f32[8,6,4,16,128]{4,3,2,1,0:T(8,128)} %get-tuple-element.286), channel_id=1, source_target_pairs={{0,1},{1,0},{2,3},{3,2},{4,5},{5,4},{6,7},{7,6},{8,9},{9,8},{10,11... | collective-permute-start | bytes 4718600 | tf_op jit(solution)/shard_map/ppermute | solution.py:805
  259.7 20.0 %collective-permute-start.27 = (f32[4,6,4,16,128]{4,3,2,1,0:T(8,128)S(1)}, f32[4,6,4,16,128]{4,3,2,1,0:T(8,128)}, u32[]{:S(2)}, u32[]{:S(2)}) collective-permute-start(f32[4,6,4,16,128]{4,3,2,1,0:T(8,128)S(1)} %get-tuple-element.295), channel_id=1, source_target_pairs={{0,2},{1,3},{2,0},{3,1},{4,6},{5,7},{6,4},{7,5},{8,10},{9,11},{10,... | collective-permute-start | bytes 2359304 | tf_op jit(solution)/shard_map/ppermute | solution.py:805
  260.2 34.1 %collective-permute-start.30 = (f32[4,32,2816]{2,1,0:T(8,128)}, f32[4,32,2816]{2,1,0:T(8,128)}, u32[]{:S(2)}, u32[]{:S(2)}) collective-permute-start(f32[4,32,2816]{2,1,0:T(8,128)} %get-tuple-element.301), channel_id=1, source_target_pairs={{0,16},{16,0},{1,17},{17,1},{2,18},{18,2},{3,19},{19,3},{4,20},{20... | collective-permute-start | bytes 4325384 | tf_op jit(solution)/shard_map/ppermute | solution.py:805
  281.9 33.4 %collective-permute-start.32 = (f32[4,32,2816]{2,1,0:T(8,128)}, f32[4,32,2816]{2,1,0:T(8,128)}, u32[]{:S(2)}, u32[]{:S(2)}) collective-permute-start(f32[4,32,2816]{2,1,0:T(8,128)} %get-tuple-element.309), channel_id=1, source_target_pairs={{0,2},{1,3},{2,0},{3,1},{4,6},{5,7},{6,4},{7,5},{8,10},{9,11},{10,... | collective-permute-start | bytes 4325384 | tf_op jit(solution)/shard_map/ppermute | solution.py:805
  296.3 23.6 %collective-permute-start.31 = (f32[2,6,4,16,128]{4,3,2,1,0:T(8,128)S(1)}, f32[2,6,4,16,128]{4,3,2,1,0:T(8,128)S(1)}, u32[]{:S(2)}, u32[]{:S(2)}) collective-permute-start(f32[2,6,4,16,128]{4,3,2,1,0:T(8,128)S(1)} %add_select_fusion.14), channel_id=1, source_target_pairs={{8,0},{9,1},{10,2},{11,3},{12,4},{13,5},{14,6},{15,7},{24,16},{25,... | collective-permute-start | bytes 1179656 | tf_op jit(solution)/shard_map/ppermute | solution.py:913
  297.6 47.2 %collective-permute-start.34 = (f32[8,64,1024]{2,1,0:T(8,128)}, f32[8,64,1024]{2,1,0:T(8,128)S(1)}, u32[]{:S(2)}, u32[]{:S(2)}) collective-permute-start(f32[8,64,1024]{2,1,0:T(8,128)} %get-tuple-element.316), channel_id=1, source_target_pairs={{0,16},{16,0},{1,17},{17,1},{2,18},{18,2},{3,19},{19,3},{4,20},{20... | collective-permute-start | bytes 6291464 | tf_op jit(solution)/shard_map/ppermute | solution.py:805
  331.1 17.0 %collective-permute-start.35 = (f32[4,6,4,16,128]{4,3,2,1,0:T(8,128)S(1)}, f32[4,6,4,16,128]{4,3,2,1,0:T(8,128)S(1)}, u32[]{:S(2)}, u32[]{:S(2)}) collective-permute-start(f32[4,6,4,16,128]{4,3,2,1,0:T(8,128)S(1)} %get-tuple-element.314), channel_id=1, source_target_pairs={{0,2},{1,3},{2,0},{3,1},{4,6},{5,7},{6,4},{7,5},{8,10},{9,11},{10,... | collective-permute-start | bytes 2359304 | tf_op jit(solution)/shard_map/ppermute | solution.py:805
  349.0 19.0 %collective-permute-start.37 = (f32[2,32,2816]{2,1,0:T(8,128)S(1)}, f32[2,32,2816]{2,1,0:T(8,128)S(1)}, u32[]{:S(2)}, u32[]{:S(2)}) collective-permute-start(f32[2,32,2816]{2,1,0:T(8,128)S(1)} %get-tuple-element.335), channel_id=1, source_target_pairs={{0,4},{1,5},{2,6},{3,7},{4,0},{5,1},{6,2},{7,3},{8,12},{9,13},{10,... | collective-permute-start | bytes 2162696 | tf_op jit(solution)/shard_map/ppermute | solution.py:805
  349.6 33.7 %collective-permute-start.39 = (f32[4,88,1024]{2,1,0:T(8,128)S(1)}, f32[4,88,1024]{2,1,0:T(8,128)S(1)}, u32[]{:S(2)}, u32[]{:S(2)}) collective-permute-start(f32[4,88,1024]{2,1,0:T(8,128)S(1)} %copy-done.56), channel_id=1, source_target_pairs={{0,16},{16,0},{1,17},{17,1},{2,18},{18,2},{3,19},{19,3},{4,20},{20... | collective-permute-start | bytes 4325384 | tf_op jit(solution)/shard_map/ppermute | solution.py:805
  349.9 33.1 %collective-permute-start.38 = (f32[2,32,2816]{2,1,0:T(8,128)S(1)}, f32[2,32,2816]{2,1,0:T(8,128)S(1)}, u32[]{:S(2)}, u32[]{:S(2)}) collective-permute-start(f32[2,32,2816]{2,1,0:T(8,128)S(1)} %get-tuple-element.337), channel_id=1, source_target_pairs={{0,4},{1,5},{2,6},{3,7},{4,0},{5,1},{6,2},{7,3},{8,12},{9,13},{10,... | collective-permute-start | bytes 2162696 | tf_op jit(solution)/shard_map/ppermute | solution.py:805
  351.3 32.3 %collective-permute-start.40 = (f32[4,64,1024]{2,1,0:T(8,128)S(1)}, f32[4,64,1024]{2,1,0:T(8,128)S(1)}, u32[]{:S(2)}, u32[]{:S(2)}) collective-permute-start(f32[4,64,1024]{2,1,0:T(8,128)S(1)} %get-tuple-element.341), channel_id=1, source_target_pairs={{0,2},{1,3},{2,0},{3,1},{4,6},{5,7},{6,4},{7,5},{8,10},{9,11},{10,... | collective-permute-start | bytes 3145736 | tf_op jit(solution)/shard_map/ppermute | solution.py:805
  391.5 25.3 %collective-permute-start.43 = (f32[8,64,512]{2,1,0:T(8,128)S(1)}, f32[8,64,512]{2,1,0:T(8,128)S(1)}, u32[]{:S(2)}, u32[]{:S(2)}) collective-permute-start(f32[8,64,512]{2,1,0:T(8,128)S(1)} %get-tuple-element.346), channel_id=1, source_target_pairs={{0,16},{16,0},{1,17},{17,1},{2,18},{18,2},{3,19},{19,3},{4,20},{20... | collective-permute-start | bytes 3145736 | tf_op jit(solution)/shard_map/ppermute | solution.py:805
  391.9 25.1 %collective-permute-start.44 = (f32[8,32,1024]{2,1,0:T(8,128)S(1)}, f32[8,32,1024]{2,1,0:T(8,128)S(1)}, u32[]{:S(2)}, u32[]{:S(2)}) collective-permute-start(f32[8,32,1024]{2,1,0:T(8,128)S(1)} %get-tuple-element.359), channel_id=1, source_target_pairs={{0,2},{1,3},{2,0},{3,1},{4,6},{5,7},{6,4},{7,5},{8,10},{9,11},{10,... | collective-permute-start | bytes 3145736 | tf_op jit(solution)/shard_map/ppermute | solution.py:805
  393.6 29.1 %collective-permute-start.45 = (f32[1,32,2816]{2,1,0:T(8,128)S(1)}, f32[1,32,2816]{2,1,0:T(8,128)S(1)}, u32[]{:S(2)}, u32[]{:S(2)}) collective-permute-start(f32[1,32,2816]{2,1,0:T(8,128)S(1)} %get-tuple-element.362), channel_id=1, source_target_pairs={{0,8},{1,9},{2,10},{3,11},{4,12},{5,13},{6,14},{7,15},{8,0},{9,1},... | collective-permute-start | bytes 1081352 | tf_op jit(solution)/shard_map/ppermute | solution.py:805
  399.1 31.2 %collective-permute-start.46 = (f32[1,32,2816]{2,1,0:T(8,128)S(1)}, f32[1,32,2816]{2,1,0:T(8,128)S(1)}, u32[]{:S(2)}, u32[]{:S(2)}) collective-permute-start(f32[1,32,2816]{2,1,0:T(8,128)S(1)} %get-tuple-element.364), channel_id=1, source_target_pairs={{0,8},{1,9},{2,10},{3,11},{4,12},{5,13},{6,14},{7,15},{8,0},{9,1},... | collective-permute-start | bytes 1081352 | tf_op jit(solution)/shard_map/ppermute | solution.py:805
  399.2 31.9 %collective-permute-start.47 = (f32[2,64,1024]{2,1,0:T(8,128)S(1)}, f32[2,64,1024]{2,1,0:T(8,128)S(1)}, u32[]{:S(2)}, u32[]{:S(2)}) collective-permute-start(f32[2,64,1024]{2,1,0:T(8,128)S(1)} %get-tuple-element.367), channel_id=1, source_target_pairs={{0,4},{1,5},{2,6},{3,7},{4,0},{5,1},{6,2},{7,3},{8,12},{9,13},{10,... | collective-permute-start | bytes 1572872 | tf_op jit(solution)/shard_map/ppermute | solution.py:805
  431.9 14.9 %collective-permute-start.51 = (f32[2,64,512]{2,1,0:T(8,128)S(1)}, f32[2,64,512]{2,1,0:T(8,128)S(1)}, u32[]{:S(2)}, u32[]{:S(2)}) collective-permute-start(f32[2,64,512]{2,1,0:T(8,128)S(1)} %get-tuple-element.372), channel_id=1, source_target_pairs={{0,4},{1,5},{2,6},{3,7},{4,0},{5,1},{6,2},{7,3},{8,12},{9,13},{10,... | collective-permute-start | bytes 786440 | tf_op jit(solution)/shard_map/ppermute | solution.py:805
  433.4 23.8 %collective-permute-start.55 = (f32[1,64,1024]{2,1,0:T(8,128)S(1)}, f32[1,64,1024]{2,1,0:T(8,128)S(1)}, u32[]{:S(2)}, u32[]{:S(2)}) collective-permute-start(f32[1,64,1024]{2,1,0:T(8,128)S(1)} %get-tuple-element.368), channel_id=1, source_target_pairs={{0,8},{1,9},{2,10},{3,11},{4,12},{5,13},{6,14},{7,15},{8,0},{9,1},... | collective-permute-start | bytes 786440 | tf_op jit(solution)/shard_map/ppermute | solution.py:805
  437.8 15.6 %collective-permute-start.53 = (f32[2,88,1024]{2,1,0:T(8,128)S(1)}, f32[2,88,1024]{2,1,0:T(8,128)S(1)}, u32[]{:S(2)}, u32[]{:S(2)}) collective-permute-start(f32[2,88,1024]{2,1,0:T(8,128)S(1)} %get-tuple-element.380), channel_id=1, source_target_pairs={{0,2},{1,3},{2,0},{3,1},{4,6},{5,7},{6,4},{7,5},{8,10},{9,11},{10,... | collective-permute-start | bytes 2162696 | tf_op jit(solution)/shard_map/ppermute | solution.py:805
  454.3 17.9 %collective-permute-start.57 = (f32[1,64,512]{2,1,0:T(8,128)S(1)}, f32[1,64,512]{2,1,0:T(8,128)S(1)}, u32[]{:S(2)}, u32[]{:S(2)}) collective-permute-start(f32[1,64,512]{2,1,0:T(8,128)S(1)} %get-tuple-element.378), channel_id=1, source_target_pairs={{0,8},{1,9},{2,10},{3,11},{4,12},{5,13},{6,14},{7,15},{8,0},{9,1},... | collective-permute-start | bytes 393224 | tf_op jit(solution)/shard_map/ppermute | solution.py:805
  455.9 19.1 %collective-permute-start.58 = (f32[1,32,1024]{2,1,0:T(8,128)S(1)}, f32[1,32,1024]{2,1,0:T(8,128)S(1)}, u32[]{:S(2)}, u32[]{:S(2)}) collective-permute-start(f32[1,32,1024]{2,1,0:T(8,128)S(1)} %get-tuple-element.389), channel_id=1, source_target_pairs={{0,8},{1,9},{2,10},{3,11},{4,12},{5,13},{6,14},{7,15},{8,0},{9,1},... | collective-permute-start | bytes 393224 | tf_op jit(solution)/shard_map/ppermute | solution.py:805
  458.4 17.2 %collective-permute-start.59 = (f32[2,56,128]{2,1,0:T(8,128)S(1)}, f32[2,56,128]{2,1,0:T(8,128)S(1)}, u32[]{:S(2)}, u32[]{:S(2)}) collective-permute-start(f32[2,56,128]{2,1,0:T(8,128)S(1)} %get-tuple-element.386), channel_id=1, source_target_pairs={{0,4},{1,5},{2,6},{3,7},{4,0},{5,1},{6,2},{7,3},{8,12},{9,13},{10,... | collective-permute-start | bytes 172040 | tf_op jit(solution)/shard_map/ppermute | solution.py:805
  461.3 21.2 %collective-permute-start.60 = (f32[1,88,1024]{2,1,0:T(8,128)S(1)}, f32[1,88,1024]{2,1,0:T(8,128)S(1)}, u32[]{:S(2)}, u32[]{:S(2)}) collective-permute-start(f32[1,88,1024]{2,1,0:T(8,128)S(1)} %get-tuple-element.381), channel_id=1, source_target_pairs={{0,8},{1,9},{2,10},{3,11},{4,12},{5,13},{6,14},{7,15},{8,0},{9,1},... | collective-permute-start | bytes 1081352 | tf_op jit(solution)/shard_map/ppermute | solution.py:805
  (118 other events, 1233.0 us)
